TPU v7x, 32 devices: a whole 2x2x4 slice. The times are simulated.
32 devices in a mesh: groups: 2 (over y), ka: 4 (over x, core), pw: 4 (over z).
Axes of the slice: x: 2, y: 2, z: 4, core: 2. Of those that a mesh axis runs over, the one named last changes fastest.
Arguments:
- coefficients: bfloat16 [8, 2, 256, 40960], P(('groups', 'ka'), None, None, 'pw'), parts along dimension 0, may hold values from -0.375 to 0.375
- shifts: int32 [8, 2, 40960], P(('groups', 'ka'), None, 'pw'), parts along dimension 0, may hold values from 0 to 40959, as said below
Outputs:
- correlations: float32 [8, 2, 2, 256, 256], P(('groups', 'ka')), parts along dimension 0
There are 2 independent parts, one for each index of `groups`. A program takes and returns all parts, laid end to end along the dimension named above; each array names one. Nothing has to cross between parts.
Inputs may be any that keep to these rules, and one draw needn't show every extreme that they name: For every k, shifts[k, 0] maps each aligned block of 256 plane waves onto itself, one to one; shifts[k, 1] is the inverse permutation of shifts[(k - 1) mod 4, 0].
All inputs are finite; a program needn't handle non-finite values.
Results may differ from a plain program's by a relative error of at most 0.0003.
Values may be sent and summed in bfloat16 or wider, within the bound.
No kernel may reach another device: no remote copies, remote signals or barrier semaphores. Data moves between devices by JAX's collectives and lax.ppermute only.
A program may use at most 128 MiB of HBM per device.

v0:
```python
import jax
import jax.numpy as jnp
from jax import lax
from jax.sharding import PartitionSpec as P

PWB = 256


def passed_along(block, axis, distance):
    devices = range(lax.axis_size(axis))
    route = [((i - distance) % len(devices), i) for i in devices]
    return lax.ppermute(block, axis, route)


def correlation_of(own_bands, partner):
    bands = own_bands.shape[1]
    product = lax.dot_general(
        own_bands.reshape(2 * bands, -1),
        partner.reshape(2 * bands, -1),
        (((1,), (1,)), ((), ())),
        preferred_element_type=jnp.float32,
    )
    real_part = product[:bands, :bands] + product[bands:, bands:]
    imag_part = product[:bands, bands:] - product[bands:, :bands]
    return jnp.stack([real_part, imag_part])


def permuted(bands_block, table):
    width = bands_block.shape[2]
    block_count = width // PWB
    block_start = (jnp.arange(block_count, dtype=jnp.int32) * PWB)[:, None]
    inside = table.reshape(block_count, PWB) - block_start
    selector = (inside[:, :, None] == jnp.arange(PWB, dtype=jnp.int32)[None, None, :]).astype(
        jnp.bfloat16
    )
    rows = bands_block.reshape(-1, block_count, PWB)
    moved = jnp.einsum("rbi,boi->rbo", rows, selector, preferred_element_type=jnp.float32)
    return moved.astype(jnp.bfloat16).reshape(bands_block.shape)


def local(coefficients, shifts):
    local_count = coefficients.shape[0]
    pw_width = coefficients.shape[3]
    local_shift = shifts - lax.axis_index("pw") * pw_width
    following = passed_along(coefficients[0], "ka", -1)
    position = 0
    forward = [
        correlation_of(coefficients[position], permuted(following, local_shift[position, 0]))
    ]
    preceding = passed_along(coefficients[local_count - 1], "ka", 1)
    position = 0
    backward = correlation_of(coefficients[position], permuted(preceding, local_shift[position, 1]))
    pairs = [jnp.stack([forward[position], backward])]
    return lax.psum(jnp.stack(pairs), "pw")


def solution(mesh):
    return jax.shard_map(
        local,
        mesh=mesh,
        in_specs=(P(("groups", "ka"), None, None, "pw"), P(("groups", "ka"), None, "pw")),
        out_specs=P(("groups", "ka"), None, None, None, None),
        check_vma=False,
    )
```

profile of v0, /device:TPU:0, one launch (start us, length us, event | category | flops | bytes accessed | tf_op | source)
XLA Modules:
  0.0 392.8 jit_solution(17026476969545740125)
XLA Ops:
  6.5 0.0 all-reduce.2.cloned.1.call-start
  6.5 0.5 collective-permute-start.1
  7.0 1.9 collective-permute-start
  8.9 0.9 broadcast_subtract_fusion
  9.8 0.2 slice_reduce_fusion.1
  10.1 0.1 broadcast_subtract_fusion.2
  10.2 222.3 %collective-permute-done.1 = bf16[2,256,10240]{2,1,0:T(8,128)(2,1)} collective-permute-done((bf16[2,256,10240]{2,1,0:T(8,128)(2,1)}, bf16[2,256,10240]{2,1,0:T(8,128)(2,1)}, u32[]{:S(2)}, u32[]{:S(2)}) %collective-permute-start.1) | collective-permute-done | bytes 10485792 | tf_op jit(solution)/shard_map/ppermute | solution.py:12
  232.5 11.6 %copy.8 = bf16[64,8,40,256]{3,2,1,0:T(8,128)(2,1)} copy(bf16[64,8,40,256]{3,1,2,0:T(8,128)(2,1)} %bitcast.21) | data formatting | bytes 20971520
  244.1 23.7 %fusion.7 = bf16[40,256,512]{2,1,0:T(8,128)(2,1)} fusion(bf16[512,40,256]{2,1,0:T(8,128)(2,1)} %bitcast.37, s32[40,256]{1,0:T(8,128)S(1)} %get-tuple-element.12), kind=kOutput, calls=%fused_computation.7 | convolution fusion | flops 2692218880 | bytes 21012480 | tf_op jit(solution)/shard_map/rbi,boi->rbo/dot_general | solution.py:37
  267.8 11.7 %convolution_bitcast_fusion = f32[512,512]{0,1:T(8,128)S(1)} fusion(bf16[512,10240]{0,1:T(8,128)(2,1)} %bitcast.42, bf16[512,10240]{1,0:T(8,128)(2,1)} %bitcast.40), kind=kOutput, calls=%fused_computation.10 | convolution fusion | flops 5368709120 | bytes 22020096 | tf_op jit(solution)/shard_map/dot_general | solution.py:17
  279.5 0.1 fusion.13
  279.6 0.0 collective-permute-done
  279.6 11.4 %copy.7 = bf16[64,8,40,256]{3,2,1,0:T(8,128)(2,1)} copy(bf16[64,8,40,256]{3,1,2,0:T(8,128)(2,1)} %bitcast.18) | data formatting | bytes 20971520
  291.0 23.8 %fusion.4 = bf16[40,256,512]{2,1,0:T(8,128)(2,1)} fusion(bf16[512,40,256]{2,1,0:T(8,128)(2,1)} %bitcast.36, s32[40,256]{1,0:T(8,128)S(1)} %get-tuple-element.11), kind=kOutput, calls=%fused_computation.6 | convolution fusion | flops 2692218880 | bytes 21012480 | tf_op jit(solution)/shard_map/rbi,boi->rbo/dot_general | solution.py:37
  314.8 11.5 %convolution_bitcast_fusion.1 = f32[512,512]{0,1:T(8,128)S(1)} fusion(bf16[512,10240]{0,1:T(8,128)(2,1)} %bitcast.43, bf16[512,10240]{1,0:T(8,128)(2,1)} %bitcast.41), kind=kOutput, calls=%fused_computation.11 | convolution fusion | flops 5368709120 | bytes 22020096 | tf_op jit(solution)/shard_map/dot_general | solution.py:17
  326.3 0.1 fusion.15
  326.4 0.1 maximum_bitcast_fusion.1
  326.5 1.0 maximum_bitcast_fusion
  327.5 0.0 all-reduce.2.cloned.1.call-update
  327.6 55.9 %all-reduce.2.cloned.1.call-done = f32[1,2,2,256,256]{3,4,2,1,0:T(8,128)} async-done(((f32[1,2,2,256,256]{3,4,2,1,0:T(8,128)}), f32[1,2,2,256,256]{3,4,2,1,0:T(8,128)}) %all-reduce.2.cloned.1.call-update) | async-done | bytes 1048592 | tf_op jit(solution)/shard_map/psum | solution.py:54
  383.5 2.5 copy.6
  (3 shorter events, 0.0 us)
Async XLA Ops:
  6.5 376.9 %all-reduce.2.cloned.1.call-start = ((), (), s32[]{:S(2)}) async-start(), calls=%async_computation | async-start | bytes 2097152 | tf_op jit(solution)/shard_map/psum | solution.py:54
  6.5 226.0 %collective-permute-start.1 = (bf16[2,256,10240]{2,1,0:T(8,128)(2,1)}, bf16[2,256,10240]{2,1,0:T(8,128)(2,1)}, u32[]{:S(2)}, u32[]{:S(2)}) collective-permute-start(bf16[2,256,10240]{2,1,0:T(8,128)(2,1)} %bitcast.38), channel_id=1, source_target_pairs={{12,0},{0,4},{4,8},{8,12},{13,1},{1,5},{5,9},{9,13},{14,2},{2,6},{... | collective-permute-start | bytes 31457288 | tf_op jit(solution)/shard_map/ppermute | solution.py:12
  7.0 272.6 %collective-permute-start = (bf16[2,256,10240]{2,1,0:T(8,128)(2,1)}, bf16[2,256,10240]{2,1,0:T(8,128)(2,1)}, u32[]{:S(2)}, u32[]{:S(2)}) collective-permute-start(bf16[2,256,10240]{2,1,0:T(8,128)(2,1)} %bitcast.39), channel_id=1, source_target_pairs={{4,0},{8,4},{12,8},{0,12},{5,1},{9,5},{13,9},{1,13},{6,2},{10,6},{... | collective-permute-start | bytes 31457288 | tf_op jit(solution)/shard_map/ppermute | solution.py:12
Sparse Core Ops, SparseCore 0:
  327.7 55.7 all-reduce.1
where the time goes:
time: 393 us
  waiting for transfers between devices  278 us (71%)
  matrix products  70.7 us (18%)
  local copies, waits for them, and re-layouts  25.8 us (7%)
  between operations  13.5 us (3%)
    ppermute x2, waiting for transfers between devices, passed_along(): return lax.ppermute(block, axis, route)  222 us
    psum x1, waiting for transfers between devices, local(): return lax.psum(jnp.stack(pairs), 'pw')  55.9 us
    dot_general x2, matrix products, permuted(): jnp.einsum('rbi,boi->rbo', rows, selector, preferred_element_type=jnp.flo...  47.5 us
    dot_general x2, matrix products, correlation_of(): lax.dot_general(own_bands.reshape(2 * bands, -1), partner.reshape(2 * ban...  23.2 us
    unnamed x2, local copies, waits for them, and re-layouts  23 us
  transfers between devices with their start and end apart: 3, of which 2 were waited for; matrix products, arithmetic and copies ran while one was open for 12% of the time, Pallas kernels for 0%

commit v1 on v0

v1 whole, which is shorter than its diff:
```python
import jax
import jax.numpy as jnp
from jax import lax
from jax.sharding import PartitionSpec as P

PWB = 256
SIXTEENTHS = (2, 4, 4, 3, 2, 1)
IN_FLIGHT = 2


def moved(block, axis, distance):
    count = lax.axis_size(axis)
    return lax.ppermute(block, axis, [(i, (i + distance) % count) for i in range(count)])


def moved_both(block, ka_distance, pw_distance):
    ka, pw = lax.axis_size("ka"), lax.axis_size("pw")
    route = [
        (k * pw + p, (k + ka_distance) % ka * pw + (p + pw_distance) % pw)
        for k in range(ka)
        for p in range(pw)
    ]
    return lax.ppermute(block, ("ka", "pw"), route)


def unpermuted(bands_block, table):
    width = bands_block.shape[2]
    block_count = width // PWB
    block_start = (jnp.arange(block_count, dtype=jnp.int32) * PWB)[:, None]
    inside = table.reshape(block_count, PWB) - block_start
    selector = (inside[:, :, None] == jnp.arange(PWB, dtype=jnp.int32)[None, None, :]).astype(
        jnp.bfloat16
    )
    rows = bands_block.reshape(-1, block_count, PWB)
    placed = jnp.einsum("rbo,boi->rbi", rows, selector, preferred_element_type=jnp.float32)
    return placed.astype(jnp.bfloat16).reshape(bands_block.shape)


def correlation_of(own, partner):
    bands = own.shape[1]
    some = partner.shape[1]
    product = lax.dot_general(
        own.reshape(2 * bands, -1),
        partner.reshape(2 * some, -1),
        (((1,), (1,)), ((), ())),
        preferred_element_type=jnp.float32,
    )
    real_part = product[:bands, :some] + product[bands:, some:]
    imag_part = product[:bands, some:] - product[bands:, :some]
    return jnp.stack([real_part, imag_part])


def mirrored(matrix):
    turned = jnp.swapaxes(matrix, -1, -2)
    return jnp.stack([turned[..., 0, :, :], -turned[..., 1, :, :]], axis=-3)


def summed_in_shares(partial):
    pw = lax.axis_size("pw")
    me = lax.axis_index("pw")
    bands, some = partial.shape[1:]
    rows = bands // pw
    share = lax.dynamic_slice_in_dim(partial, me * rows, rows, 1)
    for d in range(1, pw):
        piece = lax.dynamic_slice_in_dim(partial, lax.rem(me + d, pw) * rows, rows, 1)
        share = share + moved(piece, "pw", d)
    pair = jnp.stack([share, moved(share, "ka", 1)])
    whole = jnp.zeros((2, 2, bands, some), jnp.float32)
    whole = lax.dynamic_update_slice_in_dim(whole, pair, me * rows, 2)
    for d in range(1, pw):
        got = moved(pair, "pw", d)
        whole = lax.dynamic_update_slice_in_dim(whole, got, lax.rem(me + pw - d, pw) * rows, 2)
    return whole[0], whole[1]


def summed_at_once(partial):
    pw = lax.axis_size("pw")
    here = partial
    for d in range(1, pw):
        here = here + moved(partial, "pw", d)
    before = moved_both(partial, 1, 0)
    for d in range(1, pw):
        before = before + moved_both(partial, 1, d)
    return here, before


def local(coefficients, shifts):
    own = coefficients[0]
    bands, pw_width = own.shape[1:]
    table = shifts[0, 0] - lax.axis_index("pw") * pw_width
    unit = bands // sum(SIXTEENTHS)
    arrived = []
    start = 0
    for index, size in enumerate(SIXTEENTHS):
        block = own[:, start : start + size * unit]
        if index >= IN_FLIGHT:
            block, arrived[index - IN_FLIGHT] = lax.optimization_barrier(
                (block, arrived[index - IN_FLIGHT])
            )
        arrived.append(moved(block, "ka", -1))
        start += size * unit
    placed = unpermuted(own, table)
    partials = [correlation_of(placed, block) for block in arrived]
    most_ahead, most_behind = summed_in_shares(jnp.concatenate(partials[:-1], axis=2))
    last_ahead, last_behind = summed_at_once(partials[-1])
    ahead = jnp.concatenate([most_ahead, last_ahead], axis=2)
    behind = jnp.concatenate([mirrored(most_behind), mirrored(last_behind)], axis=1)
    return jnp.stack([ahead, behind])[None]


def solution(mesh):
    return jax.shard_map(
        local,
        mesh=mesh,
        in_specs=(P(("groups", "ka"), None, None, "pw"), P(("groups", "ka"), None, "pw")),
        out_specs=P(("groups", "ka"), None, None, None, None),
        check_vma=False,
    )
```

time: 393 us -> 206 us (0.52)
  the two profiles are of different devices: /device:TPU:0 before, /device:TPU:28 now
where the time goes in v1:
time: 206 us
  waiting for transfers between devices  120 us (58%)
  matrix products  31.7 us (15%)
  local copies, waits for them, and re-layouts  31.5 us (15%)
  starting transfers between devices  20.8 us (10%)
    ppermute x16, waiting for transfers between devices, moved(): lax.ppermute(block, axis, [(i, (i + distance) % count) for i in range(cou...  117 us
    ppermute x16, starting transfers between devices, moved(): lax.ppermute(block, axis, [(i, (i + distance) % count) for i in range(cou...  19.2 us
    dot_general x6, matrix products, correlation_of(): lax.dot_general(own.reshape(2 * bands, -1), partner.reshape(2 * some, -1)...  18.3 us
    slice x4, local copies, waits for them, and re-layouts, local(): block = own[:, start:start + size * unit]  13.6 us
    dot_general x1, matrix products, unpermuted(): jnp.einsum('rbo,boi->rbi', rows, selector, preferred_element_type=jnp.flo...  13.4 us
    unnamed x15, local copies, waits for them, and re-layouts  11.5 us
  transfers between devices with their start and end apart: 20, of which 11 were waited for; matrix products, arithmetic and copies ran while one was open for 28% of the time, Pallas kernels for 0%

profile of v1, /device:TPU:28, one launch (start us, length us, event | category | flops | bytes accessed | tf_op | source)
XLA Modules:
  0.0 205.8 jit_solution(17694662314482507573)
XLA Ops:
  0.0 3.0 %fusion.18 = (bf16[2,32,10240]{2,1,0:T(8,128)(2,1)}, bf16[2,32,10240]{2,1,0:T(8,128)(2,1)S(1)}) fusion(bf16[2,256,10240]{2,1,0:T(8,128)(2,1)} %bitcast.74), kind=kLoop, calls=%fused_computation.52 | loop fusion | bytes 5242880 | tf_op jit(solution)/shard_map/slice | solution.py:95
  4.0 5.5 %fusion.19 = (bf16[2,64,10240]{2,1,0:T(8,128)(2,1)}, bf16[2,64,10240]{2,1,0:T(8,128)(2,1)}) fusion(bf16[2,256,10240]{2,1,0:T(8,128)(2,1)} %bitcast.75), kind=kLoop, calls=%fused_computation.53 | loop fusion | bytes 10485760 | tf_op jit(solution)/shard_map/slice | solution.py:95
  10.3 11.5 %copy.5 = bf16[64,8,40,256]{3,2,1,0:T(8,128)(2,1)} copy(bf16[64,8,40,256]{3,1,2,0:T(8,128)(2,1)} %bitcast.76) | data formatting | bytes 20971520
  21.8 13.4 %fusion.2 = bf16[40,256,512]{2,1,0:T(8,128)(2,1)} fusion(bf16[512,40,256]{2,1,0:T(8,128)(2,1)} %bitcast.79, s32[40,256]{1,0:T(8,128)S(1)} %broadcast_subtract_fusion), kind=kOutput, calls=%fused_computation.3 | convolution fusion | flops 2692218880 | bytes 21012480 | tf_op jit(solution)/shard_map/rbo,boi->rbi/dot_general | solution.py:35
  35.2 3.0 %slice.154 = bf16[2,48,10240]{2,1,0:T(8,128)(2,1)} slice(bf16[2,256,10240]{2,1,0:T(8,128)(2,1)} %bitcast.77), slice={[0:2], [160:208], [0:10240]} | slice | bytes 3932160 | tf_op jit(solution)/shard_map/slice | solution.py:95
  38.2 2.1 %slice.165 = bf16[2,16,10240]{2,1,0:T(8,128)(2,1)} slice(bf16[2,256,10240]{2,1,0:T(8,128)(2,1)} %bitcast.78), slice={[0:2], [240:256], [0:10240]} | slice | bytes 1310720 | tf_op jit(solution)/shard_map/slice | solution.py:95
  40.3 6.0 %fusion.22 = f32[512,64]{0,1:T(8,128)S(1)} fusion(bf16[64,10240]{1,0:T(8,128)(2,1)S(1)} %bitcast.81, bf16[512,10240]{0,1:T(8,128)(2,1)} %bitcast.66), kind=kOutput, calls=%fused_computation.56 | convolution fusion | flops 671088640 | bytes 11927552 | tf_op jit(solution)/shard_map/dot_general | solution.py:42
  47.3 1.9 collective-permute-start.3
  49.2 3.4 %fusion.23 = f32[512,128]{0,1:T(8,128)S(1)} fusion(bf16[128,10240]{1,0:T(8,128)(2,1)} %bitcast.7, bf16[512,10240]{0,1:T(8,128)(2,1)S(1)} %bitcast.69), kind=kOutput, calls=%fused_computation.57 | convolution fusion | flops 1342177280 | bytes 13369344 | tf_op jit(solution)/shard_map/dot_general | solution.py:42
  52.6 22.7 %collective-permute-done.2 = bf16[2,64,10240]{2,1,0:T(8,128)(2,1)} collective-permute-done((bf16[2,64,10240]{2,1,0:T(8,128)(2,1)}, bf16[2,64,10240]{2,1,0:T(8,128)(2,1)}, u32[]{:S(2)}, u32[]{:S(2)}) %collective-permute-start.2) | collective-permute-done | bytes 2621472 | tf_op jit(solution)/shard_map/ppermute | solution.py:13
  75.4 1.9 collective-permute-start.4
  77.3 3.3 %fusion.24 = f32[512,128]{0,1:T(8,128)S(1)} fusion(bf16[128,10240]{1,0:T(8,128)(2,1)} %bitcast.10, bf16[512,10240]{0,1:T(8,128)(2,1)S(1)} %bitcast.70), kind=kOutput, calls=%fused_computation.58 | convolution fusion | flops 1342177280 | bytes 13369344 | tf_op jit(solution)/shard_map/dot_general | solution.py:42
  80.7 15.7 %collective-permute-done.3 = bf16[2,48,10240]{2,1,0:T(8,128)(2,1)S(1)} collective-permute-done((bf16[2,48,10240]{2,1,0:T(8,128)(2,1)S(1)}, bf16[2,48,10240]{2,1,0:T(8,128)(2,1)S(1)}, u32[]{:S(2)}, u32[]{:S(2)}) %collective-permute-start.3) | collective-permute-done | bytes 1966112 | tf_op jit(solution)/shard_map/ppermute | solution.py:13
  96.3 1.9 collective-permute-start.12
  98.2 1.8 fusion.25
  100.1 17.3 %collective-permute-done.12 = bf16[2,16,10240]{2,1,0:T(8,128)(2,1)S(1)} collective-permute-done((bf16[2,16,10240]{2,1,0:T(8,128)(2,1)S(1)}, bf16[2,16,10240]{2,1,0:T(8,128)(2,1)S(1)}, u32[]{:S(2)}, u32[]{:S(2)}) %collective-permute-start.12) | collective-permute-done | bytes 655392 | tf_op jit(solution)/shard_map/ppermute | solution.py:13
  117.4 1.9 fusion.27
  119.3 1.9 fusion.26
  121.8 1.7 collective-permute-start.6
  123.9 3.4 %collective-permute-start.13 = (f32[2,256,16]{1,2,0:T(8,128)S(1)}, f32[2,256,16]{1,2,0:T(8,128)S(1)}, u32[]{:S(2)}, u32[]{:S(2)}) collective-permute-start(f32[2,256,16]{1,2,0:T(8,128)S(1)} %pad_maximum_fusion.1), channel_id=1, source_target_pairs={{0,1},{1,2},{2,3},{3,0},{4,5},{5,6},{6,7},{7,4},{8,9},{9,10},{10,1... | collective-permute-start | bytes 98312 | tf_op jit(solution)/shard_map/ppermute | solution.py:13
  127.4 3.1 %collective-permute-done.5 = f32[2,64,240]{1,2,0:T(8,128)S(1)} collective-permute-done((f32[2,64,240]{1,2,0:T(8,128)S(1)}, f32[2,64,240]{1,2,0:T(8,128)S(1)}, u32[]{:S(2)}, u32[]{:S(2)}) %collective-permute-start.5) | collective-permute-done | bytes 122912 | tf_op jit(solution)/shard_map/ppermute | solution.py:13
  130.4 1.6 collective-permute-start.17
  132.1 14.7 %collective-permute-done.6 = f32[2,64,240]{1,2,0:T(8,128)S(1)} collective-permute-done((f32[2,64,240]{1,2,0:T(8,128)S(1)}, f32[2,64,240]{1,2,0:T(8,128)S(1)}, u32[]{:S(2)}, u32[]{:S(2)}) %collective-permute-start.6) | collective-permute-done | bytes 122912 | tf_op jit(solution)/shard_map/ppermute | solution.py:13
  146.9 2.4 %collective-permute-start.14 = (f32[2,256,16]{1,2,0:T(8,128)S(1)}, f32[2,256,16]{1,2,0:T(8,128)S(1)}, u32[]{:S(2)}, u32[]{:S(2)}) collective-permute-start(f32[2,256,16]{1,2,0:T(8,128)S(1)} %pad_maximum_fusion.1), channel_id=1, source_target_pairs={{0,2},{1,3},{2,0},{3,1},{4,6},{5,7},{6,4},{7,5},{8,10},{9,11},{10,... | collective-permute-start | bytes 98312 | tf_op jit(solution)/shard_map/ppermute | solution.py:13
  149.4 1.5 collective-permute-start.15
  150.9 1.4 collective-permute-done.18
  153.1 4.7 %collective-permute-done.8 = f32[2,64,240]{1,2,0:T(8,128)S(1)} collective-permute-done((f32[2,64,240]{1,2,0:T(8,128)S(1)}, f32[2,64,240]{1,2,0:T(8,128)S(1)}, u32[]{:S(2)}, u32[]{:S(2)}) %collective-permute-start.8) | collective-permute-done | bytes 122912 | tf_op jit(solution)/shard_map/ppermute | solution.py:13
  160.1 1.8 dynamic_update_slice.12
  161.9 8.8 %collective-permute-done.9 = f32[2,2,64,240]{2,3,1,0:T(8,128)S(1)} collective-permute-done((f32[2,2,64,240]{2,3,1,0:T(8,128)S(1)}, f32[2,2,64,240]{2,3,1,0:T(8,128)S(1)}, u32[]{:S(2)}, u32[]{:S(2)}) %collective-permute-start.9) | collective-permute-done | bytes 245792 | tf_op jit(solution)/shard_map/ppermute | solution.py:13
  171.4 29.5 %collective-permute-done.10 = f32[2,2,64,240]{2,3,1,0:T(8,128)S(1)} collective-permute-done((f32[2,2,64,240]{2,3,1,0:T(8,128)S(1)}, f32[2,2,64,240]{2,3,1,0:T(8,128)S(1)}, u32[]{:S(2)}, u32[]{:S(2)}) %collective-permute-start.10) | collective-permute-done | bytes 245792 | tf_op jit(solution)/shard_map/ppermute | solution.py:13
  200.9 2.1 %dynamic_update_slice.14 = f32[2,2,256,240]{2,3,1,0:T(8,128)S(1)} dynamic-update-slice(f32[2,2,256,240]{2,3,1,0:T(8,128)S(1)} %dynamic_update_slice.13, f32[2,2,64,240]{2,3,1,0:T(8,128)S(1)} %collective-permute-done.10, s32[]{:T(128)} %constant.35.clone.1, s32[]{:T(128)} %constant.35.clone.1, s32[]{:T(128)S(6)} %select_n.18, s32[]{:T(128)} %constant.35.clone.1) | dynamic-update-slice | bytes 491524 | tf_op jit(solution)/shard_map/dynamic_update_slice | solution.py:72
  203.1 1.2 dynamic_update_slice.15
  (68 shorter events, 9.2 us)
Async XLA Ops:
  0.0 10.1 %copy-start.3 = (s32[1,2,10240]{2,1,0:T(2,128)S(1)}, s32[1,2,10240]{2,1,0:T(2,128)}, u32[]{:S(2)}) copy-start(s32[1,2,10240]{2,1,0:T(2,128)} %param.3) | copy-start | bytes 245764
  3.0 18.8 %collective-permute-start = (bf16[2,32,10240]{2,1,0:T(8,128)(2,1)S(1)}, bf16[2,32,10240]{2,1,0:T(8,128)(2,1)S(1)}, u32[]{:S(2)}, u32[]{:S(2)}) collective-permute-start(bf16[2,32,10240]{2,1,0:T(8,128)(2,1)S(1)} %get-tuple-element.22), channel_id=1, source_target_pairs={{0,12},{4,0},{8,4},{12,8},{1,13},{5,1},{9,5},{13,9},{2,14},{6,2},{... | collective-permute-start | bytes 3932168 | tf_op jit(solution)/shard_map/ppermute | solution.py:13
  9.4 37.9 %collective-permute-start.1 = (bf16[2,64,10240]{2,1,0:T(8,128)(2,1)}, bf16[2,64,10240]{2,1,0:T(8,128)(2,1)}, u32[]{:S(2)}, u32[]{:S(2)}) collective-permute-start(bf16[2,64,10240]{2,1,0:T(8,128)(2,1)} %get-tuple-element.24), channel_id=1, source_target_pairs={{0,12},{4,0},{8,4},{12,8},{1,13},{5,1},{9,5},{13,9},{2,14},{6,2},{... | collective-permute-start | bytes 7864328 | tf_op jit(solution)/shard_map/ppermute | solution.py:13
  21.8 53.6 %collective-permute-start.2 = (bf16[2,64,10240]{2,1,0:T(8,128)(2,1)}, bf16[2,64,10240]{2,1,0:T(8,128)(2,1)}, u32[]{:S(2)}, u32[]{:S(2)}) collective-permute-start(bf16[2,64,10240]{2,1,0:T(8,128)(2,1)} %get-tuple-element.15), channel_id=1, source_target_pairs={{0,12},{4,0},{8,4},{12,8},{1,13},{5,1},{9,5},{13,9},{2,14},{6,2},{... | collective-permute-start | bytes 7864328 | tf_op jit(solution)/shard_map/ppermute | solution.py:13
  38.2 11.0 %slice-start = ((s8[10485760]{0:T(1024)(128)(4,1)}), s8[2097152]{0:T(1024)(128)(4,1)S(1)}, s32[]{:S(2)}) async-start(s8[10485760]{0:T(1024)(128)(4,1)} %bitcast.67), calls=%async_computation | async-start | bytes 4194304
  40.3 6.9 %copy-start = (bf16[2,48,10240]{2,1,0:T(8,128)(2,1)S(1)}, bf16[2,48,10240]{2,1,0:T(8,128)(2,1)}, u32[]{:S(2)}) copy-start(bf16[2,48,10240]{2,1,0:T(8,128)(2,1)} %slice.154) | copy-start | bytes 5898244
  40.3 8.9 %slice-start.1 = ((s8[10485760]{0:T(1024)(128)(4,1)}), s8[4194304]{0:T(1024)(128)(4,1)S(1)}, s32[]{:S(2)}) async-start(s8[10485760]{0:T(1024)(128)(4,1)} %bitcast.67), calls=%async_computation.1 | async-start | bytes 8388608
  40.3 8.9 %slice-start.2 = ((s8[10485760]{0:T(1024)(128)(4,1)}), s8[4194304]{0:T(1024)(128)(4,1)S(1)}, s32[]{:S(2)}) async-start(s8[10485760]{0:T(1024)(128)(4,1)} %bitcast.67), calls=%async_computation.2 | async-start | bytes 8388608
  47.3 49.0 %collective-permute-start.3 = (bf16[2,48,10240]{2,1,0:T(8,128)(2,1)S(1)}, bf16[2,48,10240]{2,1,0:T(8,128)(2,1)S(1)}, u32[]{:S(2)}, u32[]{:S(2)}) collective-permute-start(bf16[2,48,10240]{2,1,0:T(8,128)(2,1)S(1)} %copy-done), channel_id=1, source_target_pairs={{0,12},{4,0},{8,4},{12,8},{1,13},{5,1},{9,5},{13,9},{2,14},{6,2},{... | collective-permute-start | bytes 5898248 | tf_op jit(solution)/shard_map/ppermute | solution.py:13
  49.2 26.2 %copy-start.1 = (bf16[2,32,10240]{2,1,0:T(8,128)(2,1)S(1)}, bf16[2,32,10240]{2,1,0:T(8,128)(2,1)}, u32[]{:S(2)}) copy-start(bf16[2,32,10240]{2,1,0:T(8,128)(2,1)} %get-tuple-element.19) | copy-start | bytes 3932164
  75.4 43.9 %collective-permute-start.4 = (bf16[2,32,10240]{2,1,0:T(8,128)(2,1)S(1)}, bf16[2,32,10240]{2,1,0:T(8,128)(2,1)S(1)}, u32[]{:S(2)}, u32[]{:S(2)}) collective-permute-start(bf16[2,32,10240]{2,1,0:T(8,128)(2,1)S(1)} %copy-done.1), channel_id=1, source_target_pairs={{0,12},{4,0},{8,4},{12,8},{1,13},{5,1},{9,5},{13,9},{2,14},{6,2},{... | collective-permute-start | bytes 3932168 | tf_op jit(solution)/shard_map/ppermute | solution.py:13
  77.3 19.1 %copy-start.2 = (bf16[2,16,10240]{2,1,0:T(8,128)(2,1)S(1)}, bf16[2,16,10240]{2,1,0:T(8,128)(2,1)}, u32[]{:S(2)}) copy-start(bf16[2,16,10240]{2,1,0:T(8,128)(2,1)} %slice.165) | copy-start | bytes 1966084
  96.3 21.1 %collective-permute-start.12 = (bf16[2,16,10240]{2,1,0:T(8,128)(2,1)S(1)}, bf16[2,16,10240]{2,1,0:T(8,128)(2,1)S(1)}, u32[]{:S(2)}, u32[]{:S(2)}) collective-permute-start(bf16[2,16,10240]{2,1,0:T(8,128)(2,1)S(1)} %copy-done.2), channel_id=1, source_target_pairs={{0,12},{4,0},{8,4},{12,8},{1,13},{5,1},{9,5},{13,9},{2,14},{6,2},{... | collective-permute-start | bytes 1966088 | tf_op jit(solution)/shard_map/ppermute | solution.py:13
  121.5 8.9 %collective-permute-start.5 = (f32[2,64,240]{1,2,0:T(8,128)S(1)}, f32[2,64,240]{1,2,0:T(8,128)S(1)}, u32[]{:S(2)}, u32[]{:S(2)}) collective-permute-start(f32[2,64,240]{1,2,0:T(8,128)S(1)} %get-tuple-element.29), channel_id=1, source_target_pairs={{0,1},{1,2},{2,3},{3,0},{4,5},{5,6},{6,7},{7,4},{8,9},{9,10},{10,1... | collective-permute-start | bytes 368648 | tf_op jit(solution)/shard_map/ppermute | solution.py:13
  121.8 25.0 %collective-permute-start.6 = (f32[2,64,240]{1,2,0:T(8,128)S(1)}, f32[2,64,240]{1,2,0:T(8,128)S(1)}, u32[]{:S(2)}, u32[]{:S(2)}) collective-permute-start(f32[2,64,240]{1,2,0:T(8,128)S(1)} %get-tuple-element.31), channel_id=1, source_target_pairs={{0,2},{1,3},{2,0},{3,1},{4,6},{5,7},{6,4},{7,5},{8,10},{9,11},{10,... | collective-permute-start | bytes 368648 | tf_op jit(solution)/shard_map/ppermute | solution.py:13
  123.5 23.3 %collective-permute-start.7 = (f32[2,64,240]{1,2,0:T(8,128)S(1)}, f32[2,64,240]{1,2,0:T(8,128)S(1)}, u32[]{:S(2)}, u32[]{:S(2)}) collective-permute-start(f32[2,64,240]{1,2,0:T(8,128)S(1)} %get-tuple-element.30), channel_id=1, source_target_pairs={{0,3},{1,0},{2,1},{3,2},{4,7},{5,4},{6,5},{7,6},{8,11},{9,8},{10,9... | collective-permute-start | bytes 368648 | tf_op jit(solution)/shard_map/ppermute | solution.py:13
  123.9 35.0 %collective-permute-start.13 = (f32[2,256,16]{1,2,0:T(8,128)S(1)}, f32[2,256,16]{1,2,0:T(8,128)S(1)}, u32[]{:S(2)}, u32[]{:S(2)}) collective-permute-start(f32[2,256,16]{1,2,0:T(8,128)S(1)} %pad_maximum_fusion.1), channel_id=1, source_target_pairs={{0,1},{1,2},{2,3},{3,0},{4,5},{5,6},{6,7},{7,4},{8,9},{9,10},{10,1... | collective-permute-start | bytes 98312 | tf_op jit(solution)/shard_map/ppermute | solution.py:13
  127.4 19.6 %collective-permute-start.16 = (f32[2,256,16]{1,2,0:T(8,128)S(1)}, f32[2,256,16]{1,2,0:T(8,128)S(1)}, u32[]{:S(2)}, u32[]{:S(2)}) collective-permute-start(f32[2,256,16]{1,2,0:T(8,128)S(1)} %pad_maximum_fusion.1), channel_id=1, source_target_pairs={{0,4},{1,5},{2,6},{3,7},{4,8},{5,9},{6,10},{7,11},{8,12},{9,13},{1... | collective-permute-start | bytes 98312 | tf_op jit(solution)/shard_map/ppermute | solution.py:23
  130.4 18.9 %collective-permute-start.17 = (f32[2,256,16]{1,2,0:T(8,128)S(1)}, f32[2,256,16]{1,2,0:T(8,128)S(1)}, u32[]{:S(2)}, u32[]{:S(2)}) collective-permute-start(f32[2,256,16]{1,2,0:T(8,128)S(1)} %pad_maximum_fusion.1), channel_id=1, source_target_pairs={{0,5},{1,6},{2,7},{3,4},{4,9},{5,10},{6,11},{7,8},{8,13},{9,14},{1... | collective-permute-start | bytes 98312 | tf_op jit(solution)/shard_map/ppermute | solution.py:23
  146.8 5.5 %collective-permute-start.18 = (f32[2,256,16]{1,2,0:T(8,128)S(1)}, f32[2,256,16]{1,2,0:T(8,128)S(1)}, u32[]{:S(2)}, u32[]{:S(2)}) collective-permute-start(f32[2,256,16]{1,2,0:T(8,128)S(1)} %pad_maximum_fusion.1), channel_id=1, source_target_pairs={{0,6},{1,7},{2,4},{3,5},{4,10},{5,11},{6,8},{7,9},{8,14},{9,15},{1... | collective-permute-start | bytes 98312 | tf_op jit(solution)/shard_map/ppermute | solution.py:23
  146.8 6.3 %collective-permute-start.19 = (f32[2,256,16]{1,2,0:T(8,128)S(1)}, f32[2,256,16]{1,2,0:T(8,128)S(1)}, u32[]{:S(2)}, u32[]{:S(2)}) collective-permute-start(f32[2,256,16]{1,2,0:T(8,128)S(1)} %pad_maximum_fusion.1), channel_id=1, source_target_pairs={{0,7},{1,4},{2,5},{3,6},{4,11},{5,8},{6,9},{7,10},{8,15},{9,12},{1... | collective-permute-start | bytes 98312 | tf_op jit(solution)/shard_map/ppermute | solution.py:23
  146.9 13.1 %collective-permute-start.14 = (f32[2,256,16]{1,2,0:T(8,128)S(1)}, f32[2,256,16]{1,2,0:T(8,128)S(1)}, u32[]{:S(2)}, u32[]{:S(2)}) collective-permute-start(f32[2,256,16]{1,2,0:T(8,128)S(1)} %pad_maximum_fusion.1), channel_id=1, source_target_pairs={{0,2},{1,3},{2,0},{3,1},{4,6},{5,7},{6,4},{7,5},{8,10},{9,11},{10,... | collective-permute-start | bytes 98312 | tf_op jit(solution)/shard_map/ppermute | solution.py:13
  149.4 10.6 %collective-permute-start.15 = (f32[2,256,16]{1,2,0:T(8,128)S(1)}, f32[2,256,16]{1,2,0:T(8,128)S(1)}, u32[]{:S(2)}, u32[]{:S(2)}) collective-permute-start(f32[2,256,16]{1,2,0:T(8,128)S(1)} %pad_maximum_fusion.1), channel_id=1, source_target_pairs={{0,3},{1,0},{2,1},{3,2},{4,7},{5,4},{6,5},{7,6},{8,11},{9,8},{10,9... | collective-permute-start | bytes 98312 | tf_op jit(solution)/shard_map/ppermute | solution.py:13
  152.3 5.6 %collective-permute-start.8 = (f32[2,64,240]{1,2,0:T(8,128)S(1)}, f32[2,64,240]{1,2,0:T(8,128)S(1)}, u32[]{:S(2)}, u32[]{:S(2)}) collective-permute-start(f32[2,64,240]{1,2,0:T(8,128)S(1)} %add_add_fusion), channel_id=1, source_target_pairs={{0,4},{4,8},{8,12},{12,0},{1,5},{5,9},{9,13},{13,1},{2,6},{6,10},{... | collective-permute-start | bytes 368648 | tf_op jit(solution)/shard_map/ppermute | solution.py:13
  157.9 12.7 %collective-permute-start.9 = (f32[2,2,64,240]{2,3,1,0:T(8,128)S(1)}, f32[2,2,64,240]{2,3,1,0:T(8,128)S(1)}, u32[]{:S(2)}, u32[]{:S(2)}) collective-permute-start(f32[2,2,64,240]{2,3,1,0:T(8,128)S(1)} %pad_maximum_fusion), channel_id=1, source_target_pairs={{0,1},{1,2},{2,3},{3,0},{4,5},{5,6},{6,7},{7,4},{8,9},{9,10},{10,1... | collective-permute-start | bytes 737288 | tf_op jit(solution)/shard_map/ppermute | solution.py:13
  158.9 42.0 %collective-permute-start.10 = (f32[2,2,64,240]{2,3,1,0:T(8,128)S(1)}, f32[2,2,64,240]{2,3,1,0:T(8,128)S(1)}, u32[]{:S(2)}, u32[]{:S(2)}) collective-permute-start(f32[2,2,64,240]{2,3,1,0:T(8,128)S(1)} %pad_maximum_fusion), channel_id=1, source_target_pairs={{0,2},{1,3},{2,0},{3,1},{4,6},{5,7},{6,4},{7,5},{8,10},{9,11},{10,... | collective-permute-start | bytes 737288 | tf_op jit(solution)/shard_map/ppermute | solution.py:13
  158.9 44.1 %collective-permute-start.11 = (f32[2,2,64,240]{2,3,1,0:T(8,128)S(1)}, f32[2,2,64,240]{2,3,1,0:T(8,128)S(1)}, u32[]{:S(2)}, u32[]{:S(2)}) collective-permute-start(f32[2,2,64,240]{2,3,1,0:T(8,128)S(1)} %pad_maximum_fusion), channel_id=1, source_target_pairs={{0,3},{1,0},{2,1},{3,2},{4,7},{5,4},{6,5},{7,6},{8,11},{9,8},{10,9... | collective-permute-start | bytes 737288 | tf_op jit(solution)/shard_map/ppermute | solution.py:13

commit v2 on v1

v2 whole, which is shorter than its diff:
```python
import jax
import jax.numpy as jnp
from jax import lax
from jax.sharding import PartitionSpec as P

PWB = 256
SIXTEENTHS = (1, 3, 4, 4, 2, 1, 1)


def moved(block, axis, distance):
    count = lax.axis_size(axis)
    return lax.ppermute(block, axis, [(i, (i + distance) % count) for i in range(count)])


def after(value, *others):
    return lax.optimization_barrier((value, *others))[0]


def unpermuted(bands_block, table):
    width = bands_block.shape[2]
    block_count = width // PWB
    block_start = (jnp.arange(block_count, dtype=jnp.int32) * PWB)[:, None]
    inside = table.reshape(block_count, PWB) - block_start
    selector = (inside[:, :, None] == jnp.arange(PWB, dtype=jnp.int32)[None, None, :]).astype(
        jnp.bfloat16
    )
    rows = bands_block.reshape(-1, block_count, PWB)
    placed = jnp.einsum("rbo,boi->rbi", rows, selector, preferred_element_type=jnp.float32)
    return placed.astype(jnp.bfloat16).reshape(bands_block.shape)


def correlation_of(own, partner):
    bands = own.shape[1]
    some = partner.shape[1]
    product = lax.dot_general(
        own.reshape(2 * bands, -1),
        partner.reshape(2 * some, -1),
        (((1,), (1,)), ((), ())),
        preferred_element_type=jnp.float32,
    )
    real_part = product[:bands, :some] + product[bands:, some:]
    imag_part = product[:bands, some:] - product[bands:, :some]
    return jnp.stack([real_part, imag_part])


def mirrored(matrix):
    turned = jnp.swapaxes(matrix, -1, -2)
    return jnp.stack([turned[0], -turned[1]])


def exchanged(pieces):
    return lax.all_to_all(pieces, "pw", 0, 0, tiled=True)


def share_of_sum(partial):
    pw = lax.axis_size("pw")
    bands, some = partial.shape[1:]
    pieces = jnp.swapaxes(partial.reshape(2, pw, bands // pw, some), 0, 1)
    return jnp.sum(exchanged(pieces), axis=0)


def all_shares(pair):
    pw = lax.axis_size("pw")
    shares = exchanged(jnp.broadcast_to(pair[None], (pw, *pair.shape)))
    whole = jnp.moveaxis(shares, 0, 2)
    return whole.reshape(*pair.shape[:2], -1, pair.shape[3])


def whole_sum(partial):
    pw = lax.axis_size("pw")
    return jnp.sum(exchanged(jnp.broadcast_to(partial[None], (pw, *partial.shape))), axis=0)


def local(coefficients, shifts):
    own = coefficients[0]
    bands, pw_width = own.shape[1:]
    table = shifts[0, 0] - lax.axis_index("pw") * pw_width
    unit = bands // sum(SIXTEENTHS)
    edges = [0]
    for size in SIXTEENTHS:
        edges.append(edges[-1] + size * unit)

    def sent(chunk, *others):
        block = own[:, edges[chunk] : edges[chunk + 1]]
        return moved(after(block, *others) if others else block, "ka", -1)

    arrived = {0: sent(0)}
    arrived[1] = sent(1)
    arrived[2] = sent(2)
    placed = unpermuted(own, table)
    partial = {}

    def correlate(chunk, *others):
        block = arrived[chunk]
        partial[chunk] = correlation_of(placed, after(block, *others) if others else block)

    correlate(0)
    arrived[3] = sent(3, arrived[0])
    correlate(1, partial[0])
    arrived[4] = sent(4, arrived[1])
    correlate(2, partial[1])
    arrived[5] = sent(5, arrived[2])
    first = share_of_sum(jnp.concatenate([partial[0], partial[1], partial[2]], axis=2))
    first_behind = moved(first, "ka", 1)
    correlate(3, first)
    arrived[6] = sent(6, arrived[3])
    second = share_of_sum(partial[3])
    second_behind = moved(second, "ka", 1)
    first_whole = all_shares(jnp.stack([first, first_behind]))
    correlate(4, first_whole, second)
    third = whole_sum(partial[4])
    third_behind = moved(third, "ka", 1)
    second_whole = all_shares(jnp.stack([second, after(second_behind, third)]))
    correlate(5, second_whole, third)
    fourth = whole_sum(partial[5])
    fourth_behind = moved(fourth, "ka", 1)
    correlate(6, fourth)
    fifth = whole_sum(partial[6])
    fifth_behind = moved(fifth, "ka", 1)
    ahead = jnp.concatenate([first_whole[0], second_whole[0], third, fourth, fifth], axis=2)
    behind = jnp.concatenate(
        [
            mirrored(before)
            for before in (
                first_whole[1],
                second_whole[1],
                third_behind,
                fourth_behind,
                fifth_behind,
            )
        ],
        axis=1,
    )
    return jnp.stack([ahead, behind])[None]


def solution(mesh):
    return jax.shard_map(
        local,
        mesh=mesh,
        in_specs=(P(("groups", "ka"), None, None, "pw"), P(("groups", "ka"), None, "pw")),
        out_specs=P(("groups", "ka"), None, None, None, None),
        check_vma=False,
    )
```

time: 206 us -> 184 us (0.89)
  the two profiles are of different devices: /device:TPU:28 before, /device:TPU:0 now
where the time goes in v2:
time: 184 us; the launch traced here: 183 us
  waiting for transfers between devices  59.5 us (32%)
  matrix products  49.6 us (27%)
  starting transfers between devices  35.6 us (19%)
  local copies, waits for them, and re-layouts  33.4 us (18%)
  other arithmetic  3.89 us (2%)
    dot_general x7, matrix products, correlation_of(): lax.dot_general(own.reshape(2 * bands, -1), partner.reshape(2 * some, -1)...  36.1 us
    all_to_all x7, waiting for transfers between devices, exchanged(): return lax.all_to_all(pieces, 'pw', 0, 0, tiled=True)  32 us
    all_to_all x7, starting transfers between devices, exchanged(): return lax.all_to_all(pieces, 'pw', 0, 0, tiled=True)  27.8 us
    ppermute x12, waiting for transfers between devices, moved(): lax.ppermute(block, axis, [(i, (i + distance) % count) for i in range(cou...  27.6 us
    unnamed x12, local copies, waits for them, and re-layouts  13.9 us
    slice x4, local copies, waits for them, and re-layouts, sent(): block = own[:, edges[chunk]:edges[chunk + 1]]  13.5 us
    dot_general x1, matrix products, unpermuted(): jnp.einsum('rbo,boi->rbi', rows, selector, preferred_element_type=jnp.flo...  13.5 us
    ppermute x12, starting transfers between devices, moved(): lax.ppermute(block, axis, [(i, (i + distance) % count) for i in range(cou...  7.8 us
  transfers between devices with their start and end apart: 19, of which 11 were waited for; matrix products, arithmetic and copies ran while one was open for 45% of the time, Pallas kernels for 0%

profile of v2, /device:TPU:0, one launch (start us, length us, event | category | flops | bytes accessed | tf_op | source)
XLA Modules:
  0.0 182.6 jit_solution(9405131054573936009)
XLA Ops:
  0.0 2.7 %fusion.18 = (bf16[2,16,10240]{2,1,0:T(8,128)(2,1)}, bf16[2,16,10240]{2,1,0:T(8,128)(2,1)}, bf16[2,16,10240]{2,1,0:T(8,128)(2,1)S(1)}) fusion(bf16[2,256,10240]{2,1,0:T(8,128)(2,1)} %bitcast.102), kind=kLoop, calls=%fused_computation.53 | loop fusion | bytes 3932160 | tf_op jit(solution)/shard_map/slice | solution.py:84
  2.7 2.4 %collective-permute-start = (bf16[2,16,10240]{2,1,0:T(8,128)(2,1)S(1)}, bf16[2,16,10240]{2,1,0:T(8,128)(2,1)S(1)}, u32[]{:S(2)}, u32[]{:S(2)}) collective-permute-start(bf16[2,16,10240]{2,1,0:T(8,128)(2,1)S(1)} %get-tuple-element.29), channel_id=1, source_target_pairs={{0,12},{4,0},{8,4},{12,8},{1,13},{5,1},{9,5},{13,9},{2,14},{6,2},{... | collective-permute-start | bytes 1966088 | tf_op jit(solution)/shard_map/ppermute | solution.py:12
  5.0 5.4 %fusion.19 = (bf16[2,64,10240]{2,1,0:T(8,128)(2,1)}, bf16[2,64,10240]{2,1,0:T(8,128)(2,1)}) fusion(bf16[2,256,10240]{2,1,0:T(8,128)(2,1)} %bitcast.103), kind=kLoop, calls=%fused_computation.54 | loop fusion | bytes 10485760 | tf_op jit(solution)/shard_map/slice | solution.py:84
  11.1 3.0 %slice.204 = bf16[2,48,10240]{2,1,0:T(8,128)(2,1)} slice(bf16[2,256,10240]{2,1,0:T(8,128)(2,1)} %bitcast.104), slice={[0:2], [16:64], [0:10240]} | slice | bytes 3932160 | tf_op jit(solution)/shard_map/slice | solution.py:84
  14.1 11.5 %copy.45 = bf16[64,8,40,256]{3,2,1,0:T(8,128)(2,1)} copy(bf16[64,8,40,256]{3,1,2,0:T(8,128)(2,1)} %bitcast.105) | data formatting | bytes 20971520
  25.8 13.5 %fusion.2 = bf16[40,256,512]{2,1,0:T(8,128)(2,1)} fusion(bf16[512,40,256]{2,1,0:T(8,128)(2,1)} %bitcast.107, s32[40,256]{1,0:T(8,128)S(1)} %broadcast_subtract_fusion), kind=kOutput, calls=%fused_computation.3 | convolution fusion | flops 2692218880 | bytes 21012480 | tf_op jit(solution)/shard_map/rbo,boi->rbi/dot_general | solution.py:28
  39.3 6.0 %fusion.28 = f32[512,32]{0,1:T(8,128)S(1)} fusion(bf16[32,10240]{1,0:T(8,128)(2,1)S(1)} %bitcast.113, bf16[512,10240]{0,1:T(8,128)(2,1)} %bitcast.95), kind=kOutput, calls=%fused_computation.66 | convolution fusion | flops 335544320 | bytes 11206656 | tf_op jit(solution)/shard_map/dot_general | solution.py:35
  45.3 17.1 %collective-permute-done.1 = bf16[2,48,10240]{2,1,0:T(8,128)(2,1)} collective-permute-done((bf16[2,48,10240]{2,1,0:T(8,128)(2,1)}, bf16[2,48,10240]{2,1,0:T(8,128)(2,1)}, u32[]{:S(2)}, u32[]{:S(2)}) %collective-permute-start.1) | collective-permute-done | bytes 1966112 | tf_op jit(solution)/shard_map/ppermute | solution.py:12
  62.4 3.3 %fusion.29 = f32[512,96]{0,1:T(8,128)S(1)} fusion(bf16[96,10240]{1,0:T(8,128)(2,1)} %bitcast.7, bf16[512,10240]{0,1:T(8,128)(2,1)S(1)} %bitcast.100), kind=kOutput, calls=%fused_computation.67 | convolution fusion | flops 1006632960 | bytes 12648448 | tf_op jit(solution)/shard_map/dot_general | solution.py:35
  65.8 3.3 %fusion.30 = f32[512,128]{0,1:T(8,128)S(1)} fusion(bf16[128,10240]{1,0:T(8,128)(2,1)} %bitcast.10, bf16[512,10240]{0,1:T(8,128)(2,1)S(1)} %bitcast.101), kind=kOutput, calls=%fused_computation.68 | convolution fusion | flops 1342177280 | bytes 13369344 | tf_op jit(solution)/shard_map/dot_general | solution.py:35
  70.0 4.9 %all-to-all-start = ((f32[4,2,64,128]{3,2,1,0:T(8,128)}), f32[4,2,64,128]{3,2,1,0:T(8,128)S(1)}, u32[]{:S(2)}, u32[]{:S(2)}) async-start(f32[4,2,64,128]{3,2,1,0:T(8,128)} %copy.35), calls=%async_computation | async-start | bytes 524288 | tf_op jit(solution)/shard_map/all_to_all | solution.py:52
  74.8 2.5 %slice.225 = bf16[2,32,10240]{2,1,0:T(8,128)(2,1)} slice(bf16[2,256,10240]{2,1,0:T(8,128)(2,1)} %bitcast.106), slice={[0:2], [192:224], [0:10240]} | slice | bytes 2621440 | tf_op jit(solution)/shard_map/slice | solution.py:84
  77.3 1.6 collective-permute-start.6
  78.9 5.8 %all-to-all-done = f32[4,2,64,128]{3,2,1,0:T(8,128)S(1)} async-done(((f32[4,2,64,128]{3,2,1,0:T(8,128)}), f32[4,2,64,128]{3,2,1,0:T(8,128)S(1)}, u32[]{:S(2)}, u32[]{:S(2)}) %all-to-all-start) | async-done | bytes 262176 | tf_op jit(solution)/shard_map/all_to_all | solution.py:52
  84.7 5.8 %collective-permute-done.4 = bf16[2,64,10240]{2,1,0:T(8,128)(2,1)S(1)} collective-permute-done((bf16[2,64,10240]{2,1,0:T(8,128)(2,1)}, bf16[2,64,10240]{2,1,0:T(8,128)(2,1)S(1)}, u32[]{:S(2)}, u32[]{:S(2)}) %collective-permute-start.4) | collective-permute-done | bytes 2621472 | tf_op jit(solution)/shard_map/ppermute | solution.py:12
  90.5 5.5 %fusion.31 = f32[512,128]{0,1:T(8,128)S(1)} fusion(bf16[128,10240]{1,0:T(8,128)(2,1)S(1)} %bitcast.108, bf16[512,10240]{0,1:T(8,128)(2,1)} %bitcast.96), kind=kOutput, calls=%fused_computation.69 | convolution fusion | flops 1342177280 | bytes 13369344 | tf_op jit(solution)/shard_map/dot_general | solution.py:35
  97.2 4.9 %all-to-all-start.2 = ((f32[4,1,8192]{2,1,0:T(1,128)}), f32[4,1,8192]{2,1,0:T(1,128)S(1)}, u32[]{:S(2)}, u32[]{:S(2)}) async-start(f32[4,1,8192]{2,1,0:T(1,128)} %reshape.87), calls=%async_computation.2 | async-start | bytes 262144 | tf_op jit(solution)/shard_map/all_to_all | solution.py:52
  103.5 5.0 %all-to-all-done.2 = f32[4,1,8192]{2,1,0:T(1,128)S(1)} async-done(((f32[4,1,8192]{2,1,0:T(1,128)}), f32[4,1,8192]{2,1,0:T(1,128)S(1)}, u32[]{:S(2)}, u32[]{:S(2)}) %all-to-all-start.2) | async-done | bytes 131104 | tf_op jit(solution)/shard_map/all_to_all | solution.py:52
  110.2 6.4 %fusion.32 = f32[512,64]{0,1:T(8,128)S(1)} fusion(bf16[64,10240]{1,0:T(8,128)(2,1)} %bitcast.22, bf16[512,10240]{0,1:T(8,128)(2,1)} %bitcast.97), kind=kOutput, calls=%fused_computation.70 | convolution fusion | flops 671088640 | bytes 11927552 | tf_op jit(solution)/shard_map/dot_general | solution.py:35
  117.4 3.4 %all-to-all-start.3 = ((f32[4,2,256,32]{2,3,1,0:T(8,128)}), f32[4,2,256,32]{2,3,1,0:T(8,128)S(1)}, u32[]{:S(2)}, u32[]{:S(2)}) async-start(f32[4,2,256,32]{2,3,1,0:T(8,128)} %broadcast_in_dim.13), calls=%async_computation.3 | async-start | bytes 524288 | tf_op jit(solution)/shard_map/all_to_all | solution.py:52
  121.4 3.1 %collective-permute-done.3 = f32[2,64,128]{2,1,0:T(8,128)S(1)} collective-permute-done((f32[2,64,128]{2,1,0:T(8,128)S(1)}, f32[2,64,128]{2,1,0:T(8,128)S(1)}, u32[]{:S(2)}, u32[]{:S(2)}) %collective-permute-start.3) | collective-permute-done | bytes 65568 | tf_op jit(solution)/shard_map/ppermute | solution.py:12
  124.6 4.9 %all-to-all-done.3 = f32[4,2,256,32]{2,3,1,0:T(8,128)S(1)} async-done(((f32[4,2,256,32]{2,3,1,0:T(8,128)}), f32[4,2,256,32]{2,3,1,0:T(8,128)S(1)}, u32[]{:S(2)}, u32[]{:S(2)}) %all-to-all-start.3) | async-done | bytes 262176 | tf_op jit(solution)/shard_map/all_to_all | solution.py:52
  130.3 3.5 %all-to-all-start.1 = ((f32[4,2,2,64,128]{4,3,2,1,0:T(8,128)}), f32[4,2,2,64,128]{4,3,2,1,0:T(8,128)S(1)}, u32[]{:S(2)}, u32[]{:S(2)}) async-start(f32[4,2,2,64,128]{4,3,2,1,0:T(8,128)} %broadcast_in_dim.12), calls=%async_computation.1 | async-start | bytes 1048576 | tf_op jit(solution)/shard_map/all_to_all | solution.py:52
  134.0 5.9 %fusion.33 = f32[512,32]{0,1:T(8,128)S(1)} fusion(bf16[32,10240]{1,0:T(8,128)(2,1)S(1)} %bitcast.112, bf16[512,10240]{0,1:T(8,128)(2,1)} %bitcast.98), kind=kOutput, calls=%fused_computation.71 | convolution fusion | flops 335544320 | bytes 11206656 | tf_op jit(solution)/shard_map/dot_general | solution.py:35
  139.9 7.0 %all-to-all-done.1 = f32[4,2,2,64,128]{4,3,2,1,0:T(8,128)S(1)} async-done(((f32[4,2,2,64,128]{4,3,2,1,0:T(8,128)}), f32[4,2,2,64,128]{4,3,2,1,0:T(8,128)S(1)}, u32[]{:S(2)}, u32[]{:S(2)}) %all-to-all-start.1) | async-done | bytes 524320 | tf_op jit(solution)/shard_map/all_to_all | solution.py:52
  147.6 3.3 %all-to-all-start.5 = ((f32[4,2,256,16]{2,3,1,0:T(8,128)}), f32[4,2,256,16]{2,3,1,0:T(8,128)S(1)}, u32[]{:S(2)}, u32[]{:S(2)}) async-start(f32[4,2,256,16]{2,3,1,0:T(8,128)} %broadcast_in_dim.15), calls=%async_computation.5 | async-start | bytes 262144 | tf_op jit(solution)/shard_map/all_to_all | solution.py:52
  152.3 4.5 %all-to-all-done.5 = f32[4,2,256,16]{2,3,1,0:T(8,128)S(1)} async-done(((f32[4,2,256,16]{2,3,1,0:T(8,128)}), f32[4,2,256,16]{2,3,1,0:T(8,128)S(1)}, u32[]{:S(2)}, u32[]{:S(2)}) %all-to-all-start.5) | async-done | bytes 131104 | tf_op jit(solution)/shard_map/all_to_all | solution.py:52
  156.8 3.4 %all-to-all-start.4 = ((f32[4,1,16384]{2,1,0:T(1,128)}), f32[4,1,16384]{2,1,0:T(1,128)S(1)}, u32[]{:S(2)}, u32[]{:S(2)}) async-start(f32[4,1,16384]{2,1,0:T(1,128)} %reshape.89), calls=%async_computation.4 | async-start | bytes 524288 | tf_op jit(solution)/shard_map/all_to_all | solution.py:52
  160.3 5.9 %fusion.34 = f32[512,32]{0,1:T(8,128)S(1)} fusion(bf16[32,10240]{1,0:T(8,128)(2,1)S(1)} %bitcast.111, bf16[512,10240]{0,1:T(8,128)(2,1)} %bitcast.99), kind=kOutput, calls=%fused_computation.72 | convolution fusion | flops 335544320 | bytes 11206656 | tf_op jit(solution)/shard_map/dot_general | solution.py:35
  167.6 4.5 %all-to-all-start.6 = ((f32[4,2,256,16]{2,3,1,0:T(8,128)}), f32[4,2,256,16]{2,3,1,0:T(8,128)S(1)}, u32[]{:S(2)}, u32[]{:S(2)}) async-start(f32[4,2,256,16]{2,3,1,0:T(8,128)} %broadcast_in_dim.16), calls=%async_computation.6 | async-start | bytes 262144 | tf_op jit(solution)/shard_map/all_to_all | solution.py:52
  173.8 4.3 %all-to-all-done.6 = f32[4,2,256,16]{2,3,1,0:T(8,128)S(1)} async-done(((f32[4,2,256,16]{2,3,1,0:T(8,128)}), f32[4,2,256,16]{2,3,1,0:T(8,128)S(1)}, u32[]{:S(2)}, u32[]{:S(2)}) %all-to-all-start.6) | async-done | bytes 131104 | tf_op jit(solution)/shard_map/all_to_all | solution.py:52
  180.0 1.5 collective-permute-done.11
  (89 shorter events, 16.7 us)
Async XLA Ops:
  2.7 36.6 %collective-permute-start = (bf16[2,16,10240]{2,1,0:T(8,128)(2,1)S(1)}, bf16[2,16,10240]{2,1,0:T(8,128)(2,1)S(1)}, u32[]{:S(2)}, u32[]{:S(2)}) collective-permute-start(bf16[2,16,10240]{2,1,0:T(8,128)(2,1)S(1)} %get-tuple-element.29), channel_id=1, source_target_pairs={{0,12},{4,0},{8,4},{12,8},{1,13},{5,1},{9,5},{13,9},{2,14},{6,2},{... | collective-permute-start | bytes 1966088 | tf_op jit(solution)/shard_map/ppermute | solution.py:12
  10.5 55.3 %collective-permute-start.2 = (bf16[2,64,10240]{2,1,0:T(8,128)(2,1)}, bf16[2,64,10240]{2,1,0:T(8,128)(2,1)}, u32[]{:S(2)}, u32[]{:S(2)}) collective-permute-start(bf16[2,64,10240]{2,1,0:T(8,128)(2,1)} %get-tuple-element.31), channel_id=1, source_target_pairs={{0,12},{4,0},{8,4},{12,8},{1,13},{5,1},{9,5},{13,9},{2,14},{6,2},{... | collective-permute-start | bytes 7864328 | tf_op jit(solution)/shard_map/ppermute | solution.py:12
  14.1 48.3 %collective-permute-start.1 = (bf16[2,48,10240]{2,1,0:T(8,128)(2,1)}, bf16[2,48,10240]{2,1,0:T(8,128)(2,1)}, u32[]{:S(2)}, u32[]{:S(2)}) collective-permute-start(bf16[2,48,10240]{2,1,0:T(8,128)(2,1)} %slice.204), channel_id=1, source_target_pairs={{0,12},{4,0},{8,4},{12,8},{1,13},{5,1},{9,5},{13,9},{2,14},{6,2},{... | collective-permute-start | bytes 5898248 | tf_op jit(solution)/shard_map/ppermute | solution.py:12
  14.1 11.5 %copy-start.2 = (s32[1,2,10240]{2,1,0:T(2,128)S(1)}, s32[1,2,10240]{2,1,0:T(2,128)}, u32[]{:S(2)}) copy-start(s32[1,2,10240]{2,1,0:T(2,128)} %param.3) | copy-start | bytes 245764
  39.3 23.1 %copy-start = (bf16[40,256,512]{2,1,0:T(8,128)(2,1)S(1)}, bf16[40,256,512]{2,1,0:T(8,128)(2,1)}, u32[]{:S(2)}) copy-start(bf16[40,256,512]{2,1,0:T(8,128)(2,1)} %fusion.2) | copy-start | bytes 31457284
  39.3 51.2 %collective-permute-start.4 = (bf16[2,64,10240]{2,1,0:T(8,128)(2,1)}, bf16[2,64,10240]{2,1,0:T(8,128)(2,1)S(1)}, u32[]{:S(2)}, u32[]{:S(2)}) collective-permute-start(bf16[2,64,10240]{2,1,0:T(8,128)(2,1)} %get-tuple-element.18), channel_id=1, source_target_pairs={{0,12},{4,0},{8,4},{12,8},{1,13},{5,1},{9,5},{13,9},{2,14},{6,2},{... | collective-permute-start | bytes 7864328 | tf_op jit(solution)/shard_map/ppermute | solution.py:12
  70.0 14.8 %all-to-all-start = ((f32[4,2,64,128]{3,2,1,0:T(8,128)}), f32[4,2,64,128]{3,2,1,0:T(8,128)S(1)}, u32[]{:S(2)}, u32[]{:S(2)}) async-start(f32[4,2,64,128]{3,2,1,0:T(8,128)} %copy.35), calls=%async_computation | async-start | bytes 524288 | tf_op jit(solution)/shard_map/all_to_all | solution.py:52
  77.3 32.9 %collective-permute-start.6 = (bf16[2,32,10240]{2,1,0:T(8,128)(2,1)}, bf16[2,32,10240]{2,1,0:T(8,128)(2,1)}, u32[]{:S(2)}, u32[]{:S(2)}) collective-permute-start(bf16[2,32,10240]{2,1,0:T(8,128)(2,1)} %slice.225), channel_id=1, source_target_pairs={{0,12},{4,0},{8,4},{12,8},{1,13},{5,1},{9,5},{13,9},{2,14},{6,2},{... | collective-permute-start | bytes 3932168 | tf_op jit(solution)/shard_map/ppermute | solution.py:12
  97.2 11.4 %all-to-all-start.2 = ((f32[4,1,8192]{2,1,0:T(1,128)}), f32[4,1,8192]{2,1,0:T(1,128)S(1)}, u32[]{:S(2)}, u32[]{:S(2)}) async-start(f32[4,1,8192]{2,1,0:T(1,128)} %reshape.87), calls=%async_computation.2 | async-start | bytes 262144 | tf_op jit(solution)/shard_map/all_to_all | solution.py:52
  102.0 32.0 %collective-permute-start.7 = (bf16[2,16,10240]{2,1,0:T(8,128)(2,1)}, bf16[2,16,10240]{2,1,0:T(8,128)(2,1)S(1)}, u32[]{:S(2)}, u32[]{:S(2)}) collective-permute-start(bf16[2,16,10240]{2,1,0:T(8,128)(2,1)} %get-tuple-element.23), channel_id=1, source_target_pairs={{0,12},{4,0},{8,4},{12,8},{1,13},{5,1},{9,5},{13,9},{2,14},{6,2},{... | collective-permute-start | bytes 1966088 | tf_op jit(solution)/shard_map/ppermute | solution.py:12
  110.2 14.3 %copy-start.1 = (bf16[2,16,10240]{2,1,0:T(8,128)(2,1)S(1)}, bf16[2,16,10240]{2,1,0:T(8,128)(2,1)}, u32[]{:S(2)}) copy-start(bf16[2,16,10240]{2,1,0:T(8,128)(2,1)} %get-tuple-element.25) | copy-start | bytes 1966084
  117.4 12.1 %all-to-all-start.3 = ((f32[4,2,256,32]{2,3,1,0:T(8,128)}), f32[4,2,256,32]{2,3,1,0:T(8,128)S(1)}, u32[]{:S(2)}, u32[]{:S(2)}) async-start(f32[4,2,256,32]{2,3,1,0:T(8,128)} %broadcast_in_dim.13), calls=%async_computation.3 | async-start | bytes 524288 | tf_op jit(solution)/shard_map/all_to_all | solution.py:52
  120.8 3.7 %collective-permute-start.3 = (f32[2,64,128]{2,1,0:T(8,128)S(1)}, f32[2,64,128]{2,1,0:T(8,128)S(1)}, u32[]{:S(2)}, u32[]{:S(2)}) collective-permute-start(f32[2,64,128]{2,1,0:T(8,128)S(1)} %reduce_sum.45), channel_id=1, source_target_pairs={{0,4},{4,8},{8,12},{12,0},{1,5},{5,9},{9,13},{13,1},{2,6},{6,10},{... | collective-permute-start | bytes 196616 | tf_op jit(solution)/shard_map/ppermute | solution.py:12
  120.8 13.2 %collective-permute-start.5 = (f32[2,64,64]{1,2,0:T(8,128)S(1)}, f32[2,64,64]{1,2,0:T(8,128)S(1)}, u32[]{:S(2)}, u32[]{:S(2)}) collective-permute-start(f32[2,64,64]{1,2,0:T(8,128)S(1)} %bitcast_reduce_fusion), channel_id=1, source_target_pairs={{0,4},{4,8},{8,12},{12,0},{1,5},{5,9},{9,13},{13,1},{2,6},{6,10},{... | collective-permute-start | bytes 98312 | tf_op jit(solution)/shard_map/ppermute | solution.py:12
  124.5 35.7 %collective-permute-start.8 = (bf16[2,16,10240]{2,1,0:T(8,128)(2,1)S(1)}, bf16[2,16,10240]{2,1,0:T(8,128)(2,1)S(1)}, u32[]{:S(2)}, u32[]{:S(2)}) collective-permute-start(bf16[2,16,10240]{2,1,0:T(8,128)(2,1)S(1)} %copy-done.1), channel_id=1, source_target_pairs={{0,12},{4,0},{8,4},{12,8},{1,13},{5,1},{9,5},{13,9},{2,14},{6,2},{... | collective-permute-start | bytes 1966088 | tf_op jit(solution)/shard_map/ppermute | solution.py:12
  130.3 16.6 %all-to-all-start.1 = ((f32[4,2,2,64,128]{4,3,2,1,0:T(8,128)}), f32[4,2,2,64,128]{4,3,2,1,0:T(8,128)S(1)}, u32[]{:S(2)}, u32[]{:S(2)}) async-start(f32[4,2,2,64,128]{4,3,2,1,0:T(8,128)} %broadcast_in_dim.12), calls=%async_computation.1 | async-start | bytes 1048576 | tf_op jit(solution)/shard_map/all_to_all | solution.py:52
  134.0 18.3 %collective-permute-start.9 = (f32[2,256,32]{1,2,0:T(8,128)S(1)}, f32[2,256,32]{1,2,0:T(8,128)S(1)}, u32[]{:S(2)}, u32[]{:S(2)}) collective-permute-start(f32[2,256,32]{1,2,0:T(8,128)S(1)} %reduce_sum.47), channel_id=1, source_target_pairs={{0,4},{4,8},{8,12},{12,0},{1,5},{5,9},{9,13},{13,1},{2,6},{6,10},{... | collective-permute-start | bytes 196616 | tf_op jit(solution)/shard_map/ppermute | solution.py:12
  147.6 9.2 %all-to-all-start.5 = ((f32[4,2,256,16]{2,3,1,0:T(8,128)}), f32[4,2,256,16]{2,3,1,0:T(8,128)S(1)}, u32[]{:S(2)}, u32[]{:S(2)}) async-start(f32[4,2,256,16]{2,3,1,0:T(8,128)} %broadcast_in_dim.15), calls=%async_computation.5 | async-start | bytes 262144 | tf_op jit(solution)/shard_map/all_to_all | solution.py:52
  156.8 10.2 %all-to-all-start.4 = ((f32[4,1,16384]{2,1,0:T(1,128)}), f32[4,1,16384]{2,1,0:T(1,128)S(1)}, u32[]{:S(2)}, u32[]{:S(2)}) async-start(f32[4,1,16384]{2,1,0:T(1,128)} %reshape.89), calls=%async_computation.4 | async-start | bytes 524288 | tf_op jit(solution)/shard_map/all_to_all | solution.py:52
  160.2 6.1 %collective-permute-start.10 = (f32[2,256,16]{1,2,0:T(8,128)S(1)}, f32[2,256,16]{1,2,0:T(8,128)S(1)}, u32[]{:S(2)}, u32[]{:S(2)}) collective-permute-start(f32[2,256,16]{1,2,0:T(8,128)S(1)} %reduce_sum.48), channel_id=1, source_target_pairs={{0,4},{4,8},{8,12},{12,0},{1,5},{5,9},{9,13},{13,1},{2,6},{6,10},{... | collective-permute-start | bytes 98312 | tf_op jit(solution)/shard_map/ppermute | solution.py:12
  167.6 10.5 %all-to-all-start.6 = ((f32[4,2,256,16]{2,3,1,0:T(8,128)}), f32[4,2,256,16]{2,3,1,0:T(8,128)S(1)}, u32[]{:S(2)}, u32[]{:S(2)}) async-start(f32[4,2,256,16]{2,3,1,0:T(8,128)} %broadcast_in_dim.16), calls=%async_computation.6 | async-start | bytes 262144 | tf_op jit(solution)/shard_map/all_to_all | solution.py:52
  178.1 3.4 %collective-permute-start.11 = (f32[2,256,16]{1,2,0:T(8,128)S(1)}, f32[2,256,16]{1,2,0:T(8,128)S(1)}, u32[]{:S(2)}, u32[]{:S(2)}) collective-permute-start(f32[2,256,16]{1,2,0:T(8,128)S(1)} %reduce_sum.49), channel_id=1, source_target_pairs={{0,4},{4,8},{8,12},{12,0},{1,5},{5,9},{9,13},{13,1},{2,6},{6,10},{... | collective-permute-start | bytes 98312 | tf_op jit(solution)/shard_map/ppermute | solution.py:12

commit v3 on v0

v3 whole, which is shorter than its diff:
```python
import functools

import jax
import jax.numpy as jnp
from jax import lax
from jax.experimental import pallas as pl
from jax.experimental.pallas import tpu as pltpu
from jax.sharding import PartitionSpec as P

PWB = 256
SIXTEENTHS = (5, 4, 3, 2, 1, 1)
MIB = 1 << 20
ANYWHERE = pl.BlockSpec(memory_space=pl.ANY)
WHOLE = pl.BlockSpec(memory_space=pltpu.VMEM)


def moved(block, axis, distance):
    count = lax.axis_size(axis)
    return lax.ppermute(block, axis, [(i, (i + distance) % count) for i in range(count)])


def cut_kernel(low, high, *refs):
    own_ref, out_ref, sems = refs[0], refs[-2], refs[-1]
    copies = [
        pltpu.make_async_copy(own_ref.at[0, c, low:high], out_ref.at[c], sems.at[c])
        for c in range(2)
    ]
    for copy in copies:
        copy.start()
    for copy in copies:
        copy.wait()


def cut(coefficients, low, high, *others):
    shape = (2, high - low, coefficients.shape[3])
    return pl.pallas_call(
        functools.partial(cut_kernel, low, high),
        out_shape=jax.ShapeDtypeStruct(shape, coefficients.dtype),
        in_specs=[ANYWHERE] * (1 + len(others)),
        out_specs=ANYWHERE,
        scratch_shapes=[pltpu.SemaphoreType.DMA((2,))],
        compiler_params=pltpu.CompilerParams(vmem_limit_bytes=MIB),
        cost_estimate=pl.CostEstimate(flops=0, bytes_accessed=1024, transcendentals=0),
        name="cut",
    )(coefficients, *others)


def place_kernel(own_ref, shift_ref, out_ref):
    bands, width = own_ref.shape[2:]
    base = pl.program_id(0) * width
    goal = lax.broadcasted_iota(jnp.int32, (PWB, PWB), 0)
    for block in range(width // PWB):
        here = pl.ds(block * PWB, PWB)
        inside = shift_ref[0, 0:1, here] & (PWB - 1)
        selector = (goal == inside).astype(jnp.float32).astype(jnp.bfloat16)
        rows = own_ref[0, :, :, here].reshape(2 * bands, PWB)
        placed = lax.dot_general(
            selector, rows, (((1,), (1,)), ((), ())), preferred_element_type=jnp.float32
        )
        there = pl.multiple_of(base + block * PWB, PWB)
        out_ref[pl.ds(there, PWB), :] = placed.astype(jnp.bfloat16)


def placed_bands(coefficients, shifts):
    bands, width = coefficients.shape[2:]
    step = 4 * PWB if width % (4 * PWB) == 0 else PWB
    return pl.pallas_call(
        place_kernel,
        grid=(width // step,),
        out_shape=pltpu.VMEM((width, 2 * bands), jnp.bfloat16),
        in_specs=[
            pl.BlockSpec((1, 2, bands, step), lambda g: (0, 0, 0, g)),
            pl.BlockSpec((1, 2, step), lambda g: (0, 0, g)),
        ],
        out_specs=WHOLE,
        compiler_params=pltpu.CompilerParams(vmem_limit_bytes=16 * MIB),
        cost_estimate=pl.CostEstimate(flops=0, bytes_accessed=1024, transcendentals=0),
        name="place",
    )(coefficients, shifts)


def correlate_kernel(steps, *refs):
    placed_ref, block_ref, out_ref, total = refs[0], refs[1], refs[-2], refs[-1]
    some, depth = block_ref.shape[1:]
    bands = out_ref.shape[2]
    step = pl.program_id(0)
    start = pl.multiple_of(step * depth, PWB)
    product = jnp.dot(
        block_ref[...].reshape(2 * some, depth),
        placed_ref[pl.ds(start, depth), :],
        preferred_element_type=jnp.float32,
    )

    @pl.when(step == 0)
    def _():
        total[...] = product

    @pl.when(step > 0)
    def _():
        total[...] += product

    @pl.when(step == steps - 1)
    def _():
        out_ref[0] = total[:some, :bands] + total[some:, bands:]
        out_ref[1] = total[some:, :bands] - total[:some, bands:]


def correlate(placed, block, *others):
    some, width = block.shape[1:]
    bands = placed.shape[1] // 2
    depth = width
    while depth % (2 * PWB) == 0 and some * depth > 1 << 18:
        depth //= 2
    steps = width // depth
    return pl.pallas_call(
        functools.partial(correlate_kernel, steps),
        grid=(steps,),
        out_shape=jax.ShapeDtypeStruct((2, some, bands), jnp.float32),
        in_specs=[WHOLE, pl.BlockSpec((2, some, depth), lambda g: (0, 0, g))]
        + [ANYWHERE] * len(others),
        out_specs=pl.BlockSpec((2, some, bands), lambda g: (0, 0, 0)),
        scratch_shapes=[pltpu.VMEM((2 * some, 2 * bands), jnp.float32)],
        compiler_params=pltpu.CompilerParams(vmem_limit_bytes=16 * MIB),
        cost_estimate=pl.CostEstimate(flops=0, bytes_accessed=1024, transcendentals=0),
        name="correlate",
    )(placed, block, *others)


def summed_over_pw(partial):
    pw = lax.axis_size("pw")
    if pw & (pw - 1):
        return partial + sum(moved(partial, "pw", d) for d in range(1, pw))
    distance = 1
    while distance < pw:
        route = [(i, i ^ distance) for i in range(pw)]
        partial = partial + lax.ppermute(partial, "pw", route)
        distance *= 2
    return partial


def local(coefficients, shifts):
    bands = coefficients.shape[2]
    unit = bands // sum(SIXTEENTHS)
    edges = [0]
    for size in SIXTEENTHS:
        edges.append(edges[-1] + size * unit)
    coefficients = pltpu.with_memory_space_constraint(coefficients, pltpu.HBM)
    placed = pltpu.with_memory_space_constraint(placed_bands(coefficients, shifts), pltpu.VMEM)
    blocks, arrived = [], []
    for chunk, (low, high) in enumerate(zip(edges, edges[1:])):
        before = blocks[-1:] + ([arrived[chunk - 3], placed] if chunk >= 3 else [])
        blocks.append(cut(coefficients, low, high, *before))
        arrived.append(moved(blocks[-1], "ka", -1))
    partial, whole = [], []
    for chunk, block in enumerate(arrived):
        before = partial[-1:] + whole[max(0, chunk - 1 - (chunk > 3)) : chunk - (chunk > 3)]
        partial.append(correlate(placed, block, *before))
        whole.append(summed_over_pw(partial[-1]))
    behind = [
        moved(jnp.concatenate(some, axis=1), "ka", 1)
        for some in (whole[:3], whole[3:5], whole[5:])
    ]
    ahead = jnp.swapaxes(jnp.concatenate(whole, axis=1), 1, 2)
    behind = jnp.concatenate(behind, axis=1)
    return jnp.stack([ahead, jnp.stack([behind[0], -behind[1]])])[None]


def solution(mesh):
    return jax.shard_map(
        local,
        mesh=mesh,
        in_specs=(P(("groups", "ka"), None, None, "pw"), P(("groups", "ka"), None, "pw")),
        out_specs=P(("groups", "ka"), None, None, None, None),
        check_vma=False,
    )
```

time: 393 us -> 145 us (0.37)
  waiting for transfers between devices: 278 us -> 72.9 us
  matrix products: 70.7 us -> 0 us
  Pallas kernels: 0 us -> 31.3 us
  starting transfers between devices: 2.38 us -> 32.3 us
  local copies, waits for them, and re-layouts: 25.8 us -> 5.24 us
  between operations: 13.5 us -> 0.29 us
    ppermute x2 -> x21, waiting for transfers between devices: 222 us -> 72.9 us  [the longest x9 46.4 us: moved(): lax.ppermute(block, axis, [(i, (i + distance) % count) for i in range(cou...]
    dot_general x4 -> x0, matrix products: 70.7 us -> none  [the longest x2 47.5 us: permuted(): jnp.einsum('rbi,boi->rbo', rows, selector, preferred_element_type=jnp.flo...]
    psum x1 -> x0, waiting for transfers between devices: 55.9 us -> none  [local(): return lax.psum(jnp.stack(pairs), 'pw')]
    pallas_call x0 -> x13, Pallas kernels: none -> 31.3 us  [the longest x6 13.3 us: correlate(): pl.pallas_call(functools.partial(correlate_kernel, steps), grid=(steps,),...]
    ppermute x2 -> x21, starting transfers between devices: 2.38 us -> 32.3 us  [the longest x12 25.1 us: summed_over_pw(): partial = partial + lax.ppermute(partial, 'pw', route)]
    unnamed x2 -> x8, local copies, waits for them, and re-layouts: 23 us -> 4.02 us
  transfers between devices with their start and end apart: 3 -> 21, of which waited for: 2 -> 14; matrix products, arithmetic and copies ran while one was open for 12% -> 2% of each run, Pallas kernels for 0% -> 20%
where the time goes in v3:
time: 145 us; the launch traced here: 144 us
  waiting for transfers between devices  72.9 us (50%)
  starting transfers between devices  32.3 us (22%)
  Pallas kernels  31.3 us (22%)
  local copies, waits for them, and re-layouts  5.24 us (4%)
  other arithmetic  2.07 us (1%)
    ppermute x9, waiting for transfers between devices, moved(): lax.ppermute(block, axis, [(i, (i + distance) % count) for i in range(cou...  46.4 us
    ppermute x12, waiting for transfers between devices, summed_over_pw(): partial = partial + lax.ppermute(partial, 'pw', route)  26.5 us
    ppermute x12, starting transfers between devices, summed_over_pw(): partial = partial + lax.ppermute(partial, 'pw', route)  25.1 us
    pallas_call x6, Pallas kernels, correlate(): pl.pallas_call(functools.partial(correlate_kernel, steps), grid=(steps,),...  13.3 us
    pallas_call x1, Pallas kernels, placed_bands(): pl.pallas_call(place_kernel, grid=(width // step,), out_shape=pltpu.VMEM(...  9.34 us
    pallas_call x6, Pallas kernels, cut(): pl.pallas_call(functools.partial(cut_kernel, low, high), out_shape=jax.Sh...  8.65 us
    ppermute x9, starting transfers between devices, moved(): lax.ppermute(block, axis, [(i, (i + distance) % count) for i in range(cou...  7.25 us
    unnamed x8, local copies, waits for them, and re-layouts  4.02 us
  transfers between devices with their start and end apart: 21, of which 14 were waited for; matrix products, arithmetic and copies ran while one was open for 2% of the time, Pallas kernels for 20%

profile of v3, /device:TPU:0, one launch (start us, length us, event | category | flops | bytes accessed | tf_op | source)
XLA Modules:
  0.0 144.1 jit_solution(9007363907541203199)
XLA Ops:
  0.0 1.9 %cut.6.refs_1_ = bf16[2,80,10240]{2,1,0:T(8,128)(2,1)S(1)} custom-call(bf16[1,2,256,10240]{3,2,1,0:T(8,128)(2,1)} %refs_0_.11), custom_call_target="tpu_custom_call" | custom-call | bytes 1024 | tf_op jit(solution)/shard_map/cut/pallas_call | solution.py:36
  1.9 2.4 %collective-permute-start = (bf16[2,80,10240]{2,1,0:T(8,128)(2,1)S(1)}, bf16[2,80,10240]{2,1,0:T(8,128)(2,1)S(1)}, u32[]{:S(2)}, u32[]{:S(2)}) collective-permute-start(bf16[2,80,10240]{2,1,0:T(8,128)(2,1)S(1)} %cut.6.refs_1_), channel_id=1, source_target_pairs={{0,12},{4,0},{8,4},{12,8},{1,13},{5,1},{9,5},{13,9},{2,14},{6,2},{... | collective-permute-start | bytes 9830408 | tf_op jit(solution)/shard_map/ppermute | solution.py:19
  4.4 1.7 %cut.7.refs_1_ = bf16[2,64,10240]{2,1,0:T(8,128)(2,1)S(1)} custom-call(bf16[1,2,256,10240]{3,2,1,0:T(8,128)(2,1)} %refs_0_.11, bf16[2,80,10240]{2,1,0:T(8,128)(2,1)S(1)} %cut.6.refs_1_), custom_call_target="tpu_custom_call" | custom-call | bytes 1024 | tf_op jit(solution)/shard_map/cut/pallas_call | solution.py:36
  8.4 9.3 %place.1.refs_0_.refs_3_ = bf16[10240,512]{1,0:T(8,128)(2,1)S(1)} custom-call(bf16[1,2,256,10240]{3,2,1,0:T(8,128)(2,1)} %refs_0_.11, s32[1,2,10240]{2,1,0:T(2,128)S(1)} %copy-done.2), custom_call_target="tpu_custom_call" | custom-call | bytes 1024 | tf_op jit(solution)/shard_map/place/pallas_call | solution.py:67
  17.8 22.8 %collective-permute-done.refs_1_.refs_2_ = bf16[2,80,10240]{2,1,0:T(8,128)(2,1)S(1)} collective-permute-done((bf16[2,80,10240]{2,1,0:T(8,128)(2,1)S(1)}, bf16[2,80,10240]{2,1,0:T(8,128)(2,1)S(1)}, u32[]{:S(2)}, u32[]{:S(2)}) %collective-permute-start) | collective-permute-done | bytes 3276832 | tf_op jit(solution)/shard_map/ppermute | solution.py:19
  41.9 2.0 %collective-permute-start.9 = (bf16[2,32,10240]{2,1,0:T(8,128)(2,1)S(1)}, bf16[2,32,10240]{2,1,0:T(8,128)(2,1)S(1)}, u32[]{:S(2)}, u32[]{:S(2)}) collective-permute-start(bf16[2,32,10240]{2,1,0:T(8,128)(2,1)S(1)} %cut.9.refs_1_), channel_id=1, source_target_pairs={{0,12},{4,0},{8,4},{12,8},{1,13},{5,1},{9,5},{13,9},{2,14},{6,2},{... | collective-permute-start | bytes 3932168 | tf_op jit(solution)/shard_map/ppermute | solution.py:19
  43.8 2.8 %correlate.6.refs_2_ = f32[2,80,256]{2,1,0:T(8,128)S(1)} custom-call(bf16[10240,512]{1,0:T(8,128)(2,1)S(1)} %place.1.refs_0_.refs_3_, bf16[2,80,10240]{2,1,0:T(8,128)(2,1)S(1)} %collective-permute-done.refs_1_.refs_2_), custom_call_target="tpu_custom_call" | custom-call | bytes 1024 | tf_op jit(solution)/shard_map/correlate/pallas_call | solution.py:115
  48.3 3.7 %collective-permute-done.1 = f32[2,80,256]{2,1,0:T(8,128)S(1)} collective-permute-done((f32[2,80,256]{2,1,0:T(8,128)S(1)}, f32[2,80,256]{2,1,0:T(8,128)S(1)}, u32[]{:S(2)}, u32[]{:S(2)}) %collective-permute-start.1) | collective-permute-done | bytes 163872 | tf_op jit(solution)/shard_map/ppermute | solution.py:136
  52.0 2.7 %collective-permute-start.2 = (f32[2,80,256]{2,1,0:T(8,128)S(1)}, f32[2,80,256]{2,1,0:T(8,128)S(1)}, u32[]{:S(2)}, u32[]{:S(2)}) collective-permute-start(f32[2,80,256]{2,1,0:T(8,128)S(1)} %add.36), channel_id=1, source_target_pairs={{0,2},{1,3},{2,0},{3,1},{4,6},{5,7},{6,4},{7,5},{8,10},{9,11},{10,... | collective-permute-start | bytes 491528 | tf_op jit(solution)/shard_map/ppermute | solution.py:136
  54.7 5.7 %collective-permute-done.2 = f32[2,80,256]{2,1,0:T(8,128)S(1)} collective-permute-done((f32[2,80,256]{2,1,0:T(8,128)S(1)}, f32[2,80,256]{2,1,0:T(8,128)S(1)}, u32[]{:S(2)}, u32[]{:S(2)}) %collective-permute-start.2) | collective-permute-done | bytes 163872 | tf_op jit(solution)/shard_map/ppermute | solution.py:136
  60.5 8.2 %collective-permute-done.3.refs_1_.refs_2_ = bf16[2,64,10240]{2,1,0:T(8,128)(2,1)S(1)} collective-permute-done((bf16[2,64,10240]{2,1,0:T(8,128)(2,1)S(1)}, bf16[2,64,10240]{2,1,0:T(8,128)(2,1)S(1)}, u32[]{:S(2)}, u32[]{:S(2)}) %collective-permute-start.3) | collective-permute-done | bytes 2621472 | tf_op jit(solution)/shard_map/ppermute | solution.py:19
  68.7 2.4 %correlate.7.refs_2_ = f32[2,64,256]{2,1,0:T(8,128)S(1)} custom-call(bf16[10240,512]{1,0:T(8,128)(2,1)S(1)} %place.1.refs_0_.refs_3_, bf16[2,64,10240]{2,1,0:T(8,128)(2,1)S(1)} %collective-permute-done.3.refs_1_.refs_2_, f32[2,80,256]{2,1,0:T(8,128)S(1)} %correlate.6.refs_2_, f32[2,80,256]{2,1,0:T(8,128)S(1)} %add.37.refs_3_), custom_call_target="tpu_custom_call" | custom-call | bytes 1024 | tf_op jit(solution)/shard_map/correlate/pallas_call | solution.py:115
  72.7 4.7 %collective-permute-done.4 = f32[2,64,256]{2,1,0:T(8,128)S(1)} collective-permute-done((f32[2,64,256]{2,1,0:T(8,128)S(1)}, f32[2,64,256]{2,1,0:T(8,128)S(1)}, u32[]{:S(2)}, u32[]{:S(2)}) %collective-permute-start.4) | collective-permute-done | bytes 131104 | tf_op jit(solution)/shard_map/ppermute | solution.py:136
  77.4 2.7 %collective-permute-start.5 = (f32[2,64,256]{2,1,0:T(8,128)S(1)}, f32[2,64,256]{2,1,0:T(8,128)S(1)}, u32[]{:S(2)}, u32[]{:S(2)}) collective-permute-start(f32[2,64,256]{2,1,0:T(8,128)S(1)} %add.38), channel_id=1, source_target_pairs={{0,2},{1,3},{2,0},{3,1},{4,6},{5,7},{6,4},{7,5},{8,10},{9,11},{10,... | collective-permute-start | bytes 393224 | tf_op jit(solution)/shard_map/ppermute | solution.py:136
  81.2 8.5 %collective-permute-done.6.refs_1_.refs_2_ = bf16[2,48,10240]{2,1,0:T(8,128)(2,1)S(1)} collective-permute-done((bf16[2,48,10240]{2,1,0:T(8,128)(2,1)S(1)}, bf16[2,48,10240]{2,1,0:T(8,128)(2,1)S(1)}, u32[]{:S(2)}, u32[]{:S(2)}) %collective-permute-start.6) | collective-permute-done | bytes 1966112 | tf_op jit(solution)/shard_map/ppermute | solution.py:19
  90.8 2.0 %collective-permute-start.15 = (bf16[2,16,10240]{2,1,0:T(8,128)(2,1)S(1)}, bf16[2,16,10240]{2,1,0:T(8,128)(2,1)S(1)}, u32[]{:S(2)}, u32[]{:S(2)}) collective-permute-start(bf16[2,16,10240]{2,1,0:T(8,128)(2,1)S(1)} %cut.11), channel_id=1, source_target_pairs={{0,12},{4,0},{8,4},{12,8},{1,13},{5,1},{9,5},{13,9},{2,14},{6,2},{... | collective-permute-start | bytes 1966088 | tf_op jit(solution)/shard_map/ppermute | solution.py:19
  92.8 2.1 %correlate.8.refs_2_ = f32[2,48,256]{2,1,0:T(8,128)S(1)} custom-call(bf16[10240,512]{1,0:T(8,128)(2,1)S(1)} %place.1.refs_0_.refs_3_, bf16[2,48,10240]{2,1,0:T(8,128)(2,1)S(1)} %collective-permute-done.6.refs_1_.refs_2_, f32[2,64,256]{2,1,0:T(8,128)S(1)} %correlate.7.refs_2_, f32[2,64,256]{2,1,0:T(8,128)S(1)} %add.39.refs_3_), custom_call_target="tpu_custom_call" | custom-call | bytes 1024 | tf_op jit(solution)/shard_map/correlate/pallas_call | solution.py:115
  96.6 3.0 %collective-permute-done.7 = f32[2,48,256]{2,1,0:T(8,128)S(1)} collective-permute-done((f32[2,48,256]{2,1,0:T(8,128)S(1)}, f32[2,48,256]{2,1,0:T(8,128)S(1)}, u32[]{:S(2)}, u32[]{:S(2)}) %collective-permute-start.7) | collective-permute-done | bytes 98336 | tf_op jit(solution)/shard_map/ppermute | solution.py:136
  99.7 2.7 %collective-permute-start.8 = (f32[2,48,256]{2,1,0:T(8,128)S(1)}, f32[2,48,256]{2,1,0:T(8,128)S(1)}, u32[]{:S(2)}, u32[]{:S(2)}) collective-permute-start(f32[2,48,256]{2,1,0:T(8,128)S(1)} %add.40), channel_id=1, source_target_pairs={{0,2},{1,3},{2,0},{3,1},{4,6},{5,7},{6,4},{7,5},{8,10},{9,11},{10,... | collective-permute-start | bytes 294920 | tf_op jit(solution)/shard_map/ppermute | solution.py:136
  102.3 2.9 %collective-permute-done.8 = f32[2,48,256]{2,1,0:T(8,128)S(1)} collective-permute-done((f32[2,48,256]{2,1,0:T(8,128)S(1)}, f32[2,48,256]{2,1,0:T(8,128)S(1)}, u32[]{:S(2)}, u32[]{:S(2)}) %collective-permute-start.8) | collective-permute-done | bytes 98336 | tf_op jit(solution)/shard_map/ppermute | solution.py:136
  106.0 2.2 %correlate.9.refs_2_ = f32[2,32,256]{2,1,0:T(8,128)S(1)} custom-call(bf16[10240,512]{1,0:T(8,128)(2,1)S(1)} %place.1.refs_0_.refs_3_, bf16[2,32,10240]{2,1,0:T(8,128)(2,1)S(1)} %collective-permute-done.9.refs_1_, f32[2,48,256]{2,1,0:T(8,128)S(1)} %correlate.8.refs_2_, f32[2,48,256]{2,1,0:T(8,128)S(1)} %add.41.refs_3_), custom_call_target="tpu_custom_call" | custom-call | bytes 1024 | tf_op jit(solution)/shard_map/correlate/pallas_call | solution.py:115
  108.3 1.8 %collective-permute-start.10 = (f32[2,32,256]{2,1,0:T(8,128)S(1)}, f32[2,32,256]{2,1,0:T(8,128)S(1)}, u32[]{:S(2)}, u32[]{:S(2)}) collective-permute-start(f32[2,32,256]{2,1,0:T(8,128)S(1)} %correlate.9.refs_2_), channel_id=1, source_target_pairs={{0,1},{1,0},{2,3},{3,2},{4,5},{5,4},{6,7},{7,6},{8,9},{9,8},{10,11... | collective-permute-start | bytes 196616 | tf_op jit(solution)/shard_map/ppermute | solution.py:136
  110.0 4.2 %collective-permute-done.12.refs_1_ = bf16[2,16,10240]{2,1,0:T(8,128)(2,1)S(1)} collective-permute-done((bf16[2,16,10240]{2,1,0:T(8,128)(2,1)S(1)}, bf16[2,16,10240]{2,1,0:T(8,128)(2,1)S(1)}, u32[]{:S(2)}, u32[]{:S(2)}) %collective-permute-start.12) | collective-permute-done | bytes 655392 | tf_op jit(solution)/shard_map/ppermute | solution.py:19
  114.2 1.9 %correlate.10.refs_2_ = f32[2,16,256]{2,1,0:T(8,128)S(1)} custom-call(bf16[10240,512]{1,0:T(8,128)(2,1)S(1)} %place.1.refs_0_.refs_3_, bf16[2,16,10240]{2,1,0:T(8,128)(2,1)S(1)} %collective-permute-done.12.refs_1_, f32[2,32,256]{2,1,0:T(8,128)S(1)} %correlate.9.refs_2_, f32[2,48,256]{2,1,0:T(8,128)S(1)} %add.41.refs_3_), custom_call_target="tpu_custom_call" | custom-call | bytes 1024 | tf_op jit(solution)/shard_map/correlate/pallas_call | solution.py:115
  117.5 1.9 %collective-permute-start.11 = (f32[2,32,256]{2,1,0:T(8,128)S(1)}, f32[2,32,256]{2,1,0:T(8,128)S(1)}, u32[]{:S(2)}, u32[]{:S(2)}) collective-permute-start(f32[2,32,256]{2,1,0:T(8,128)S(1)} %add.42), channel_id=1, source_target_pairs={{0,2},{1,3},{2,0},{3,1},{4,6},{5,7},{6,4},{7,5},{8,10},{9,11},{10,... | collective-permute-start | bytes 196616 | tf_op jit(solution)/shard_map/ppermute | solution.py:136
  120.0 2.8 %collective-permute-start.14 = (f32[2,16,256]{2,1,0:T(8,128)S(1)}, f32[2,16,256]{2,1,0:T(8,128)S(1)}, u32[]{:S(2)}, u32[]{:S(2)}) collective-permute-start(f32[2,16,256]{2,1,0:T(8,128)S(1)} %add.44), channel_id=1, source_target_pairs={{0,2},{1,3},{2,0},{3,1},{4,6},{5,7},{6,4},{7,5},{8,10},{9,11},{10,... | collective-permute-start | bytes 98312 | tf_op jit(solution)/shard_map/ppermute | solution.py:136
  123.2 1.7 %collective-permute-done.14 = f32[2,16,256]{2,1,0:T(8,128)S(1)} collective-permute-done((f32[2,16,256]{2,1,0:T(8,128)S(1)}, f32[2,16,256]{2,1,0:T(8,128)S(1)}, u32[]{:S(2)}, u32[]{:S(2)}) %collective-permute-start.14) | collective-permute-done | bytes 32800 | tf_op jit(solution)/shard_map/ppermute | solution.py:136
  125.0 4.0 %copy-done.1 = bf16[10240,512]{1,0:T(8,128)(2,1)S(1)} copy-done((bf16[10240,512]{1,0:T(8,128)(2,1)S(1)}, bf16[10240,512]{1,0:T(8,128)(2,1)}, u32[]{:S(2)}) %copy-start.1) | copy-done | bytes 10485784
  128.9 1.9 %correlate.11 = f32[2,16,256]{2,1,0:T(8,128)S(1)} custom-call(bf16[10240,512]{1,0:T(8,128)(2,1)S(1)} %copy-done.1, bf16[2,16,10240]{2,1,0:T(8,128)(2,1)S(1)} %collective-permute-done.15.refs_1_, f32[2,16,256]{2,1,0:T(8,128)S(1)} %correlate.10.refs_2_, f32[2,32,256]{2,1,0:T(8,128)S(1)} %add.43.refs_3_), custom_call_target="tpu_custom_call" | custom-call | bytes 1024 | tf_op jit(solution)/shard_map/correlate/pallas_call | solution.py:115
  132.2 2.5 %collective-permute-done.16 = f32[2,16,256]{2,1,0:T(8,128)S(1)} collective-permute-done((f32[2,16,256]{2,1,0:T(8,128)S(1)}, f32[2,16,256]{2,1,0:T(8,128)S(1)}, u32[]{:S(2)}, u32[]{:S(2)}) %collective-permute-start.16) | collective-permute-done | bytes 32800 | tf_op jit(solution)/shard_map/ppermute | solution.py:136
  134.8 2.9 %collective-permute-start.17 = (f32[2,16,256]{2,1,0:T(8,128)S(1)}, f32[2,16,256]{2,1,0:T(8,128)S(1)}, u32[]{:S(2)}, u32[]{:S(2)}) collective-permute-start(f32[2,16,256]{2,1,0:T(8,128)S(1)} %add.46), channel_id=1, source_target_pairs={{0,2},{1,3},{2,0},{3,1},{4,6},{5,7},{6,4},{7,5},{8,10},{9,11},{10,... | collective-permute-start | bytes 98312 | tf_op jit(solution)/shard_map/ppermute | solution.py:136
  140.2 2.7 %collective-permute-done.20 = f32[2,16,256]{2,1,0:T(8,128)S(1)} collective-permute-done((f32[2,16,256]{2,1,0:T(8,128)S(1)}, f32[2,16,256]{2,1,0:T(8,128)S(1)}, u32[]{:S(2)}, u32[]{:S(2)}) %collective-permute-start.20) | collective-permute-done | bytes 32800 | tf_op jit(solution)/shard_map/ppermute | solution.py:19
  (56 shorter events, 19.2 us)
Async XLA Ops:
  1.9 38.6 %collective-permute-start = (bf16[2,80,10240]{2,1,0:T(8,128)(2,1)S(1)}, bf16[2,80,10240]{2,1,0:T(8,128)(2,1)S(1)}, u32[]{:S(2)}, u32[]{:S(2)}) collective-permute-start(bf16[2,80,10240]{2,1,0:T(8,128)(2,1)S(1)} %cut.6.refs_1_), channel_id=1, source_target_pairs={{0,12},{4,0},{8,4},{12,8},{1,13},{5,1},{9,5},{13,9},{2,14},{6,2},{... | collective-permute-start | bytes 9830408 | tf_op jit(solution)/shard_map/ppermute | solution.py:19
  6.1 2.3 %copy-start.2 = (s32[1,2,10240]{2,1,0:T(2,128)S(1)}, s32[1,2,10240]{2,1,0:T(2,128)}, u32[]{:S(2)}) copy-start(s32[1,2,10240]{2,1,0:T(2,128)} %shift_ref.1) | copy-start | bytes 245764
  6.1 62.5 %collective-permute-start.3 = (bf16[2,64,10240]{2,1,0:T(8,128)(2,1)S(1)}, bf16[2,64,10240]{2,1,0:T(8,128)(2,1)S(1)}, u32[]{:S(2)}, u32[]{:S(2)}) collective-permute-start(bf16[2,64,10240]{2,1,0:T(8,128)(2,1)S(1)} %cut.7.refs_1_), channel_id=1, source_target_pairs={{0,12},{4,0},{8,4},{12,8},{1,13},{5,1},{9,5},{13,9},{2,14},{6,2},{... | collective-permute-start | bytes 7864328 | tf_op jit(solution)/shard_map/ppermute | solution.py:19
  8.4 81.4 %collective-permute-start.6 = (bf16[2,48,10240]{2,1,0:T(8,128)(2,1)S(1)}, bf16[2,48,10240]{2,1,0:T(8,128)(2,1)S(1)}, u32[]{:S(2)}, u32[]{:S(2)}) collective-permute-start(bf16[2,48,10240]{2,1,0:T(8,128)(2,1)S(1)} %cut.8.refs_1_), channel_id=1, source_target_pairs={{0,12},{4,0},{8,4},{12,8},{1,13},{5,1},{9,5},{13,9},{2,14},{6,2},{... | collective-permute-start | bytes 5898248 | tf_op jit(solution)/shard_map/ppermute | solution.py:19
  17.8 96.4 %copy-start = (bf16[10240,512]{1,0:T(8,128)(2,1)}, bf16[10240,512]{1,0:T(8,128)(2,1)S(1)}, u32[]{:S(2)}) copy-start(bf16[10240,512]{1,0:T(8,128)(2,1)S(1)} %place.1.refs_0_.refs_3_) | copy-start | bytes 31457284
  41.9 64.2 %collective-permute-start.9 = (bf16[2,32,10240]{2,1,0:T(8,128)(2,1)S(1)}, bf16[2,32,10240]{2,1,0:T(8,128)(2,1)S(1)}, u32[]{:S(2)}, u32[]{:S(2)}) collective-permute-start(bf16[2,32,10240]{2,1,0:T(8,128)(2,1)S(1)} %cut.9.refs_1_), channel_id=1, source_target_pairs={{0,12},{4,0},{8,4},{12,8},{1,13},{5,1},{9,5},{13,9},{2,14},{6,2},{... | collective-permute-start | bytes 3932168 | tf_op jit(solution)/shard_map/ppermute | solution.py:19
  46.6 5.4 %collective-permute-start.1 = (f32[2,80,256]{2,1,0:T(8,128)S(1)}, f32[2,80,256]{2,1,0:T(8,128)S(1)}, u32[]{:S(2)}, u32[]{:S(2)}) collective-permute-start(f32[2,80,256]{2,1,0:T(8,128)S(1)} %correlate.6.refs_2_), channel_id=1, source_target_pairs={{0,1},{1,0},{2,3},{3,2},{4,5},{5,4},{6,7},{7,6},{8,9},{9,8},{10,11... | collective-permute-start | bytes 491528 | tf_op jit(solution)/shard_map/ppermute | solution.py:136
  52.0 8.4 %collective-permute-start.2 = (f32[2,80,256]{2,1,0:T(8,128)S(1)}, f32[2,80,256]{2,1,0:T(8,128)S(1)}, u32[]{:S(2)}, u32[]{:S(2)}) collective-permute-start(f32[2,80,256]{2,1,0:T(8,128)S(1)} %add.36), channel_id=1, source_target_pairs={{0,2},{1,3},{2,0},{3,1},{4,6},{5,7},{6,4},{7,5},{8,10},{9,11},{10,... | collective-permute-start | bytes 491528 | tf_op jit(solution)/shard_map/ppermute | solution.py:136
  71.1 6.3 %collective-permute-start.4 = (f32[2,64,256]{2,1,0:T(8,128)S(1)}, f32[2,64,256]{2,1,0:T(8,128)S(1)}, u32[]{:S(2)}, u32[]{:S(2)}) collective-permute-start(f32[2,64,256]{2,1,0:T(8,128)S(1)} %correlate.7.refs_2_), channel_id=1, source_target_pairs={{0,1},{1,0},{2,3},{3,2},{4,5},{5,4},{6,7},{7,6},{8,9},{9,8},{10,11... | collective-permute-start | bytes 393224 | tf_op jit(solution)/shard_map/ppermute | solution.py:136
  77.4 15.4 %collective-permute-start.5 = (f32[2,64,256]{2,1,0:T(8,128)S(1)}, f32[2,64,256]{2,1,0:T(8,128)S(1)}, u32[]{:S(2)}, u32[]{:S(2)}) collective-permute-start(f32[2,64,256]{2,1,0:T(8,128)S(1)} %add.38), channel_id=1, source_target_pairs={{0,2},{1,3},{2,0},{3,1},{4,6},{5,7},{6,4},{7,5},{8,10},{9,11},{10,... | collective-permute-start | bytes 393224 | tf_op jit(solution)/shard_map/ppermute | solution.py:136
  81.1 33.1 %collective-permute-start.12 = (bf16[2,16,10240]{2,1,0:T(8,128)(2,1)S(1)}, bf16[2,16,10240]{2,1,0:T(8,128)(2,1)S(1)}, u32[]{:S(2)}, u32[]{:S(2)}) collective-permute-start(bf16[2,16,10240]{2,1,0:T(8,128)(2,1)S(1)} %cut.10.refs_1_), channel_id=1, source_target_pairs={{0,12},{4,0},{8,4},{12,8},{1,13},{5,1},{9,5},{13,9},{2,14},{6,2},{... | collective-permute-start | bytes 1966088 | tf_op jit(solution)/shard_map/ppermute | solution.py:19
  90.8 34.1 %collective-permute-start.15 = (bf16[2,16,10240]{2,1,0:T(8,128)(2,1)S(1)}, bf16[2,16,10240]{2,1,0:T(8,128)(2,1)S(1)}, u32[]{:S(2)}, u32[]{:S(2)}) collective-permute-start(bf16[2,16,10240]{2,1,0:T(8,128)(2,1)S(1)} %cut.11), channel_id=1, source_target_pairs={{0,12},{4,0},{8,4},{12,8},{1,13},{5,1},{9,5},{13,9},{2,14},{6,2},{... | collective-permute-start | bytes 1966088 | tf_op jit(solution)/shard_map/ppermute | solution.py:19
  95.0 4.7 %collective-permute-start.7 = (f32[2,48,256]{2,1,0:T(8,128)S(1)}, f32[2,48,256]{2,1,0:T(8,128)S(1)}, u32[]{:S(2)}, u32[]{:S(2)}) collective-permute-start(f32[2,48,256]{2,1,0:T(8,128)S(1)} %correlate.8.refs_2_), channel_id=1, source_target_pairs={{0,1},{1,0},{2,3},{3,2},{4,5},{5,4},{6,7},{7,6},{8,9},{9,8},{10,11... | collective-permute-start | bytes 294920 | tf_op jit(solution)/shard_map/ppermute | solution.py:136
  99.7 5.6 %collective-permute-start.8 = (f32[2,48,256]{2,1,0:T(8,128)S(1)}, f32[2,48,256]{2,1,0:T(8,128)S(1)}, u32[]{:S(2)}, u32[]{:S(2)}) collective-permute-start(f32[2,48,256]{2,1,0:T(8,128)S(1)} %add.40), channel_id=1, source_target_pairs={{0,2},{1,3},{2,0},{3,1},{4,6},{5,7},{6,4},{7,5},{8,10},{9,11},{10,... | collective-permute-start | bytes 294920 | tf_op jit(solution)/shard_map/ppermute | solution.py:136
  106.0 31.6 %collective-permute-start.18 = (f32[2,192,256]{2,1,0:T(8,128)}, f32[2,192,256]{2,1,0:T(8,128)S(1)}, u32[]{:S(2)}, u32[]{:S(2)}) collective-permute-start(f32[2,192,256]{2,1,0:T(8,128)} %pad_maximum_fusion), channel_id=1, source_target_pairs={{0,4},{4,8},{8,12},{12,0},{1,5},{5,9},{9,13},{13,1},{2,6},{6,10},{... | collective-permute-start | bytes 1179656 | tf_op jit(solution)/shard_map/ppermute | solution.py:19
  108.3 9.3 %collective-permute-start.10 = (f32[2,32,256]{2,1,0:T(8,128)S(1)}, f32[2,32,256]{2,1,0:T(8,128)S(1)}, u32[]{:S(2)}, u32[]{:S(2)}) collective-permute-start(f32[2,32,256]{2,1,0:T(8,128)S(1)} %correlate.9.refs_2_), channel_id=1, source_target_pairs={{0,1},{1,0},{2,3},{3,2},{4,5},{5,4},{6,7},{7,6},{8,9},{9,8},{10,11... | collective-permute-start | bytes 196616 | tf_op jit(solution)/shard_map/ppermute | solution.py:136
  116.1 3.9 %collective-permute-start.13 = (f32[2,16,256]{2,1,0:T(8,128)S(1)}, f32[2,16,256]{2,1,0:T(8,128)S(1)}, u32[]{:S(2)}, u32[]{:S(2)}) collective-permute-start(f32[2,16,256]{2,1,0:T(8,128)S(1)} %correlate.10.refs_2_), channel_id=1, source_target_pairs={{0,1},{1,0},{2,3},{3,2},{4,5},{5,4},{6,7},{7,6},{8,9},{9,8},{10,11... | collective-permute-start | bytes 98312 | tf_op jit(solution)/shard_map/ppermute | solution.py:136
  117.5 7.4 %collective-permute-start.11 = (f32[2,32,256]{2,1,0:T(8,128)S(1)}, f32[2,32,256]{2,1,0:T(8,128)S(1)}, u32[]{:S(2)}, u32[]{:S(2)}) collective-permute-start(f32[2,32,256]{2,1,0:T(8,128)S(1)} %add.42), channel_id=1, source_target_pairs={{0,2},{1,3},{2,0},{3,1},{4,6},{5,7},{6,4},{7,5},{8,10},{9,11},{10,... | collective-permute-start | bytes 196616 | tf_op jit(solution)/shard_map/ppermute | solution.py:136
  120.0 4.9 %collective-permute-start.14 = (f32[2,16,256]{2,1,0:T(8,128)S(1)}, f32[2,16,256]{2,1,0:T(8,128)S(1)}, u32[]{:S(2)}, u32[]{:S(2)}) collective-permute-start(f32[2,16,256]{2,1,0:T(8,128)S(1)} %add.44), channel_id=1, source_target_pairs={{0,2},{1,3},{2,0},{3,1},{4,6},{5,7},{6,4},{7,5},{8,10},{9,11},{10,... | collective-permute-start | bytes 98312 | tf_op jit(solution)/shard_map/ppermute | solution.py:136
  125.0 4.0 %copy-start.1 = (bf16[10240,512]{1,0:T(8,128)(2,1)S(1)}, bf16[10240,512]{1,0:T(8,128)(2,1)}, u32[]{:S(2)}) copy-start(bf16[10240,512]{1,0:T(8,128)(2,1)} %copy-done) | copy-start | bytes 31457284
  130.8 3.9 %collective-permute-start.16 = (f32[2,16,256]{2,1,0:T(8,128)S(1)}, f32[2,16,256]{2,1,0:T(8,128)S(1)}, u32[]{:S(2)}, u32[]{:S(2)}) collective-permute-start(f32[2,16,256]{2,1,0:T(8,128)S(1)} %correlate.11), channel_id=1, source_target_pairs={{0,1},{1,0},{2,3},{3,2},{4,5},{5,4},{6,7},{7,6},{8,9},{9,8},{10,11... | collective-permute-start | bytes 98312 | tf_op jit(solution)/shard_map/ppermute | solution.py:136
  132.2 8.0 %collective-permute-start.19 = (f32[2,48,256]{2,1,0:T(8,128)S(1)}, f32[2,48,256]{2,1,0:T(8,128)S(1)}, u32[]{:S(2)}, u32[]{:S(2)}) collective-permute-start(f32[2,48,256]{2,1,0:T(8,128)S(1)} %pad_maximum_fusion.1), channel_id=1, source_target_pairs={{0,4},{4,8},{8,12},{12,0},{1,5},{5,9},{9,13},{13,1},{2,6},{6,10},{... | collective-permute-start | bytes 294920 | tf_op jit(solution)/shard_map/ppermute | solution.py:19
  134.8 4.8 %collective-permute-start.17 = (f32[2,16,256]{2,1,0:T(8,128)S(1)}, f32[2,16,256]{2,1,0:T(8,128)S(1)}, u32[]{:S(2)}, u32[]{:S(2)}) collective-permute-start(f32[2,16,256]{2,1,0:T(8,128)S(1)} %add.46), channel_id=1, source_target_pairs={{0,2},{1,3},{2,0},{3,1},{4,6},{5,7},{6,4},{7,5},{8,10},{9,11},{10,... | collective-permute-start | bytes 98312 | tf_op jit(solution)/shard_map/ppermute | solution.py:136
  139.6 3.3 %collective-permute-start.20 = (f32[2,16,256]{2,1,0:T(8,128)S(1)}, f32[2,16,256]{2,1,0:T(8,128)S(1)}, u32[]{:S(2)}, u32[]{:S(2)}) collective-permute-start(f32[2,16,256]{2,1,0:T(8,128)S(1)} %add.47), channel_id=1, source_target_pairs={{0,4},{4,8},{8,12},{12,0},{1,5},{5,9},{9,13},{13,1},{2,6},{6,10},{... | collective-permute-start | bytes 98312 | tf_op jit(solution)/shard_map/ppermute | solution.py:19

commit v4 on v3

--- a/solution.py
+++ b/solution.py
@@ -8,7 +8,7 @@
 from jax.sharding import PartitionSpec as P
 
 PWB = 256
-SIXTEENTHS = (5, 4, 3, 2, 1, 1)
+SIXTEENTHS = (5, 4, 3, 2, 2)
 MIB = 1 << 20
 ANYWHERE = pl.BlockSpec(memory_space=pl.ANY)
 WHOLE = pl.BlockSpec(memory_space=pltpu.VMEM)
@@ -79,51 +79,53 @@
     )(coefficients, shifts)
 
 
-def correlate_kernel(steps, *refs):
-    placed_ref, block_ref, out_ref, total = refs[0], refs[1], refs[-2], refs[-1]
-    some, depth = block_ref.shape[1:]
+def correlate_kernel(out_at, depth, placed_ref, block_ref, *refs):
+    out_ref, total = refs[out_at], refs[-1]
+    some, width = block_ref.shape[1:]
     bands = out_ref.shape[2]
-    step = pl.program_id(0)
-    start = pl.multiple_of(step * depth, PWB)
-    product = jnp.dot(
-        block_ref[...].reshape(2 * some, depth),
-        placed_ref[pl.ds(start, depth), :],
-        preferred_element_type=jnp.float32,
-    )
-
-    @pl.when(step == 0)
-    def _():
-        total[...] = product
-
-    @pl.when(step > 0)
-    def _():
-        total[...] += product
-
-    @pl.when(step == steps - 1)
-    def _():
-        out_ref[0] = total[:some, :bands] + total[some:, bands:]
-        out_ref[1] = total[some:, :bands] - total[:some, bands:]
-
-
-def correlate(placed, block, *others):
+
+    def product_of(start):
+        return jnp.dot(
+            block_ref[:, :, pl.ds(start, depth)].reshape(2 * some, depth),
+            placed_ref[pl.ds(start, depth), :],
+            preferred_element_type=jnp.float32,
+        )
+
+    total[...] = product_of(0)
+
+    @pl.loop(1, width // depth)
+    def _(step):
+        total[...] += product_of(pl.multiple_of(step * depth, depth))
+
+    out_ref[0] = total[:some, :bands] + total[some:, bands:]
+    out_ref[1] = total[some:, :bands] - total[:some, bands:]
+
+
+def correlate(placed, block, *others, held=None):
     some, width = block.shape[1:]
     bands = placed.shape[1] // 2
     depth = width
-    while depth % (2 * PWB) == 0 and some * depth > 1 << 18:
+    while depth % (2 * PWB) == 0 and some * depth > 1 << 19:
         depth //= 2
-    steps = width // depth
-    return pl.pallas_call(
-        functools.partial(correlate_kernel, steps),
-        grid=(steps,),
-        out_shape=jax.ShapeDtypeStruct((2, some, bands), jnp.float32),
-        in_specs=[WHOLE, pl.BlockSpec((2, some, depth), lambda g: (0, 0, g))]
-        + [ANYWHERE] * len(others),
-        out_specs=pl.BlockSpec((2, some, bands), lambda g: (0, 0, 0)),
+    block = pltpu.with_memory_space_constraint(block, pltpu.VMEM)
+    out_shape = [jax.ShapeDtypeStruct((2, some, bands), jnp.float32)]
+    aliases = {}
+    if held is not None:
+        others = (*others, held)
+        aliases = {1 + len(others): 1}
+        out_shape.append(jax.ShapeDtypeStruct(held.shape, held.dtype))
+    out = pl.pallas_call(
+        functools.partial(correlate_kernel, len(others), depth),
+        out_shape=out_shape,
+        in_specs=[WHOLE, WHOLE] + [ANYWHERE] * len(others),
+        out_specs=[WHOLE, ANYWHERE][: len(out_shape)],
         scratch_shapes=[pltpu.VMEM((2 * some, 2 * bands), jnp.float32)],
+        input_output_aliases=aliases,
         compiler_params=pltpu.CompilerParams(vmem_limit_bytes=16 * MIB),
         cost_estimate=pl.CostEstimate(flops=0, bytes_accessed=1024, transcendentals=0),
         name="correlate",
     )(placed, block, *others)
+    return out[0] if held is None else out
 
 
 def summed_over_pw(partial):
@@ -132,10 +134,69 @@
         return partial + sum(moved(partial, "pw", d) for d in range(1, pw))
     distance = 1
     while distance < pw:
-        route = [(i, i ^ distance) for i in range(pw)]
-        partial = partial + lax.ppermute(partial, "pw", route)
+        partial = partial + lax.ppermute(partial, "pw", [(i, i ^ distance) for i in range(pw)])
         distance *= 2
     return partial
+
+
+def sums_here_and_next(partial):
+    ka, pw = lax.axis_size("ka"), lax.axis_size("pw")
+    if pw & (pw - 1) or pw == 1:
+        whole = summed_over_pw(partial)
+        return [whole], [moved(whole, "ka", 1)]
+    distance = 1
+    while 2 * distance < pw:
+        partial = partial + lax.ppermute(partial, "pw", [(i, i ^ distance) for i in range(pw)])
+        distance *= 2
+    here = lax.ppermute(partial, "pw", [(i, i ^ distance) for i in range(pw)])
+    across = [
+        (k * pw + p, (k + 1) % ka * pw + (p ^ distance)) for k in range(ka) for p in range(pw)
+    ]
+    before = [moved(partial, "ka", 1), lax.ppermute(partial, ("ka", "pw"), across)]
+    return [partial, here], before
+
+
+def assemble_kernel(ahead_count, *refs):
+    ins, (out_ref, made, sems) = refs[:-3], refs[-3:]
+    most_ref, most_before_ref = ins[:2]
+    last_refs = ins[2 : 2 + ahead_count], ins[2 + ahead_count :]
+    copies = []
+    for side in (1, 0):
+        for c in (0, 1):
+            early = (most_ref, most_before_ref)[side][c]
+            late = sum(ref[c] for ref in last_refs[side])
+            matrix = jnp.concatenate([early, late], axis=0)
+            if side == 0:
+                matrix = matrix.T
+            elif c == 1:
+                matrix = -matrix
+            made[2 * side + c] = matrix
+            copies.append(
+                pltpu.make_async_copy(
+                    made.at[2 * side + c], out_ref.at[0, side, c], sems.at[2 * side + c]
+                )
+            )
+            copies[-1].start()
+    for copy in copies:
+        copy.wait()
+
+
+def assembled(most, most_before, last, last_before):
+    bands = most.shape[2]
+    count = 2 + len(last) + len(last_before)
+    return pl.pallas_call(
+        functools.partial(assemble_kernel, len(last)),
+        out_shape=jax.ShapeDtypeStruct((1, 2, 2, bands, bands), jnp.float32),
+        in_specs=[WHOLE] * count,
+        out_specs=ANYWHERE,
+        scratch_shapes=[
+            pltpu.VMEM((4, bands, bands), jnp.float32),
+            pltpu.SemaphoreType.DMA((4,)),
+        ],
+        compiler_params=pltpu.CompilerParams(vmem_limit_bytes=16 * MIB),
+        cost_estimate=pl.CostEstimate(flops=0, bytes_accessed=1024, transcendentals=0),
+        name="assemble",
+    )(most, most_before, *last, *last_before)
 
 
 def local(coefficients, shifts):
@@ -146,23 +207,25 @@
         edges.append(edges[-1] + size * unit)
     coefficients = pltpu.with_memory_space_constraint(coefficients, pltpu.HBM)
     placed = pltpu.with_memory_space_constraint(placed_bands(coefficients, shifts), pltpu.VMEM)
-    blocks, arrived = [], []
-    for chunk, (low, high) in enumerate(zip(edges, edges[1:])):
-        before = blocks[-1:] + ([arrived[chunk - 3], placed] if chunk >= 3 else [])
-        blocks.append(cut(coefficients, low, high, *before))
+    blocks, arrived, whole = [], [], []
+
+    def send(chunk, *others):
+        blocks.append(
+            cut(coefficients, edges[chunk], edges[chunk + 1], *blocks[-1:], *others)
+        )
         arrived.append(moved(blocks[-1], "ka", -1))
-    partial, whole = [], []
-    for chunk, block in enumerate(arrived):
-        before = partial[-1:] + whole[max(0, chunk - 1 - (chunk > 3)) : chunk - (chunk > 3)]
-        partial.append(correlate(placed, block, *before))
-        whole.append(summed_over_pw(partial[-1]))
-    behind = [
-        moved(jnp.concatenate(some, axis=1), "ka", 1)
-        for some in (whole[:3], whole[3:5], whole[5:])
-    ]
-    ahead = jnp.swapaxes(jnp.concatenate(whole, axis=1), 1, 2)
-    behind = jnp.concatenate(behind, axis=1)
-    return jnp.stack([ahead, jnp.stack([behind[0], -behind[1]])])[None]
+
+    for chunk in range(3):
+        send(chunk)
+    send(3, arrived[0], placed)
+    for chunk in range(4):
+        if chunk == 1:
+            send(4, arrived[1], whole[0])
+        whole.append(summed_over_pw(correlate(placed, arrived[chunk], *whole[-1:])))
+    most = jnp.concatenate(whole, axis=1)
+    last, most = correlate(placed, arrived[-1], held=most)
+    most_before = moved(most, "ka", 1)
+    return assembled(most, most_before, *sums_here_and_next(last))
 
 
 def solution(mesh):

time: 145 us -> 136 us (0.938)
  local copies, waits for them, and re-layouts: 5.24 us -> 0.01 us
  waiting for transfers between devices: 72.9 us -> 77.3 us
  Pallas kernels: 31.3 us -> 27.1 us
  starting transfers between devices: 32.3 us -> 29.3 us
  other arithmetic: 2.07 us -> 0.16 us
    ppermute x12 -> x11, waiting for transfers between devices: 26.5 us -> 39.6 us  [the longest x8 34.1 us: summed_over_pw(): lax.ppermute(partial, 'pw', [(i, i ^ distance) for i in range(pw)])]
    ppermute x9 -> x7, waiting for transfers between devices: 46.4 us -> 37.7 us  [moved(): lax.ppermute(block, axis, [(i, (i + distance) % count) for i in range(cou...]
    unnamed x8 -> x2, local copies, waits for them, and re-layouts: 4.02 us -> 0.01 us
    ppermute x12 -> x11, starting transfers between devices: 25.1 us -> 21.6 us  [the longest x8 15.8 us: summed_over_pw(): lax.ppermute(partial, 'pw', [(i, i ^ distance) for i in range(pw)])]
    pallas_call x6, Pallas kernels: 13.3 us -> 10 us  [the longest x5 8.99 us: correlate(): pl.pallas_call(functools.partial(correlate_kernel, len(others), depth), o...]
    pallas_call x6 -> x5, Pallas kernels: 8.65 us -> 7.78 us  [cut(): pl.pallas_call(functools.partial(cut_kernel, low, high), out_shape=jax.Sh...]
    ppermute x9 -> x7, starting transfers between devices: 7.25 us -> 7.76 us  [moved(): lax.ppermute(block, axis, [(i, (i + distance) % count) for i in range(cou...]
  transfers between devices with their start and end apart: 21 -> 18, of which waited for: 14 -> 16; matrix products, arithmetic and copies ran while one was open for 2% -> 0% of each run, Pallas kernels for 20% -> 17%
where the time goes in v4:
time: 136 us; the launch traced here: 134 us
  waiting for transfers between devices  77.3 us (57%)
  starting transfers between devices  29.3 us (22%)
  Pallas kernels  27.1 us (20%)
    ppermute x7, waiting for transfers between devices, moved(): lax.ppermute(block, axis, [(i, (i + distance) % count) for i in range(cou...  37.7 us
    ppermute x8, waiting for transfers between devices, summed_over_pw(): lax.ppermute(partial, 'pw', [(i, i ^ distance) for i in range(pw)])  34.1 us
    ppermute x8, starting transfers between devices, summed_over_pw(): lax.ppermute(partial, 'pw', [(i, i ^ distance) for i in range(pw)])  15.8 us
    pallas_call x1, Pallas kernels, placed_bands(): pl.pallas_call(place_kernel, grid=(width // step,), out_shape=pltpu.VMEM(...  9.34 us
    pallas_call x5, Pallas kernels, correlate(): pl.pallas_call(functools.partial(correlate_kernel, len(others), depth), o...  8.99 us
    pallas_call x5, Pallas kernels, cut(): pl.pallas_call(functools.partial(cut_kernel, low, high), out_shape=jax.Sh...  7.78 us
    ppermute x7, starting transfers between devices, moved(): lax.ppermute(block, axis, [(i, (i + distance) % count) for i in range(cou...  7.76 us
  transfers between devices with their start and end apart: 18, of which 16 were waited for; matrix products, arithmetic and copies ran while one was open for 0% of the time, Pallas kernels for 17%

profile of v4, /device:TPU:0, one launch (start us, length us, event | category | flops | bytes accessed | tf_op | source)
XLA Modules:
  0.0 134.1 jit_solution(6853318114082774001)
XLA Ops:
  0.0 1.9 %cut.5.refs_1_ = bf16[2,80,10240]{2,1,0:T(8,128)(2,1)S(1)} custom-call(bf16[1,2,256,10240]{3,2,1,0:T(8,128)(2,1)} %refs_0_.9), custom_call_target="tpu_custom_call" | custom-call | bytes 1024 | tf_op jit(solution)/shard_map/cut/pallas_call | solution.py:36
  1.9 2.4 %collective-permute-start = (bf16[2,80,10240]{2,1,0:T(8,128)(2,1)S(1)}, bf16[2,80,10240]{2,1,0:T(8,128)(2,1)S(1)}, u32[]{:S(2)}, u32[]{:S(2)}) collective-permute-start(bf16[2,80,10240]{2,1,0:T(8,128)(2,1)S(1)} %cut.5.refs_1_), channel_id=1, source_target_pairs={{0,12},{4,0},{8,4},{12,8},{1,13},{5,1},{9,5},{13,9},{2,14},{6,2},{... | collective-permute-start | bytes 9830408 | tf_op jit(solution)/shard_map/ppermute | solution.py:19
  4.4 1.7 %cut.6.refs_1_ = bf16[2,64,10240]{2,1,0:T(8,128)(2,1)S(1)} custom-call(bf16[1,2,256,10240]{3,2,1,0:T(8,128)(2,1)} %refs_0_.9, bf16[2,80,10240]{2,1,0:T(8,128)(2,1)S(1)} %cut.5.refs_1_), custom_call_target="tpu_custom_call" | custom-call | bytes 1024 | tf_op jit(solution)/shard_map/cut/pallas_call | solution.py:36
  8.4 9.3 %place.1.refs_3_.placed_ref = bf16[10240,512]{1,0:T(8,128)(2,1)S(1)} custom-call(bf16[1,2,256,10240]{3,2,1,0:T(8,128)(2,1)} %refs_0_.9, s32[1,2,10240]{2,1,0:T(2,128)S(1)} %copy-done), custom_call_target="tpu_custom_call" | custom-call | bytes 1024 | tf_op jit(solution)/shard_map/place/pallas_call | solution.py:67
  17.8 22.8 %collective-permute-done.refs_2_.block_ref = bf16[2,80,10240]{2,1,0:T(8,128)(2,1)S(1)} collective-permute-done((bf16[2,80,10240]{2,1,0:T(8,128)(2,1)S(1)}, bf16[2,80,10240]{2,1,0:T(8,128)(2,1)S(1)}, u32[]{:S(2)}, u32[]{:S(2)}) %collective-permute-start) | collective-permute-done | bytes 3276832 | tf_op jit(solution)/shard_map/ppermute | solution.py:19
  40.6 1.9 %correlate.5 = f32[2,80,256]{2,1,0:T(8,128)S(1)} custom-call(bf16[10240,512]{1,0:T(8,128)(2,1)S(1)} %place.1.refs_3_.placed_ref, bf16[2,80,10240]{2,1,0:T(8,128)(2,1)S(1)} %collective-permute-done.refs_2_.block_ref), custom_call_target="tpu_custom_call" | custom-call | bytes 1024 | tf_op jit(solution)/shard_map/correlate/pallas_call | solution.py:117
  42.4 1.6 %collective-permute-start.2 = (f32[2,80,256]{2,1,0:T(8,128)S(1)}, f32[2,80,256]{2,1,0:T(8,128)S(1)}, u32[]{:S(2)}, u32[]{:S(2)}) collective-permute-start(f32[2,80,256]{2,1,0:T(8,128)S(1)} %correlate.5), channel_id=1, source_target_pairs={{0,1},{1,0},{2,3},{3,2},{4,5},{5,4},{6,7},{7,6},{8,9},{9,8},{10,11... | collective-permute-start | bytes 491528 | tf_op jit(solution)/shard_map/ppermute | solution.py:137
  45.4 1.7 %collective-permute-start.10 = (bf16[2,32,10240]{2,1,0:T(8,128)(2,1)S(1)}, bf16[2,32,10240]{2,1,0:T(8,128)(2,1)S(1)}, u32[]{:S(2)}, u32[]{:S(2)}) collective-permute-start(bf16[2,32,10240]{2,1,0:T(8,128)(2,1)S(1)} %cut.8.refs_1_), channel_id=1, source_target_pairs={{0,12},{4,0},{8,4},{12,8},{1,13},{5,1},{9,5},{13,9},{2,14},{6,2},{... | collective-permute-start | bytes 3932168 | tf_op jit(solution)/shard_map/ppermute | solution.py:19
  47.1 2.4 %collective-permute-done.2 = f32[2,80,256]{2,1,0:T(8,128)S(1)} collective-permute-done((f32[2,80,256]{2,1,0:T(8,128)S(1)}, f32[2,80,256]{2,1,0:T(8,128)S(1)}, u32[]{:S(2)}, u32[]{:S(2)}) %collective-permute-start.2) | collective-permute-done | bytes 163872 | tf_op jit(solution)/shard_map/ppermute | solution.py:137
  49.5 2.7 %collective-permute-start.3 = (f32[2,80,256]{2,1,0:T(8,128)S(1)}, f32[2,80,256]{2,1,0:T(8,128)S(1)}, u32[]{:S(2)}, u32[]{:S(2)}) collective-permute-start(f32[2,80,256]{2,1,0:T(8,128)S(1)} %add.27), channel_id=1, source_target_pairs={{0,2},{1,3},{2,0},{3,1},{4,6},{5,7},{6,4},{7,5},{8,10},{9,11},{10,... | collective-permute-start | bytes 491528 | tf_op jit(solution)/shard_map/ppermute | solution.py:137
  52.1 7.9 %collective-permute-done.3 = f32[2,80,256]{2,1,0:T(8,128)S(1)} collective-permute-done((f32[2,80,256]{2,1,0:T(8,128)S(1)}, f32[2,80,256]{2,1,0:T(8,128)S(1)}, u32[]{:S(2)}, u32[]{:S(2)}) %collective-permute-start.3) | collective-permute-done | bytes 163872 | tf_op jit(solution)/shard_map/ppermute | solution.py:137
  60.1 8.6 %collective-permute-done.1.refs_2_.block_ref = bf16[2,64,10240]{2,1,0:T(8,128)(2,1)S(1)} collective-permute-done((bf16[2,64,10240]{2,1,0:T(8,128)(2,1)S(1)}, bf16[2,64,10240]{2,1,0:T(8,128)(2,1)S(1)}, u32[]{:S(2)}, u32[]{:S(2)}) %collective-permute-start.1) | collective-permute-done | bytes 2621472 | tf_op jit(solution)/shard_map/ppermute | solution.py:19
  70.0 2.0 %collective-permute-start.4 = (bf16[2,32,10240]{2,1,0:T(8,128)(2,1)S(1)}, bf16[2,32,10240]{2,1,0:T(8,128)(2,1)S(1)}, u32[]{:S(2)}, u32[]{:S(2)}) collective-permute-start(bf16[2,32,10240]{2,1,0:T(8,128)(2,1)S(1)} %cut.9), channel_id=1, source_target_pairs={{0,12},{4,0},{8,4},{12,8},{1,13},{5,1},{9,5},{13,9},{2,14},{6,2},{... | collective-permute-start | bytes 3932168 | tf_op jit(solution)/shard_map/ppermute | solution.py:19
  73.5 1.6 %collective-permute-start.5 = (f32[2,64,256]{2,1,0:T(8,128)S(1)}, f32[2,64,256]{2,1,0:T(8,128)S(1)}, u32[]{:S(2)}, u32[]{:S(2)}) collective-permute-start(f32[2,64,256]{2,1,0:T(8,128)S(1)} %correlate.6), channel_id=1, source_target_pairs={{0,1},{1,0},{2,3},{3,2},{4,5},{5,4},{6,7},{7,6},{8,9},{9,8},{10,11... | collective-permute-start | bytes 393224 | tf_op jit(solution)/shard_map/ppermute | solution.py:137
  75.1 3.4 %collective-permute-done.5 = f32[2,64,256]{2,1,0:T(8,128)S(1)} collective-permute-done((f32[2,64,256]{2,1,0:T(8,128)S(1)}, f32[2,64,256]{2,1,0:T(8,128)S(1)}, u32[]{:S(2)}, u32[]{:S(2)}) %collective-permute-start.5) | collective-permute-done | bytes 131104 | tf_op jit(solution)/shard_map/ppermute | solution.py:137
  78.5 2.7 %collective-permute-start.6 = (f32[2,64,256]{2,1,0:T(8,128)S(1)}, f32[2,64,256]{2,1,0:T(8,128)S(1)}, u32[]{:S(2)}, u32[]{:S(2)}) collective-permute-start(f32[2,64,256]{2,1,0:T(8,128)S(1)} %add.29), channel_id=1, source_target_pairs={{0,2},{1,3},{2,0},{3,1},{4,6},{5,7},{6,4},{7,5},{8,10},{9,11},{10,... | collective-permute-start | bytes 393224 | tf_op jit(solution)/shard_map/ppermute | solution.py:137
  81.2 4.7 %collective-permute-done.6 = f32[2,64,256]{2,1,0:T(8,128)S(1)} collective-permute-done((f32[2,64,256]{2,1,0:T(8,128)S(1)}, f32[2,64,256]{2,1,0:T(8,128)S(1)}, u32[]{:S(2)}, u32[]{:S(2)}) %collective-permute-start.6) | collective-permute-done | bytes 131104 | tf_op jit(solution)/shard_map/ppermute | solution.py:137
  85.9 3.9 %collective-permute-done.7.block_ref = bf16[2,48,10240]{2,1,0:T(8,128)(2,1)S(1)} collective-permute-done((bf16[2,48,10240]{2,1,0:T(8,128)(2,1)S(1)}, bf16[2,48,10240]{2,1,0:T(8,128)(2,1)S(1)}, u32[]{:S(2)}, u32[]{:S(2)}) %collective-permute-start.7) | collective-permute-done | bytes 1966112 | tf_op jit(solution)/shard_map/ppermute | solution.py:19
  89.7 1.8 %correlate.7 = f32[2,48,256]{2,1,0:T(8,128)S(1)} custom-call(bf16[10240,512]{1,0:T(8,128)(2,1)S(1)} %place.1.refs_3_.placed_ref, bf16[2,48,10240]{2,1,0:T(8,128)(2,1)S(1)} %collective-permute-done.7.block_ref, f32[2,64,256]{2,1,0:T(8,128)S(1)} %add.30.refs_0_), custom_call_target="tpu_custom_call" | custom-call | bytes 1024 | tf_op jit(solution)/shard_map/correlate/pallas_call | solution.py:117
  91.5 1.6 %collective-permute-start.8 = (f32[2,48,256]{2,1,0:T(8,128)S(1)}, f32[2,48,256]{2,1,0:T(8,128)S(1)}, u32[]{:S(2)}, u32[]{:S(2)}) collective-permute-start(f32[2,48,256]{2,1,0:T(8,128)S(1)} %correlate.7), channel_id=1, source_target_pairs={{0,1},{1,0},{2,3},{3,2},{4,5},{5,4},{6,7},{7,6},{8,9},{9,8},{10,11... | collective-permute-start | bytes 294920 | tf_op jit(solution)/shard_map/ppermute | solution.py:137
  93.2 4.0 %collective-permute-done.8 = f32[2,48,256]{2,1,0:T(8,128)S(1)} collective-permute-done((f32[2,48,256]{2,1,0:T(8,128)S(1)}, f32[2,48,256]{2,1,0:T(8,128)S(1)}, u32[]{:S(2)}, u32[]{:S(2)}) %collective-permute-start.8) | collective-permute-done | bytes 98336 | tf_op jit(solution)/shard_map/ppermute | solution.py:137
  97.2 2.7 %collective-permute-start.9 = (f32[2,48,256]{2,1,0:T(8,128)S(1)}, f32[2,48,256]{2,1,0:T(8,128)S(1)}, u32[]{:S(2)}, u32[]{:S(2)}) collective-permute-start(f32[2,48,256]{2,1,0:T(8,128)S(1)} %add.31), channel_id=1, source_target_pairs={{0,2},{1,3},{2,0},{3,1},{4,6},{5,7},{6,4},{7,5},{8,10},{9,11},{10,... | collective-permute-start | bytes 294920 | tf_op jit(solution)/shard_map/ppermute | solution.py:137
  99.8 5.1 %collective-permute-done.9 = f32[2,48,256]{2,1,0:T(8,128)S(1)} collective-permute-done((f32[2,48,256]{2,1,0:T(8,128)S(1)}, f32[2,48,256]{2,1,0:T(8,128)S(1)}, u32[]{:S(2)}, u32[]{:S(2)}) %collective-permute-start.9) | collective-permute-done | bytes 98336 | tf_op jit(solution)/shard_map/ppermute | solution.py:137
  104.9 1.9 %correlate.8 = f32[2,32,256]{2,1,0:T(8,128)S(1)} custom-call(bf16[10240,512]{1,0:T(8,128)(2,1)S(1)} %place.1.refs_3_.placed_ref, bf16[2,32,10240]{2,1,0:T(8,128)(2,1)S(1)} %collective-permute-done.10.block_ref, f32[2,48,256]{2,1,0:T(8,128)S(1)} %add.32.refs_0_), custom_call_target="tpu_custom_call" | custom-call | bytes 1024 | tf_op jit(solution)/shard_map/correlate/pallas_call | solution.py:117
  107.6 3.6 %collective-permute-done.11 = f32[2,32,256]{2,1,0:T(8,128)S(1)} collective-permute-done((f32[2,32,256]{2,1,0:T(8,128)S(1)}, f32[2,32,256]{2,1,0:T(8,128)S(1)}, u32[]{:S(2)}, u32[]{:S(2)}) %collective-permute-start.11) | collective-permute-done | bytes 65568 | tf_op jit(solution)/shard_map/ppermute | solution.py:137
  111.2 2.2 %collective-permute-start.12 = (f32[2,32,256]{2,1,0:T(8,128)S(1)}, f32[2,32,256]{2,1,0:T(8,128)S(1)}, u32[]{:S(2)}, u32[]{:S(2)}) collective-permute-start(f32[2,32,256]{2,1,0:T(8,128)S(1)} %add.33), channel_id=1, source_target_pairs={{0,2},{1,3},{2,0},{3,1},{4,6},{5,7},{6,4},{7,5},{8,10},{9,11},{10,... | collective-permute-start | bytes 196616 | tf_op jit(solution)/shard_map/ppermute | solution.py:137
  113.4 3.1 %collective-permute-done.12 = f32[2,32,256]{2,1,0:T(8,128)S(1)} collective-permute-done((f32[2,32,256]{2,1,0:T(8,128)S(1)}, f32[2,32,256]{2,1,0:T(8,128)S(1)}, u32[]{:S(2)}, u32[]{:S(2)}) %collective-permute-start.12) | collective-permute-done | bytes 65568 | tf_op jit(solution)/shard_map/ppermute | solution.py:137
  117.8 1.9 %correlate.9 = (f32[2,32,256]{2,1,0:T(8,128)S(1)}, f32[2,224,256]{2,1,0:T(8,128)S(1)}) custom-call(bf16[10240,512]{1,0:T(8,128)(2,1)S(1)} %place.1.refs_3_.placed_ref, bf16[2,32,10240]{2,1,0:T(8,128)(2,1)S(1)} %collective-permute-done.4.block_ref, f32[2,224,256]{2,1,0:T(8,128)S(1)} %pad_maximum_fusion.refs_0_), custom_call_target="tpu_custom_call", output_to_operand_aliasing={{1}: (2, {})} | custom-call | bytes 1024 | tf_op jit(solution)/shard_map/correlate/pallas_call | solution.py:117
  120.6 1.6 %collective-permute-start.14 = (f32[2,32,256]{2,1,0:T(8,128)S(1)}, f32[2,32,256]{2,1,0:T(8,128)S(1)}, u32[]{:S(2)}, u32[]{:S(2)}) collective-permute-start(f32[2,32,256]{2,1,0:T(8,128)S(1)} %get-tuple-element.8), channel_id=1, source_target_pairs={{0,1},{1,0},{2,3},{3,2},{4,5},{5,4},{6,7},{7,6},{8,9},{9,8},{10,11... | collective-permute-start | bytes 196616 | tf_op jit(solution)/shard_map/ppermute | solution.py:149
  122.2 2.7 %collective-permute-done.14 = f32[2,32,256]{2,1,0:T(8,128)S(1)} collective-permute-done((f32[2,32,256]{2,1,0:T(8,128)S(1)}, f32[2,32,256]{2,1,0:T(8,128)S(1)}, u32[]{:S(2)}, u32[]{:S(2)}) %collective-permute-start.14) | collective-permute-done | bytes 65568 | tf_op jit(solution)/shard_map/ppermute | solution.py:149
  124.9 2.7 %collective-permute-start.15 = (f32[2,32,256]{2,1,0:T(8,128)S(1)}, f32[2,32,256]{2,1,0:T(8,128)S(1)}, u32[]{:S(2)}, u32[]{:S(2)}) collective-permute-start(f32[2,32,256]{2,1,0:T(8,128)S(1)} %add.35.refs_2_), channel_id=1, source_target_pairs={{0,2},{1,3},{2,0},{3,1},{4,6},{5,7},{6,4},{7,5},{8,10},{9,11},{10,... | collective-permute-start | bytes 196616 | tf_op jit(solution)/shard_map/ppermute | solution.py:151
  131.2 1.8 %collective-permute-done.17.refs_5_ = f32[2,32,256]{2,1,0:T(8,128)S(1)} collective-permute-done((f32[2,32,256]{2,1,0:T(8,128)S(1)}, f32[2,32,256]{2,1,0:T(8,128)S(1)}, u32[]{:S(2)}, u32[]{:S(2)}) %collective-permute-start.17) | collective-permute-done | bytes 65568 | tf_op jit(solution)/shard_map/ppermute | solution.py:155
  (28 shorter events, 14.3 us)
Async XLA Ops:
  1.9 38.6 %collective-permute-start = (bf16[2,80,10240]{2,1,0:T(8,128)(2,1)S(1)}, bf16[2,80,10240]{2,1,0:T(8,128)(2,1)S(1)}, u32[]{:S(2)}, u32[]{:S(2)}) collective-permute-start(bf16[2,80,10240]{2,1,0:T(8,128)(2,1)S(1)} %cut.5.refs_1_), channel_id=1, source_target_pairs={{0,12},{4,0},{8,4},{12,8},{1,13},{5,1},{9,5},{13,9},{2,14},{6,2},{... | collective-permute-start | bytes 9830408 | tf_op jit(solution)/shard_map/ppermute | solution.py:19
  6.1 2.3 %copy-start = (s32[1,2,10240]{2,1,0:T(2,128)S(1)}, s32[1,2,10240]{2,1,0:T(2,128)}, u32[]{:S(2)}) copy-start(s32[1,2,10240]{2,1,0:T(2,128)} %shift_ref.1) | copy-start | bytes 245764
  6.1 62.5 %collective-permute-start.1 = (bf16[2,64,10240]{2,1,0:T(8,128)(2,1)S(1)}, bf16[2,64,10240]{2,1,0:T(8,128)(2,1)S(1)}, u32[]{:S(2)}, u32[]{:S(2)}) collective-permute-start(bf16[2,64,10240]{2,1,0:T(8,128)(2,1)S(1)} %cut.6.refs_1_), channel_id=1, source_target_pairs={{0,12},{4,0},{8,4},{12,8},{1,13},{5,1},{9,5},{13,9},{2,14},{6,2},{... | collective-permute-start | bytes 7864328 | tf_op jit(solution)/shard_map/ppermute | solution.py:19
  8.4 81.4 %collective-permute-start.7 = (bf16[2,48,10240]{2,1,0:T(8,128)(2,1)S(1)}, bf16[2,48,10240]{2,1,0:T(8,128)(2,1)S(1)}, u32[]{:S(2)}, u32[]{:S(2)}) collective-permute-start(bf16[2,48,10240]{2,1,0:T(8,128)(2,1)S(1)} %cut.7.refs_1_), channel_id=1, source_target_pairs={{0,12},{4,0},{8,4},{12,8},{1,13},{5,1},{9,5},{13,9},{2,14},{6,2},{... | collective-permute-start | bytes 5898248 | tf_op jit(solution)/shard_map/ppermute | solution.py:19
  42.4 7.0 %collective-permute-start.2 = (f32[2,80,256]{2,1,0:T(8,128)S(1)}, f32[2,80,256]{2,1,0:T(8,128)S(1)}, u32[]{:S(2)}, u32[]{:S(2)}) collective-permute-start(f32[2,80,256]{2,1,0:T(8,128)S(1)} %correlate.5), channel_id=1, source_target_pairs={{0,1},{1,0},{2,3},{3,2},{4,5},{5,4},{6,7},{7,6},{8,9},{9,8},{10,11... | collective-permute-start | bytes 491528 | tf_op jit(solution)/shard_map/ppermute | solution.py:137
  45.4 59.6 %collective-permute-start.10 = (bf16[2,32,10240]{2,1,0:T(8,128)(2,1)S(1)}, bf16[2,32,10240]{2,1,0:T(8,128)(2,1)S(1)}, u32[]{:S(2)}, u32[]{:S(2)}) collective-permute-start(bf16[2,32,10240]{2,1,0:T(8,128)(2,1)S(1)} %cut.8.refs_1_), channel_id=1, source_target_pairs={{0,12},{4,0},{8,4},{12,8},{1,13},{5,1},{9,5},{13,9},{2,14},{6,2},{... | collective-permute-start | bytes 3932168 | tf_op jit(solution)/shard_map/ppermute | solution.py:19
  49.5 10.6 %collective-permute-start.3 = (f32[2,80,256]{2,1,0:T(8,128)S(1)}, f32[2,80,256]{2,1,0:T(8,128)S(1)}, u32[]{:S(2)}, u32[]{:S(2)}) collective-permute-start(f32[2,80,256]{2,1,0:T(8,128)S(1)} %add.27), channel_id=1, source_target_pairs={{0,2},{1,3},{2,0},{3,1},{4,6},{5,7},{6,4},{7,5},{8,10},{9,11},{10,... | collective-permute-start | bytes 491528 | tf_op jit(solution)/shard_map/ppermute | solution.py:137
  70.0 47.8 %collective-permute-start.4 = (bf16[2,32,10240]{2,1,0:T(8,128)(2,1)S(1)}, bf16[2,32,10240]{2,1,0:T(8,128)(2,1)S(1)}, u32[]{:S(2)}, u32[]{:S(2)}) collective-permute-start(bf16[2,32,10240]{2,1,0:T(8,128)(2,1)S(1)} %cut.9), channel_id=1, source_target_pairs={{0,12},{4,0},{8,4},{12,8},{1,13},{5,1},{9,5},{13,9},{2,14},{6,2},{... | collective-permute-start | bytes 3932168 | tf_op jit(solution)/shard_map/ppermute | solution.py:19
  73.5 5.0 %collective-permute-start.5 = (f32[2,64,256]{2,1,0:T(8,128)S(1)}, f32[2,64,256]{2,1,0:T(8,128)S(1)}, u32[]{:S(2)}, u32[]{:S(2)}) collective-permute-start(f32[2,64,256]{2,1,0:T(8,128)S(1)} %correlate.6), channel_id=1, source_target_pairs={{0,1},{1,0},{2,3},{3,2},{4,5},{5,4},{6,7},{7,6},{8,9},{9,8},{10,11... | collective-permute-start | bytes 393224 | tf_op jit(solution)/shard_map/ppermute | solution.py:137
  78.5 7.3 %collective-permute-start.6 = (f32[2,64,256]{2,1,0:T(8,128)S(1)}, f32[2,64,256]{2,1,0:T(8,128)S(1)}, u32[]{:S(2)}, u32[]{:S(2)}) collective-permute-start(f32[2,64,256]{2,1,0:T(8,128)S(1)} %add.29), channel_id=1, source_target_pairs={{0,2},{1,3},{2,0},{3,1},{4,6},{5,7},{6,4},{7,5},{8,10},{9,11},{10,... | collective-permute-start | bytes 393224 | tf_op jit(solution)/shard_map/ppermute | solution.py:137
  91.5 5.6 %collective-permute-start.8 = (f32[2,48,256]{2,1,0:T(8,128)S(1)}, f32[2,48,256]{2,1,0:T(8,128)S(1)}, u32[]{:S(2)}, u32[]{:S(2)}) collective-permute-start(f32[2,48,256]{2,1,0:T(8,128)S(1)} %correlate.7), channel_id=1, source_target_pairs={{0,1},{1,0},{2,3},{3,2},{4,5},{5,4},{6,7},{7,6},{8,9},{9,8},{10,11... | collective-permute-start | bytes 294920 | tf_op jit(solution)/shard_map/ppermute | solution.py:137
  97.2 7.8 %collective-permute-start.9 = (f32[2,48,256]{2,1,0:T(8,128)S(1)}, f32[2,48,256]{2,1,0:T(8,128)S(1)}, u32[]{:S(2)}, u32[]{:S(2)}) collective-permute-start(f32[2,48,256]{2,1,0:T(8,128)S(1)} %add.31), channel_id=1, source_target_pairs={{0,2},{1,3},{2,0},{3,1},{4,6},{5,7},{6,4},{7,5},{8,10},{9,11},{10,... | collective-permute-start | bytes 294920 | tf_op jit(solution)/shard_map/ppermute | solution.py:137
  106.9 4.3 %collective-permute-start.11 = (f32[2,32,256]{2,1,0:T(8,128)S(1)}, f32[2,32,256]{2,1,0:T(8,128)S(1)}, u32[]{:S(2)}, u32[]{:S(2)}) collective-permute-start(f32[2,32,256]{2,1,0:T(8,128)S(1)} %correlate.8), channel_id=1, source_target_pairs={{0,1},{1,0},{2,3},{3,2},{4,5},{5,4},{6,7},{7,6},{8,9},{9,8},{10,11... | collective-permute-start | bytes 196616 | tf_op jit(solution)/shard_map/ppermute | solution.py:137
  111.2 5.2 %collective-permute-start.12 = (f32[2,32,256]{2,1,0:T(8,128)S(1)}, f32[2,32,256]{2,1,0:T(8,128)S(1)}, u32[]{:S(2)}, u32[]{:S(2)}) collective-permute-start(f32[2,32,256]{2,1,0:T(8,128)S(1)} %add.33), channel_id=1, source_target_pairs={{0,2},{1,3},{2,0},{3,1},{4,6},{5,7},{6,4},{7,5},{8,10},{9,11},{10,... | collective-permute-start | bytes 196616 | tf_op jit(solution)/shard_map/ppermute | solution.py:137
  119.7 13.3 %collective-permute-start.13 = (f32[2,224,256]{2,1,0:T(8,128)S(1)}, f32[2,224,256]{2,1,0:T(8,128)S(1)}, u32[]{:S(2)}, u32[]{:S(2)}) collective-permute-start(f32[2,224,256]{2,1,0:T(8,128)S(1)} %get-tuple-element.7.refs_0_), channel_id=1, source_target_pairs={{0,4},{4,8},{8,12},{12,0},{1,5},{5,9},{9,13},{13,1},{2,6},{6,10},{... | collective-permute-start | bytes 1376264 | tf_op jit(solution)/shard_map/ppermute | solution.py:19
  120.6 4.3 %collective-permute-start.14 = (f32[2,32,256]{2,1,0:T(8,128)S(1)}, f32[2,32,256]{2,1,0:T(8,128)S(1)}, u32[]{:S(2)}, u32[]{:S(2)}) collective-permute-start(f32[2,32,256]{2,1,0:T(8,128)S(1)} %get-tuple-element.8), channel_id=1, source_target_pairs={{0,1},{1,0},{2,3},{3,2},{4,5},{5,4},{6,7},{7,6},{8,9},{9,8},{10,11... | collective-permute-start | bytes 196616 | tf_op jit(solution)/shard_map/ppermute | solution.py:149
  124.9 5.2 %collective-permute-start.15 = (f32[2,32,256]{2,1,0:T(8,128)S(1)}, f32[2,32,256]{2,1,0:T(8,128)S(1)}, u32[]{:S(2)}, u32[]{:S(2)}) collective-permute-start(f32[2,32,256]{2,1,0:T(8,128)S(1)} %add.35.refs_2_), channel_id=1, source_target_pairs={{0,2},{1,3},{2,0},{3,1},{4,6},{5,7},{6,4},{7,5},{8,10},{9,11},{10,... | collective-permute-start | bytes 196616 | tf_op jit(solution)/shard_map/ppermute | solution.py:151
  127.6 3.7 %collective-permute-start.16 = (f32[2,32,256]{2,1,0:T(8,128)S(1)}, f32[2,32,256]{2,1,0:T(8,128)S(1)}, u32[]{:S(2)}, u32[]{:S(2)}) collective-permute-start(f32[2,32,256]{2,1,0:T(8,128)S(1)} %add.35.refs_2_), channel_id=1, source_target_pairs={{0,4},{4,8},{8,12},{12,0},{1,5},{5,9},{9,13},{13,1},{2,6},{6,10},{... | collective-permute-start | bytes 196616 | tf_op jit(solution)/shard_map/ppermute | solution.py:19
  127.6 5.5 %collective-permute-start.17 = (f32[2,32,256]{2,1,0:T(8,128)S(1)}, f32[2,32,256]{2,1,0:T(8,128)S(1)}, u32[]{:S(2)}, u32[]{:S(2)}) collective-permute-start(f32[2,32,256]{2,1,0:T(8,128)S(1)} %add.35.refs_2_), channel_id=1, source_target_pairs={{0,6},{1,7},{2,4},{3,5},{4,10},{5,11},{6,8},{7,9},{8,14},{9,15},{1... | collective-permute-start | bytes 196616 | tf_op jit(solution)/shard_map/ppermute | solution.py:155

commit v5 on v4

v5 whole, which is shorter than its diff:
```python
import functools

import jax
import jax.numpy as jnp
from jax import lax
from jax.experimental import pallas as pl
from jax.experimental.pallas import tpu as pltpu
from jax.sharding import PartitionSpec as P

PWB = 256
SIXTEENTHS = (5, 4, 3, 2, 2)
MIB = 1 << 20
ANYWHERE = pl.BlockSpec(memory_space=pl.ANY)
WHOLE = pl.BlockSpec(memory_space=pltpu.VMEM)


def moved(block, axis, distance):
    count = lax.axis_size(axis)
    return lax.ppermute(block, axis, [(i, (i + distance) % count) for i in range(count)])


def cut_kernel(bands, waves, *refs):
    own_ref, out_ref, sems = refs[0], refs[-2], refs[-1]
    copies = [
        pltpu.make_async_copy(own_ref.at[0, c, bands, waves], out_ref.at[c], sems.at[c])
        for c in range(2)
    ]
    for copy in copies:
        copy.start()
    for copy in copies:
        copy.wait()


def cut(coefficients, bands, waves, *others):
    shape = (2, bands.stop - bands.start, waves.stop - waves.start)
    return pl.pallas_call(
        functools.partial(cut_kernel, bands, waves),
        out_shape=jax.ShapeDtypeStruct(shape, coefficients.dtype),
        in_specs=[ANYWHERE] * (1 + len(others)),
        out_specs=ANYWHERE,
        scratch_shapes=[pltpu.SemaphoreType.DMA((2,))],
        compiler_params=pltpu.CompilerParams(vmem_limit_bytes=MIB),
        cost_estimate=pl.CostEstimate(flops=0, bytes_accessed=1024, transcendentals=0),
        name="cut",
    )(coefficients, *others)


def place_kernel(own_ref, shift_ref, out_ref):
    bands, width = own_ref.shape[2:]
    base = pl.program_id(0) * width
    goal = lax.broadcasted_iota(jnp.int32, (PWB, PWB), 0)
    for block in range(width // PWB):
        here = pl.ds(block * PWB, PWB)
        inside = shift_ref[0, 0:1, here] & (PWB - 1)
        selector = (goal == inside).astype(jnp.float32).astype(jnp.bfloat16)
        rows = own_ref[0, :, :, here].reshape(2 * bands, PWB)
        placed = lax.dot_general(
            selector, rows, (((1,), (1,)), ((), ())), preferred_element_type=jnp.float32
        )
        there = pl.multiple_of(base + block * PWB, PWB)
        out_ref[pl.ds(there, PWB), :] = placed.astype(jnp.bfloat16)


def placed_bands(coefficients, shifts):
    bands, width = coefficients.shape[2:]
    step = 4 * PWB if width % (4 * PWB) == 0 else PWB
    return pl.pallas_call(
        place_kernel,
        grid=(width // step,),
        out_shape=pltpu.VMEM((width, 2 * bands), jnp.bfloat16),
        in_specs=[
            pl.BlockSpec((1, 2, bands, step), lambda g: (0, 0, 0, g)),
            pl.BlockSpec((1, 2, step), lambda g: (0, 0, g)),
        ],
        out_specs=WHOLE,
        compiler_params=pltpu.CompilerParams(vmem_limit_bytes=16 * MIB),
        cost_estimate=pl.CostEstimate(flops=0, bytes_accessed=1024, transcendentals=0),
        name="place",
    )(coefficients, shifts)


def correlate_kernel(first, depth, begun, held, placed_ref, block_ref, *refs):
    out_ref, total = refs[-2 - held], refs[-1]
    some, width = block_ref.shape[1:]
    bands = out_ref.shape[2]

    def product_of(start):
        return jnp.dot(
            block_ref[:, :, pl.ds(start, depth)].reshape(2 * some, depth),
            placed_ref[pl.ds(first + start, depth), :],
            preferred_element_type=jnp.float32,
        )

    total[...] = product_of(0)

    @pl.loop(1, width // depth)
    def _(step):
        total[...] += product_of(pl.multiple_of(step * depth, depth))

    real_part = total[:some, :bands] + total[some:, bands:]
    imag_part = total[some:, :bands] - total[:some, bands:]
    out_ref[0] = refs[0][0] + real_part if begun else real_part
    out_ref[1] = refs[0][1] + imag_part if begun else imag_part


def correlate(placed, block, *others, first=0, begun=None, held=()):
    some, width = block.shape[1:]
    bands = placed.shape[1] // 2
    depth = width
    while depth % (2 * PWB) == 0 and some * depth > 1 << 19:
        depth //= 2
    block = pltpu.with_memory_space_constraint(block, pltpu.VMEM)
    ins = [placed, block] if begun is None else [placed, block, begun]
    in_specs = [WHOLE] * len(ins) + [ANYWHERE] * (len(others) + len(held))
    before = len(ins) + len(others)
    product = jax.ShapeDtypeStruct((2, some, bands), jnp.float32)
    out = pl.pallas_call(
        functools.partial(correlate_kernel, first, depth, begun is not None, len(held)),
        out_shape=[product] + [jax.ShapeDtypeStruct(kept.shape, kept.dtype) for kept in held],
        in_specs=in_specs,
        out_specs=[WHOLE] + [ANYWHERE] * len(held),
        scratch_shapes=[pltpu.VMEM((2 * some, 2 * bands), jnp.float32)],
        input_output_aliases={before + index: 1 + index for index in range(len(held))},
        compiler_params=pltpu.CompilerParams(vmem_limit_bytes=16 * MIB),
        cost_estimate=pl.CostEstimate(flops=0, bytes_accessed=1024, transcendentals=0),
        name="correlate",
    )(*ins, *others, *held)
    return out if held else out[0]


def summed_over_pw(partial):
    pw = lax.axis_size("pw")
    if pw & (pw - 1):
        return partial + sum(moved(partial, "pw", d) for d in range(1, pw))
    distance = pw // 2
    while distance:
        partial = partial + lax.ppermute(partial, "pw", [(i, i ^ distance) for i in range(pw)])
        distance //= 2
    return partial


def sums_here_and_next(partial):
    ka, pw = lax.axis_size("ka"), lax.axis_size("pw")
    if pw & (pw - 1) or pw == 1:
        whole = summed_over_pw(partial)
        return [whole], [moved(whole, "ka", 1)]
    distance = pw // 2
    while distance > 1:
        partial = partial + lax.ppermute(partial, "pw", [(i, i ^ distance) for i in range(pw)])
        distance //= 2
    here = lax.ppermute(partial, "pw", [(i, i ^ 1) for i in range(pw)])
    across = [(k * pw + p, (k + 1) % ka * pw + (p ^ 1)) for k in range(ka) for p in range(pw)]
    before = [moved(partial, "ka", 1), lax.ppermute(partial, ("ka", "pw"), across)]
    return [partial, here], before


def assemble_kernel(counts, *refs):
    ins, (out_ref, made, sems) = list(refs[:-3]), refs[-3:]
    most, most_before, *last_refs = [[ins.pop(0) for _ in range(count)] for count in counts]
    copies = []
    for side in (1, 0):
        for c in (0, 1):
            early = [ref[c] for ref in (most, most_before)[side]]
            late = sum(ref[c] for ref in last_refs[side])
            matrix = jnp.concatenate([*early, late], axis=0)
            if side == 0:
                matrix = matrix.T
            elif c == 1:
                matrix = -matrix
            made[2 * side + c] = matrix
            copies.append(
                pltpu.make_async_copy(
                    made.at[2 * side + c], out_ref.at[0, side, c], sems.at[2 * side + c]
                )
            )
            copies[-1].start()
    for copy in copies:
        copy.wait()


def assembled(*parts):
    bands = parts[0][0].shape[2]
    counts = [len(part) for part in parts]
    return pl.pallas_call(
        functools.partial(assemble_kernel, counts),
        out_shape=jax.ShapeDtypeStruct((1, 2, 2, bands, bands), jnp.float32),
        in_specs=[WHOLE] * sum(counts),
        out_specs=ANYWHERE,
        scratch_shapes=[
            pltpu.VMEM((4, bands, bands), jnp.float32),
            pltpu.SemaphoreType.DMA((4,)),
        ],
        compiler_params=pltpu.CompilerParams(vmem_limit_bytes=16 * MIB),
        cost_estimate=pl.CostEstimate(flops=0, bytes_accessed=1024, transcendentals=0),
        name="assemble",
    )(*[array for part in parts for array in part])


def local(coefficients, shifts):
    bands, width = coefficients.shape[2:]
    unit = bands // sum(SIXTEENTHS)
    edges = [0]
    for size in SIXTEENTHS:
        edges.append(edges[-1] + size * unit)
    late = width // PWB * 3 // 4 * PWB
    coefficients = pltpu.with_memory_space_constraint(coefficients, pltpu.HBM)
    placed = pltpu.with_memory_space_constraint(placed_bands(coefficients, shifts), pltpu.VMEM)
    blocks, arrived, whole = [], [], []

    def send(chunk, low, high, *others):
        some = slice(edges[chunk], edges[chunk + 1])
        blocks.append(cut(coefficients, some, slice(low, high), *blocks[-1:], *others))
        arrived.append(moved(blocks[-1], "ka", -1))

    for chunk in range(3):
        send(chunk, 0, width)
    send(3, 0, width, arrived[0], placed)
    for chunk in range(4):
        if chunk == 1:
            send(4, 0, late, arrived[1], whole[0])
        if chunk == 2:
            send(4, late, width, arrived[2], whole[1])
        whole.append(summed_over_pw(correlate(placed, arrived[chunk], *whole[-1:])))
    halves = [jnp.concatenate(whole[:2], axis=1), jnp.concatenate(whole[2:], axis=1)]
    last = correlate(placed, arrived[4], *halves)
    last, *halves = correlate(placed, arrived[5], first=late, begun=last, held=halves)
    halves_before = [moved(half, "ka", 1) for half in halves]
    return assembled(halves, halves_before, *sums_here_and_next(last))


def solution(mesh):
    return jax.shard_map(
        local,
        mesh=mesh,
        in_specs=(P(("groups", "ka"), None, None, "pw"), P(("groups", "ka"), None, "pw")),
        out_specs=P(("groups", "ka"), None, None, None, None),
        check_vma=False,
    )
```

time: 136 us -> 134 us (0.985); the launches traced: 134 us -> 134 us
  starting transfers between devices: 29.3 us -> 26.3 us
  waiting for transfers between devices: 77.3 us -> 79.2 us
    ppermute x8, waiting for transfers between devices: 34.1 us -> 38 us  [summed_over_pw(): lax.ppermute(partial, 'pw', [(i, i ^ distance) for i in range(pw)])]
    ppermute x7 -> x9, waiting for transfers between devices: 37.7 us -> 33.9 us  [moved(): lax.ppermute(block, axis, [(i, (i + distance) % count) for i in range(cou...]
    ppermute x8, starting transfers between devices: 15.8 us -> 13.1 us  [summed_over_pw(): lax.ppermute(partial, 'pw', [(i, i ^ distance) for i in range(pw)])]
    ppermute x1, waiting for transfers between devices: 2.69 us -> 4.38 us  [sums_here_and_next(): lax.ppermute(partial, 'pw', [(i, i ^ distance) for i in range(pw)])]
    ppermute x1, starting transfers between devices: 1.51 us -> 0.06 us  [sums_here_and_next(): lax.ppermute(partial, ('ka', 'pw'), across)]
    ppermute x7 -> x9, starting transfers between devices: 7.76 us -> 8.89 us  [moved(): lax.ppermute(block, axis, [(i, (i + distance) % count) for i in range(cou...]
    pallas_call x11 -> x13, Pallas kernels: 17.8 us -> 18.8 us  [the longest x6 9.11 us: correlate(): pl.pallas_call(functools.partial(correlate_kernel, first, depth, begun is...]
  transfers between devices with their start and end apart: 18 -> 20, of which waited for: 16 -> 14; matrix products, arithmetic and copies ran while one was open for 0% -> 0% of each run, Pallas kernels for 17% -> 18%
where the time goes in v5:
time: 134 us
  waiting for transfers between devices  79.2 us (59%)
  Pallas kernels  28.2 us (21%)
  starting transfers between devices  26.3 us (20%)
    ppermute x8, waiting for transfers between devices, summed_over_pw(): lax.ppermute(partial, 'pw', [(i, i ^ distance) for i in range(pw)])  38 us
    ppermute x9, waiting for transfers between devices, moved(): lax.ppermute(block, axis, [(i, (i + distance) % count) for i in range(cou...  33.9 us
    ppermute x8, starting transfers between devices, summed_over_pw(): lax.ppermute(partial, 'pw', [(i, i ^ distance) for i in range(pw)])  13.1 us
    pallas_call x1, Pallas kernels, placed_bands(): pl.pallas_call(place_kernel, grid=(width // step,), out_shape=pltpu.VMEM(...  9.34 us
    pallas_call x6, Pallas kernels, correlate(): pl.pallas_call(functools.partial(correlate_kernel, first, depth, begun is...  9.11 us
    ppermute x9, starting transfers between devices, moved(): lax.ppermute(block, axis, [(i, (i + distance) % count) for i in range(cou...  8.89 us
    pallas_call x6, Pallas kernels, cut(): pl.pallas_call(functools.partial(cut_kernel, bands, waves), out_shape=jax...  8.68 us
    ppermute x1, waiting for transfers between devices, sums_here_and_next(): lax.ppermute(partial, 'pw', [(i, i ^ distance) for i in range(pw)])  4.38 us
  transfers between devices with their start and end apart: 20, of which 14 were waited for; matrix products, arithmetic and copies ran while one was open for 0% of the time, Pallas kernels for 18%

profile of v5, /device:TPU:0, one launch (start us, length us, event | category | flops | bytes accessed | tf_op | source)
XLA Modules:
  0.0 134.0 jit_solution(5431327053141867478)
XLA Ops:
  0.0 1.9 %cut.6.refs_1_ = bf16[2,80,10240]{2,1,0:T(8,128)(2,1)S(1)} custom-call(bf16[1,2,256,10240]{3,2,1,0:T(8,128)(2,1)} %refs_0_.11), custom_call_target="tpu_custom_call" | custom-call | bytes 1024 | tf_op jit(solution)/shard_map/cut/pallas_call | solution.py:36
  1.9 2.4 %collective-permute-start = (bf16[2,80,10240]{2,1,0:T(8,128)(2,1)S(1)}, bf16[2,80,10240]{2,1,0:T(8,128)(2,1)S(1)}, u32[]{:S(2)}, u32[]{:S(2)}) collective-permute-start(bf16[2,80,10240]{2,1,0:T(8,128)(2,1)S(1)} %cut.6.refs_1_), channel_id=1, source_target_pairs={{0,12},{4,0},{8,4},{12,8},{1,13},{5,1},{9,5},{13,9},{2,14},{6,2},{... | collective-permute-start | bytes 9830408 | tf_op jit(solution)/shard_map/ppermute | solution.py:19
  4.4 1.7 %cut.7.refs_1_ = bf16[2,64,10240]{2,1,0:T(8,128)(2,1)S(1)} custom-call(bf16[1,2,256,10240]{3,2,1,0:T(8,128)(2,1)} %refs_0_.11, bf16[2,80,10240]{2,1,0:T(8,128)(2,1)S(1)} %cut.6.refs_1_), custom_call_target="tpu_custom_call" | custom-call | bytes 1024 | tf_op jit(solution)/shard_map/cut/pallas_call | solution.py:36
  6.9 1.5 %cut.8.refs_1_ = bf16[2,48,10240]{2,1,0:T(8,128)(2,1)S(1)} custom-call(bf16[1,2,256,10240]{3,2,1,0:T(8,128)(2,1)} %refs_0_.11, bf16[2,64,10240]{2,1,0:T(8,128)(2,1)S(1)} %cut.7.refs_1_), custom_call_target="tpu_custom_call" | custom-call | bytes 1024 | tf_op jit(solution)/shard_map/cut/pallas_call | solution.py:36
  8.4 9.3 %place.1.refs_3_.placed_ref = bf16[10240,512]{1,0:T(8,128)(2,1)S(1)} custom-call(bf16[1,2,256,10240]{3,2,1,0:T(8,128)(2,1)} %refs_0_.11, s32[1,2,10240]{2,1,0:T(2,128)S(1)} %copy-done), custom_call_target="tpu_custom_call" | custom-call | bytes 1024 | tf_op jit(solution)/shard_map/place/pallas_call | solution.py:67
  17.8 22.8 %collective-permute-done.refs_2_.block_ref = bf16[2,80,10240]{2,1,0:T(8,128)(2,1)S(1)} collective-permute-done((bf16[2,80,10240]{2,1,0:T(8,128)(2,1)S(1)}, bf16[2,80,10240]{2,1,0:T(8,128)(2,1)S(1)}, u32[]{:S(2)}, u32[]{:S(2)}) %collective-permute-start) | collective-permute-done | bytes 3276832 | tf_op jit(solution)/shard_map/ppermute | solution.py:19
  40.6 1.3 cut.9.refs_1_
  41.9 2.0 %collective-permute-start.11 = (bf16[2,32,10240]{2,1,0:T(8,128)(2,1)S(1)}, bf16[2,32,10240]{2,1,0:T(8,128)(2,1)S(1)}, u32[]{:S(2)}, u32[]{:S(2)}) collective-permute-start(bf16[2,32,10240]{2,1,0:T(8,128)(2,1)S(1)} %cut.9.refs_1_), channel_id=1, source_target_pairs={{0,12},{4,0},{8,4},{12,8},{1,13},{5,1},{9,5},{13,9},{2,14},{6,2},{... | collective-permute-start | bytes 3932168 | tf_op jit(solution)/shard_map/ppermute | solution.py:19
  43.8 1.9 %correlate.6 = f32[2,80,256]{2,1,0:T(8,128)S(1)} custom-call(bf16[10240,512]{1,0:T(8,128)(2,1)S(1)} %place.1.refs_3_.placed_ref, bf16[2,80,10240]{2,1,0:T(8,128)(2,1)S(1)} %collective-permute-done.refs_2_.block_ref), custom_call_target="tpu_custom_call" | custom-call | bytes 1024 | tf_op jit(solution)/shard_map/correlate/pallas_call | solution.py:117
  45.7 2.7 %collective-permute-start.2 = (f32[2,80,256]{2,1,0:T(8,128)S(1)}, f32[2,80,256]{2,1,0:T(8,128)S(1)}, u32[]{:S(2)}, u32[]{:S(2)}) collective-permute-start(f32[2,80,256]{2,1,0:T(8,128)S(1)} %correlate.6), channel_id=1, source_target_pairs={{0,2},{1,3},{2,0},{3,1},{4,6},{5,7},{6,4},{7,5},{8,10},{9,11},{10,... | collective-permute-start | bytes 491528 | tf_op jit(solution)/shard_map/ppermute | solution.py:137
  48.4 6.9 %collective-permute-done.2 = f32[2,80,256]{2,1,0:T(8,128)S(1)} collective-permute-done((f32[2,80,256]{2,1,0:T(8,128)S(1)}, f32[2,80,256]{2,1,0:T(8,128)S(1)}, u32[]{:S(2)}, u32[]{:S(2)}) %collective-permute-start.2) | collective-permute-done | bytes 163872 | tf_op jit(solution)/shard_map/ppermute | solution.py:137
  56.0 4.6 %collective-permute-done.3 = f32[2,80,256]{2,1,0:T(8,128)S(1)} collective-permute-done((f32[2,80,256]{2,1,0:T(8,128)S(1)}, f32[2,80,256]{2,1,0:T(8,128)S(1)}, u32[]{:S(2)}, u32[]{:S(2)}) %collective-permute-start.3) | collective-permute-done | bytes 163872 | tf_op jit(solution)/shard_map/ppermute | solution.py:137
  60.7 8.0 %collective-permute-done.1.refs_2_.block_ref = bf16[2,64,10240]{2,1,0:T(8,128)(2,1)S(1)} collective-permute-done((bf16[2,64,10240]{2,1,0:T(8,128)(2,1)S(1)}, bf16[2,64,10240]{2,1,0:T(8,128)(2,1)S(1)}, u32[]{:S(2)}, u32[]{:S(2)}) %collective-permute-start.1) | collective-permute-done | bytes 2621472 | tf_op jit(solution)/shard_map/ppermute | solution.py:19
  69.9 2.0 %collective-permute-start.8 = (bf16[2,32,7680]{2,1,0:T(8,128)(2,1)S(1)}, bf16[2,32,7680]{2,1,0:T(8,128)(2,1)S(1)}, u32[]{:S(2)}, u32[]{:S(2)}) collective-permute-start(bf16[2,32,7680]{2,1,0:T(8,128)(2,1)S(1)} %cut.10.refs_1_), channel_id=1, source_target_pairs={{0,12},{4,0},{8,4},{12,8},{1,13},{5,1},{9,5},{13,9},{2,14},{6,2},{... | collective-permute-start | bytes 2949128 | tf_op jit(solution)/shard_map/ppermute | solution.py:19
  71.8 1.5 %correlate.7 = f32[2,64,256]{2,1,0:T(8,128)S(1)} custom-call(bf16[10240,512]{1,0:T(8,128)(2,1)S(1)} %place.1.refs_3_.placed_ref, bf16[2,64,10240]{2,1,0:T(8,128)(2,1)S(1)} %collective-permute-done.1.refs_2_.block_ref, f32[2,80,256]{2,1,0:T(8,128)S(1)} %add.28.refs_3_.refs_0_), custom_call_target="tpu_custom_call" | custom-call | bytes 1024 | tf_op jit(solution)/shard_map/correlate/pallas_call | solution.py:117
  73.3 2.7 %collective-permute-start.5 = (f32[2,64,256]{2,1,0:T(8,128)S(1)}, f32[2,64,256]{2,1,0:T(8,128)S(1)}, u32[]{:S(2)}, u32[]{:S(2)}) collective-permute-start(f32[2,64,256]{2,1,0:T(8,128)S(1)} %correlate.7), channel_id=1, source_target_pairs={{0,2},{1,3},{2,0},{3,1},{4,6},{5,7},{6,4},{7,5},{8,10},{9,11},{10,... | collective-permute-start | bytes 393224 | tf_op jit(solution)/shard_map/ppermute | solution.py:137
  76.0 5.5 %collective-permute-done.5 = f32[2,64,256]{2,1,0:T(8,128)S(1)} collective-permute-done((f32[2,64,256]{2,1,0:T(8,128)S(1)}, f32[2,64,256]{2,1,0:T(8,128)S(1)}, u32[]{:S(2)}, u32[]{:S(2)}) %collective-permute-start.5) | collective-permute-done | bytes 131104 | tf_op jit(solution)/shard_map/ppermute | solution.py:137
  82.2 4.3 %collective-permute-done.6 = f32[2,64,256]{2,1,0:T(8,128)S(1)} collective-permute-done((f32[2,64,256]{2,1,0:T(8,128)S(1)}, f32[2,64,256]{2,1,0:T(8,128)S(1)}, u32[]{:S(2)}, u32[]{:S(2)}) %collective-permute-start.6) | collective-permute-done | bytes 131104 | tf_op jit(solution)/shard_map/ppermute | solution.py:137
  86.6 3.2 %collective-permute-done.4.refs_2_.block_ref = bf16[2,48,10240]{2,1,0:T(8,128)(2,1)S(1)} collective-permute-done((bf16[2,48,10240]{2,1,0:T(8,128)(2,1)S(1)}, bf16[2,48,10240]{2,1,0:T(8,128)(2,1)S(1)}, u32[]{:S(2)}, u32[]{:S(2)}) %collective-permute-start.4) | collective-permute-done | bytes 1966112 | tf_op jit(solution)/shard_map/ppermute | solution.py:19
  89.7 1.8 %correlate.8 = f32[2,48,256]{2,1,0:T(8,128)S(1)} custom-call(bf16[10240,512]{1,0:T(8,128)(2,1)S(1)} %place.1.refs_3_.placed_ref, bf16[2,48,10240]{2,1,0:T(8,128)(2,1)S(1)} %collective-permute-done.4.refs_2_.block_ref, f32[2,64,256]{2,1,0:T(8,128)S(1)} %add.30.refs_3_.refs_0_), custom_call_target="tpu_custom_call" | custom-call | bytes 1024 | tf_op jit(solution)/shard_map/correlate/pallas_call | solution.py:117
  91.5 2.6 %collective-permute-start.9 = (f32[2,48,256]{2,1,0:T(8,128)S(1)}, f32[2,48,256]{2,1,0:T(8,128)S(1)}, u32[]{:S(2)}, u32[]{:S(2)}) collective-permute-start(f32[2,48,256]{2,1,0:T(8,128)S(1)} %correlate.8), channel_id=1, source_target_pairs={{0,2},{1,3},{2,0},{3,1},{4,6},{5,7},{6,4},{7,5},{8,10},{9,11},{10,... | collective-permute-start | bytes 294920 | tf_op jit(solution)/shard_map/ppermute | solution.py:137
  94.2 6.0 %collective-permute-done.9 = f32[2,48,256]{2,1,0:T(8,128)S(1)} collective-permute-done((f32[2,48,256]{2,1,0:T(8,128)S(1)}, f32[2,48,256]{2,1,0:T(8,128)S(1)}, u32[]{:S(2)}, u32[]{:S(2)}) %collective-permute-start.9) | collective-permute-done | bytes 98336 | tf_op jit(solution)/shard_map/ppermute | solution.py:137
  102.1 2.8 %collective-permute-done.10 = f32[2,48,256]{2,1,0:T(8,128)S(1)} collective-permute-done((f32[2,48,256]{2,1,0:T(8,128)S(1)}, f32[2,48,256]{2,1,0:T(8,128)S(1)}, u32[]{:S(2)}, u32[]{:S(2)}) %collective-permute-start.10) | collective-permute-done | bytes 98336 | tf_op jit(solution)/shard_map/ppermute | solution.py:137
  104.9 1.9 %correlate.9 = f32[2,32,256]{2,1,0:T(8,128)S(1)} custom-call(bf16[10240,512]{1,0:T(8,128)(2,1)S(1)} %place.1.refs_3_.placed_ref, bf16[2,32,10240]{2,1,0:T(8,128)(2,1)S(1)} %collective-permute-done.11.block_ref, f32[2,48,256]{2,1,0:T(8,128)S(1)} %add.32.refs_0_), custom_call_target="tpu_custom_call" | custom-call | bytes 1024 | tf_op jit(solution)/shard_map/correlate/pallas_call | solution.py:117
  106.9 2.5 %collective-permute-start.12 = (f32[2,32,256]{2,1,0:T(8,128)S(1)}, f32[2,32,256]{2,1,0:T(8,128)S(1)}, u32[]{:S(2)}, u32[]{:S(2)}) collective-permute-start(f32[2,32,256]{2,1,0:T(8,128)S(1)} %correlate.9), channel_id=1, source_target_pairs={{0,2},{1,3},{2,0},{3,1},{4,6},{5,7},{6,4},{7,5},{8,10},{9,11},{10,... | collective-permute-start | bytes 196616 | tf_op jit(solution)/shard_map/ppermute | solution.py:137
  109.4 4.1 %collective-permute-done.12 = f32[2,32,256]{2,1,0:T(8,128)S(1)} collective-permute-done((f32[2,32,256]{2,1,0:T(8,128)S(1)}, f32[2,32,256]{2,1,0:T(8,128)S(1)}, u32[]{:S(2)}, u32[]{:S(2)}) %collective-permute-start.12) | collective-permute-done | bytes 65568 | tf_op jit(solution)/shard_map/ppermute | solution.py:137
  113.9 3.9 %collective-permute-done.13 = f32[2,32,256]{2,1,0:T(8,128)S(1)} collective-permute-done((f32[2,32,256]{2,1,0:T(8,128)S(1)}, f32[2,32,256]{2,1,0:T(8,128)S(1)}, u32[]{:S(2)}, u32[]{:S(2)}) %collective-permute-start.13) | collective-permute-done | bytes 65568 | tf_op jit(solution)/shard_map/ppermute | solution.py:137
  117.8 1.5 %correlate.10.refs_0_ = f32[2,32,256]{2,1,0:T(8,128)S(1)} custom-call(bf16[10240,512]{1,0:T(8,128)(2,1)S(1)} %place.1.refs_3_.placed_ref, bf16[2,32,7680]{2,1,0:T(8,128)(2,1)S(1)} %collective-permute-done.8.block_ref, f32[2,144,256]{2,1,0:T(8,128)S(1)} %pad_maximum_fusion.refs_0_.refs_1_, f32[2,80,256]{2,1,0:T(8,128)S(1)} %pad_maximum_fusion.1.refs_1_.refs_2_), custom_call_target="tpu_custom_call" | custom-call | bytes 1024 | tf_op jit(solution)/shard_map/correlate/pallas_call | solution.py:117
  121.0 2.1 %collective-permute-start.16 = (f32[2,32,256]{2,1,0:T(8,128)S(1)}, f32[2,32,256]{2,1,0:T(8,128)S(1)}, u32[]{:S(2)}, u32[]{:S(2)}) collective-permute-start(f32[2,32,256]{2,1,0:T(8,128)S(1)} %get-tuple-element.10), channel_id=1, source_target_pairs={{0,2},{1,3},{2,0},{3,1},{4,6},{5,7},{6,4},{7,5},{8,10},{9,11},{10,... | collective-permute-start | bytes 196616 | tf_op jit(solution)/shard_map/ppermute | solution.py:149
  123.1 4.4 %collective-permute-done.16 = f32[2,32,256]{2,1,0:T(8,128)S(1)} collective-permute-done((f32[2,32,256]{2,1,0:T(8,128)S(1)}, f32[2,32,256]{2,1,0:T(8,128)S(1)}, u32[]{:S(2)}, u32[]{:S(2)}) %collective-permute-start.16) | collective-permute-done | bytes 65568 | tf_op jit(solution)/shard_map/ppermute | solution.py:149
  128.0 2.1 %collective-permute-start.17 = (f32[2,32,256]{2,1,0:T(8,128)S(1)}, f32[2,32,256]{2,1,0:T(8,128)S(1)}, u32[]{:S(2)}, u32[]{:S(2)}) collective-permute-start(f32[2,32,256]{2,1,0:T(8,128)S(1)} %add.35.refs_4_), channel_id=1, source_target_pairs={{0,1},{1,0},{2,3},{3,2},{4,5},{5,4},{6,7},{7,6},{8,9},{9,8},{10,11... | collective-permute-start | bytes 196616 | tf_op jit(solution)/shard_map/ppermute | solution.py:151
  130.1 2.0 %collective-permute-done.19.refs_7_ = f32[2,32,256]{2,1,0:T(8,128)S(1)} collective-permute-done((f32[2,32,256]{2,1,0:T(8,128)S(1)}, f32[2,32,256]{2,1,0:T(8,128)S(1)}, u32[]{:S(2)}, u32[]{:S(2)}) %collective-permute-start.19) | collective-permute-done | bytes 65568 | tf_op jit(solution)/shard_map/ppermute | solution.py:153
  (35 shorter events, 10.1 us)
Async XLA Ops:
  1.9 38.6 %collective-permute-start = (bf16[2,80,10240]{2,1,0:T(8,128)(2,1)S(1)}, bf16[2,80,10240]{2,1,0:T(8,128)(2,1)S(1)}, u32[]{:S(2)}, u32[]{:S(2)}) collective-permute-start(bf16[2,80,10240]{2,1,0:T(8,128)(2,1)S(1)} %cut.6.refs_1_), channel_id=1, source_target_pairs={{0,12},{4,0},{8,4},{12,8},{1,13},{5,1},{9,5},{13,9},{2,14},{6,2},{... | collective-permute-start | bytes 9830408 | tf_op jit(solution)/shard_map/ppermute | solution.py:19
  6.1 2.3 %copy-start = (s32[1,2,10240]{2,1,0:T(2,128)S(1)}, s32[1,2,10240]{2,1,0:T(2,128)}, u32[]{:S(2)}) copy-start(s32[1,2,10240]{2,1,0:T(2,128)} %shift_ref.1) | copy-start | bytes 245764
  6.1 62.5 %collective-permute-start.1 = (bf16[2,64,10240]{2,1,0:T(8,128)(2,1)S(1)}, bf16[2,64,10240]{2,1,0:T(8,128)(2,1)S(1)}, u32[]{:S(2)}, u32[]{:S(2)}) collective-permute-start(bf16[2,64,10240]{2,1,0:T(8,128)(2,1)S(1)} %cut.7.refs_1_), channel_id=1, source_target_pairs={{0,12},{4,0},{8,4},{12,8},{1,13},{5,1},{9,5},{13,9},{2,14},{6,2},{... | collective-permute-start | bytes 7864328 | tf_op jit(solution)/shard_map/ppermute | solution.py:19
  8.4 81.4 %collective-permute-start.4 = (bf16[2,48,10240]{2,1,0:T(8,128)(2,1)S(1)}, bf16[2,48,10240]{2,1,0:T(8,128)(2,1)S(1)}, u32[]{:S(2)}, u32[]{:S(2)}) collective-permute-start(bf16[2,48,10240]{2,1,0:T(8,128)(2,1)S(1)} %cut.8.refs_1_), channel_id=1, source_target_pairs={{0,12},{4,0},{8,4},{12,8},{1,13},{5,1},{9,5},{13,9},{2,14},{6,2},{... | collective-permute-start | bytes 5898248 | tf_op jit(solution)/shard_map/ppermute | solution.py:19
  41.9 63.1 %collective-permute-start.11 = (bf16[2,32,10240]{2,1,0:T(8,128)(2,1)S(1)}, bf16[2,32,10240]{2,1,0:T(8,128)(2,1)S(1)}, u32[]{:S(2)}, u32[]{:S(2)}) collective-permute-start(bf16[2,32,10240]{2,1,0:T(8,128)(2,1)S(1)} %cut.9.refs_1_), channel_id=1, source_target_pairs={{0,12},{4,0},{8,4},{12,8},{1,13},{5,1},{9,5},{13,9},{2,14},{6,2},{... | collective-permute-start | bytes 3932168 | tf_op jit(solution)/shard_map/ppermute | solution.py:19
  45.7 9.5 %collective-permute-start.2 = (f32[2,80,256]{2,1,0:T(8,128)S(1)}, f32[2,80,256]{2,1,0:T(8,128)S(1)}, u32[]{:S(2)}, u32[]{:S(2)}) collective-permute-start(f32[2,80,256]{2,1,0:T(8,128)S(1)} %correlate.6), channel_id=1, source_target_pairs={{0,2},{1,3},{2,0},{3,1},{4,6},{5,7},{6,4},{7,5},{8,10},{9,11},{10,... | collective-permute-start | bytes 491528 | tf_op jit(solution)/shard_map/ppermute | solution.py:137
  55.3 5.4 %collective-permute-start.3 = (f32[2,80,256]{2,1,0:T(8,128)S(1)}, f32[2,80,256]{2,1,0:T(8,128)S(1)}, u32[]{:S(2)}, u32[]{:S(2)}) collective-permute-start(f32[2,80,256]{2,1,0:T(8,128)S(1)} %add.27), channel_id=1, source_target_pairs={{0,1},{1,0},{2,3},{3,2},{4,5},{5,4},{6,7},{7,6},{8,9},{9,8},{10,11... | collective-permute-start | bytes 491528 | tf_op jit(solution)/shard_map/ppermute | solution.py:137
  69.9 48.0 %collective-permute-start.8 = (bf16[2,32,7680]{2,1,0:T(8,128)(2,1)S(1)}, bf16[2,32,7680]{2,1,0:T(8,128)(2,1)S(1)}, u32[]{:S(2)}, u32[]{:S(2)}) collective-permute-start(bf16[2,32,7680]{2,1,0:T(8,128)(2,1)S(1)} %cut.10.refs_1_), channel_id=1, source_target_pairs={{0,12},{4,0},{8,4},{12,8},{1,13},{5,1},{9,5},{13,9},{2,14},{6,2},{... | collective-permute-start | bytes 2949128 | tf_op jit(solution)/shard_map/ppermute | solution.py:19
  73.3 8.1 %collective-permute-start.5 = (f32[2,64,256]{2,1,0:T(8,128)S(1)}, f32[2,64,256]{2,1,0:T(8,128)S(1)}, u32[]{:S(2)}, u32[]{:S(2)}) collective-permute-start(f32[2,64,256]{2,1,0:T(8,128)S(1)} %correlate.7), channel_id=1, source_target_pairs={{0,2},{1,3},{2,0},{3,1},{4,6},{5,7},{6,4},{7,5},{8,10},{9,11},{10,... | collective-permute-start | bytes 393224 | tf_op jit(solution)/shard_map/ppermute | solution.py:137
  81.5 5.0 %collective-permute-start.6 = (f32[2,64,256]{2,1,0:T(8,128)S(1)}, f32[2,64,256]{2,1,0:T(8,128)S(1)}, u32[]{:S(2)}, u32[]{:S(2)}) collective-permute-start(f32[2,64,256]{2,1,0:T(8,128)S(1)} %add.29), channel_id=1, source_target_pairs={{0,1},{1,0},{2,3},{3,2},{4,5},{5,4},{6,7},{7,6},{8,9},{9,8},{10,11... | collective-permute-start | bytes 393224 | tf_op jit(solution)/shard_map/ppermute | solution.py:137
  91.5 8.6 %collective-permute-start.9 = (f32[2,48,256]{2,1,0:T(8,128)S(1)}, f32[2,48,256]{2,1,0:T(8,128)S(1)}, u32[]{:S(2)}, u32[]{:S(2)}) collective-permute-start(f32[2,48,256]{2,1,0:T(8,128)S(1)} %correlate.8), channel_id=1, source_target_pairs={{0,2},{1,3},{2,0},{3,1},{4,6},{5,7},{6,4},{7,5},{8,10},{9,11},{10,... | collective-permute-start | bytes 294920 | tf_op jit(solution)/shard_map/ppermute | solution.py:137
  100.2 4.7 %collective-permute-start.10 = (f32[2,48,256]{2,1,0:T(8,128)S(1)}, f32[2,48,256]{2,1,0:T(8,128)S(1)}, u32[]{:S(2)}, u32[]{:S(2)}) collective-permute-start(f32[2,48,256]{2,1,0:T(8,128)S(1)} %add.31), channel_id=1, source_target_pairs={{0,1},{1,0},{2,3},{3,2},{4,5},{5,4},{6,7},{7,6},{8,9},{9,8},{10,11... | collective-permute-start | bytes 294920 | tf_op jit(solution)/shard_map/ppermute | solution.py:137
  101.9 17.4 %collective-permute-start.7 = (bf16[2,32,2560]{2,1,0:T(8,128)(2,1)S(1)}, bf16[2,32,2560]{2,1,0:T(8,128)(2,1)S(1)}, u32[]{:S(2)}, u32[]{:S(2)}) collective-permute-start(bf16[2,32,2560]{2,1,0:T(8,128)(2,1)S(1)} %cut.11), channel_id=1, source_target_pairs={{0,12},{4,0},{8,4},{12,8},{1,13},{5,1},{9,5},{13,9},{2,14},{6,2},{... | collective-permute-start | bytes 983048 | tf_op jit(solution)/shard_map/ppermute | solution.py:19
  106.9 6.6 %collective-permute-start.12 = (f32[2,32,256]{2,1,0:T(8,128)S(1)}, f32[2,32,256]{2,1,0:T(8,128)S(1)}, u32[]{:S(2)}, u32[]{:S(2)}) collective-permute-start(f32[2,32,256]{2,1,0:T(8,128)S(1)} %correlate.9), channel_id=1, source_target_pairs={{0,2},{1,3},{2,0},{3,1},{4,6},{5,7},{6,4},{7,5},{8,10},{9,11},{10,... | collective-permute-start | bytes 196616 | tf_op jit(solution)/shard_map/ppermute | solution.py:137
  113.5 4.3 %collective-permute-start.13 = (f32[2,32,256]{2,1,0:T(8,128)S(1)}, f32[2,32,256]{2,1,0:T(8,128)S(1)}, u32[]{:S(2)}, u32[]{:S(2)}) collective-permute-start(f32[2,32,256]{2,1,0:T(8,128)S(1)} %add.33), channel_id=1, source_target_pairs={{0,1},{1,0},{2,3},{3,2},{4,5},{5,4},{6,7},{7,6},{8,9},{9,8},{10,11... | collective-permute-start | bytes 196616 | tf_op jit(solution)/shard_map/ppermute | solution.py:137
  119.9 13.1 %collective-permute-start.14 = (f32[2,144,256]{2,1,0:T(8,128)S(1)}, f32[2,144,256]{2,1,0:T(8,128)S(1)}, u32[]{:S(2)}, u32[]{:S(2)}) collective-permute-start(f32[2,144,256]{2,1,0:T(8,128)S(1)} %get-tuple-element.8.refs_0_), channel_id=1, source_target_pairs={{0,4},{4,8},{8,12},{12,0},{1,5},{5,9},{9,13},{13,1},{2,6},{6,10},{... | collective-permute-start | bytes 884744 | tf_op jit(solution)/shard_map/ppermute | solution.py:19
  119.9 13.0 %collective-permute-start.15 = (f32[2,80,256]{2,1,0:T(8,128)S(1)}, f32[2,80,256]{2,1,0:T(8,128)S(1)}, u32[]{:S(2)}, u32[]{:S(2)}) collective-permute-start(f32[2,80,256]{2,1,0:T(8,128)S(1)} %get-tuple-element.9.refs_1_), channel_id=1, source_target_pairs={{0,4},{4,8},{8,12},{12,0},{1,5},{5,9},{9,13},{13,1},{2,6},{6,10},{... | collective-permute-start | bytes 491528 | tf_op jit(solution)/shard_map/ppermute | solution.py:19
  121.0 6.5 %collective-permute-start.16 = (f32[2,32,256]{2,1,0:T(8,128)S(1)}, f32[2,32,256]{2,1,0:T(8,128)S(1)}, u32[]{:S(2)}, u32[]{:S(2)}) collective-permute-start(f32[2,32,256]{2,1,0:T(8,128)S(1)} %get-tuple-element.10), channel_id=1, source_target_pairs={{0,2},{1,3},{2,0},{3,1},{4,6},{5,7},{6,4},{7,5},{8,10},{9,11},{10,... | collective-permute-start | bytes 196616 | tf_op jit(solution)/shard_map/ppermute | solution.py:149
  127.5 4.6 %collective-permute-start.19 = (f32[2,32,256]{2,1,0:T(8,128)S(1)}, f32[2,32,256]{2,1,0:T(8,128)S(1)}, u32[]{:S(2)}, u32[]{:S(2)}) collective-permute-start(f32[2,32,256]{2,1,0:T(8,128)S(1)} %add.35.refs_4_), channel_id=1, source_target_pairs={{0,5},{1,4},{2,7},{3,6},{4,9},{5,8},{6,11},{7,10},{8,13},{9,12},{1... | collective-permute-start | bytes 196616 | tf_op jit(solution)/shard_map/ppermute | solution.py:153
  127.5 4.6 %collective-permute-start.18 = (f32[2,32,256]{2,1,0:T(8,128)S(1)}, f32[2,32,256]{2,1,0:T(8,128)S(1)}, u32[]{:S(2)}, u32[]{:S(2)}) collective-permute-start(f32[2,32,256]{2,1,0:T(8,128)S(1)} %add.35.refs_4_), channel_id=1, source_target_pairs={{0,4},{4,8},{8,12},{12,0},{1,5},{5,9},{9,13},{13,1},{2,6},{6,10},{... | collective-permute-start | bytes 196616 | tf_op jit(solution)/shard_map/ppermute | solution.py:19
  128.0 5.0 %collective-permute-start.17 = (f32[2,32,256]{2,1,0:T(8,128)S(1)}, f32[2,32,256]{2,1,0:T(8,128)S(1)}, u32[]{:S(2)}, u32[]{:S(2)}) collective-permute-start(f32[2,32,256]{2,1,0:T(8,128)S(1)} %add.35.refs_4_), channel_id=1, source_target_pairs={{0,1},{1,0},{2,3},{3,2},{4,5},{5,4},{6,7},{7,6},{8,9},{9,8},{10,11... | collective-permute-start | bytes 196616 | tf_op jit(solution)/shard_map/ppermute | solution.py:151

commit v6 on v5

--- a/solution.py
+++ b/solution.py
@@ -8,15 +8,30 @@
 from jax.sharding import PartitionSpec as P
 
 PWB = 256
-SIXTEENTHS = (5, 4, 3, 2, 2)
+SIXTEENTHS = (6, 4, 4, 2)
+EVEN, ODD = 0, 1
 MIB = 1 << 20
 ANYWHERE = pl.BlockSpec(memory_space=pl.ANY)
 WHOLE = pl.BlockSpec(memory_space=pltpu.VMEM)
 
 
-def moved(block, axis, distance):
-    count = lax.axis_size(axis)
-    return lax.ppermute(block, axis, [(i, (i + distance) % count) for i in range(count)])
+def sent(block, kind, points=0, waves=0):
+    ka, pw = lax.axis_size("ka"), lax.axis_size("pw")
+    route = [
+        (k * pw + p, (k + points) % ka * pw + (p ^ waves))
+        for k in range(ka)
+        for p in range(pw)
+        if k % 2 == kind
+    ]
+    return lax.ppermute(block, ("ka", "pw"), route)
+
+
+def fetched(block, kind):
+    ka, pw = lax.axis_size("ka"), lax.axis_size("pw")
+    route = [
+        ((k + 1) % ka * pw + p, k * pw + p) for k in range(ka) for p in range(pw) if k % 2 == kind
+    ]
+    return lax.ppermute(block, ("ka", "pw"), route)
 
 
 def cut_kernel(bands, waves, *refs):
@@ -128,41 +143,23 @@
     return out if held else out[0]
 
 
-def summed_over_pw(partial):
-    pw = lax.axis_size("pw")
-    if pw & (pw - 1):
-        return partial + sum(moved(partial, "pw", d) for d in range(1, pw))
-    distance = pw // 2
-    while distance:
-        partial = partial + lax.ppermute(partial, "pw", [(i, i ^ distance) for i in range(pw)])
+def summed_over_pw(partial, kind, nearest=1):
+    distance = lax.axis_size("pw") // 2
+    while distance >= nearest:
+        partial = partial + sent(partial, kind, waves=distance)
         distance //= 2
     return partial
 
 
-def sums_here_and_next(partial):
-    ka, pw = lax.axis_size("ka"), lax.axis_size("pw")
-    if pw & (pw - 1) or pw == 1:
-        whole = summed_over_pw(partial)
-        return [whole], [moved(whole, "ka", 1)]
-    distance = pw // 2
-    while distance > 1:
-        partial = partial + lax.ppermute(partial, "pw", [(i, i ^ distance) for i in range(pw)])
-        distance //= 2
-    here = lax.ppermute(partial, "pw", [(i, i ^ 1) for i in range(pw)])
-    across = [(k * pw + p, (k + 1) % ka * pw + (p ^ 1)) for k in range(ka) for p in range(pw)]
-    before = [moved(partial, "ka", 1), lax.ppermute(partial, ("ka", "pw"), across)]
-    return [partial, here], before
-
-
 def assemble_kernel(counts, *refs):
     ins, (out_ref, made, sems) = list(refs[:-3]), refs[-3:]
-    most, most_before, *last_refs = [[ins.pop(0) for _ in range(count)] for count in counts]
+    parts = [[ins.pop(0) for _ in range(count)] for count in counts]
     copies = []
     for side in (1, 0):
+        near, early, late = parts[3 * side : 3 * side + 3]
         for c in (0, 1):
-            early = [ref[c] for ref in (most, most_before)[side]]
-            late = sum(ref[c] for ref in last_refs[side])
-            matrix = jnp.concatenate([*early, late], axis=0)
+            far = jnp.concatenate([ref[c] for ref in early] + [sum(ref[c] for ref in late)], axis=0)
+            matrix = near[0][c] + far
             if side == 0:
                 matrix = matrix.T
             elif c == 1:
@@ -203,6 +200,7 @@
     for size in SIXTEENTHS:
         edges.append(edges[-1] + size * unit)
     late = width // PWB * 3 // 4 * PWB
+    near_block = fetched(coefficients[0], EVEN)
     coefficients = pltpu.with_memory_space_constraint(coefficients, pltpu.HBM)
     placed = pltpu.with_memory_space_constraint(placed_bands(coefficients, shifts), pltpu.VMEM)
     blocks, arrived, whole = [], [], []
@@ -210,22 +208,26 @@
     def send(chunk, low, high, *others):
         some = slice(edges[chunk], edges[chunk + 1])
         blocks.append(cut(coefficients, some, slice(low, high), *blocks[-1:], *others))
-        arrived.append(moved(blocks[-1], "ka", -1))
+        arrived.append(fetched(blocks[-1], ODD))
 
     for chunk in range(3):
         send(chunk, 0, width)
-    send(3, 0, width, arrived[0], placed)
-    for chunk in range(4):
-        if chunk == 1:
-            send(4, 0, late, arrived[1], whole[0])
+    near = summed_over_pw(correlate(placed, near_block), EVEN)
+    near_before = sent(near, EVEN, points=1)
+    send(3, 0, late, arrived[0], placed)
+    for chunk in range(3):
         if chunk == 2:
-            send(4, late, width, arrived[2], whole[1])
-        whole.append(summed_over_pw(correlate(placed, arrived[chunk], *whole[-1:])))
-    halves = [jnp.concatenate(whole[:2], axis=1), jnp.concatenate(whole[2:], axis=1)]
-    last = correlate(placed, arrived[4], *halves)
-    last, *halves = correlate(placed, arrived[5], first=late, begun=last, held=halves)
-    halves_before = [moved(half, "ka", 1) for half in halves]
-    return assembled(halves, halves_before, *sums_here_and_next(last))
+            send(3, late, width, arrived[1], whole[0])
+        before = whole[-1] if whole else near
+        whole.append(summed_over_pw(correlate(placed, arrived[chunk], before), ODD))
+    halves = [jnp.concatenate(whole[:2], axis=1), whole[2]]
+    last = correlate(placed, arrived[3], *halves)
+    last, *halves = correlate(placed, arrived[4], first=late, begun=last, held=halves)
+    halves_before = [sent(half, ODD, points=1) for half in halves]
+    last = summed_over_pw(last, ODD, nearest=2)
+    ahead = [last, sent(last, ODD, waves=1)]
+    behind = [sent(last, ODD, points=1), sent(last, ODD, points=1, waves=1)]
+    return assembled([near], halves, ahead, [near_before], halves_before, behind)
 
 
 def solution(mesh):

time: 134 us -> 145 us (1.082)
  starting transfers between devices: 26.3 us -> 51.6 us
  waiting for transfers between devices: 79.2 us -> 59.6 us
  Pallas kernels: 28.2 us -> 32.3 us
    ppermute x20 -> x21, starting transfers between devices: 26.3 us -> 51.6 us  [the longest x6 27.7 us: fetched(): return lax.ppermute(block, ('ka', 'pw'), route)]
    ppermute x20 -> x21, waiting for transfers between devices: 79.2 us -> 59.6 us  [the longest x6 30.1 us: fetched(): return lax.ppermute(block, ('ka', 'pw'), route)]
    pallas_call x6, Pallas kernels: 9.11 us -> 14.1 us  [correlate(): pl.pallas_call(functools.partial(correlate_kernel, first, depth, begun is...]
    pallas_call x6 -> x5, Pallas kernels: 8.68 us -> 7.84 us  [cut(): pl.pallas_call(functools.partial(cut_kernel, bands, waves), out_shape=jax...]
  transfers between devices with their start and end apart: 20 -> 21, of which waited for: 14 -> 8; matrix products, arithmetic and copies ran while one was open for 0% -> 0% of each run, Pallas kernels for 18% -> 22%
where the time goes in v6:
time: 145 us; the launch traced here: 144 us
  waiting for transfers between devices  59.6 us (41%)
  starting transfers between devices  51.6 us (36%)
  Pallas kernels  32.3 us (22%)
    ppermute x6, waiting for transfers between devices, fetched(): return lax.ppermute(block, ('ka', 'pw'), route)  30.1 us
    ppermute x15, waiting for transfers between devices, sent(): return lax.ppermute(block, ('ka', 'pw'), route)  29.5 us
    ppermute x6, starting transfers between devices, fetched(): return lax.ppermute(block, ('ka', 'pw'), route)  27.7 us
    ppermute x15, starting transfers between devices, sent(): return lax.ppermute(block, ('ka', 'pw'), route)  23.9 us
    pallas_call x6, Pallas kernels, correlate(): pl.pallas_call(functools.partial(correlate_kernel, first, depth, begun is...  14.1 us
    pallas_call x1, Pallas kernels, placed_bands(): pl.pallas_call(place_kernel, grid=(width // step,), out_shape=pltpu.VMEM(...  9.35 us
    pallas_call x5, Pallas kernels, cut(): pl.pallas_call(functools.partial(cut_kernel, bands, waves), out_shape=jax...  7.84 us
  transfers between devices with their start and end apart: 21, of which 8 were waited for; matrix products, arithmetic and copies ran while one was open for 0% of the time, Pallas kernels for 22%

profile of v6, /device:TPU:0, one launch (start us, length us, event | category | flops | bytes accessed | tf_op | source)
XLA Modules:
  0.0 144.3 jit_solution(2190907935811957778)
XLA Ops:
  0.0 1.3 collective-permute-start
  1.3 2.2 %cut.5.refs_1_ = bf16[2,96,10240]{2,1,0:T(8,128)(2,1)S(1)} custom-call(bf16[1,2,256,10240]{3,2,1,0:T(8,128)(2,1)} %refs_0_.9), custom_call_target="tpu_custom_call" | custom-call | bytes 1024 | tf_op jit(solution)/shard_map/cut/pallas_call | solution.py:51
  3.5 6.5 %collective-permute-start.3 = (bf16[2,96,10240]{2,1,0:T(8,128)(2,1)S(1)}, bf16[2,96,10240]{2,1,0:T(8,128)(2,1)S(1)}, u32[]{:S(2)}, u32[]{:S(2)}) collective-permute-start(bf16[2,96,10240]{2,1,0:T(8,128)(2,1)S(1)} %cut.5.refs_1_), channel_id=1, source_target_pairs={{8,4},{9,5},{10,6},{11,7},{0,12},{1,13},{2,14},{3,15},{24,20},{25,... | collective-permute-start | bytes 11796488 | tf_op jit(solution)/shard_map/ppermute | solution.py:34
  10.0 1.7 %cut.6.refs_1_ = bf16[2,64,10240]{2,1,0:T(8,128)(2,1)S(1)} custom-call(bf16[1,2,256,10240]{3,2,1,0:T(8,128)(2,1)} %refs_0_.9, bf16[2,96,10240]{2,1,0:T(8,128)(2,1)S(1)} %cut.5.refs_1_), custom_call_target="tpu_custom_call" | custom-call | bytes 1024 | tf_op jit(solution)/shard_map/cut/pallas_call | solution.py:51
  11.7 1.6 %collective-permute-start.4 = (bf16[2,64,10240]{2,1,0:T(8,128)(2,1)S(1)}, bf16[2,64,10240]{2,1,0:T(8,128)(2,1)S(1)}, u32[]{:S(2)}, u32[]{:S(2)}) collective-permute-start(bf16[2,64,10240]{2,1,0:T(8,128)(2,1)S(1)} %cut.6.refs_1_), channel_id=1, source_target_pairs={{8,4},{9,5},{10,6},{11,7},{0,12},{1,13},{2,14},{3,15},{24,20},{25,... | collective-permute-start | bytes 7864328 | tf_op jit(solution)/shard_map/ppermute | solution.py:34
  13.3 1.7 %cut.7.refs_1_ = bf16[2,64,10240]{2,1,0:T(8,128)(2,1)S(1)} custom-call(bf16[1,2,256,10240]{3,2,1,0:T(8,128)(2,1)} %refs_0_.9, bf16[2,64,10240]{2,1,0:T(8,128)(2,1)S(1)} %cut.6.refs_1_), custom_call_target="tpu_custom_call" | custom-call | bytes 1024 | tf_op jit(solution)/shard_map/cut/pallas_call | solution.py:51
  15.0 1.5 %collective-permute-start.11 = (bf16[2,64,10240]{2,1,0:T(8,128)(2,1)S(1)}, bf16[2,64,10240]{2,1,0:T(8,128)(2,1)S(1)}, u32[]{:S(2)}, u32[]{:S(2)}) collective-permute-start(bf16[2,64,10240]{2,1,0:T(8,128)(2,1)S(1)} %cut.7.refs_1_), channel_id=1, source_target_pairs={{8,4},{9,5},{10,6},{11,7},{0,12},{1,13},{2,14},{3,15},{24,20},{25,... | collective-permute-start | bytes 7864328 | tf_op jit(solution)/shard_map/ppermute | solution.py:34
  16.5 9.4 %place.1.placed_ref.refs_3_ = bf16[10240,512]{1,0:T(8,128)(2,1)S(1)} custom-call(bf16[1,2,256,10240]{3,2,1,0:T(8,128)(2,1)} %refs_0_.9, s32[1,2,10240]{2,1,0:T(2,128)S(1)} %copy-done), custom_call_target="tpu_custom_call" | custom-call | bytes 1024 | tf_op jit(solution)/shard_map/place/pallas_call | solution.py:82
  25.9 6.8 %correlate.6 = f32[2,256,256]{2,1,0:T(8,128)S(1)} custom-call(bf16[10240,512]{1,0:T(8,128)(2,1)S(1)} %place.1.placed_ref.refs_3_, bf16[2,256,10240]{2,1,0:T(8,128)(2,1)S(1)} %collective-permute-done.block_ref), custom_call_target="tpu_custom_call" | custom-call | bytes 1024 | tf_op jit(solution)/shard_map/correlate/pallas_call | solution.py:132
  32.7 4.5 %collective-permute-start.1 = (f32[2,256,256]{2,1,0:T(8,128)S(1)}, f32[2,256,256]{2,1,0:T(8,128)S(1)}, u32[]{:S(2)}, u32[]{:S(2)}) collective-permute-start(f32[2,256,256]{2,1,0:T(8,128)S(1)} %correlate.6), channel_id=1, source_target_pairs={{0,2},{1,3},{2,0},{3,1},{8,10},{9,11},{10,8},{11,9},{16,18},{17,19... | collective-permute-start | bytes 1572872 | tf_op jit(solution)/shard_map/ppermute | solution.py:26
  37.2 13.1 %collective-permute-done.1 = f32[2,256,256]{2,1,0:T(8,128)S(1)} collective-permute-done((f32[2,256,256]{2,1,0:T(8,128)S(1)}, f32[2,256,256]{2,1,0:T(8,128)S(1)}, u32[]{:S(2)}, u32[]{:S(2)}) %collective-permute-start.1) | collective-permute-done | bytes 524320 | tf_op jit(solution)/shard_map/ppermute | solution.py:26
  50.4 2.6 %collective-permute-start.2 = (f32[2,256,256]{2,1,0:T(8,128)S(1)}, f32[2,256,256]{2,1,0:T(8,128)S(1)}, u32[]{:S(2)}, u32[]{:S(2)}) collective-permute-start(f32[2,256,256]{2,1,0:T(8,128)S(1)} %add.27), channel_id=1, source_target_pairs={{0,1},{1,0},{2,3},{3,2},{8,9},{9,8},{10,11},{11,10},{16,17},{17,16... | collective-permute-start | bytes 1572872 | tf_op jit(solution)/shard_map/ppermute | solution.py:26
  53.0 1.2 cut.8.refs_1_
  54.2 3.8 %collective-permute-start.8 = (bf16[2,32,7680]{2,1,0:T(8,128)(2,1)S(1)}, bf16[2,32,7680]{2,1,0:T(8,128)(2,1)S(1)}, u32[]{:S(2)}, u32[]{:S(2)}) collective-permute-start(bf16[2,32,7680]{2,1,0:T(8,128)(2,1)S(1)} %cut.8.refs_1_), channel_id=1, source_target_pairs={{8,4},{9,5},{10,6},{11,7},{0,12},{1,13},{2,14},{3,15},{24,20},{25,... | collective-permute-start | bytes 2949128 | tf_op jit(solution)/shard_map/ppermute | solution.py:34
  58.0 3.5 %collective-permute-done.2 = f32[2,256,256]{2,1,0:T(8,128)S(1)} collective-permute-done((f32[2,256,256]{2,1,0:T(8,128)S(1)}, f32[2,256,256]{2,1,0:T(8,128)S(1)}, u32[]{:S(2)}, u32[]{:S(2)}) %collective-permute-start.2) | collective-permute-done | bytes 524320 | tf_op jit(solution)/shard_map/ppermute | solution.py:26
  61.5 2.2 %correlate.7 = f32[2,96,256]{2,1,0:T(8,128)S(1)} custom-call(bf16[10240,512]{1,0:T(8,128)(2,1)S(1)} %place.1.placed_ref.refs_3_, bf16[2,96,10240]{2,1,0:T(8,128)(2,1)S(1)} %collective-permute-done.3.refs_2_.block_ref, f32[2,256,256]{2,1,0:T(8,128)S(1)} %add.28.refs_0_), custom_call_target="tpu_custom_call" | custom-call | bytes 1024 | tf_op jit(solution)/shard_map/correlate/pallas_call | solution.py:132
  65.2 15.8 %collective-permute-done.4.refs_2_.block_ref = bf16[2,64,10240]{2,1,0:T(8,128)(2,1)S(1)} collective-permute-done((bf16[2,64,10240]{2,1,0:T(8,128)(2,1)S(1)}, bf16[2,64,10240]{2,1,0:T(8,128)(2,1)S(1)}, u32[]{:S(2)}, u32[]{:S(2)}) %collective-permute-start.4) | collective-permute-done | bytes 2621472 | tf_op jit(solution)/shard_map/ppermute | solution.py:34
  81.0 1.5 %correlate.8 = f32[2,64,256]{2,1,0:T(8,128)S(1)} custom-call(bf16[10240,512]{1,0:T(8,128)(2,1)S(1)} %place.1.placed_ref.refs_3_, bf16[2,64,10240]{2,1,0:T(8,128)(2,1)S(1)} %collective-permute-done.4.refs_2_.block_ref, f32[2,96,256]{2,1,0:T(8,128)S(1)} %add.30.refs_3_.refs_0_), custom_call_target="tpu_custom_call" | custom-call | bytes 1024 | tf_op jit(solution)/shard_map/correlate/pallas_call | solution.py:132
  84.9 13.1 %collective-permute-start.7 = (bf16[2,32,2560]{2,1,0:T(8,128)(2,1)S(1)}, bf16[2,32,2560]{2,1,0:T(8,128)(2,1)S(1)}, u32[]{:S(2)}, u32[]{:S(2)}) collective-permute-start(bf16[2,32,2560]{2,1,0:T(8,128)(2,1)S(1)} %cut.9), channel_id=1, source_target_pairs={{8,4},{9,5},{10,6},{11,7},{0,12},{1,13},{2,14},{3,15},{24,20},{25,... | collective-permute-start | bytes 983048 | tf_op jit(solution)/shard_map/ppermute | solution.py:34
  98.1 11.0 %collective-permute-done.11.block_ref = bf16[2,64,10240]{2,1,0:T(8,128)(2,1)S(1)} collective-permute-done((bf16[2,64,10240]{2,1,0:T(8,128)(2,1)S(1)}, bf16[2,64,10240]{2,1,0:T(8,128)(2,1)S(1)}, u32[]{:S(2)}, u32[]{:S(2)}) %collective-permute-start.11) | collective-permute-done | bytes 2621472 | tf_op jit(solution)/shard_map/ppermute | solution.py:34
  109.1 1.5 %correlate.9 = f32[2,64,256]{2,1,0:T(8,128)S(1)} custom-call(bf16[10240,512]{1,0:T(8,128)(2,1)S(1)} %place.1.placed_ref.refs_3_, bf16[2,64,10240]{2,1,0:T(8,128)(2,1)S(1)} %collective-permute-done.11.block_ref, f32[2,64,256]{2,1,0:T(8,128)S(1)} %add.32.refs_0_), custom_call_target="tpu_custom_call" | custom-call | bytes 1024 | tf_op jit(solution)/shard_map/correlate/pallas_call | solution.py:132
  111.3 6.3 %collective-permute-start.16 = (f32[2,256,256]{2,1,0:T(8,128)S(1)}, f32[2,256,256]{2,1,0:T(8,128)S(1)}, u32[]{:S(2)}, u32[]{:S(2)}) collective-permute-start(f32[2,256,256]{2,1,0:T(8,128)S(1)} %add.28.refs_0_), channel_id=1, source_target_pairs={{0,4},{1,5},{2,6},{3,7},{8,12},{9,13},{10,14},{11,15},{16,20},{17,... | collective-permute-start | bytes 1572872 | tf_op jit(solution)/shard_map/ppermute | solution.py:26
  118.4 1.2 collective-permute-done.8.block_ref
  119.6 1.5 %correlate.10.refs_0_ = f32[2,32,256]{2,1,0:T(8,128)S(1)} custom-call(bf16[10240,512]{1,0:T(8,128)(2,1)S(1)} %place.1.placed_ref.refs_3_, bf16[2,32,7680]{2,1,0:T(8,128)(2,1)S(1)} %collective-permute-done.8.block_ref, f32[2,160,256]{2,1,0:T(8,128)S(1)} %pad_maximum_fusion.refs_0_.refs_1_, f32[2,64,256]{2,1,0:T(8,128)S(1)} %add.34.refs_1_.refs_2_), custom_call_target="tpu_custom_call" | custom-call | bytes 1024 | tf_op jit(solution)/shard_map/correlate/pallas_call | solution.py:132
  121.1 2.0 %collective-permute-done.7.block_ref = bf16[2,32,2560]{2,1,0:T(8,128)(2,1)S(1)} collective-permute-done((bf16[2,32,2560]{2,1,0:T(8,128)(2,1)S(1)}, bf16[2,32,2560]{2,1,0:T(8,128)(2,1)S(1)}, u32[]{:S(2)}, u32[]{:S(2)}) %collective-permute-start.7) | collective-permute-done | bytes 327712 | tf_op jit(solution)/shard_map/ppermute | solution.py:34
  123.7 1.3 collective-permute-start.17
  125.7 1.3 collective-permute-start.18
  127.7 1.3 collective-permute-start.19
  129.0 1.3 collective-permute-start.20
  130.3 11.6 %collective-permute-done.19.refs_8_ = f32[2,32,256]{2,1,0:T(8,128)S(1)} collective-permute-done((f32[2,32,256]{2,1,0:T(8,128)S(1)}, f32[2,32,256]{2,1,0:T(8,128)S(1)}, u32[]{:S(2)}, u32[]{:S(2)}) %collective-permute-start.19) | collective-permute-done | bytes 65568 | tf_op jit(solution)/shard_map/ppermute | solution.py:26
  141.9 1.4 collective-permute-done.20.refs_9_
  143.2 1.1 assemble.1
  (35 shorter events, 7.3 us)
Async XLA Ops:
  0.0 25.9 %collective-permute-start = (bf16[2,256,10240]{2,1,0:T(8,128)(2,1)}, bf16[2,256,10240]{2,1,0:T(8,128)(2,1)S(1)}, u32[]{:S(2)}, u32[]{:S(2)}) collective-permute-start(bf16[2,256,10240]{2,1,0:T(8,128)(2,1)} %bitcast.1), channel_id=1, source_target_pairs={{4,0},{5,1},{6,2},{7,3},{12,8},{13,9},{14,10},{15,11},{20,16},{21,... | collective-permute-start | bytes 31457288 | tf_op jit(solution)/shard_map/ppermute | solution.py:34
  3.5 49.5 %collective-permute-start.3 = (bf16[2,96,10240]{2,1,0:T(8,128)(2,1)S(1)}, bf16[2,96,10240]{2,1,0:T(8,128)(2,1)S(1)}, u32[]{:S(2)}, u32[]{:S(2)}) collective-permute-start(bf16[2,96,10240]{2,1,0:T(8,128)(2,1)S(1)} %cut.5.refs_1_), channel_id=1, source_target_pairs={{8,4},{9,5},{10,6},{11,7},{0,12},{1,13},{2,14},{3,15},{24,20},{25,... | collective-permute-start | bytes 11796488 | tf_op jit(solution)/shard_map/ppermute | solution.py:34
  11.7 4.8 %copy-start = (s32[1,2,10240]{2,1,0:T(2,128)S(1)}, s32[1,2,10240]{2,1,0:T(2,128)}, u32[]{:S(2)}) copy-start(s32[1,2,10240]{2,1,0:T(2,128)} %shift_ref.1) | copy-start | bytes 245764
  11.7 69.3 %collective-permute-start.4 = (bf16[2,64,10240]{2,1,0:T(8,128)(2,1)S(1)}, bf16[2,64,10240]{2,1,0:T(8,128)(2,1)S(1)}, u32[]{:S(2)}, u32[]{:S(2)}) collective-permute-start(bf16[2,64,10240]{2,1,0:T(8,128)(2,1)S(1)} %cut.6.refs_1_), channel_id=1, source_target_pairs={{8,4},{9,5},{10,6},{11,7},{0,12},{1,13},{2,14},{3,15},{24,20},{25,... | collective-permute-start | bytes 7864328 | tf_op jit(solution)/shard_map/ppermute | solution.py:34
  15.0 94.0 %collective-permute-start.11 = (bf16[2,64,10240]{2,1,0:T(8,128)(2,1)S(1)}, bf16[2,64,10240]{2,1,0:T(8,128)(2,1)S(1)}, u32[]{:S(2)}, u32[]{:S(2)}) collective-permute-start(bf16[2,64,10240]{2,1,0:T(8,128)(2,1)S(1)} %cut.7.refs_1_), channel_id=1, source_target_pairs={{8,4},{9,5},{10,6},{11,7},{0,12},{1,13},{2,14},{3,15},{24,20},{25,... | collective-permute-start | bytes 7864328 | tf_op jit(solution)/shard_map/ppermute | solution.py:34
  32.7 17.6 %collective-permute-start.1 = (f32[2,256,256]{2,1,0:T(8,128)S(1)}, f32[2,256,256]{2,1,0:T(8,128)S(1)}, u32[]{:S(2)}, u32[]{:S(2)}) collective-permute-start(f32[2,256,256]{2,1,0:T(8,128)S(1)} %correlate.6), channel_id=1, source_target_pairs={{0,2},{1,3},{2,0},{3,1},{8,10},{9,11},{10,8},{11,9},{16,18},{17,19... | collective-permute-start | bytes 1572872 | tf_op jit(solution)/shard_map/ppermute | solution.py:26
  50.4 11.1 %collective-permute-start.2 = (f32[2,256,256]{2,1,0:T(8,128)S(1)}, f32[2,256,256]{2,1,0:T(8,128)S(1)}, u32[]{:S(2)}, u32[]{:S(2)}) collective-permute-start(f32[2,256,256]{2,1,0:T(8,128)S(1)} %add.27), channel_id=1, source_target_pairs={{0,1},{1,0},{2,3},{3,2},{8,9},{9,8},{10,11},{11,10},{16,17},{17,16... | collective-permute-start | bytes 1572872 | tf_op jit(solution)/shard_map/ppermute | solution.py:26
  54.2 65.4 %collective-permute-start.8 = (bf16[2,32,7680]{2,1,0:T(8,128)(2,1)S(1)}, bf16[2,32,7680]{2,1,0:T(8,128)(2,1)S(1)}, u32[]{:S(2)}, u32[]{:S(2)}) collective-permute-start(bf16[2,32,7680]{2,1,0:T(8,128)(2,1)S(1)} %cut.8.refs_1_), channel_id=1, source_target_pairs={{8,4},{9,5},{10,6},{11,7},{0,12},{1,13},{2,14},{3,15},{24,20},{25,... | collective-permute-start | bytes 2949128 | tf_op jit(solution)/shard_map/ppermute | solution.py:34
  63.7 0.7 collective-permute-start.5
  64.5 0.7 collective-permute-start.6
  82.5 0.7 collective-permute-start.9
  83.2 14.8 %collective-permute-start.10 = (f32[2,64,256]{2,1,0:T(8,128)S(1)}, f32[2,64,256]{2,1,0:T(8,128)S(1)}, u32[]{:S(2)}, u32[]{:S(2)}) collective-permute-start(f32[2,64,256]{2,1,0:T(8,128)S(1)} %add.31), channel_id=1, source_target_pairs={{4,5},{5,4},{6,7},{7,6},{12,13},{13,12},{14,15},{15,14},{20,21},{2... | collective-permute-start | bytes 393224 | tf_op jit(solution)/shard_map/ppermute | solution.py:26
  84.9 38.2 %collective-permute-start.7 = (bf16[2,32,2560]{2,1,0:T(8,128)(2,1)S(1)}, bf16[2,32,2560]{2,1,0:T(8,128)(2,1)S(1)}, u32[]{:S(2)}, u32[]{:S(2)}) collective-permute-start(bf16[2,32,2560]{2,1,0:T(8,128)(2,1)S(1)} %cut.9), channel_id=1, source_target_pairs={{8,4},{9,5},{10,6},{11,7},{0,12},{1,13},{2,14},{3,15},{24,20},{25,... | collective-permute-start | bytes 983048 | tf_op jit(solution)/shard_map/ppermute | solution.py:34
  110.6 7.0 %collective-permute-start.12 = (f32[2,64,256]{2,1,0:T(8,128)S(1)}, f32[2,64,256]{2,1,0:T(8,128)S(1)}, u32[]{:S(2)}, u32[]{:S(2)}) collective-permute-start(f32[2,64,256]{2,1,0:T(8,128)S(1)} %correlate.9), channel_id=1, source_target_pairs={{4,6},{5,7},{6,4},{7,5},{12,14},{13,15},{14,12},{15,13},{20,22},{2... | collective-permute-start | bytes 393224 | tf_op jit(solution)/shard_map/ppermute | solution.py:26
  111.3 17.7 %collective-permute-start.16 = (f32[2,256,256]{2,1,0:T(8,128)S(1)}, f32[2,256,256]{2,1,0:T(8,128)S(1)}, u32[]{:S(2)}, u32[]{:S(2)}) collective-permute-start(f32[2,256,256]{2,1,0:T(8,128)S(1)} %add.28.refs_0_), channel_id=1, source_target_pairs={{0,4},{1,5},{2,6},{3,7},{8,12},{9,13},{10,14},{11,15},{16,20},{17,... | collective-permute-start | bytes 1572872 | tf_op jit(solution)/shard_map/ppermute | solution.py:26
  117.6 0.7 collective-permute-start.13
  123.7 19.5 %collective-permute-start.17 = (f32[2,160,256]{2,1,0:T(8,128)S(1)}, f32[2,160,256]{2,1,0:T(8,128)S(1)}, u32[]{:S(2)}, u32[]{:S(2)}) collective-permute-start(f32[2,160,256]{2,1,0:T(8,128)S(1)} %get-tuple-element.8.refs_1_), channel_id=1, source_target_pairs={{4,8},{5,9},{6,10},{7,11},{12,0},{13,1},{14,2},{15,3},{20,24},{21,... | collective-permute-start | bytes 983048 | tf_op jit(solution)/shard_map/ppermute | solution.py:26
  125.0 2.0 %collective-permute-start.14 = (f32[2,32,256]{2,1,0:T(8,128)S(1)}, f32[2,32,256]{2,1,0:T(8,128)S(1)}, u32[]{:S(2)}, u32[]{:S(2)}) collective-permute-start(f32[2,32,256]{2,1,0:T(8,128)S(1)} %get-tuple-element.10), channel_id=1, source_target_pairs={{4,6},{5,7},{6,4},{7,5},{12,14},{13,15},{14,12},{15,13},{20,22},{2... | collective-permute-start | bytes 196616 | tf_op jit(solution)/shard_map/ppermute | solution.py:26
  125.7 17.6 %collective-permute-start.18 = (f32[2,64,256]{2,1,0:T(8,128)S(1)}, f32[2,64,256]{2,1,0:T(8,128)S(1)}, u32[]{:S(2)}, u32[]{:S(2)}) collective-permute-start(f32[2,64,256]{2,1,0:T(8,128)S(1)} %get-tuple-element.9.refs_2_), channel_id=1, source_target_pairs={{4,8},{5,9},{6,10},{7,11},{12,0},{13,1},{14,2},{15,3},{20,24},{21,... | collective-permute-start | bytes 393224 | tf_op jit(solution)/shard_map/ppermute | solution.py:26
  127.0 3.3 %collective-permute-start.15 = (f32[2,32,256]{2,1,0:T(8,128)S(1)}, f32[2,32,256]{2,1,0:T(8,128)S(1)}, u32[]{:S(2)}, u32[]{:S(2)}) collective-permute-start(f32[2,32,256]{2,1,0:T(8,128)S(1)} %add.35.refs_3_), channel_id=1, source_target_pairs={{4,5},{5,4},{6,7},{7,6},{12,13},{13,12},{14,15},{15,14},{20,21},{2... | collective-permute-start | bytes 196616 | tf_op jit(solution)/shard_map/ppermute | solution.py:26
  127.7 14.2 %collective-permute-start.19 = (f32[2,32,256]{2,1,0:T(8,128)S(1)}, f32[2,32,256]{2,1,0:T(8,128)S(1)}, u32[]{:S(2)}, u32[]{:S(2)}) collective-permute-start(f32[2,32,256]{2,1,0:T(8,128)S(1)} %add.35.refs_3_), channel_id=1, source_target_pairs={{4,8},{5,9},{6,10},{7,11},{12,0},{13,1},{14,2},{15,3},{20,24},{21,... | collective-permute-start | bytes 196616 | tf_op jit(solution)/shard_map/ppermute | solution.py:26
  129.0 14.2 %collective-permute-start.20 = (f32[2,32,256]{2,1,0:T(8,128)S(1)}, f32[2,32,256]{2,1,0:T(8,128)S(1)}, u32[]{:S(2)}, u32[]{:S(2)}) collective-permute-start(f32[2,32,256]{2,1,0:T(8,128)S(1)} %add.35.refs_3_), channel_id=1, source_target_pairs={{4,9},{5,8},{6,11},{7,10},{12,1},{13,0},{14,3},{15,2},{20,25},{21,... | collective-permute-start | bytes 196616 | tf_op jit(solution)/shard_map/ppermute | solution.py:26

commit v7 on v6

--- a/solution.py
+++ b/solution.py
@@ -8,30 +8,33 @@
 from jax.sharding import PartitionSpec as P
 
 PWB = 256
-SIXTEENTHS = (6, 4, 4, 2)
-EVEN, ODD = 0, 1
+SIXTEENTHS = (6, 4, 2, 2, 2)
+EVEN, ODD, ALL = (0,), (1,), (0, 1)
 MIB = 1 << 20
 ANYWHERE = pl.BlockSpec(memory_space=pl.ANY)
 WHOLE = pl.BlockSpec(memory_space=pltpu.VMEM)
 
 
-def sent(block, kind, points=0, waves=0):
+def routed(block, goal):
     ka, pw = lax.axis_size("ka"), lax.axis_size("pw")
-    route = [
-        (k * pw + p, (k + points) % ka * pw + (p ^ waves))
-        for k in range(ka)
-        for p in range(pw)
-        if k % 2 == kind
-    ]
+    route = []
+    for k in range(ka):
+        for p in range(pw):
+            point, share = goal(k, p)
+            route.append((k * pw + p, point % ka * pw + share))
     return lax.ppermute(block, ("ka", "pw"), route)
 
 
-def fetched(block, kind):
-    ka, pw = lax.axis_size("ka"), lax.axis_size("pw")
-    route = [
-        ((k + 1) % ka * pw + p, k * pw + p) for k in range(ka) for p in range(pw) if k % 2 == kind
-    ]
-    return lax.ppermute(block, ("ka", "pw"), route)
+def fetched(block):
+    return routed(block, lambda k, p: (k - 1, p))
+
+
+def swapped(block):
+    return routed(block, lambda k, p: (k ^ 1, p))
+
+
+def exchanged(block, kinds, distance):
+    return routed(block, lambda k, p: (k, p ^ distance if k % 2 in kinds else p))
 
 
 def cut_kernel(bands, waves, *refs):
@@ -143,23 +146,29 @@
     return out if held else out[0]
 
 
-def summed_over_pw(partial, kind, nearest=1):
+def summed_over_pw(partial, kinds, nearest=1):
     distance = lax.axis_size("pw") // 2
     while distance >= nearest:
-        partial = partial + sent(partial, kind, waves=distance)
+        partial = partial + exchanged(partial, kinds, distance)
         distance //= 2
     return partial
 
 
-def assemble_kernel(counts, *refs):
+def stepped(block, kinds=(), distance=0):
+    return routed(block, lambda k, p: (k + 1, p ^ distance if k % 2 in kinds else p))
+
+
+def assemble_kernel(counts, kind_ref, *refs):
     ins, (out_ref, made, sems) = list(refs[:-3]), refs[-3:]
     parts = [[ins.pop(0) for _ in range(count)] for count in counts]
+    odd = kind_ref[0] == 1
     copies = []
     for side in (1, 0):
-        near, early, late = parts[3 * side : 3 * side + 3]
+        early, near, far = parts[3 * side : 3 * side + 3]
         for c in (0, 1):
-            far = jnp.concatenate([ref[c] for ref in early] + [sum(ref[c] for ref in late)], axis=0)
-            matrix = near[0][c] + far
+            terms = near[0][c], far[0][c] + far[1][c]
+            late = jnp.where(odd, terms[1 - side], terms[side])
+            matrix = jnp.concatenate([ref[c] for ref in early] + [late], axis=0)
             if side == 0:
                 matrix = matrix.T
             elif c == 1:
@@ -178,10 +187,11 @@
 def assembled(*parts):
     bands = parts[0][0].shape[2]
     counts = [len(part) for part in parts]
+    kind = (lax.axis_index("ka") % 2).astype(jnp.int32).reshape(1)
     return pl.pallas_call(
         functools.partial(assemble_kernel, counts),
         out_shape=jax.ShapeDtypeStruct((1, 2, 2, bands, bands), jnp.float32),
-        in_specs=[WHOLE] * sum(counts),
+        in_specs=[pl.BlockSpec(memory_space=pltpu.SMEM)] + [WHOLE] * sum(counts),
         out_specs=ANYWHERE,
         scratch_shapes=[
             pltpu.VMEM((4, bands, bands), jnp.float32),
@@ -190,7 +200,7 @@
         compiler_params=pltpu.CompilerParams(vmem_limit_bytes=16 * MIB),
         cost_estimate=pl.CostEstimate(flops=0, bytes_accessed=1024, transcendentals=0),
         name="assemble",
-    )(*[array for part in parts for array in part])
+    )(kind, *[array for part in parts for array in part])
 
 
 def local(coefficients, shifts):
@@ -200,7 +210,6 @@
     for size in SIXTEENTHS:
         edges.append(edges[-1] + size * unit)
     late = width // PWB * 3 // 4 * PWB
-    near_block = fetched(coefficients[0], EVEN)
     coefficients = pltpu.with_memory_space_constraint(coefficients, pltpu.HBM)
     placed = pltpu.with_memory_space_constraint(placed_bands(coefficients, shifts), pltpu.VMEM)
     blocks, arrived, whole = [], [], []
@@ -208,26 +217,29 @@
     def send(chunk, low, high, *others):
         some = slice(edges[chunk], edges[chunk + 1])
         blocks.append(cut(coefficients, some, slice(low, high), *blocks[-1:], *others))
-        arrived.append(fetched(blocks[-1], ODD))
+        return blocks[-1]
 
     for chunk in range(3):
-        send(chunk, 0, width)
-    near = summed_over_pw(correlate(placed, near_block), EVEN)
-    near_before = sent(near, EVEN, points=1)
-    send(3, 0, late, arrived[0], placed)
-    for chunk in range(3):
-        if chunk == 2:
-            send(3, late, width, arrived[1], whole[0])
-        before = whole[-1] if whole else near
-        whole.append(summed_over_pw(correlate(placed, arrived[chunk], before), ODD))
-    halves = [jnp.concatenate(whole[:2], axis=1), whole[2]]
-    last = correlate(placed, arrived[3], *halves)
-    last, *halves = correlate(placed, arrived[4], first=late, begun=last, held=halves)
-    halves_before = [sent(half, ODD, points=1) for half in halves]
+        arrived.append(fetched(send(chunk, 0, width)))
+    arrived.append(fetched(send(3, 0, width, arrived[0], placed)))
+    near_block = swapped(send(4, 0, width))
+    whole.append(summed_over_pw(correlate(placed, arrived[0]), ALL))
+    near = summed_over_pw(correlate(placed, near_block, whole[0]), EVEN)
+    near_before = swapped(near)
+    arrived.append(fetched(send(4, 0, late, arrived[1], near)))
+    whole.append(summed_over_pw(correlate(placed, arrived[1], near), ALL))
+    arrived.append(fetched(send(4, late, width, arrived[2], whole[1])))
+    for chunk in (2, 3):
+        partial = correlate(placed, arrived[chunk], whole[-1], near_before)
+        whole.append(summed_over_pw(partial, ALL))
+    halves = [jnp.concatenate(whole[:2], axis=1), jnp.concatenate(whole[2:], axis=1)]
+    last = correlate(placed, arrived[4], *halves)
+    last, *halves = correlate(placed, arrived[5], first=late, begun=last, held=halves)
+    halves_before = [stepped(half) for half in halves]
     last = summed_over_pw(last, ODD, nearest=2)
-    ahead = [last, sent(last, ODD, waves=1)]
-    behind = [sent(last, ODD, points=1), sent(last, ODD, points=1, waves=1)]
-    return assembled([near], halves, ahead, [near_before], halves_before, behind)
+    ahead = [last, exchanged(last, ODD, 1)]
+    behind = [stepped(last), stepped(last, ODD, 1)]
+    return assembled(halves, [near], ahead, halves_before, [near_before], behind)
 
 
 def solution(mesh):

time: 145 us -> 147 us (1.014); the launches traced: 144 us -> 145 us
  waiting for transfers between devices: 59.6 us -> 73 us
  starting transfers between devices: 51.6 us -> 39.4 us
    ppermute x21 -> x24, waiting for transfers between devices: 59.6 us -> 73 us  [routed(): return lax.ppermute(block, ('ka', 'pw'), route)]
    ppermute x21 -> x24, starting transfers between devices: 51.6 us -> 39.4 us  [routed(): return lax.ppermute(block, ('ka', 'pw'), route)]
    pallas_call x6 -> x7, Pallas kernels: 14.1 us -> 11.4 us  [correlate(): pl.pallas_call(functools.partial(correlate_kernel, first, depth, begun is...]
    pallas_call x5 -> x7, Pallas kernels: 7.84 us -> 10 us  [cut(): pl.pallas_call(functools.partial(cut_kernel, bands, waves), out_shape=jax...]
  transfers between devices with their start and end apart: 21 -> 24, of which waited for: 8 -> 12; matrix products, arithmetic and copies ran while one was open for 0% -> 0% of each run, Pallas kernels for 22% -> 19%
where the time goes in v7:
time: 147 us; the launch traced here: 145 us
  waiting for transfers between devices  73 us (50%)
  starting transfers between devices  39.4 us (27%)
  Pallas kernels  31.8 us (22%)
    ppermute x24, waiting for transfers between devices, routed(): return lax.ppermute(block, ('ka', 'pw'), route)  73 us
    ppermute x24, starting transfers between devices, routed(): return lax.ppermute(block, ('ka', 'pw'), route)  39.4 us
    pallas_call x7, Pallas kernels, correlate(): pl.pallas_call(functools.partial(correlate_kernel, first, depth, begun is...  11.4 us
    pallas_call x7, Pallas kernels, cut(): pl.pallas_call(functools.partial(cut_kernel, bands, waves), out_shape=jax...  10 us
    pallas_call x1, Pallas kernels, placed_bands(): pl.pallas_call(place_kernel, grid=(width // step,), out_shape=pltpu.VMEM(...  9.35 us
  transfers between devices with their start and end apart: 24, of which 12 were waited for; matrix products, arithmetic and copies ran while one was open for 0% of the time, Pallas kernels for 19%

profile of v7, /device:TPU:0, one launch (start us, length us, event | category | flops | bytes accessed | tf_op | source)
XLA Modules:
  0.0 144.8 jit_solution(13531659265070416729)
XLA Ops:
  0.0 2.2 %cut.7.refs_1_ = bf16[2,96,10240]{2,1,0:T(8,128)(2,1)S(1)} custom-call(bf16[1,2,256,10240]{3,2,1,0:T(8,128)(2,1)} %refs_0_.13), custom_call_target="tpu_custom_call" | custom-call | bytes 1024 | tf_op jit(solution)/shard_map/cut/pallas_call | solution.py:54
  2.2 2.4 %collective-permute-start = (bf16[2,96,10240]{2,1,0:T(8,128)(2,1)S(1)}, bf16[2,96,10240]{2,1,0:T(8,128)(2,1)S(1)}, u32[]{:S(2)}, u32[]{:S(2)}) collective-permute-start(bf16[2,96,10240]{2,1,0:T(8,128)(2,1)S(1)} %cut.7.refs_1_), channel_id=1, source_target_pairs={{0,12},{1,13},{2,14},{3,15},{4,0},{5,1},{6,2},{7,3},{8,4},{9,5},{1... | collective-permute-start | bytes 11796488 | tf_op jit(solution)/shard_map/ppermute | solution.py:25
  4.6 1.7 %cut.8.refs_1_ = bf16[2,64,10240]{2,1,0:T(8,128)(2,1)S(1)} custom-call(bf16[1,2,256,10240]{3,2,1,0:T(8,128)(2,1)} %refs_0_.13, bf16[2,96,10240]{2,1,0:T(8,128)(2,1)S(1)} %cut.7.refs_1_), custom_call_target="tpu_custom_call" | custom-call | bytes 1024 | tf_op jit(solution)/shard_map/cut/pallas_call | solution.py:54
  8.4 9.3 %place.1.refs_3_.placed_ref = bf16[10240,512]{1,0:T(8,128)(2,1)S(1)} custom-call(bf16[1,2,256,10240]{3,2,1,0:T(8,128)(2,1)} %refs_0_.13, s32[1,2,10240]{2,1,0:T(2,128)S(1)} %copy-done), custom_call_target="tpu_custom_call" | custom-call | bytes 1024 | tf_op jit(solution)/shard_map/place/pallas_call | solution.py:85
  17.7 30.1 %collective-permute-done.refs_2_.block_ref = bf16[2,96,10240]{2,1,0:T(8,128)(2,1)S(1)} collective-permute-done((bf16[2,96,10240]{2,1,0:T(8,128)(2,1)S(1)}, bf16[2,96,10240]{2,1,0:T(8,128)(2,1)S(1)}, u32[]{:S(2)}, u32[]{:S(2)}) %collective-permute-start) | collective-permute-done | bytes 3932192 | tf_op jit(solution)/shard_map/ppermute | solution.py:25
  52.9 2.2 %correlate.7 = f32[2,96,256]{2,1,0:T(8,128)S(1)} custom-call(bf16[10240,512]{1,0:T(8,128)(2,1)S(1)} %place.1.refs_3_.placed_ref, bf16[2,96,10240]{2,1,0:T(8,128)(2,1)S(1)} %collective-permute-done.refs_2_.block_ref), custom_call_target="tpu_custom_call" | custom-call | bytes 1024 | tf_op jit(solution)/shard_map/correlate/pallas_call | solution.py:135
  55.1 2.7 %collective-permute-start.3 = (f32[2,96,256]{2,1,0:T(8,128)S(1)}, f32[2,96,256]{2,1,0:T(8,128)S(1)}, u32[]{:S(2)}, u32[]{:S(2)}) collective-permute-start(f32[2,96,256]{2,1,0:T(8,128)S(1)} %correlate.7), channel_id=1, source_target_pairs={{0,2},{1,3},{2,0},{3,1},{4,6},{5,7},{6,4},{7,5},{8,10},{9,11},{10,... | collective-permute-start | bytes 589832 | tf_op jit(solution)/shard_map/ppermute | solution.py:25
  57.8 9.4 %collective-permute-done.3 = f32[2,96,256]{2,1,0:T(8,128)S(1)} collective-permute-done((f32[2,96,256]{2,1,0:T(8,128)S(1)}, f32[2,96,256]{2,1,0:T(8,128)S(1)}, u32[]{:S(2)}, u32[]{:S(2)}) %collective-permute-start.3) | collective-permute-done | bytes 196640 | tf_op jit(solution)/shard_map/ppermute | solution.py:25
  67.9 5.4 %collective-permute-done.4 = f32[2,96,256]{2,1,0:T(8,128)S(1)} collective-permute-done((f32[2,96,256]{2,1,0:T(8,128)S(1)}, f32[2,96,256]{2,1,0:T(8,128)S(1)}, u32[]{:S(2)}, u32[]{:S(2)}) %collective-permute-start.4) | collective-permute-done | bytes 196640 | tf_op jit(solution)/shard_map/ppermute | solution.py:25
  73.3 1.9 %correlate.8 = f32[2,32,256]{2,1,0:T(8,128)S(1)} custom-call(bf16[10240,512]{1,0:T(8,128)(2,1)S(1)} %place.1.refs_3_.placed_ref, bf16[2,32,10240]{2,1,0:T(8,128)(2,1)S(1)} %collective-permute-done.2.block_ref, f32[2,96,256]{2,1,0:T(8,128)S(1)} %add.39.refs_0_), custom_call_target="tpu_custom_call" | custom-call | bytes 1024 | tf_op jit(solution)/shard_map/correlate/pallas_call | solution.py:135
  75.2 5.0 %collective-permute-start.5 = (f32[2,32,256]{2,1,0:T(8,128)S(1)}, f32[2,32,256]{2,1,0:T(8,128)S(1)}, u32[]{:S(2)}, u32[]{:S(2)}) collective-permute-start(f32[2,32,256]{2,1,0:T(8,128)S(1)} %correlate.8), channel_id=1, source_target_pairs={{0,2},{1,3},{2,0},{3,1},{4,4},{5,5},{6,6},{7,7},{8,10},{9,11},{10,... | collective-permute-start | bytes 196616 | tf_op jit(solution)/shard_map/ppermute | solution.py:25
  80.3 2.2 %collective-permute-done.5 = f32[2,32,256]{2,1,0:T(8,128)S(1)} collective-permute-done((f32[2,32,256]{2,1,0:T(8,128)S(1)}, f32[2,32,256]{2,1,0:T(8,128)S(1)}, u32[]{:S(2)}, u32[]{:S(2)}) %collective-permute-start.5) | collective-permute-done | bytes 65568 | tf_op jit(solution)/shard_map/ppermute | solution.py:25
  82.5 3.6 %collective-permute-start.6 = (f32[2,32,256]{2,1,0:T(8,128)S(1)}, f32[2,32,256]{2,1,0:T(8,128)S(1)}, u32[]{:S(2)}, u32[]{:S(2)}) collective-permute-start(f32[2,32,256]{2,1,0:T(8,128)S(1)} %add.40), channel_id=1, source_target_pairs={{0,1},{1,0},{2,3},{3,2},{4,4},{5,5},{6,6},{7,7},{8,9},{9,8},{10,11... | collective-permute-start | bytes 196616 | tf_op jit(solution)/shard_map/ppermute | solution.py:25
  86.2 2.5 %collective-permute-done.6 = f32[2,32,256]{2,1,0:T(8,128)S(1)} collective-permute-done((f32[2,32,256]{2,1,0:T(8,128)S(1)}, f32[2,32,256]{2,1,0:T(8,128)S(1)}, u32[]{:S(2)}, u32[]{:S(2)}) %collective-permute-start.6) | collective-permute-done | bytes 65568 | tf_op jit(solution)/shard_map/ppermute | solution.py:25
  90.0 1.5 %correlate.9 = f32[2,64,256]{2,1,0:T(8,128)S(1)} custom-call(bf16[10240,512]{1,0:T(8,128)(2,1)S(1)} %place.1.refs_3_.placed_ref, bf16[2,64,10240]{2,1,0:T(8,128)(2,1)S(1)} %collective-permute-done.1.refs_2_.block_ref, f32[2,32,256]{2,1,0:T(8,128)S(1)} %add.41.refs_3_.refs_0_.refs_2_), custom_call_target="tpu_custom_call" | custom-call | bytes 1024 | tf_op jit(solution)/shard_map/correlate/pallas_call | solution.py:135
  91.5 3.1 %collective-permute-start.8 = (f32[2,64,256]{2,1,0:T(8,128)S(1)}, f32[2,64,256]{2,1,0:T(8,128)S(1)}, u32[]{:S(2)}, u32[]{:S(2)}) collective-permute-start(f32[2,64,256]{2,1,0:T(8,128)S(1)} %correlate.9), channel_id=1, source_target_pairs={{0,2},{1,3},{2,0},{3,1},{4,6},{5,7},{6,4},{7,5},{8,10},{9,11},{10,... | collective-permute-start | bytes 393224 | tf_op jit(solution)/shard_map/ppermute | solution.py:25
  94.6 7.0 %collective-permute-done.8 = f32[2,64,256]{2,1,0:T(8,128)S(1)} collective-permute-done((f32[2,64,256]{2,1,0:T(8,128)S(1)}, f32[2,64,256]{2,1,0:T(8,128)S(1)}, u32[]{:S(2)}, u32[]{:S(2)}) %collective-permute-start.8) | collective-permute-done | bytes 131104 | tf_op jit(solution)/shard_map/ppermute | solution.py:25
  102.4 4.6 %collective-permute-done.9 = f32[2,64,256]{2,1,0:T(8,128)S(1)} collective-permute-done((f32[2,64,256]{2,1,0:T(8,128)S(1)}, f32[2,64,256]{2,1,0:T(8,128)S(1)}, u32[]{:S(2)}, u32[]{:S(2)}) %collective-permute-start.9) | collective-permute-done | bytes 131104 | tf_op jit(solution)/shard_map/ppermute | solution.py:25
  107.0 1.9 %correlate.10 = f32[2,32,256]{2,1,0:T(8,128)S(1)} custom-call(bf16[10240,512]{1,0:T(8,128)(2,1)S(1)} %place.1.refs_3_.placed_ref, bf16[2,32,10240]{2,1,0:T(8,128)(2,1)S(1)} %collective-permute-done.7.refs_2_.block_ref, f32[2,64,256]{2,1,0:T(8,128)S(1)} %add.43.refs_3_.refs_0_, f32[2,32,256]{2,1,0:T(8,128)S(1)} %collective-permute-done.12.refs_1_.refs_7_), custom_call_target="tpu_custom_call" | custom-call | bytes 1024 | tf_op jit(solution)/shard_map/correlate/pallas_call | solution.py:135
  109.0 2.6 %collective-permute-start.13 = (f32[2,32,256]{2,1,0:T(8,128)S(1)}, f32[2,32,256]{2,1,0:T(8,128)S(1)}, u32[]{:S(2)}, u32[]{:S(2)}) collective-permute-start(f32[2,32,256]{2,1,0:T(8,128)S(1)} %correlate.10), channel_id=1, source_target_pairs={{0,2},{1,3},{2,0},{3,1},{4,6},{5,7},{6,4},{7,5},{8,10},{9,11},{10,... | collective-permute-start | bytes 196616 | tf_op jit(solution)/shard_map/ppermute | solution.py:25
  111.5 2.7 %collective-permute-done.13 = f32[2,32,256]{2,1,0:T(8,128)S(1)} collective-permute-done((f32[2,32,256]{2,1,0:T(8,128)S(1)}, f32[2,32,256]{2,1,0:T(8,128)S(1)}, u32[]{:S(2)}, u32[]{:S(2)}) %collective-permute-start.13) | collective-permute-done | bytes 65568 | tf_op jit(solution)/shard_map/ppermute | solution.py:25
  116.7 1.9 %collective-permute-done.14 = f32[2,32,256]{2,1,0:T(8,128)S(1)} collective-permute-done((f32[2,32,256]{2,1,0:T(8,128)S(1)}, f32[2,32,256]{2,1,0:T(8,128)S(1)}, u32[]{:S(2)}, u32[]{:S(2)}) %collective-permute-start.14) | collective-permute-done | bytes 65568 | tf_op jit(solution)/shard_map/ppermute | solution.py:25
  118.6 1.9 %correlate.11 = f32[2,32,256]{2,1,0:T(8,128)S(1)} custom-call(bf16[10240,512]{1,0:T(8,128)(2,1)S(1)} %place.1.refs_3_.placed_ref, bf16[2,32,10240]{2,1,0:T(8,128)(2,1)S(1)} %collective-permute-done.15.block_ref, f32[2,32,256]{2,1,0:T(8,128)S(1)} %add.45.refs_0_, f32[2,32,256]{2,1,0:T(8,128)S(1)} %collective-permute-done.12.refs_1_.refs_7_), custom_call_target="tpu_custom_call" | custom-call | bytes 1024 | tf_op jit(solution)/shard_map/correlate/pallas_call | solution.py:135
  120.5 2.7 %collective-permute-start.16 = (f32[2,32,256]{2,1,0:T(8,128)S(1)}, f32[2,32,256]{2,1,0:T(8,128)S(1)}, u32[]{:S(2)}, u32[]{:S(2)}) collective-permute-start(f32[2,32,256]{2,1,0:T(8,128)S(1)} %correlate.11), channel_id=1, source_target_pairs={{0,2},{1,3},{2,0},{3,1},{4,6},{5,7},{6,4},{7,5},{8,10},{9,11},{10,... | collective-permute-start | bytes 196616 | tf_op jit(solution)/shard_map/ppermute | solution.py:25
  123.2 2.5 %collective-permute-done.16 = f32[2,32,256]{2,1,0:T(8,128)S(1)} collective-permute-done((f32[2,32,256]{2,1,0:T(8,128)S(1)}, f32[2,32,256]{2,1,0:T(8,128)S(1)}, u32[]{:S(2)}, u32[]{:S(2)}) %collective-permute-start.16) | collective-permute-done | bytes 65568 | tf_op jit(solution)/shard_map/ppermute | solution.py:25
  125.7 1.8 %collective-permute-start.17 = (f32[2,32,256]{2,1,0:T(8,128)S(1)}, f32[2,32,256]{2,1,0:T(8,128)S(1)}, u32[]{:S(2)}, u32[]{:S(2)}) collective-permute-start(f32[2,32,256]{2,1,0:T(8,128)S(1)} %add.46), channel_id=1, source_target_pairs={{0,1},{1,0},{2,3},{3,2},{4,5},{5,4},{6,7},{7,6},{8,9},{9,8},{10,11... | collective-permute-start | bytes 196616 | tf_op jit(solution)/shard_map/ppermute | solution.py:25
  127.6 2.5 %collective-permute-done.17 = f32[2,32,256]{2,1,0:T(8,128)S(1)} collective-permute-done((f32[2,32,256]{2,1,0:T(8,128)S(1)}, f32[2,32,256]{2,1,0:T(8,128)S(1)}, u32[]{:S(2)}, u32[]{:S(2)}) %collective-permute-start.17) | collective-permute-done | bytes 65568 | tf_op jit(solution)/shard_map/ppermute | solution.py:25
  130.1 1.5 %correlate.12.refs_0_ = f32[2,32,256]{2,1,0:T(8,128)S(1)} custom-call(bf16[10240,512]{1,0:T(8,128)(2,1)S(1)} %place.1.refs_3_.placed_ref, bf16[2,32,7680]{2,1,0:T(8,128)(2,1)S(1)} %collective-permute-done.11.block_ref, f32[2,160,256]{2,1,0:T(8,128)S(1)} %pad_maximum_fusion.refs_0_.refs_1_, f32[2,64,256]{2,1,0:T(8,128)S(1)} %pad_maximum_fusion.1.refs_1_.refs_2_), custom_call_target="tpu_custom_call" | custom-call | bytes 1024 | tf_op jit(solution)/shard_map/correlate/pallas_call | solution.py:135
  132.9 4.8 %collective-permute-start.21 = (f32[2,64,256]{2,1,0:T(8,128)S(1)}, f32[2,64,256]{2,1,0:T(8,128)S(1)}, u32[]{:S(2)}, u32[]{:S(2)}) collective-permute-start(f32[2,64,256]{2,1,0:T(8,128)S(1)} %get-tuple-element.9.refs_1_), channel_id=1, source_target_pairs={{0,4},{1,5},{2,6},{3,7},{4,8},{5,9},{6,10},{7,11},{8,12},{9,13},{1... | collective-permute-start | bytes 393224 | tf_op jit(solution)/shard_map/ppermute | solution.py:25
  137.7 1.6 %collective-permute-start.23 = (f32[2,32,256]{2,1,0:T(8,128)S(1)}, f32[2,32,256]{2,1,0:T(8,128)S(1)}, u32[]{:S(2)}, u32[]{:S(2)}) collective-permute-start(f32[2,32,256]{2,1,0:T(8,128)S(1)} %add.48.refs_3_), channel_id=1, source_target_pairs={{0,4},{1,5},{2,6},{3,7},{4,9},{5,8},{6,11},{7,10},{8,12},{9,13},{1... | collective-permute-start | bytes 196616 | tf_op jit(solution)/shard_map/ppermute | solution.py:25
  139.3 1.4 collective-permute-start.22
  141.4 2.4 %collective-permute-done.23.refs_9_ = f32[2,32,256]{2,1,0:T(8,128)S(1)} collective-permute-done((f32[2,32,256]{2,1,0:T(8,128)S(1)}, f32[2,32,256]{2,1,0:T(8,128)S(1)}, u32[]{:S(2)}, u32[]{:S(2)}) %collective-permute-start.23) | collective-permute-done | bytes 65568 | tf_op jit(solution)/shard_map/ppermute | solution.py:25
  (47 shorter events, 15.6 us)
Async XLA Ops:
  2.2 45.6 %collective-permute-start = (bf16[2,96,10240]{2,1,0:T(8,128)(2,1)S(1)}, bf16[2,96,10240]{2,1,0:T(8,128)(2,1)S(1)}, u32[]{:S(2)}, u32[]{:S(2)}) collective-permute-start(bf16[2,96,10240]{2,1,0:T(8,128)(2,1)S(1)} %cut.7.refs_1_), channel_id=1, source_target_pairs={{0,12},{1,13},{2,14},{3,15},{4,0},{5,1},{6,2},{7,3},{8,4},{9,5},{1... | collective-permute-start | bytes 11796488 | tf_op jit(solution)/shard_map/ppermute | solution.py:25
  6.3 2.0 %copy-start = (s32[1,2,10240]{2,1,0:T(2,128)S(1)}, s32[1,2,10240]{2,1,0:T(2,128)}, u32[]{:S(2)}) copy-start(s32[1,2,10240]{2,1,0:T(2,128)} %shift_ref.1) | copy-start | bytes 245764
  6.3 82.4 %collective-permute-start.1 = (bf16[2,64,10240]{2,1,0:T(8,128)(2,1)S(1)}, bf16[2,64,10240]{2,1,0:T(8,128)(2,1)S(1)}, u32[]{:S(2)}, u32[]{:S(2)}) collective-permute-start(bf16[2,64,10240]{2,1,0:T(8,128)(2,1)S(1)} %cut.8.refs_1_), channel_id=1, source_target_pairs={{0,12},{1,13},{2,14},{3,15},{4,0},{5,1},{6,2},{7,3},{8,4},{9,5},{1... | collective-permute-start | bytes 7864328 | tf_op jit(solution)/shard_map/ppermute | solution.py:25
  50.4 22.9 %collective-permute-start.2 = (bf16[2,32,10240]{2,1,0:T(8,128)(2,1)S(1)}, bf16[2,32,10240]{2,1,0:T(8,128)(2,1)S(1)}, u32[]{:S(2)}, u32[]{:S(2)}) collective-permute-start(bf16[2,32,10240]{2,1,0:T(8,128)(2,1)S(1)} %cut.11.refs_1_), channel_id=1, source_target_pairs={{0,4},{1,5},{2,6},{3,7},{4,0},{5,1},{6,2},{7,3},{8,12},{9,13},{10,... | collective-permute-start | bytes 3932168 | tf_op jit(solution)/shard_map/ppermute | solution.py:25
  51.3 55.7 %collective-permute-start.7 = (bf16[2,32,10240]{2,1,0:T(8,128)(2,1)S(1)}, bf16[2,32,10240]{2,1,0:T(8,128)(2,1)S(1)}, u32[]{:S(2)}, u32[]{:S(2)}) collective-permute-start(bf16[2,32,10240]{2,1,0:T(8,128)(2,1)S(1)} %cut.9.refs_1_), channel_id=1, source_target_pairs={{0,12},{1,13},{2,14},{3,15},{4,0},{5,1},{6,2},{7,3},{8,4},{9,5},{1... | collective-permute-start | bytes 3932168 | tf_op jit(solution)/shard_map/ppermute | solution.py:25
  52.5 66.1 %collective-permute-start.15 = (bf16[2,32,10240]{2,1,0:T(8,128)(2,1)S(1)}, bf16[2,32,10240]{2,1,0:T(8,128)(2,1)S(1)}, u32[]{:S(2)}, u32[]{:S(2)}) collective-permute-start(bf16[2,32,10240]{2,1,0:T(8,128)(2,1)S(1)} %cut.10.refs_1_), channel_id=1, source_target_pairs={{0,12},{1,13},{2,14},{3,15},{4,0},{5,1},{6,2},{7,3},{8,4},{9,5},{1... | collective-permute-start | bytes 3932168 | tf_op jit(solution)/shard_map/ppermute | solution.py:25
  55.1 12.0 %collective-permute-start.3 = (f32[2,96,256]{2,1,0:T(8,128)S(1)}, f32[2,96,256]{2,1,0:T(8,128)S(1)}, u32[]{:S(2)}, u32[]{:S(2)}) collective-permute-start(f32[2,96,256]{2,1,0:T(8,128)S(1)} %correlate.7), channel_id=1, source_target_pairs={{0,2},{1,3},{2,0},{3,1},{4,6},{5,7},{6,4},{7,5},{8,10},{9,11},{10,... | collective-permute-start | bytes 589832 | tf_op jit(solution)/shard_map/ppermute | solution.py:25
  67.2 6.1 %collective-permute-start.4 = (f32[2,96,256]{2,1,0:T(8,128)S(1)}, f32[2,96,256]{2,1,0:T(8,128)S(1)}, u32[]{:S(2)}, u32[]{:S(2)}) collective-permute-start(f32[2,96,256]{2,1,0:T(8,128)S(1)} %add.38), channel_id=1, source_target_pairs={{0,1},{1,0},{2,3},{3,2},{4,5},{5,4},{6,7},{7,6},{8,9},{9,8},{10,11... | collective-permute-start | bytes 589832 | tf_op jit(solution)/shard_map/ppermute | solution.py:25
  75.2 7.3 %collective-permute-start.5 = (f32[2,32,256]{2,1,0:T(8,128)S(1)}, f32[2,32,256]{2,1,0:T(8,128)S(1)}, u32[]{:S(2)}, u32[]{:S(2)}) collective-permute-start(f32[2,32,256]{2,1,0:T(8,128)S(1)} %correlate.8), channel_id=1, source_target_pairs={{0,2},{1,3},{2,0},{3,1},{4,4},{5,5},{6,6},{7,7},{8,10},{9,11},{10,... | collective-permute-start | bytes 196616 | tf_op jit(solution)/shard_map/ppermute | solution.py:25
  82.5 6.2 %collective-permute-start.6 = (f32[2,32,256]{2,1,0:T(8,128)S(1)}, f32[2,32,256]{2,1,0:T(8,128)S(1)}, u32[]{:S(2)}, u32[]{:S(2)}) collective-permute-start(f32[2,32,256]{2,1,0:T(8,128)S(1)} %add.40), channel_id=1, source_target_pairs={{0,1},{1,0},{2,3},{3,2},{4,4},{5,5},{6,6},{7,7},{8,9},{9,8},{10,11... | collective-permute-start | bytes 196616 | tf_op jit(solution)/shard_map/ppermute | solution.py:25
  89.9 40.2 %collective-permute-start.11 = (bf16[2,32,7680]{2,1,0:T(8,128)(2,1)S(1)}, bf16[2,32,7680]{2,1,0:T(8,128)(2,1)S(1)}, u32[]{:S(2)}, u32[]{:S(2)}) collective-permute-start(bf16[2,32,7680]{2,1,0:T(8,128)(2,1)S(1)} %cut.12.refs_1_), channel_id=1, source_target_pairs={{0,12},{1,13},{2,14},{3,15},{4,0},{5,1},{6,2},{7,3},{8,4},{9,5},{1... | collective-permute-start | bytes 2949128 | tf_op jit(solution)/shard_map/ppermute | solution.py:25
  91.5 10.1 %collective-permute-start.8 = (f32[2,64,256]{2,1,0:T(8,128)S(1)}, f32[2,64,256]{2,1,0:T(8,128)S(1)}, u32[]{:S(2)}, u32[]{:S(2)}) collective-permute-start(f32[2,64,256]{2,1,0:T(8,128)S(1)} %correlate.9), channel_id=1, source_target_pairs={{0,2},{1,3},{2,0},{3,1},{4,6},{5,7},{6,4},{7,5},{8,10},{9,11},{10,... | collective-permute-start | bytes 393224 | tf_op jit(solution)/shard_map/ppermute | solution.py:25
  101.6 5.4 %collective-permute-start.9 = (f32[2,64,256]{2,1,0:T(8,128)S(1)}, f32[2,64,256]{2,1,0:T(8,128)S(1)}, u32[]{:S(2)}, u32[]{:S(2)}) collective-permute-start(f32[2,64,256]{2,1,0:T(8,128)S(1)} %add.42), channel_id=1, source_target_pairs={{0,1},{1,0},{2,3},{3,2},{4,5},{5,4},{6,7},{7,6},{8,9},{9,8},{10,11... | collective-permute-start | bytes 393224 | tf_op jit(solution)/shard_map/ppermute | solution.py:25
  102.4 4.6 %collective-permute-start.12 = (f32[2,32,256]{2,1,0:T(8,128)S(1)}, f32[2,32,256]{2,1,0:T(8,128)S(1)}, u32[]{:S(2)}, u32[]{:S(2)}) collective-permute-start(f32[2,32,256]{2,1,0:T(8,128)S(1)} %add.41.refs_3_.refs_0_.refs_2_), channel_id=1, source_target_pairs={{0,4},{1,5},{2,6},{3,7},{4,0},{5,1},{6,2},{7,3},{8,12},{9,13},{10,... | collective-permute-start | bytes 196616 | tf_op jit(solution)/shard_map/ppermute | solution.py:25
  109.0 5.2 %collective-permute-start.13 = (f32[2,32,256]{2,1,0:T(8,128)S(1)}, f32[2,32,256]{2,1,0:T(8,128)S(1)}, u32[]{:S(2)}, u32[]{:S(2)}) collective-permute-start(f32[2,32,256]{2,1,0:T(8,128)S(1)} %correlate.10), channel_id=1, source_target_pairs={{0,2},{1,3},{2,0},{3,1},{4,6},{5,7},{6,4},{7,5},{8,10},{9,11},{10,... | collective-permute-start | bytes 196616 | tf_op jit(solution)/shard_map/ppermute | solution.py:25
  114.2 4.3 %collective-permute-start.14 = (f32[2,32,256]{2,1,0:T(8,128)S(1)}, f32[2,32,256]{2,1,0:T(8,128)S(1)}, u32[]{:S(2)}, u32[]{:S(2)}) collective-permute-start(f32[2,32,256]{2,1,0:T(8,128)S(1)} %add.44), channel_id=1, source_target_pairs={{0,1},{1,0},{2,3},{3,2},{4,5},{5,4},{6,7},{7,6},{8,9},{9,8},{10,11... | collective-permute-start | bytes 196616 | tf_op jit(solution)/shard_map/ppermute | solution.py:25
  116.6 14.9 %collective-permute-start.10 = (bf16[2,32,2560]{2,1,0:T(8,128)(2,1)S(1)}, bf16[2,32,2560]{2,1,0:T(8,128)(2,1)S(1)}, u32[]{:S(2)}, u32[]{:S(2)}) collective-permute-start(bf16[2,32,2560]{2,1,0:T(8,128)(2,1)S(1)} %cut.13), channel_id=1, source_target_pairs={{0,12},{1,13},{2,14},{3,15},{4,0},{5,1},{6,2},{7,3},{8,4},{9,5},{1... | collective-permute-start | bytes 983048 | tf_op jit(solution)/shard_map/ppermute | solution.py:25
  120.5 5.2 %collective-permute-start.16 = (f32[2,32,256]{2,1,0:T(8,128)S(1)}, f32[2,32,256]{2,1,0:T(8,128)S(1)}, u32[]{:S(2)}, u32[]{:S(2)}) collective-permute-start(f32[2,32,256]{2,1,0:T(8,128)S(1)} %correlate.11), channel_id=1, source_target_pairs={{0,2},{1,3},{2,0},{3,1},{4,6},{5,7},{6,4},{7,5},{8,10},{9,11},{10,... | collective-permute-start | bytes 196616 | tf_op jit(solution)/shard_map/ppermute | solution.py:25
  125.7 4.3 %collective-permute-start.17 = (f32[2,32,256]{2,1,0:T(8,128)S(1)}, f32[2,32,256]{2,1,0:T(8,128)S(1)}, u32[]{:S(2)}, u32[]{:S(2)}) collective-permute-start(f32[2,32,256]{2,1,0:T(8,128)S(1)} %add.46), channel_id=1, source_target_pairs={{0,1},{1,0},{2,3},{3,2},{4,5},{5,4},{6,7},{7,6},{8,9},{9,8},{10,11... | collective-permute-start | bytes 196616 | tf_op jit(solution)/shard_map/ppermute | solution.py:25
  132.1 11.6 %collective-permute-start.20 = (f32[2,160,256]{2,1,0:T(8,128)S(1)}, f32[2,160,256]{2,1,0:T(8,128)S(1)}, u32[]{:S(2)}, u32[]{:S(2)}) collective-permute-start(f32[2,160,256]{2,1,0:T(8,128)S(1)} %get-tuple-element.8.refs_0_), channel_id=1, source_target_pairs={{0,4},{1,5},{2,6},{3,7},{4,8},{5,9},{6,10},{7,11},{8,12},{9,13},{1... | collective-permute-start | bytes 983048 | tf_op jit(solution)/shard_map/ppermute | solution.py:25
  132.2 5.4 %collective-permute-start.18 = (f32[2,32,256]{2,1,0:T(8,128)S(1)}, f32[2,32,256]{2,1,0:T(8,128)S(1)}, u32[]{:S(2)}, u32[]{:S(2)}) collective-permute-start(f32[2,32,256]{2,1,0:T(8,128)S(1)} %get-tuple-element.10), channel_id=1, source_target_pairs={{0,0},{1,1},{2,2},{3,3},{4,6},{5,7},{6,4},{7,5},{8,8},{9,9},{10,10... | collective-permute-start | bytes 196616 | tf_op jit(solution)/shard_map/ppermute | solution.py:25
  132.9 10.9 %collective-permute-start.21 = (f32[2,64,256]{2,1,0:T(8,128)S(1)}, f32[2,64,256]{2,1,0:T(8,128)S(1)}, u32[]{:S(2)}, u32[]{:S(2)}) collective-permute-start(f32[2,64,256]{2,1,0:T(8,128)S(1)} %get-tuple-element.9.refs_1_), channel_id=1, source_target_pairs={{0,4},{1,5},{2,6},{3,7},{4,8},{5,9},{6,10},{7,11},{8,12},{9,13},{1... | collective-permute-start | bytes 393224 | tf_op jit(solution)/shard_map/ppermute | solution.py:25
  137.7 6.1 %collective-permute-start.23 = (f32[2,32,256]{2,1,0:T(8,128)S(1)}, f32[2,32,256]{2,1,0:T(8,128)S(1)}, u32[]{:S(2)}, u32[]{:S(2)}) collective-permute-start(f32[2,32,256]{2,1,0:T(8,128)S(1)} %add.48.refs_3_), channel_id=1, source_target_pairs={{0,4},{1,5},{2,6},{3,7},{4,9},{5,8},{6,11},{7,10},{8,12},{9,13},{1... | collective-permute-start | bytes 196616 | tf_op jit(solution)/shard_map/ppermute | solution.py:25
  139.3 4.4 %collective-permute-start.22 = (f32[2,32,256]{2,1,0:T(8,128)S(1)}, f32[2,32,256]{2,1,0:T(8,128)S(1)}, u32[]{:S(2)}, u32[]{:S(2)}) collective-permute-start(f32[2,32,256]{2,1,0:T(8,128)S(1)} %add.48.refs_3_), channel_id=1, source_target_pairs={{0,4},{1,5},{2,6},{3,7},{4,8},{5,9},{6,10},{7,11},{8,12},{9,13},{1... | collective-permute-start | bytes 196616 | tf_op jit(solution)/shard_map/ppermute | solution.py:25
  140.7 3.0 %collective-permute-start.19 = (f32[2,32,256]{2,1,0:T(8,128)S(1)}, f32[2,32,256]{2,1,0:T(8,128)S(1)}, u32[]{:S(2)}, u32[]{:S(2)}) collective-permute-start(f32[2,32,256]{2,1,0:T(8,128)S(1)} %add.48.refs_3_), channel_id=1, source_target_pairs={{0,0},{1,1},{2,2},{3,3},{4,5},{5,4},{6,7},{7,6},{8,8},{9,9},{10,10... | collective-permute-start | bytes 196616 | tf_op jit(solution)/shard_map/ppermute | solution.py:25

commit v8 on v5

--- a/solution.py
+++ b/solution.py
@@ -8,7 +8,8 @@
 from jax.sharding import PartitionSpec as P
 
 PWB = 256
-SIXTEENTHS = (5, 4, 3, 2, 2)
+SIXTEENTHS = (6, 4, 2, 2, 2)
+PIECES = 1
 MIB = 1 << 20
 ANYWHERE = pl.BlockSpec(memory_space=pl.ANY)
 WHOLE = pl.BlockSpec(memory_space=pltpu.VMEM)
@@ -221,11 +222,11 @@
         if chunk == 2:
             send(4, late, width, arrived[2], whole[1])
         whole.append(summed_over_pw(correlate(placed, arrived[chunk], *whole[-1:])))
-    halves = [jnp.concatenate(whole[:2], axis=1), jnp.concatenate(whole[2:], axis=1)]
-    last = correlate(placed, arrived[4], *halves)
-    last, *halves = correlate(placed, arrived[5], first=late, begun=last, held=halves)
-    halves_before = [moved(half, "ka", 1) for half in halves]
-    return assembled(halves, halves_before, *sums_here_and_next(last))
+    pieces = jnp.split(jnp.concatenate(whole, axis=1), PIECES, axis=1)
+    last = correlate(placed, arrived[4], *pieces)
+    last, *pieces = correlate(placed, arrived[5], first=late, begun=last, held=pieces)
+    pieces_before = [moved(piece, "ka", 1) for piece in pieces]
+    return assembled(pieces, pieces_before, *sums_here_and_next(last))
 
 
 def solution(mesh):

time: 134 us -> 135 us (level)
  starting transfers between devices: 26.3 us -> 23.4 us
  waiting for transfers between devices: 79.2 us -> 81.9 us
    ppermute x9 -> x8, waiting for transfers between devices: 33.9 us -> 35.8 us  [moved(): lax.ppermute(block, axis, [(i, (i + distance) % count) for i in range(cou...]
    ppermute x8, starting transfers between devices: 13.1 us -> 11.3 us  [summed_over_pw(): lax.ppermute(partial, 'pw', [(i, i ^ distance) for i in range(pw)])]
    ppermute x9 -> x8, starting transfers between devices: 8.89 us -> 8.76 us  [moved(): lax.ppermute(block, axis, [(i, (i + distance) % count) for i in range(cou...]
  transfers between devices with their start and end apart: 20 -> 19, of which waited for: 14 -> 13; matrix products, arithmetic and copies ran while one was open for 0% -> 0% of each run, Pallas kernels for 18% -> 19%
where the time goes in v8:
time: 135 us; the launch traced here: 134 us
  waiting for transfers between devices  81.9 us (61%)
  Pallas kernels  28.6 us (21%)
  starting transfers between devices  23.4 us (17%)
    ppermute x8, waiting for transfers between devices, summed_over_pw(): lax.ppermute(partial, 'pw', [(i, i ^ distance) for i in range(pw)])  37.1 us
    ppermute x8, waiting for transfers between devices, moved(): lax.ppermute(block, axis, [(i, (i + distance) % count) for i in range(cou...  35.8 us
    ppermute x8, starting transfers between devices, summed_over_pw(): lax.ppermute(partial, 'pw', [(i, i ^ distance) for i in range(pw)])  11.3 us
    pallas_call x6, Pallas kernels, correlate(): pl.pallas_call(functools.partial(correlate_kernel, first, depth, begun is...  9.54 us
    pallas_call x1, Pallas kernels, placed_bands(): pl.pallas_call(place_kernel, grid=(width // step,), out_shape=pltpu.VMEM(...  9.35 us
    ppermute x8, starting transfers between devices, moved(): lax.ppermute(block, axis, [(i, (i + distance) % count) for i in range(cou...  8.76 us
    pallas_call x6, Pallas kernels, cut(): pl.pallas_call(functools.partial(cut_kernel, bands, waves), out_shape=jax...  8.68 us
    ppermute x1, waiting for transfers between devices, sums_here_and_next(): lax.ppermute(partial, 'pw', [(i, i ^ distance) for i in range(pw)])  5.3 us
  transfers between devices with their start and end apart: 19, of which 13 were waited for; matrix products, arithmetic and copies ran while one was open for 0% of the time, Pallas kernels for 19%

profile of v8, /device:TPU:0, one launch (start us, length us, event | category | flops | bytes accessed | tf_op | source)
XLA Modules:
  0.0 134.2 jit_solution(4600047754514749458)
XLA Ops:
  0.0 2.2 %cut.6.refs_1_ = bf16[2,96,10240]{2,1,0:T(8,128)(2,1)S(1)} custom-call(bf16[1,2,256,10240]{3,2,1,0:T(8,128)(2,1)} %refs_0_.11), custom_call_target="tpu_custom_call" | custom-call | bytes 1024 | tf_op jit(solution)/shard_map/cut/pallas_call | solution.py:37
  2.2 2.4 %collective-permute-start = (bf16[2,96,10240]{2,1,0:T(8,128)(2,1)S(1)}, bf16[2,96,10240]{2,1,0:T(8,128)(2,1)S(1)}, u32[]{:S(2)}, u32[]{:S(2)}) collective-permute-start(bf16[2,96,10240]{2,1,0:T(8,128)(2,1)S(1)} %cut.6.refs_1_), channel_id=1, source_target_pairs={{0,12},{4,0},{8,4},{12,8},{1,13},{5,1},{9,5},{13,9},{2,14},{6,2},{... | collective-permute-start | bytes 11796488 | tf_op jit(solution)/shard_map/ppermute | solution.py:20
  4.6 1.7 %cut.7.refs_1_ = bf16[2,64,10240]{2,1,0:T(8,128)(2,1)S(1)} custom-call(bf16[1,2,256,10240]{3,2,1,0:T(8,128)(2,1)} %refs_0_.11, bf16[2,96,10240]{2,1,0:T(8,128)(2,1)S(1)} %cut.6.refs_1_), custom_call_target="tpu_custom_call" | custom-call | bytes 1024 | tf_op jit(solution)/shard_map/cut/pallas_call | solution.py:37
  7.1 1.3 cut.8.refs_1_
  8.4 9.3 %place.1.refs_3_.placed_ref = bf16[10240,512]{1,0:T(8,128)(2,1)S(1)} custom-call(bf16[1,2,256,10240]{3,2,1,0:T(8,128)(2,1)} %refs_0_.11, s32[1,2,10240]{2,1,0:T(2,128)S(1)} %copy-done), custom_call_target="tpu_custom_call" | custom-call | bytes 1024 | tf_op jit(solution)/shard_map/place/pallas_call | solution.py:68
  17.8 30.0 %collective-permute-done.refs_2_.block_ref = bf16[2,96,10240]{2,1,0:T(8,128)(2,1)S(1)} collective-permute-done((bf16[2,96,10240]{2,1,0:T(8,128)(2,1)S(1)}, bf16[2,96,10240]{2,1,0:T(8,128)(2,1)S(1)}, u32[]{:S(2)}, u32[]{:S(2)}) %collective-permute-start) | collective-permute-done | bytes 3932192 | tf_op jit(solution)/shard_map/ppermute | solution.py:20
  47.8 1.3 cut.9.refs_1_
  49.1 2.0 %collective-permute-start.11 = (bf16[2,32,10240]{2,1,0:T(8,128)(2,1)S(1)}, bf16[2,32,10240]{2,1,0:T(8,128)(2,1)S(1)}, u32[]{:S(2)}, u32[]{:S(2)}) collective-permute-start(bf16[2,32,10240]{2,1,0:T(8,128)(2,1)S(1)} %cut.9.refs_1_), channel_id=1, source_target_pairs={{0,12},{4,0},{8,4},{12,8},{1,13},{5,1},{9,5},{13,9},{2,14},{6,2},{... | collective-permute-start | bytes 3932168 | tf_op jit(solution)/shard_map/ppermute | solution.py:20
  51.1 2.2 %correlate.6 = f32[2,96,256]{2,1,0:T(8,128)S(1)} custom-call(bf16[10240,512]{1,0:T(8,128)(2,1)S(1)} %place.1.refs_3_.placed_ref, bf16[2,96,10240]{2,1,0:T(8,128)(2,1)S(1)} %collective-permute-done.refs_2_.block_ref), custom_call_target="tpu_custom_call" | custom-call | bytes 1024 | tf_op jit(solution)/shard_map/correlate/pallas_call | solution.py:118
  53.3 2.7 %collective-permute-start.2 = (f32[2,96,256]{2,1,0:T(8,128)S(1)}, f32[2,96,256]{2,1,0:T(8,128)S(1)}, u32[]{:S(2)}, u32[]{:S(2)}) collective-permute-start(f32[2,96,256]{2,1,0:T(8,128)S(1)} %correlate.6), channel_id=1, source_target_pairs={{0,2},{1,3},{2,0},{3,1},{4,6},{5,7},{6,4},{7,5},{8,10},{9,11},{10,... | collective-permute-start | bytes 589832 | tf_op jit(solution)/shard_map/ppermute | solution.py:138
  55.9 8.3 %collective-permute-done.2 = f32[2,96,256]{2,1,0:T(8,128)S(1)} collective-permute-done((f32[2,96,256]{2,1,0:T(8,128)S(1)}, f32[2,96,256]{2,1,0:T(8,128)S(1)}, u32[]{:S(2)}, u32[]{:S(2)}) %collective-permute-start.2) | collective-permute-done | bytes 196640 | tf_op jit(solution)/shard_map/ppermute | solution.py:138
  65.0 5.1 %collective-permute-done.3 = f32[2,96,256]{2,1,0:T(8,128)S(1)} collective-permute-done((f32[2,96,256]{2,1,0:T(8,128)S(1)}, f32[2,96,256]{2,1,0:T(8,128)S(1)}, u32[]{:S(2)}, u32[]{:S(2)}) %collective-permute-start.3) | collective-permute-done | bytes 196640 | tf_op jit(solution)/shard_map/ppermute | solution.py:138
  70.1 5.8 %collective-permute-done.1.refs_2_.block_ref = bf16[2,64,10240]{2,1,0:T(8,128)(2,1)S(1)} collective-permute-done((bf16[2,64,10240]{2,1,0:T(8,128)(2,1)S(1)}, bf16[2,64,10240]{2,1,0:T(8,128)(2,1)S(1)}, u32[]{:S(2)}, u32[]{:S(2)}) %collective-permute-start.1) | collective-permute-done | bytes 2621472 | tf_op jit(solution)/shard_map/ppermute | solution.py:20
  75.9 1.2 cut.10.refs_1_
  77.1 2.0 %collective-permute-start.8 = (bf16[2,32,7680]{2,1,0:T(8,128)(2,1)S(1)}, bf16[2,32,7680]{2,1,0:T(8,128)(2,1)S(1)}, u32[]{:S(2)}, u32[]{:S(2)}) collective-permute-start(bf16[2,32,7680]{2,1,0:T(8,128)(2,1)S(1)} %cut.10.refs_1_), channel_id=1, source_target_pairs={{0,12},{4,0},{8,4},{12,8},{1,13},{5,1},{9,5},{13,9},{2,14},{6,2},{... | collective-permute-start | bytes 2949128 | tf_op jit(solution)/shard_map/ppermute | solution.py:20
  79.1 1.5 %correlate.7 = f32[2,64,256]{2,1,0:T(8,128)S(1)} custom-call(bf16[10240,512]{1,0:T(8,128)(2,1)S(1)} %place.1.refs_3_.placed_ref, bf16[2,64,10240]{2,1,0:T(8,128)(2,1)S(1)} %collective-permute-done.1.refs_2_.block_ref, f32[2,96,256]{2,1,0:T(8,128)S(1)} %add.28.refs_3_.refs_0_), custom_call_target="tpu_custom_call" | custom-call | bytes 1024 | tf_op jit(solution)/shard_map/correlate/pallas_call | solution.py:118
  80.6 2.7 %collective-permute-start.5 = (f32[2,64,256]{2,1,0:T(8,128)S(1)}, f32[2,64,256]{2,1,0:T(8,128)S(1)}, u32[]{:S(2)}, u32[]{:S(2)}) collective-permute-start(f32[2,64,256]{2,1,0:T(8,128)S(1)} %correlate.7), channel_id=1, source_target_pairs={{0,2},{1,3},{2,0},{3,1},{4,6},{5,7},{6,4},{7,5},{8,10},{9,11},{10,... | collective-permute-start | bytes 393224 | tf_op jit(solution)/shard_map/ppermute | solution.py:138
  83.2 5.5 %collective-permute-done.5 = f32[2,64,256]{2,1,0:T(8,128)S(1)} collective-permute-done((f32[2,64,256]{2,1,0:T(8,128)S(1)}, f32[2,64,256]{2,1,0:T(8,128)S(1)}, u32[]{:S(2)}, u32[]{:S(2)}) %collective-permute-start.5) | collective-permute-done | bytes 131104 | tf_op jit(solution)/shard_map/ppermute | solution.py:138
  89.5 4.3 %collective-permute-done.6 = f32[2,64,256]{2,1,0:T(8,128)S(1)} collective-permute-done((f32[2,64,256]{2,1,0:T(8,128)S(1)}, f32[2,64,256]{2,1,0:T(8,128)S(1)}, u32[]{:S(2)}, u32[]{:S(2)}) %collective-permute-start.6) | collective-permute-done | bytes 131104 | tf_op jit(solution)/shard_map/ppermute | solution.py:138
  93.8 1.9 %correlate.8 = f32[2,32,256]{2,1,0:T(8,128)S(1)} custom-call(bf16[10240,512]{1,0:T(8,128)(2,1)S(1)} %place.1.refs_3_.placed_ref, bf16[2,32,10240]{2,1,0:T(8,128)(2,1)S(1)} %collective-permute-done.4.refs_2_.block_ref, f32[2,64,256]{2,1,0:T(8,128)S(1)} %add.30.refs_3_.refs_0_), custom_call_target="tpu_custom_call" | custom-call | bytes 1024 | tf_op jit(solution)/shard_map/correlate/pallas_call | solution.py:118
  95.7 2.1 %collective-permute-start.9 = (f32[2,32,256]{2,1,0:T(8,128)S(1)}, f32[2,32,256]{2,1,0:T(8,128)S(1)}, u32[]{:S(2)}, u32[]{:S(2)}) collective-permute-start(f32[2,32,256]{2,1,0:T(8,128)S(1)} %correlate.8), channel_id=1, source_target_pairs={{0,2},{1,3},{2,0},{3,1},{4,6},{5,7},{6,4},{7,5},{8,10},{9,11},{10,... | collective-permute-start | bytes 196616 | tf_op jit(solution)/shard_map/ppermute | solution.py:138
  99.9 1.8 %collective-permute-done.9 = f32[2,32,256]{2,1,0:T(8,128)S(1)} collective-permute-done((f32[2,32,256]{2,1,0:T(8,128)S(1)}, f32[2,32,256]{2,1,0:T(8,128)S(1)}, u32[]{:S(2)}, u32[]{:S(2)}) %collective-permute-start.9) | collective-permute-done | bytes 65568 | tf_op jit(solution)/shard_map/ppermute | solution.py:138
  102.3 3.7 %collective-permute-done.10 = f32[2,32,256]{2,1,0:T(8,128)S(1)} collective-permute-done((f32[2,32,256]{2,1,0:T(8,128)S(1)}, f32[2,32,256]{2,1,0:T(8,128)S(1)}, u32[]{:S(2)}, u32[]{:S(2)}) %collective-permute-start.10) | collective-permute-done | bytes 65568 | tf_op jit(solution)/shard_map/ppermute | solution.py:138
  106.0 1.9 %correlate.9 = f32[2,32,256]{2,1,0:T(8,128)S(1)} custom-call(bf16[10240,512]{1,0:T(8,128)(2,1)S(1)} %place.1.refs_3_.placed_ref, bf16[2,32,10240]{2,1,0:T(8,128)(2,1)S(1)} %collective-permute-done.11.block_ref, f32[2,32,256]{2,1,0:T(8,128)S(1)} %add.32.refs_0_), custom_call_target="tpu_custom_call" | custom-call | bytes 1024 | tf_op jit(solution)/shard_map/correlate/pallas_call | solution.py:118
  107.9 1.6 %collective-permute-start.12 = (f32[2,32,256]{2,1,0:T(8,128)S(1)}, f32[2,32,256]{2,1,0:T(8,128)S(1)}, u32[]{:S(2)}, u32[]{:S(2)}) collective-permute-start(f32[2,32,256]{2,1,0:T(8,128)S(1)} %correlate.9), channel_id=1, source_target_pairs={{0,2},{1,3},{2,0},{3,1},{4,6},{5,7},{6,4},{7,5},{8,10},{9,11},{10,... | collective-permute-start | bytes 196616 | tf_op jit(solution)/shard_map/ppermute | solution.py:138
  109.5 4.3 %collective-permute-done.12 = f32[2,32,256]{2,1,0:T(8,128)S(1)} collective-permute-done((f32[2,32,256]{2,1,0:T(8,128)S(1)}, f32[2,32,256]{2,1,0:T(8,128)S(1)}, u32[]{:S(2)}, u32[]{:S(2)}) %collective-permute-start.12) | collective-permute-done | bytes 65568 | tf_op jit(solution)/shard_map/ppermute | solution.py:138
  114.1 4.1 %collective-permute-done.13 = f32[2,32,256]{2,1,0:T(8,128)S(1)} collective-permute-done((f32[2,32,256]{2,1,0:T(8,128)S(1)}, f32[2,32,256]{2,1,0:T(8,128)S(1)}, u32[]{:S(2)}, u32[]{:S(2)}) %collective-permute-start.13) | collective-permute-done | bytes 65568 | tf_op jit(solution)/shard_map/ppermute | solution.py:138
  118.3 1.5 %correlate.10.refs_0_ = f32[2,32,256]{2,1,0:T(8,128)S(1)} custom-call(bf16[10240,512]{1,0:T(8,128)(2,1)S(1)} %place.1.refs_3_.placed_ref, bf16[2,32,7680]{2,1,0:T(8,128)(2,1)S(1)} %collective-permute-done.8.block_ref, f32[2,224,256]{2,1,0:T(8,128)S(1)} %pad_maximum_fusion.refs_0_.refs_1_), custom_call_target="tpu_custom_call" | custom-call | bytes 1024 | tf_op jit(solution)/shard_map/correlate/pallas_call | solution.py:118
  120.4 1.7 %collective-permute-start.15 = (f32[2,32,256]{2,1,0:T(8,128)S(1)}, f32[2,32,256]{2,1,0:T(8,128)S(1)}, u32[]{:S(2)}, u32[]{:S(2)}) collective-permute-start(f32[2,32,256]{2,1,0:T(8,128)S(1)} %get-tuple-element.8), channel_id=1, source_target_pairs={{0,2},{1,3},{2,0},{3,1},{4,6},{5,7},{6,4},{7,5},{8,10},{9,11},{10,... | collective-permute-start | bytes 196616 | tf_op jit(solution)/shard_map/ppermute | solution.py:150
  122.1 5.3 %collective-permute-done.15 = f32[2,32,256]{2,1,0:T(8,128)S(1)} collective-permute-done((f32[2,32,256]{2,1,0:T(8,128)S(1)}, f32[2,32,256]{2,1,0:T(8,128)S(1)}, u32[]{:S(2)}, u32[]{:S(2)}) %collective-permute-start.15) | collective-permute-done | bytes 65568 | tf_op jit(solution)/shard_map/ppermute | solution.py:150
  128.0 1.5 %collective-permute-start.16 = (f32[2,32,256]{2,1,0:T(8,128)S(1)}, f32[2,32,256]{2,1,0:T(8,128)S(1)}, u32[]{:S(2)}, u32[]{:S(2)}) collective-permute-start(f32[2,32,256]{2,1,0:T(8,128)S(1)} %add.35.refs_2_), channel_id=1, source_target_pairs={{0,1},{1,0},{2,3},{3,2},{4,5},{5,4},{6,7},{7,6},{8,9},{9,8},{10,11... | collective-permute-start | bytes 196616 | tf_op jit(solution)/shard_map/ppermute | solution.py:152
  129.6 2.9 %collective-permute-done.18.refs_5_ = f32[2,32,256]{2,1,0:T(8,128)S(1)} collective-permute-done((f32[2,32,256]{2,1,0:T(8,128)S(1)}, f32[2,32,256]{2,1,0:T(8,128)S(1)}, u32[]{:S(2)}, u32[]{:S(2)}) %collective-permute-start.18) | collective-permute-done | bytes 65568 | tf_op jit(solution)/shard_map/ppermute | solution.py:154
  (32 shorter events, 8.3 us)
Async XLA Ops:
  2.2 45.6 %collective-permute-start = (bf16[2,96,10240]{2,1,0:T(8,128)(2,1)S(1)}, bf16[2,96,10240]{2,1,0:T(8,128)(2,1)S(1)}, u32[]{:S(2)}, u32[]{:S(2)}) collective-permute-start(bf16[2,96,10240]{2,1,0:T(8,128)(2,1)S(1)} %cut.6.refs_1_), channel_id=1, source_target_pairs={{0,12},{4,0},{8,4},{12,8},{1,13},{5,1},{9,5},{13,9},{2,14},{6,2},{... | collective-permute-start | bytes 11796488 | tf_op jit(solution)/shard_map/ppermute | solution.py:20
  6.3 2.1 %copy-start = (s32[1,2,10240]{2,1,0:T(2,128)S(1)}, s32[1,2,10240]{2,1,0:T(2,128)}, u32[]{:S(2)}) copy-start(s32[1,2,10240]{2,1,0:T(2,128)} %shift_ref.1) | copy-start | bytes 245764
  6.3 69.6 %collective-permute-start.1 = (bf16[2,64,10240]{2,1,0:T(8,128)(2,1)S(1)}, bf16[2,64,10240]{2,1,0:T(8,128)(2,1)S(1)}, u32[]{:S(2)}, u32[]{:S(2)}) collective-permute-start(bf16[2,64,10240]{2,1,0:T(8,128)(2,1)S(1)} %cut.7.refs_1_), channel_id=1, source_target_pairs={{0,12},{4,0},{8,4},{12,8},{1,13},{5,1},{9,5},{13,9},{2,14},{6,2},{... | collective-permute-start | bytes 7864328 | tf_op jit(solution)/shard_map/ppermute | solution.py:20
  8.4 85.4 %collective-permute-start.4 = (bf16[2,32,10240]{2,1,0:T(8,128)(2,1)S(1)}, bf16[2,32,10240]{2,1,0:T(8,128)(2,1)S(1)}, u32[]{:S(2)}, u32[]{:S(2)}) collective-permute-start(bf16[2,32,10240]{2,1,0:T(8,128)(2,1)S(1)} %cut.8.refs_1_), channel_id=1, source_target_pairs={{0,12},{4,0},{8,4},{12,8},{1,13},{5,1},{9,5},{13,9},{2,14},{6,2},{... | collective-permute-start | bytes 3932168 | tf_op jit(solution)/shard_map/ppermute | solution.py:20
  49.1 56.9 %collective-permute-start.11 = (bf16[2,32,10240]{2,1,0:T(8,128)(2,1)S(1)}, bf16[2,32,10240]{2,1,0:T(8,128)(2,1)S(1)}, u32[]{:S(2)}, u32[]{:S(2)}) collective-permute-start(bf16[2,32,10240]{2,1,0:T(8,128)(2,1)S(1)} %cut.9.refs_1_), channel_id=1, source_target_pairs={{0,12},{4,0},{8,4},{12,8},{1,13},{5,1},{9,5},{13,9},{2,14},{6,2},{... | collective-permute-start | bytes 3932168 | tf_op jit(solution)/shard_map/ppermute | solution.py:20
  53.3 10.9 %collective-permute-start.2 = (f32[2,96,256]{2,1,0:T(8,128)S(1)}, f32[2,96,256]{2,1,0:T(8,128)S(1)}, u32[]{:S(2)}, u32[]{:S(2)}) collective-permute-start(f32[2,96,256]{2,1,0:T(8,128)S(1)} %correlate.6), channel_id=1, source_target_pairs={{0,2},{1,3},{2,0},{3,1},{4,6},{5,7},{6,4},{7,5},{8,10},{9,11},{10,... | collective-permute-start | bytes 589832 | tf_op jit(solution)/shard_map/ppermute | solution.py:138
  64.2 5.8 %collective-permute-start.3 = (f32[2,96,256]{2,1,0:T(8,128)S(1)}, f32[2,96,256]{2,1,0:T(8,128)S(1)}, u32[]{:S(2)}, u32[]{:S(2)}) collective-permute-start(f32[2,96,256]{2,1,0:T(8,128)S(1)} %add.27), channel_id=1, source_target_pairs={{0,1},{1,0},{2,3},{3,2},{4,5},{5,4},{6,7},{7,6},{8,9},{9,8},{10,11... | collective-permute-start | bytes 589832 | tf_op jit(solution)/shard_map/ppermute | solution.py:138
  77.1 41.2 %collective-permute-start.8 = (bf16[2,32,7680]{2,1,0:T(8,128)(2,1)S(1)}, bf16[2,32,7680]{2,1,0:T(8,128)(2,1)S(1)}, u32[]{:S(2)}, u32[]{:S(2)}) collective-permute-start(bf16[2,32,7680]{2,1,0:T(8,128)(2,1)S(1)} %cut.10.refs_1_), channel_id=1, source_target_pairs={{0,12},{4,0},{8,4},{12,8},{1,13},{5,1},{9,5},{13,9},{2,14},{6,2},{... | collective-permute-start | bytes 2949128 | tf_op jit(solution)/shard_map/ppermute | solution.py:20
  80.6 8.1 %collective-permute-start.5 = (f32[2,64,256]{2,1,0:T(8,128)S(1)}, f32[2,64,256]{2,1,0:T(8,128)S(1)}, u32[]{:S(2)}, u32[]{:S(2)}) collective-permute-start(f32[2,64,256]{2,1,0:T(8,128)S(1)} %correlate.7), channel_id=1, source_target_pairs={{0,2},{1,3},{2,0},{3,1},{4,6},{5,7},{6,4},{7,5},{8,10},{9,11},{10,... | collective-permute-start | bytes 393224 | tf_op jit(solution)/shard_map/ppermute | solution.py:138
  88.7 5.0 %collective-permute-start.6 = (f32[2,64,256]{2,1,0:T(8,128)S(1)}, f32[2,64,256]{2,1,0:T(8,128)S(1)}, u32[]{:S(2)}, u32[]{:S(2)}) collective-permute-start(f32[2,64,256]{2,1,0:T(8,128)S(1)} %add.29), channel_id=1, source_target_pairs={{0,1},{1,0},{2,3},{3,2},{4,5},{5,4},{6,7},{7,6},{8,9},{9,8},{10,11... | collective-permute-start | bytes 393224 | tf_op jit(solution)/shard_map/ppermute | solution.py:138
  95.7 5.9 %collective-permute-start.9 = (f32[2,32,256]{2,1,0:T(8,128)S(1)}, f32[2,32,256]{2,1,0:T(8,128)S(1)}, u32[]{:S(2)}, u32[]{:S(2)}) collective-permute-start(f32[2,32,256]{2,1,0:T(8,128)S(1)} %correlate.8), channel_id=1, source_target_pairs={{0,2},{1,3},{2,0},{3,1},{4,6},{5,7},{6,4},{7,5},{8,10},{9,11},{10,... | collective-permute-start | bytes 196616 | tf_op jit(solution)/shard_map/ppermute | solution.py:138
  98.9 20.9 %collective-permute-start.7 = (bf16[2,32,2560]{2,1,0:T(8,128)(2,1)S(1)}, bf16[2,32,2560]{2,1,0:T(8,128)(2,1)S(1)}, u32[]{:S(2)}, u32[]{:S(2)}) collective-permute-start(bf16[2,32,2560]{2,1,0:T(8,128)(2,1)S(1)} %cut.11), channel_id=1, source_target_pairs={{0,12},{4,0},{8,4},{12,8},{1,13},{5,1},{9,5},{13,9},{2,14},{6,2},{... | collective-permute-start | bytes 983048 | tf_op jit(solution)/shard_map/ppermute | solution.py:20
  101.7 4.3 %collective-permute-start.10 = (f32[2,32,256]{2,1,0:T(8,128)S(1)}, f32[2,32,256]{2,1,0:T(8,128)S(1)}, u32[]{:S(2)}, u32[]{:S(2)}) collective-permute-start(f32[2,32,256]{2,1,0:T(8,128)S(1)} %add.31), channel_id=1, source_target_pairs={{0,1},{1,0},{2,3},{3,2},{4,5},{5,4},{6,7},{7,6},{8,9},{9,8},{10,11... | collective-permute-start | bytes 196616 | tf_op jit(solution)/shard_map/ppermute | solution.py:138
  107.9 5.9 %collective-permute-start.12 = (f32[2,32,256]{2,1,0:T(8,128)S(1)}, f32[2,32,256]{2,1,0:T(8,128)S(1)}, u32[]{:S(2)}, u32[]{:S(2)}) collective-permute-start(f32[2,32,256]{2,1,0:T(8,128)S(1)} %correlate.9), channel_id=1, source_target_pairs={{0,2},{1,3},{2,0},{3,1},{4,6},{5,7},{6,4},{7,5},{8,10},{9,11},{10,... | collective-permute-start | bytes 196616 | tf_op jit(solution)/shard_map/ppermute | solution.py:138
  113.9 4.3 %collective-permute-start.13 = (f32[2,32,256]{2,1,0:T(8,128)S(1)}, f32[2,32,256]{2,1,0:T(8,128)S(1)}, u32[]{:S(2)}, u32[]{:S(2)}) collective-permute-start(f32[2,32,256]{2,1,0:T(8,128)S(1)} %add.33), channel_id=1, source_target_pairs={{0,1},{1,0},{2,3},{3,2},{4,5},{5,4},{6,7},{7,6},{8,9},{9,8},{10,11... | collective-permute-start | bytes 196616 | tf_op jit(solution)/shard_map/ppermute | solution.py:138
  120.3 12.9 %collective-permute-start.14 = (f32[2,224,256]{2,1,0:T(8,128)S(1)}, f32[2,224,256]{2,1,0:T(8,128)S(1)}, u32[]{:S(2)}, u32[]{:S(2)}) collective-permute-start(f32[2,224,256]{2,1,0:T(8,128)S(1)} %get-tuple-element.7.refs_0_), channel_id=1, source_target_pairs={{0,4},{4,8},{8,12},{12,0},{1,5},{5,9},{9,13},{13,1},{2,6},{6,10},{... | collective-permute-start | bytes 1376264 | tf_op jit(solution)/shard_map/ppermute | solution.py:20
  120.4 7.0 %collective-permute-start.15 = (f32[2,32,256]{2,1,0:T(8,128)S(1)}, f32[2,32,256]{2,1,0:T(8,128)S(1)}, u32[]{:S(2)}, u32[]{:S(2)}) collective-permute-start(f32[2,32,256]{2,1,0:T(8,128)S(1)} %get-tuple-element.8), channel_id=1, source_target_pairs={{0,2},{1,3},{2,0},{3,1},{4,6},{5,7},{6,4},{7,5},{8,10},{9,11},{10,... | collective-permute-start | bytes 196616 | tf_op jit(solution)/shard_map/ppermute | solution.py:150
  127.4 5.0 %collective-permute-start.18 = (f32[2,32,256]{2,1,0:T(8,128)S(1)}, f32[2,32,256]{2,1,0:T(8,128)S(1)}, u32[]{:S(2)}, u32[]{:S(2)}) collective-permute-start(f32[2,32,256]{2,1,0:T(8,128)S(1)} %add.35.refs_2_), channel_id=1, source_target_pairs={{0,5},{1,4},{2,7},{3,6},{4,9},{5,8},{6,11},{7,10},{8,13},{9,12},{1... | collective-permute-start | bytes 196616 | tf_op jit(solution)/shard_map/ppermute | solution.py:154
  127.5 5.0 %collective-permute-start.17 = (f32[2,32,256]{2,1,0:T(8,128)S(1)}, f32[2,32,256]{2,1,0:T(8,128)S(1)}, u32[]{:S(2)}, u32[]{:S(2)}) collective-permute-start(f32[2,32,256]{2,1,0:T(8,128)S(1)} %add.35.refs_2_), channel_id=1, source_target_pairs={{0,4},{4,8},{8,12},{12,0},{1,5},{5,9},{9,13},{13,1},{2,6},{6,10},{... | collective-permute-start | bytes 196616 | tf_op jit(solution)/shard_map/ppermute | solution.py:20
  128.0 5.2 %collective-permute-start.16 = (f32[2,32,256]{2,1,0:T(8,128)S(1)}, f32[2,32,256]{2,1,0:T(8,128)S(1)}, u32[]{:S(2)}, u32[]{:S(2)}) collective-permute-start(f32[2,32,256]{2,1,0:T(8,128)S(1)} %add.35.refs_2_), channel_id=1, source_target_pairs={{0,1},{1,0},{2,3},{3,2},{4,5},{5,4},{6,7},{7,6},{8,9},{9,8},{10,11... | collective-permute-start | bytes 196616 | tf_op jit(solution)/shard_map/ppermute | solution.py:152

commit v9 on v5

--- a/solution.py
+++ b/solution.py
@@ -8,7 +8,7 @@
 from jax.sharding import PartitionSpec as P
 
 PWB = 256
-SIXTEENTHS = (5, 4, 3, 2, 2)
+SIXTEENTHS = (6, 4, 3, 2, 1)
 MIB = 1 << 20
 ANYWHERE = pl.BlockSpec(memory_space=pl.ANY)
 WHOLE = pl.BlockSpec(memory_space=pltpu.VMEM)
@@ -128,45 +128,38 @@
     return out if held else out[0]
 
 
-def summed_over_pw(partial):
-    pw = lax.axis_size("pw")
-    if pw & (pw - 1):
-        return partial + sum(moved(partial, "pw", d) for d in range(1, pw))
-    distance = pw // 2
-    while distance:
-        partial = partial + lax.ppermute(partial, "pw", [(i, i ^ distance) for i in range(pw)])
+def exchanged(block, distance):
+    return lax.ppermute(block, "pw", [(i, i ^ distance) for i in range(lax.axis_size("pw"))])
+
+
+def summed_over_pw(partial, nearest=1, farthest=None):
+    distance = farthest or lax.axis_size("pw") // 2
+    while distance >= nearest:
+        partial = partial + exchanged(partial, distance)
         distance //= 2
     return partial
 
 
-def sums_here_and_next(partial):
+def crossed(block):
     ka, pw = lax.axis_size("ka"), lax.axis_size("pw")
-    if pw & (pw - 1) or pw == 1:
-        whole = summed_over_pw(partial)
-        return [whole], [moved(whole, "ka", 1)]
-    distance = pw // 2
-    while distance > 1:
-        partial = partial + lax.ppermute(partial, "pw", [(i, i ^ distance) for i in range(pw)])
-        distance //= 2
-    here = lax.ppermute(partial, "pw", [(i, i ^ 1) for i in range(pw)])
-    across = [(k * pw + p, (k + 1) % ka * pw + (p ^ 1)) for k in range(ka) for p in range(pw)]
-    before = [moved(partial, "ka", 1), lax.ppermute(partial, ("ka", "pw"), across)]
-    return [partial, here], before
-
-
-def assemble_kernel(counts, *refs):
-    ins, (out_ref, made, sems) = list(refs[:-3]), refs[-3:]
-    most, most_before, *last_refs = [[ins.pop(0) for _ in range(count)] for count in counts]
+    route = [(k * pw + p, (k + 1) % ka * pw + (p ^ 1)) for k in range(ka) for p in range(pw)]
+    return lax.ppermute(block, ("ka", "pw"), route)
+
+
+def assemble_kernel(
+    most_ref, some_ref, last_ref, here_ref, most_before_ref, joint_ref, crossed_ref, out_ref, made, sems
+):
+    some = some_ref.shape[1]
     copies = []
     for side in (1, 0):
         for c in (0, 1):
-            early = [ref[c] for ref in (most, most_before)[side]]
-            late = sum(ref[c] for ref in last_refs[side])
-            matrix = jnp.concatenate([*early, late], axis=0)
-            if side == 0:
-                matrix = matrix.T
-            elif c == 1:
-                matrix = -matrix
+            if side == 1:
+                late = joint_ref[c, some:] + crossed_ref[c]
+                matrix = jnp.concatenate([most_before_ref[c], joint_ref[c, :some], late], axis=0)
+                matrix = -matrix if c == 1 else matrix
+            else:
+                late = last_ref[c] + here_ref[c]
+                matrix = jnp.concatenate([most_ref[c], some_ref[c], late], axis=0).T
             made[2 * side + c] = matrix
             copies.append(
                 pltpu.make_async_copy(
@@ -179,12 +172,11 @@
 
 
 def assembled(*parts):
-    bands = parts[0][0].shape[2]
-    counts = [len(part) for part in parts]
+    bands = parts[0].shape[2]
     return pl.pallas_call(
-        functools.partial(assemble_kernel, counts),
+        assemble_kernel,
         out_shape=jax.ShapeDtypeStruct((1, 2, 2, bands, bands), jnp.float32),
-        in_specs=[WHOLE] * sum(counts),
+        in_specs=[WHOLE] * len(parts),
         out_specs=ANYWHERE,
         scratch_shapes=[
             pltpu.VMEM((4, bands, bands), jnp.float32),
@@ -193,7 +185,7 @@
         compiler_params=pltpu.CompilerParams(vmem_limit_bytes=16 * MIB),
         cost_estimate=pl.CostEstimate(flops=0, bytes_accessed=1024, transcendentals=0),
         name="assemble",
-    )(*[array for part in parts for array in part])
+    )(*parts)
 
 
 def local(coefficients, shifts):
@@ -202,7 +194,7 @@
     edges = [0]
     for size in SIXTEENTHS:
         edges.append(edges[-1] + size * unit)
-    late = width // PWB * 3 // 4 * PWB
+    half, late = (width // PWB * quarters // 4 * PWB for quarters in (2, 3))
     coefficients = pltpu.with_memory_space_constraint(coefficients, pltpu.HBM)
     placed = pltpu.with_memory_space_constraint(placed_bands(coefficients, shifts), pltpu.VMEM)
     blocks, arrived, whole = [], [], []
@@ -214,18 +206,26 @@
 
     for chunk in range(3):
         send(chunk, 0, width)
-    send(3, 0, width, arrived[0], placed)
-    for chunk in range(4):
-        if chunk == 1:
-            send(4, 0, late, arrived[1], whole[0])
-        if chunk == 2:
-            send(4, late, width, arrived[2], whole[1])
-        whole.append(summed_over_pw(correlate(placed, arrived[chunk], *whole[-1:])))
-    halves = [jnp.concatenate(whole[:2], axis=1), jnp.concatenate(whole[2:], axis=1)]
-    last = correlate(placed, arrived[4], *halves)
-    last, *halves = correlate(placed, arrived[5], first=late, begun=last, held=halves)
-    halves_before = [moved(half, "ka", 1) for half in halves]
-    return assembled(halves, halves_before, *sums_here_and_next(last))
+    send(3, 0, half, arrived[0], placed)
+    whole.append(summed_over_pw(correlate(placed, arrived[0])))
+    send(3, half, width, arrived[1], whole[0])
+    whole.append(summed_over_pw(correlate(placed, arrived[1], whole[0])))
+    send(4, 0, late, arrived[2], whole[1])
+    whole.append(summed_over_pw(correlate(placed, arrived[2], whole[1])))
+    send(4, late, width, arrived[2], whole[1])
+    some = correlate(placed, arrived[3], whole[2])
+    some = correlate(placed, arrived[4], first=half, begun=some)
+    farthest = lax.axis_size("pw") // 2
+    more = exchanged(some, farthest)
+    most = jnp.concatenate(whole, axis=1)
+    last, some = correlate(placed, arrived[5], most, held=[some])
+    some = summed_over_pw(some + more, nearest=2, farthest=farthest // 2)
+    last, some, most = correlate(placed, arrived[6], first=late, begun=last, held=[some, most])
+    most_before = moved(most, "ka", 1)
+    last = summed_over_pw(last, nearest=2)
+    some = some + exchanged(some, 1)
+    joint = moved(jnp.concatenate([some, last], axis=1), "ka", 1)
+    return assembled(most, some, last, exchanged(last, 1), most_before, joint, crossed(last))
 
 
 def solution(mesh):

time: 134 us -> 137 us (1.022)
    ppermute x11, waiting for transfers between devices: 45.3 us -> 39.9 us  [the longest x10 38.3 us: exchanged(): lax.ppermute(block, 'pw', [(i, i ^ distance) for i in range(lax.axis_size...]
    ppermute x9, waiting for transfers between devices: 33.9 us -> 39.2 us  [moved(): lax.ppermute(block, axis, [(i, (i + distance) % count) for i in range(cou...]
    pallas_call x6 -> x7, Pallas kernels: 8.68 us -> 9.59 us  [cut(): pl.pallas_call(functools.partial(cut_kernel, bands, waves), out_shape=jax...]
    pallas_call x6 -> x7, Pallas kernels: 9.11 us -> 9.5 us  [correlate(): pl.pallas_call(functools.partial(correlate_kernel, first, depth, begun is...]
  transfers between devices with their start and end apart: 20 -> 20, of which waited for: 14 -> 13; matrix products, arithmetic and copies ran while one was open for 0% -> 0% of each run, Pallas kernels for 18% -> 19%
where the time goes in v9:
time: 137 us
  waiting for transfers between devices  79.2 us (58%)
  Pallas kernels  29.4 us (21%)
  starting transfers between devices  27.6 us (20%)
    ppermute x9, waiting for transfers between devices, moved(): lax.ppermute(block, axis, [(i, (i + distance) % count) for i in range(cou...  39.2 us
    ppermute x10, waiting for transfers between devices, exchanged(): lax.ppermute(block, 'pw', [(i, i ^ distance) for i in range(lax.axis_size...  38.3 us
    ppermute x10, starting transfers between devices, exchanged(): lax.ppermute(block, 'pw', [(i, i ^ distance) for i in range(lax.axis_size...  16.5 us
    pallas_call x7, Pallas kernels, cut(): pl.pallas_call(functools.partial(cut_kernel, bands, waves), out_shape=jax...  9.59 us
    pallas_call x7, Pallas kernels, correlate(): pl.pallas_call(functools.partial(correlate_kernel, first, depth, begun is...  9.5 us
    pallas_call x1, Pallas kernels, placed_bands(): pl.pallas_call(place_kernel, grid=(width // step,), out_shape=pltpu.VMEM(...  9.34 us
    ppermute x9, starting transfers between devices, moved(): lax.ppermute(block, axis, [(i, (i + distance) % count) for i in range(cou...  9.28 us
  transfers between devices with their start and end apart: 20, of which 13 were waited for; matrix products, arithmetic and copies ran while one was open for 0% of the time, Pallas kernels for 19%

profile of v9, /device:TPU:0, one launch (start us, length us, event | category | flops | bytes accessed | tf_op | source)
XLA Modules:
  0.0 136.6 jit_solution(17686154378267398158)
XLA Ops:
  0.0 2.2 %cut.7.refs_1_ = bf16[2,96,10240]{2,1,0:T(8,128)(2,1)S(1)} custom-call(bf16[1,2,256,10240]{3,2,1,0:T(8,128)(2,1)} %refs_0_.13), custom_call_target="tpu_custom_call" | custom-call | bytes 1024 | tf_op jit(solution)/shard_map/cut/pallas_call | solution.py:36
  2.2 2.4 %collective-permute-start = (bf16[2,96,10240]{2,1,0:T(8,128)(2,1)S(1)}, bf16[2,96,10240]{2,1,0:T(8,128)(2,1)S(1)}, u32[]{:S(2)}, u32[]{:S(2)}) collective-permute-start(bf16[2,96,10240]{2,1,0:T(8,128)(2,1)S(1)} %cut.7.refs_1_), channel_id=1, source_target_pairs={{0,12},{4,0},{8,4},{12,8},{1,13},{5,1},{9,5},{13,9},{2,14},{6,2},{... | collective-permute-start | bytes 11796488 | tf_op jit(solution)/shard_map/ppermute | solution.py:19
  4.6 1.7 %cut.8.refs_1_ = bf16[2,64,10240]{2,1,0:T(8,128)(2,1)S(1)} custom-call(bf16[1,2,256,10240]{3,2,1,0:T(8,128)(2,1)} %refs_0_.13, bf16[2,96,10240]{2,1,0:T(8,128)(2,1)S(1)} %cut.7.refs_1_), custom_call_target="tpu_custom_call" | custom-call | bytes 1024 | tf_op jit(solution)/shard_map/cut/pallas_call | solution.py:36
  7.1 1.5 %cut.9.refs_1_ = bf16[2,48,10240]{2,1,0:T(8,128)(2,1)S(1)} custom-call(bf16[1,2,256,10240]{3,2,1,0:T(8,128)(2,1)} %refs_0_.13, bf16[2,64,10240]{2,1,0:T(8,128)(2,1)S(1)} %cut.8.refs_1_), custom_call_target="tpu_custom_call" | custom-call | bytes 1024 | tf_op jit(solution)/shard_map/cut/pallas_call | solution.py:36
  8.7 9.3 %place.1.refs_3_.placed_ref = bf16[10240,512]{1,0:T(8,128)(2,1)S(1)} custom-call(bf16[1,2,256,10240]{3,2,1,0:T(8,128)(2,1)} %refs_0_.13, s32[1,2,10240]{2,1,0:T(2,128)S(1)} %copy-done), custom_call_target="tpu_custom_call" | custom-call | bytes 1024 | tf_op jit(solution)/shard_map/place/pallas_call | solution.py:67
  18.0 29.8 %collective-permute-done.refs_2_.block_ref = bf16[2,96,10240]{2,1,0:T(8,128)(2,1)S(1)} collective-permute-done((bf16[2,96,10240]{2,1,0:T(8,128)(2,1)S(1)}, bf16[2,96,10240]{2,1,0:T(8,128)(2,1)S(1)}, u32[]{:S(2)}, u32[]{:S(2)}) %collective-permute-start) | collective-permute-done | bytes 3932192 | tf_op jit(solution)/shard_map/ppermute | solution.py:19
  47.8 2.2 %correlate.7 = f32[2,96,256]{2,1,0:T(8,128)S(1)} custom-call(bf16[10240,512]{1,0:T(8,128)(2,1)S(1)} %place.1.refs_3_.placed_ref, bf16[2,96,10240]{2,1,0:T(8,128)(2,1)S(1)} %collective-permute-done.refs_2_.block_ref), custom_call_target="tpu_custom_call" | custom-call | bytes 1024 | tf_op jit(solution)/shard_map/correlate/pallas_call | solution.py:117
  50.0 2.7 %collective-permute-start.2 = (f32[2,96,256]{2,1,0:T(8,128)S(1)}, f32[2,96,256]{2,1,0:T(8,128)S(1)}, u32[]{:S(2)}, u32[]{:S(2)}) collective-permute-start(f32[2,96,256]{2,1,0:T(8,128)S(1)} %correlate.7), channel_id=1, source_target_pairs={{0,2},{1,3},{2,0},{3,1},{4,6},{5,7},{6,4},{7,5},{8,10},{9,11},{10,... | collective-permute-start | bytes 589832 | tf_op jit(solution)/shard_map/ppermute | solution.py:132
  52.7 10.2 %collective-permute-done.2 = f32[2,96,256]{2,1,0:T(8,128)S(1)} collective-permute-done((f32[2,96,256]{2,1,0:T(8,128)S(1)}, f32[2,96,256]{2,1,0:T(8,128)S(1)}, u32[]{:S(2)}, u32[]{:S(2)}) %collective-permute-start.2) | collective-permute-done | bytes 196640 | tf_op jit(solution)/shard_map/ppermute | solution.py:132
  63.6 1.1 cut.10.refs_1_
  65.0 4.8 %collective-permute-done.3 = f32[2,96,256]{2,1,0:T(8,128)S(1)} collective-permute-done((f32[2,96,256]{2,1,0:T(8,128)S(1)}, f32[2,96,256]{2,1,0:T(8,128)S(1)}, u32[]{:S(2)}, u32[]{:S(2)}) %collective-permute-start.3) | collective-permute-done | bytes 196640 | tf_op jit(solution)/shard_map/ppermute | solution.py:132
  69.7 6.1 %collective-permute-done.1.refs_2_.block_ref = bf16[2,64,10240]{2,1,0:T(8,128)(2,1)S(1)} collective-permute-done((bf16[2,64,10240]{2,1,0:T(8,128)(2,1)S(1)}, bf16[2,64,10240]{2,1,0:T(8,128)(2,1)S(1)}, u32[]{:S(2)}, u32[]{:S(2)}) %collective-permute-start.1) | collective-permute-done | bytes 2621472 | tf_op jit(solution)/shard_map/ppermute | solution.py:19
  75.9 1.1 cut.11.refs_1_
  77.0 2.0 %collective-permute-start.11 = (bf16[2,32,5120]{2,1,0:T(8,128)(2,1)S(1)}, bf16[2,32,5120]{2,1,0:T(8,128)(2,1)S(1)}, u32[]{:S(2)}, u32[]{:S(2)}) collective-permute-start(bf16[2,32,5120]{2,1,0:T(8,128)(2,1)S(1)} %cut.11.refs_1_), channel_id=1, source_target_pairs={{0,12},{4,0},{8,4},{12,8},{1,13},{5,1},{9,5},{13,9},{2,14},{6,2},{... | collective-permute-start | bytes 1966088 | tf_op jit(solution)/shard_map/ppermute | solution.py:19
  78.9 1.5 %correlate.8 = f32[2,64,256]{2,1,0:T(8,128)S(1)} custom-call(bf16[10240,512]{1,0:T(8,128)(2,1)S(1)} %place.1.refs_3_.placed_ref, bf16[2,64,10240]{2,1,0:T(8,128)(2,1)S(1)} %collective-permute-done.1.refs_2_.block_ref, f32[2,96,256]{2,1,0:T(8,128)S(1)} %add.28.refs_3_.refs_0_), custom_call_target="tpu_custom_call" | custom-call | bytes 1024 | tf_op jit(solution)/shard_map/correlate/pallas_call | solution.py:117
  80.5 2.7 %collective-permute-start.5 = (f32[2,64,256]{2,1,0:T(8,128)S(1)}, f32[2,64,256]{2,1,0:T(8,128)S(1)}, u32[]{:S(2)}, u32[]{:S(2)}) collective-permute-start(f32[2,64,256]{2,1,0:T(8,128)S(1)} %correlate.8), channel_id=1, source_target_pairs={{0,2},{1,3},{2,0},{3,1},{4,6},{5,7},{6,4},{7,5},{8,10},{9,11},{10,... | collective-permute-start | bytes 393224 | tf_op jit(solution)/shard_map/ppermute | solution.py:132
  83.1 5.5 %collective-permute-done.5 = f32[2,64,256]{2,1,0:T(8,128)S(1)} collective-permute-done((f32[2,64,256]{2,1,0:T(8,128)S(1)}, f32[2,64,256]{2,1,0:T(8,128)S(1)}, u32[]{:S(2)}, u32[]{:S(2)}) %collective-permute-start.5) | collective-permute-done | bytes 131104 | tf_op jit(solution)/shard_map/ppermute | solution.py:132
  89.4 4.3 %collective-permute-done.6 = f32[2,64,256]{2,1,0:T(8,128)S(1)} collective-permute-done((f32[2,64,256]{2,1,0:T(8,128)S(1)}, f32[2,64,256]{2,1,0:T(8,128)S(1)}, u32[]{:S(2)}, u32[]{:S(2)}) %collective-permute-start.6) | collective-permute-done | bytes 131104 | tf_op jit(solution)/shard_map/ppermute | solution.py:132
  93.7 3.3 %collective-permute-done.4.refs_2_.block_ref = bf16[2,48,10240]{2,1,0:T(8,128)(2,1)S(1)} collective-permute-done((bf16[2,48,10240]{2,1,0:T(8,128)(2,1)S(1)}, bf16[2,48,10240]{2,1,0:T(8,128)(2,1)S(1)}, u32[]{:S(2)}, u32[]{:S(2)}) %collective-permute-start.4) | collective-permute-done | bytes 1966112 | tf_op jit(solution)/shard_map/ppermute | solution.py:19
  98.0 2.0 %collective-permute-start.8 = (bf16[2,16,7680]{2,1,0:T(8,128)(2,1)S(1)}, bf16[2,16,7680]{2,1,0:T(8,128)(2,1)S(1)}, u32[]{:S(2)}, u32[]{:S(2)}) collective-permute-start(bf16[2,16,7680]{2,1,0:T(8,128)(2,1)S(1)} %cut.12.refs_1_), channel_id=1, source_target_pairs={{0,12},{4,0},{8,4},{12,8},{1,13},{5,1},{9,5},{13,9},{2,14},{6,2},{... | collective-permute-start | bytes 1474568 | tf_op jit(solution)/shard_map/ppermute | solution.py:19
  100.0 1.8 %correlate.9 = f32[2,48,256]{2,1,0:T(8,128)S(1)} custom-call(bf16[10240,512]{1,0:T(8,128)(2,1)S(1)} %place.1.refs_3_.placed_ref, bf16[2,48,10240]{2,1,0:T(8,128)(2,1)S(1)} %collective-permute-done.4.refs_2_.block_ref, f32[2,64,256]{2,1,0:T(8,128)S(1)} %add.30.refs_3_.refs_0_), custom_call_target="tpu_custom_call" | custom-call | bytes 1024 | tf_op jit(solution)/shard_map/correlate/pallas_call | solution.py:117
  101.8 2.7 %collective-permute-start.9 = (f32[2,48,256]{2,1,0:T(8,128)S(1)}, f32[2,48,256]{2,1,0:T(8,128)S(1)}, u32[]{:S(2)}, u32[]{:S(2)}) collective-permute-start(f32[2,48,256]{2,1,0:T(8,128)S(1)} %correlate.9), channel_id=1, source_target_pairs={{0,2},{1,3},{2,0},{3,1},{4,6},{5,7},{6,4},{7,5},{8,10},{9,11},{10,... | collective-permute-start | bytes 294920 | tf_op jit(solution)/shard_map/ppermute | solution.py:132
  104.5 4.2 %collective-permute-done.9 = f32[2,48,256]{2,1,0:T(8,128)S(1)} collective-permute-done((f32[2,48,256]{2,1,0:T(8,128)S(1)}, f32[2,48,256]{2,1,0:T(8,128)S(1)}, u32[]{:S(2)}, u32[]{:S(2)}) %collective-permute-start.9) | collective-permute-done | bytes 98336 | tf_op jit(solution)/shard_map/ppermute | solution.py:132
  111.1 2.3 %collective-permute-done.10 = f32[2,48,256]{2,1,0:T(8,128)S(1)} collective-permute-done((f32[2,48,256]{2,1,0:T(8,128)S(1)}, f32[2,48,256]{2,1,0:T(8,128)S(1)}, u32[]{:S(2)}, u32[]{:S(2)}) %collective-permute-start.10) | collective-permute-done | bytes 98336 | tf_op jit(solution)/shard_map/ppermute | solution.py:132
  115.4 2.0 %collective-permute-start.13 = (f32[2,32,256]{2,1,0:T(8,128)S(1)}, f32[2,32,256]{2,1,0:T(8,128)S(1)}, u32[]{:S(2)}, u32[]{:S(2)}) collective-permute-start(f32[2,32,256]{2,1,0:T(8,128)S(1)} %correlate.11.refs_1_), channel_id=1, source_target_pairs={{0,2},{1,3},{2,0},{3,1},{4,6},{5,7},{6,4},{7,5},{8,10},{9,11},{10,... | collective-permute-start | bytes 196616 | tf_op jit(solution)/shard_map/ppermute | solution.py:132
  117.4 3.9 %collective-permute-done.13 = f32[2,32,256]{2,1,0:T(8,128)S(1)} collective-permute-done((f32[2,32,256]{2,1,0:T(8,128)S(1)}, f32[2,32,256]{2,1,0:T(8,128)S(1)}, u32[]{:S(2)}, u32[]{:S(2)}) %collective-permute-start.13) | collective-permute-done | bytes 65568 | tf_op jit(solution)/shard_map/ppermute | solution.py:132
  121.3 1.4 %correlate.12 = (f32[2,16,256]{2,1,0:T(8,128)S(1)}, f32[2,32,256]{2,1,0:T(8,128)S(1)}) custom-call(bf16[10240,512]{1,0:T(8,128)(2,1)S(1)} %place.1.refs_3_.placed_ref, bf16[2,16,7680]{2,1,0:T(8,128)(2,1)S(1)} %collective-permute-done.8.block_ref, f32[2,208,256]{2,1,0:T(8,128)S(1)} %pad_maximum_fusion.refs_0_.refs_2_, ...), custom_call_target="tpu_custom_call", output_to_operand_aliasing={{1}: (3, {})} | custom-call | bytes 1024 | tf_op jit(solution)/shard_map/correlate/pallas_call | solution.py:117
  123.9 3.0 %collective-permute-start.15 = (f32[2,16,256]{2,1,0:T(8,128)S(1)}, f32[2,16,256]{2,1,0:T(8,128)S(1)}, u32[]{:S(2)}, u32[]{:S(2)}) collective-permute-start(f32[2,16,256]{2,1,0:T(8,128)S(1)} %get-tuple-element.14), channel_id=1, source_target_pairs={{0,2},{1,3},{2,0},{3,1},{4,6},{5,7},{6,4},{7,5},{8,10},{9,11},{10,... | collective-permute-start | bytes 98312 | tf_op jit(solution)/shard_map/ppermute | solution.py:132
  126.8 1.9 %collective-permute-done.15 = f32[2,16,256]{2,1,0:T(8,128)S(1)} collective-permute-done((f32[2,16,256]{2,1,0:T(8,128)S(1)}, f32[2,16,256]{2,1,0:T(8,128)S(1)}, u32[]{:S(2)}, u32[]{:S(2)}) %collective-permute-start.15) | collective-permute-done | bytes 32800 | tf_op jit(solution)/shard_map/ppermute | solution.py:132
  129.8 1.8 %collective-permute-start.19 = (f32[2,16,256]{2,1,0:T(8,128)S(1)}, f32[2,16,256]{2,1,0:T(8,128)S(1)}, u32[]{:S(2)}, u32[]{:S(2)}) collective-permute-start(f32[2,16,256]{2,1,0:T(8,128)S(1)} %add.35.last_ref), channel_id=1, source_target_pairs={{0,5},{1,4},{2,7},{3,6},{4,9},{5,8},{6,11},{7,10},{8,13},{9,12},{1... | collective-permute-start | bytes 98312 | tf_op jit(solution)/shard_map/ppermute | solution.py:146
  132.6 1.7 %collective-permute-done.19.crossed_ref = f32[2,16,256]{2,1,0:T(8,128)S(1)} collective-permute-done((f32[2,16,256]{2,1,0:T(8,128)S(1)}, f32[2,16,256]{2,1,0:T(8,128)S(1)}, u32[]{:S(2)}, u32[]{:S(2)}) %collective-permute-start.19) | collective-permute-done | bytes 32800 | tf_op jit(solution)/shard_map/ppermute | solution.py:146
  134.3 1.3 collective-permute-done.16.here_ref
  (37 shorter events, 12.3 us)
Async XLA Ops:
  2.2 45.6 %collective-permute-start = (bf16[2,96,10240]{2,1,0:T(8,128)(2,1)S(1)}, bf16[2,96,10240]{2,1,0:T(8,128)(2,1)S(1)}, u32[]{:S(2)}, u32[]{:S(2)}) collective-permute-start(bf16[2,96,10240]{2,1,0:T(8,128)(2,1)S(1)} %cut.7.refs_1_), channel_id=1, source_target_pairs={{0,12},{4,0},{8,4},{12,8},{1,13},{5,1},{9,5},{13,9},{2,14},{6,2},{... | collective-permute-start | bytes 11796488 | tf_op jit(solution)/shard_map/ppermute | solution.py:19
  6.3 2.3 %copy-start = (s32[1,2,10240]{2,1,0:T(2,128)S(1)}, s32[1,2,10240]{2,1,0:T(2,128)}, u32[]{:S(2)}) copy-start(s32[1,2,10240]{2,1,0:T(2,128)} %shift_ref.1) | copy-start | bytes 245764
  6.3 69.6 %collective-permute-start.1 = (bf16[2,64,10240]{2,1,0:T(8,128)(2,1)S(1)}, bf16[2,64,10240]{2,1,0:T(8,128)(2,1)S(1)}, u32[]{:S(2)}, u32[]{:S(2)}) collective-permute-start(bf16[2,64,10240]{2,1,0:T(8,128)(2,1)S(1)} %cut.8.refs_1_), channel_id=1, source_target_pairs={{0,12},{4,0},{8,4},{12,8},{1,13},{5,1},{9,5},{13,9},{2,14},{6,2},{... | collective-permute-start | bytes 7864328 | tf_op jit(solution)/shard_map/ppermute | solution.py:19
  8.6 88.4 %collective-permute-start.4 = (bf16[2,48,10240]{2,1,0:T(8,128)(2,1)S(1)}, bf16[2,48,10240]{2,1,0:T(8,128)(2,1)S(1)}, u32[]{:S(2)}, u32[]{:S(2)}) collective-permute-start(bf16[2,48,10240]{2,1,0:T(8,128)(2,1)S(1)} %cut.9.refs_1_), channel_id=1, source_target_pairs={{0,12},{4,0},{8,4},{12,8},{1,13},{5,1},{9,5},{13,9},{2,14},{6,2},{... | collective-permute-start | bytes 5898248 | tf_op jit(solution)/shard_map/ppermute | solution.py:19
  50.0 12.8 %collective-permute-start.2 = (f32[2,96,256]{2,1,0:T(8,128)S(1)}, f32[2,96,256]{2,1,0:T(8,128)S(1)}, u32[]{:S(2)}, u32[]{:S(2)}) collective-permute-start(f32[2,96,256]{2,1,0:T(8,128)S(1)} %correlate.7), channel_id=1, source_target_pairs={{0,2},{1,3},{2,0},{3,1},{4,6},{5,7},{6,4},{7,5},{8,10},{9,11},{10,... | collective-permute-start | bytes 589832 | tf_op jit(solution)/shard_map/ppermute | solution.py:132
  62.9 6.9 %collective-permute-start.3 = (f32[2,96,256]{2,1,0:T(8,128)S(1)}, f32[2,96,256]{2,1,0:T(8,128)S(1)}, u32[]{:S(2)}, u32[]{:S(2)}) collective-permute-start(f32[2,96,256]{2,1,0:T(8,128)S(1)} %add.27), channel_id=1, source_target_pairs={{0,1},{1,0},{2,3},{3,2},{4,5},{5,4},{6,7},{7,6},{8,9},{9,8},{10,11... | collective-permute-start | bytes 589832 | tf_op jit(solution)/shard_map/ppermute | solution.py:132
  64.7 48.7 %collective-permute-start.12 = (bf16[2,32,5120]{2,1,0:T(8,128)(2,1)S(1)}, bf16[2,32,5120]{2,1,0:T(8,128)(2,1)S(1)}, u32[]{:S(2)}, u32[]{:S(2)}) collective-permute-start(bf16[2,32,5120]{2,1,0:T(8,128)(2,1)S(1)} %cut.10.refs_1_), channel_id=1, source_target_pairs={{0,12},{4,0},{8,4},{12,8},{1,13},{5,1},{9,5},{13,9},{2,14},{6,2},{... | collective-permute-start | bytes 1966088 | tf_op jit(solution)/shard_map/ppermute | solution.py:19
  77.0 37.4 %collective-permute-start.11 = (bf16[2,32,5120]{2,1,0:T(8,128)(2,1)S(1)}, bf16[2,32,5120]{2,1,0:T(8,128)(2,1)S(1)}, u32[]{:S(2)}, u32[]{:S(2)}) collective-permute-start(bf16[2,32,5120]{2,1,0:T(8,128)(2,1)S(1)} %cut.11.refs_1_), channel_id=1, source_target_pairs={{0,12},{4,0},{8,4},{12,8},{1,13},{5,1},{9,5},{13,9},{2,14},{6,2},{... | collective-permute-start | bytes 1966088 | tf_op jit(solution)/shard_map/ppermute | solution.py:19
  80.5 8.1 %collective-permute-start.5 = (f32[2,64,256]{2,1,0:T(8,128)S(1)}, f32[2,64,256]{2,1,0:T(8,128)S(1)}, u32[]{:S(2)}, u32[]{:S(2)}) collective-permute-start(f32[2,64,256]{2,1,0:T(8,128)S(1)} %correlate.8), channel_id=1, source_target_pairs={{0,2},{1,3},{2,0},{3,1},{4,6},{5,7},{6,4},{7,5},{8,10},{9,11},{10,... | collective-permute-start | bytes 393224 | tf_op jit(solution)/shard_map/ppermute | solution.py:132
  88.6 5.0 %collective-permute-start.6 = (f32[2,64,256]{2,1,0:T(8,128)S(1)}, f32[2,64,256]{2,1,0:T(8,128)S(1)}, u32[]{:S(2)}, u32[]{:S(2)}) collective-permute-start(f32[2,64,256]{2,1,0:T(8,128)S(1)} %add.29), channel_id=1, source_target_pairs={{0,1},{1,0},{2,3},{3,2},{4,5},{5,4},{6,7},{7,6},{8,9},{9,8},{10,11... | collective-permute-start | bytes 393224 | tf_op jit(solution)/shard_map/ppermute | solution.py:132
  98.0 23.3 %collective-permute-start.8 = (bf16[2,16,7680]{2,1,0:T(8,128)(2,1)S(1)}, bf16[2,16,7680]{2,1,0:T(8,128)(2,1)S(1)}, u32[]{:S(2)}, u32[]{:S(2)}) collective-permute-start(bf16[2,16,7680]{2,1,0:T(8,128)(2,1)S(1)} %cut.12.refs_1_), channel_id=1, source_target_pairs={{0,12},{4,0},{8,4},{12,8},{1,13},{5,1},{9,5},{13,9},{2,14},{6,2},{... | collective-permute-start | bytes 1474568 | tf_op jit(solution)/shard_map/ppermute | solution.py:19
  101.8 6.8 %collective-permute-start.9 = (f32[2,48,256]{2,1,0:T(8,128)S(1)}, f32[2,48,256]{2,1,0:T(8,128)S(1)}, u32[]{:S(2)}, u32[]{:S(2)}) collective-permute-start(f32[2,48,256]{2,1,0:T(8,128)S(1)} %correlate.9), channel_id=1, source_target_pairs={{0,2},{1,3},{2,0},{3,1},{4,6},{5,7},{6,4},{7,5},{8,10},{9,11},{10,... | collective-permute-start | bytes 294920 | tf_op jit(solution)/shard_map/ppermute | solution.py:132
  108.7 4.7 %collective-permute-start.10 = (f32[2,48,256]{2,1,0:T(8,128)S(1)}, f32[2,48,256]{2,1,0:T(8,128)S(1)}, u32[]{:S(2)}, u32[]{:S(2)}) collective-permute-start(f32[2,48,256]{2,1,0:T(8,128)S(1)} %add.31), channel_id=1, source_target_pairs={{0,1},{1,0},{2,3},{3,2},{4,5},{5,4},{6,7},{7,6},{8,9},{9,8},{10,11... | collective-permute-start | bytes 294920 | tf_op jit(solution)/shard_map/ppermute | solution.py:132
  110.2 12.6 %collective-permute-start.7 = (bf16[2,16,2560]{2,1,0:T(8,128)(2,1)S(1)}, bf16[2,16,2560]{2,1,0:T(8,128)(2,1)S(1)}, u32[]{:S(2)}, u32[]{:S(2)}) collective-permute-start(bf16[2,16,2560]{2,1,0:T(8,128)(2,1)S(1)} %cut.13), channel_id=1, source_target_pairs={{0,12},{4,0},{8,4},{12,8},{1,13},{5,1},{9,5},{13,9},{2,14},{6,2},{... | collective-permute-start | bytes 491528 | tf_op jit(solution)/shard_map/ppermute | solution.py:19
  115.4 5.9 %collective-permute-start.13 = (f32[2,32,256]{2,1,0:T(8,128)S(1)}, f32[2,32,256]{2,1,0:T(8,128)S(1)}, u32[]{:S(2)}, u32[]{:S(2)}) collective-permute-start(f32[2,32,256]{2,1,0:T(8,128)S(1)} %correlate.11.refs_1_), channel_id=1, source_target_pairs={{0,2},{1,3},{2,0},{3,1},{4,6},{5,7},{6,4},{7,5},{8,10},{9,11},{10,... | collective-permute-start | bytes 196616 | tf_op jit(solution)/shard_map/ppermute | solution.py:132
  123.4 12.3 %collective-permute-start.17 = (f32[2,208,256]{2,1,0:T(8,128)S(1)}, f32[2,208,256]{2,1,0:T(8,128)S(1)}, u32[]{:S(2)}, u32[]{:S(2)}) collective-permute-start(f32[2,208,256]{2,1,0:T(8,128)S(1)} %get-tuple-element.12.most_ref), channel_id=1, source_target_pairs={{0,4},{4,8},{8,12},{12,0},{1,5},{5,9},{9,13},{13,1},{2,6},{6,10},{... | collective-permute-start | bytes 1277960 | tf_op jit(solution)/shard_map/ppermute | solution.py:19
  123.4 5.4 %collective-permute-start.14 = (f32[2,32,256]{2,1,0:T(8,128)S(1)}, f32[2,32,256]{2,1,0:T(8,128)S(1)}, u32[]{:S(2)}, u32[]{:S(2)}) collective-permute-start(f32[2,32,256]{2,1,0:T(8,128)S(1)} %get-tuple-element.13), channel_id=1, source_target_pairs={{0,1},{1,0},{2,3},{3,2},{4,5},{5,4},{6,7},{7,6},{8,9},{9,8},{10,11... | collective-permute-start | bytes 196616 | tf_op jit(solution)/shard_map/ppermute | solution.py:132
  123.9 4.9 %collective-permute-start.15 = (f32[2,16,256]{2,1,0:T(8,128)S(1)}, f32[2,16,256]{2,1,0:T(8,128)S(1)}, u32[]{:S(2)}, u32[]{:S(2)}) collective-permute-start(f32[2,16,256]{2,1,0:T(8,128)S(1)} %get-tuple-element.14), channel_id=1, source_target_pairs={{0,2},{1,3},{2,0},{3,1},{4,6},{5,7},{6,4},{7,5},{8,10},{9,11},{10,... | collective-permute-start | bytes 98312 | tf_op jit(solution)/shard_map/ppermute | solution.py:132
  128.8 6.8 %collective-permute-start.18 = (f32[2,48,256]{2,1,0:T(8,128)S(1)}, f32[2,48,256]{2,1,0:T(8,128)S(1)}, u32[]{:S(2)}, u32[]{:S(2)}) collective-permute-start(f32[2,48,256]{2,1,0:T(8,128)S(1)} %pad_maximum_fusion.1), channel_id=1, source_target_pairs={{0,4},{4,8},{8,12},{12,0},{1,5},{5,9},{9,13},{13,1},{2,6},{6,10},{... | collective-permute-start | bytes 294920 | tf_op jit(solution)/shard_map/ppermute | solution.py:19
  129.8 4.4 %collective-permute-start.19 = (f32[2,16,256]{2,1,0:T(8,128)S(1)}, f32[2,16,256]{2,1,0:T(8,128)S(1)}, u32[]{:S(2)}, u32[]{:S(2)}) collective-permute-start(f32[2,16,256]{2,1,0:T(8,128)S(1)} %add.35.last_ref), channel_id=1, source_target_pairs={{0,5},{1,4},{2,7},{3,6},{4,9},{5,8},{6,11},{7,10},{8,13},{9,12},{1... | collective-permute-start | bytes 98312 | tf_op jit(solution)/shard_map/ppermute | solution.py:146
  131.7 3.9 %collective-permute-start.16 = (f32[2,16,256]{2,1,0:T(8,128)S(1)}, f32[2,16,256]{2,1,0:T(8,128)S(1)}, u32[]{:S(2)}, u32[]{:S(2)}) collective-permute-start(f32[2,16,256]{2,1,0:T(8,128)S(1)} %add.35.last_ref), channel_id=1, source_target_pairs={{0,1},{1,0},{2,3},{3,2},{4,5},{5,4},{6,7},{7,6},{8,9},{9,8},{10,11... | collective-permute-start | bytes 98312 | tf_op jit(solution)/shard_map/ppermute | solution.py:132

commit v10 on v8

--- a/solution.py
+++ b/solution.py
@@ -9,7 +9,6 @@
 
 PWB = 256
 SIXTEENTHS = (6, 4, 2, 2, 2)
-PIECES = 1
 MIB = 1 << 20
 ANYWHERE = pl.BlockSpec(memory_space=pl.ANY)
 WHOLE = pl.BlockSpec(memory_space=pltpu.VMEM)
@@ -46,7 +45,8 @@
     )(coefficients, *others)
 
 
-def place_kernel(own_ref, shift_ref, out_ref):
+def place_kernel(own_ref, shift_ref, *refs):
+    out_ref = refs[-1]
     bands, width = own_ref.shape[2:]
     base = pl.program_id(0) * width
     goal = lax.broadcasted_iota(jnp.int32, (PWB, PWB), 0)
@@ -62,7 +62,7 @@
         out_ref[pl.ds(there, PWB), :] = placed.astype(jnp.bfloat16)
 
 
-def placed_bands(coefficients, shifts):
+def placed_bands(coefficients, shifts, *others):
     bands, width = coefficients.shape[2:]
     step = 4 * PWB if width % (4 * PWB) == 0 else PWB
     return pl.pallas_call(
@@ -72,12 +72,13 @@
         in_specs=[
             pl.BlockSpec((1, 2, bands, step), lambda g: (0, 0, 0, g)),
             pl.BlockSpec((1, 2, step), lambda g: (0, 0, g)),
-        ],
+        ]
+        + [ANYWHERE] * len(others),
         out_specs=WHOLE,
         compiler_params=pltpu.CompilerParams(vmem_limit_bytes=16 * MIB),
         cost_estimate=pl.CostEstimate(flops=0, bytes_accessed=1024, transcendentals=0),
         name="place",
-    )(coefficients, shifts)
+    )(coefficients, shifts, *others)
 
 
 def correlate_kernel(first, depth, begun, held, placed_ref, block_ref, *refs):
@@ -205,28 +206,26 @@
         edges.append(edges[-1] + size * unit)
     late = width // PWB * 3 // 4 * PWB
     coefficients = pltpu.with_memory_space_constraint(coefficients, pltpu.HBM)
-    placed = pltpu.with_memory_space_constraint(placed_bands(coefficients, shifts), pltpu.VMEM)
-    blocks, arrived, whole = [], [], []
-
-    def send(chunk, low, high, *others):
+    ranges = [(chunk, 0, width) for chunk in range(4)] + [(4, 0, late), (4, late, width)]
+    blocks = []
+    for chunk, low, high in ranges:
         some = slice(edges[chunk], edges[chunk + 1])
-        blocks.append(cut(coefficients, some, slice(low, high), *blocks[-1:], *others))
-        arrived.append(moved(blocks[-1], "ka", -1))
-
-    for chunk in range(3):
-        send(chunk, 0, width)
-    send(3, 0, width, arrived[0], placed)
+        blocks.append(cut(coefficients, some, slice(low, high), *blocks[-1:]))
+    placed = placed_bands(coefficients, shifts, *blocks[-1:])
+    placed = pltpu.with_memory_space_constraint(placed, pltpu.VMEM)
+    arrived = [moved(block, "ka", -1) for block in blocks[:3]]
+    whole = []
     for chunk in range(4):
-        if chunk == 1:
-            send(4, 0, late, arrived[1], whole[0])
-        if chunk == 2:
-            send(4, late, width, arrived[2], whole[1])
-        whole.append(summed_over_pw(correlate(placed, arrived[chunk], *whole[-1:])))
-    pieces = jnp.split(jnp.concatenate(whole, axis=1), PIECES, axis=1)
-    last = correlate(placed, arrived[4], *pieces)
-    last, *pieces = correlate(placed, arrived[5], first=late, begun=last, held=pieces)
-    pieces_before = [moved(piece, "ka", 1) for piece in pieces]
-    return assembled(pieces, pieces_before, *sums_here_and_next(last))
+        waiting = blocks[3 + chunk : 4 + chunk]
+        partial = correlate(placed, arrived[chunk], *whole[-1:], held=waiting)
+        if waiting:
+            partial, waiting = partial
+            arrived.append(moved(waiting, "ka", -1))
+        whole.append(summed_over_pw(partial))
+    most = jnp.concatenate(whole, axis=1)
+    last = correlate(placed, arrived[4], most)
+    last, most = correlate(placed, arrived[5], first=late, begun=last, held=[most])
+    return assembled([most], [moved(most, "ka", 1)], *sums_here_and_next(last))
 
 
 def solution(mesh):

time: 135 us -> 134 us (level)
  waiting for transfers between devices: 81.9 us -> 80.2 us
  starting transfers between devices: 23.4 us -> 24.8 us
    ppermute x8, waiting for transfers between devices: 35.8 us -> 33.6 us  [moved(): lax.ppermute(block, axis, [(i, (i + distance) % count) for i in range(cou...]
    ppermute x8, waiting for transfers between devices: 37.1 us -> 38.7 us  [summed_over_pw(): lax.ppermute(partial, 'pw', [(i, i ^ distance) for i in range(pw)])]
where the time goes in v10:
time: 134 us
  waiting for transfers between devices  80.2 us (60%)
  Pallas kernels  28.6 us (21%)
  starting transfers between devices  24.8 us (19%)
    ppermute x8, waiting for transfers between devices, summed_over_pw(): lax.ppermute(partial, 'pw', [(i, i ^ distance) for i in range(pw)])  38.7 us
    ppermute x8, waiting for transfers between devices, moved(): lax.ppermute(block, axis, [(i, (i + distance) % count) for i in range(cou...  33.6 us
    ppermute x8, starting transfers between devices, summed_over_pw(): lax.ppermute(partial, 'pw', [(i, i ^ distance) for i in range(pw)])  11.6 us
    pallas_call x6, Pallas kernels, correlate(): pl.pallas_call(functools.partial(correlate_kernel, first, depth, begun is...  9.54 us
    pallas_call x1, Pallas kernels, placed_bands(): pl.pallas_call(place_kernel, grid=(width // step,), out_shape=pltpu.VMEM(...  9.33 us
    ppermute x8, starting transfers between devices, moved(): lax.ppermute(block, axis, [(i, (i + distance) % count) for i in range(cou...  8.73 us
    pallas_call x6, Pallas kernels, cut(): pl.pallas_call(functools.partial(cut_kernel, bands, waves), out_shape=jax...  8.73 us
    ppermute x1, waiting for transfers between devices, sums_here_and_next(): lax.ppermute(partial, 'pw', [(i, i ^ distance) for i in range(pw)])  4.96 us
  transfers between devices with their start and end apart: 19, of which 13 were waited for; matrix products, arithmetic and copies ran while one was open for 0% of the time, Pallas kernels for 19%

profile of v10, /device:TPU:0, one launch (start us, length us, event | category | flops | bytes accessed | tf_op | source)
XLA Modules:
  0.0 133.9 jit_solution(12036219054562030830)
XLA Ops:
  0.0 2.2 %cut.6.refs_1_ = bf16[2,96,10240]{2,1,0:T(8,128)(2,1)S(1)} custom-call(bf16[1,2,256,10240]{3,2,1,0:T(8,128)(2,1)} %own_ref.1), custom_call_target="tpu_custom_call" | custom-call | bytes 1024 | tf_op jit(solution)/shard_map/cut/pallas_call | solution.py:36
  2.2 2.4 %collective-permute-start.2 = (bf16[2,96,10240]{2,1,0:T(8,128)(2,1)S(1)}, bf16[2,96,10240]{2,1,0:T(8,128)(2,1)S(1)}, u32[]{:S(2)}, u32[]{:S(2)}) collective-permute-start(bf16[2,96,10240]{2,1,0:T(8,128)(2,1)S(1)} %cut.6.refs_1_), channel_id=1, source_target_pairs={{0,12},{4,0},{8,4},{12,8},{1,13},{5,1},{9,5},{13,9},{2,14},{6,2},{... | collective-permute-start | bytes 11796488 | tf_op jit(solution)/shard_map/ppermute | solution.py:19
  4.6 1.7 %cut.7.refs_1_ = bf16[2,64,10240]{2,1,0:T(8,128)(2,1)S(1)} custom-call(bf16[1,2,256,10240]{3,2,1,0:T(8,128)(2,1)} %own_ref.1, bf16[2,96,10240]{2,1,0:T(8,128)(2,1)S(1)} %cut.6.refs_1_), custom_call_target="tpu_custom_call" | custom-call | bytes 1024 | tf_op jit(solution)/shard_map/cut/pallas_call | solution.py:36
  7.1 1.3 cut.8.refs_1_
  8.4 1.3 cut.9.refs_1_.refs_0_
  9.7 1.2 cut.10.refs_1_
  12.0 9.3 %place.1.placed_ref = bf16[10240,512]{1,0:T(8,128)(2,1)S(1)} custom-call(bf16[1,2,256,10240]{3,2,1,0:T(8,128)(2,1)} %own_ref.1, s32[1,2,10240]{2,1,0:T(2,128)S(1)} %copy-done, bf16[2,32,2560]{2,1,0:T(8,128)(2,1)S(1)} %cut.11.refs_0_.refs_1_), custom_call_target="tpu_custom_call" | custom-call | bytes 1024 | tf_op jit(solution)/shard_map/place/pallas_call | solution.py:68
  21.4 26.4 %collective-permute-done.2.block_ref = bf16[2,96,10240]{2,1,0:T(8,128)(2,1)S(1)} collective-permute-done((bf16[2,96,10240]{2,1,0:T(8,128)(2,1)S(1)}, bf16[2,96,10240]{2,1,0:T(8,128)(2,1)S(1)}, u32[]{:S(2)}, u32[]{:S(2)}) %collective-permute-start.2) | collective-permute-done | bytes 3932192 | tf_op jit(solution)/shard_map/ppermute | solution.py:19
  47.8 2.2 %correlate.6 = (f32[2,96,256]{2,1,0:T(8,128)S(1)}, bf16[2,32,10240]{2,1,0:T(8,128)(2,1)S(1)}) custom-call(bf16[10240,512]{1,0:T(8,128)(2,1)S(1)} %place.1.placed_ref, bf16[2,96,10240]{2,1,0:T(8,128)(2,1)S(1)} %collective-permute-done.2.block_ref, bf16[2,32,10240]{2,1,0:T(8,128)(2,1)S(1)} %cut.9.refs_1_.refs_0_), custom_call_target="tpu_custom_call", output_to_operand_aliasing={{1}: (2, {})} | custom-call | bytes 1024 | tf_op jit(solution)/shard_map/correlate/pallas_call | solution.py:119
  50.0 2.0 %collective-permute-start.11 = (bf16[2,32,10240]{2,1,0:T(8,128)(2,1)S(1)}, bf16[2,32,10240]{2,1,0:T(8,128)(2,1)S(1)}, u32[]{:S(2)}, u32[]{:S(2)}) collective-permute-start(bf16[2,32,10240]{2,1,0:T(8,128)(2,1)S(1)} %get-tuple-element.18), channel_id=1, source_target_pairs={{0,12},{4,0},{8,4},{12,8},{1,13},{5,1},{9,5},{13,9},{2,14},{6,2},{... | collective-permute-start | bytes 3932168 | tf_op jit(solution)/shard_map/ppermute | solution.py:19
  52.0 2.6 %collective-permute-start.3 = (f32[2,96,256]{2,1,0:T(8,128)S(1)}, f32[2,96,256]{2,1,0:T(8,128)S(1)}, u32[]{:S(2)}, u32[]{:S(2)}) collective-permute-start(f32[2,96,256]{2,1,0:T(8,128)S(1)} %get-tuple-element.13), channel_id=1, source_target_pairs={{0,2},{1,3},{2,0},{3,1},{4,6},{5,7},{6,4},{7,5},{8,10},{9,11},{10,... | collective-permute-start | bytes 589832 | tf_op jit(solution)/shard_map/ppermute | solution.py:139
  54.6 8.3 %collective-permute-done.3 = f32[2,96,256]{2,1,0:T(8,128)S(1)} collective-permute-done((f32[2,96,256]{2,1,0:T(8,128)S(1)}, f32[2,96,256]{2,1,0:T(8,128)S(1)}, u32[]{:S(2)}, u32[]{:S(2)}) %collective-permute-start.3) | collective-permute-done | bytes 196640 | tf_op jit(solution)/shard_map/ppermute | solution.py:139
  63.7 5.1 %collective-permute-done.4 = f32[2,96,256]{2,1,0:T(8,128)S(1)} collective-permute-done((f32[2,96,256]{2,1,0:T(8,128)S(1)}, f32[2,96,256]{2,1,0:T(8,128)S(1)}, u32[]{:S(2)}, u32[]{:S(2)}) %collective-permute-start.4) | collective-permute-done | bytes 196640 | tf_op jit(solution)/shard_map/ppermute | solution.py:139
  68.8 7.1 %collective-permute-done.1.block_ref = bf16[2,64,10240]{2,1,0:T(8,128)(2,1)S(1)} collective-permute-done((bf16[2,64,10240]{2,1,0:T(8,128)(2,1)S(1)}, bf16[2,64,10240]{2,1,0:T(8,128)(2,1)S(1)}, u32[]{:S(2)}, u32[]{:S(2)}) %collective-permute-start.1) | collective-permute-done | bytes 2621472 | tf_op jit(solution)/shard_map/ppermute | solution.py:19
  75.9 1.5 %correlate.7 = (f32[2,64,256]{2,1,0:T(8,128)S(1)}, bf16[2,32,7680]{2,1,0:T(8,128)(2,1)S(1)}) custom-call(bf16[10240,512]{1,0:T(8,128)(2,1)S(1)} %place.1.placed_ref, bf16[2,64,10240]{2,1,0:T(8,128)(2,1)S(1)} %collective-permute-done.1.block_ref, f32[2,96,256]{2,1,0:T(8,128)S(1)} %add.28.refs_0_, ...), custom_call_target="tpu_custom_call", output_to_operand_aliasing={{1}: (3, {})} | custom-call | bytes 1024 | tf_op jit(solution)/shard_map/correlate/pallas_call | solution.py:119
  77.4 2.0 %collective-permute-start.8 = (bf16[2,32,7680]{2,1,0:T(8,128)(2,1)S(1)}, bf16[2,32,7680]{2,1,0:T(8,128)(2,1)S(1)}, u32[]{:S(2)}, u32[]{:S(2)}) collective-permute-start(bf16[2,32,7680]{2,1,0:T(8,128)(2,1)S(1)} %get-tuple-element.16), channel_id=1, source_target_pairs={{0,12},{4,0},{8,4},{12,8},{1,13},{5,1},{9,5},{13,9},{2,14},{6,2},{... | collective-permute-start | bytes 2949128 | tf_op jit(solution)/shard_map/ppermute | solution.py:19
  79.4 2.6 %collective-permute-start.5 = (f32[2,64,256]{2,1,0:T(8,128)S(1)}, f32[2,64,256]{2,1,0:T(8,128)S(1)}, u32[]{:S(2)}, u32[]{:S(2)}) collective-permute-start(f32[2,64,256]{2,1,0:T(8,128)S(1)} %get-tuple-element.14), channel_id=1, source_target_pairs={{0,2},{1,3},{2,0},{3,1},{4,6},{5,7},{6,4},{7,5},{8,10},{9,11},{10,... | collective-permute-start | bytes 393224 | tf_op jit(solution)/shard_map/ppermute | solution.py:139
  82.0 5.5 %collective-permute-done.5 = f32[2,64,256]{2,1,0:T(8,128)S(1)} collective-permute-done((f32[2,64,256]{2,1,0:T(8,128)S(1)}, f32[2,64,256]{2,1,0:T(8,128)S(1)}, u32[]{:S(2)}, u32[]{:S(2)}) %collective-permute-start.5) | collective-permute-done | bytes 131104 | tf_op jit(solution)/shard_map/ppermute | solution.py:139
  88.3 4.3 %collective-permute-done.6 = f32[2,64,256]{2,1,0:T(8,128)S(1)} collective-permute-done((f32[2,64,256]{2,1,0:T(8,128)S(1)}, f32[2,64,256]{2,1,0:T(8,128)S(1)}, u32[]{:S(2)}, u32[]{:S(2)}) %collective-permute-start.6) | collective-permute-done | bytes 131104 | tf_op jit(solution)/shard_map/ppermute | solution.py:139
  92.6 1.9 %correlate.8 = (f32[2,32,256]{2,1,0:T(8,128)S(1)}, bf16[2,32,2560]{2,1,0:T(8,128)(2,1)S(1)}) custom-call(bf16[10240,512]{1,0:T(8,128)(2,1)S(1)} %place.1.placed_ref, bf16[2,32,10240]{2,1,0:T(8,128)(2,1)S(1)} %collective-permute-done.block_ref, f32[2,64,256]{2,1,0:T(8,128)S(1)} %add.30.refs_0_, ...), custom_call_target="tpu_custom_call", output_to_operand_aliasing={{1}: (3, {})} | custom-call | bytes 1024 | tf_op jit(solution)/shard_map/correlate/pallas_call | solution.py:119
  94.5 2.2 %collective-permute-start.9 = (f32[2,32,256]{2,1,0:T(8,128)S(1)}, f32[2,32,256]{2,1,0:T(8,128)S(1)}, u32[]{:S(2)}, u32[]{:S(2)}) collective-permute-start(f32[2,32,256]{2,1,0:T(8,128)S(1)} %get-tuple-element.17), channel_id=1, source_target_pairs={{0,2},{1,3},{2,0},{3,1},{4,6},{5,7},{6,4},{7,5},{8,10},{9,11},{10,... | collective-permute-start | bytes 196616 | tf_op jit(solution)/shard_map/ppermute | solution.py:139
  97.6 2.9 %collective-permute-done.9 = f32[2,32,256]{2,1,0:T(8,128)S(1)} collective-permute-done((f32[2,32,256]{2,1,0:T(8,128)S(1)}, f32[2,32,256]{2,1,0:T(8,128)S(1)}, u32[]{:S(2)}, u32[]{:S(2)}) %collective-permute-start.9) | collective-permute-done | bytes 65568 | tf_op jit(solution)/shard_map/ppermute | solution.py:139
  101.0 3.8 %collective-permute-done.10 = f32[2,32,256]{2,1,0:T(8,128)S(1)} collective-permute-done((f32[2,32,256]{2,1,0:T(8,128)S(1)}, f32[2,32,256]{2,1,0:T(8,128)S(1)}, u32[]{:S(2)}, u32[]{:S(2)}) %collective-permute-start.10) | collective-permute-done | bytes 65568 | tf_op jit(solution)/shard_map/ppermute | solution.py:139
  104.9 1.9 %correlate.9 = f32[2,32,256]{2,1,0:T(8,128)S(1)} custom-call(bf16[10240,512]{1,0:T(8,128)(2,1)S(1)} %place.1.placed_ref, bf16[2,32,10240]{2,1,0:T(8,128)(2,1)S(1)} %collective-permute-done.11.block_ref, f32[2,32,256]{2,1,0:T(8,128)S(1)} %add.32.refs_0_), custom_call_target="tpu_custom_call" | custom-call | bytes 1024 | tf_op jit(solution)/shard_map/correlate/pallas_call | solution.py:119
  106.8 1.7 %collective-permute-start.12 = (f32[2,32,256]{2,1,0:T(8,128)S(1)}, f32[2,32,256]{2,1,0:T(8,128)S(1)}, u32[]{:S(2)}, u32[]{:S(2)}) collective-permute-start(f32[2,32,256]{2,1,0:T(8,128)S(1)} %correlate.9), channel_id=1, source_target_pairs={{0,2},{1,3},{2,0},{3,1},{4,6},{5,7},{6,4},{7,5},{8,10},{9,11},{10,... | collective-permute-start | bytes 196616 | tf_op jit(solution)/shard_map/ppermute | solution.py:139
  108.5 4.9 %collective-permute-done.12 = f32[2,32,256]{2,1,0:T(8,128)S(1)} collective-permute-done((f32[2,32,256]{2,1,0:T(8,128)S(1)}, f32[2,32,256]{2,1,0:T(8,128)S(1)}, u32[]{:S(2)}, u32[]{:S(2)}) %collective-permute-start.12) | collective-permute-done | bytes 65568 | tf_op jit(solution)/shard_map/ppermute | solution.py:139
  113.9 3.9 %collective-permute-done.13 = f32[2,32,256]{2,1,0:T(8,128)S(1)} collective-permute-done((f32[2,32,256]{2,1,0:T(8,128)S(1)}, f32[2,32,256]{2,1,0:T(8,128)S(1)}, u32[]{:S(2)}, u32[]{:S(2)}) %collective-permute-start.13) | collective-permute-done | bytes 65568 | tf_op jit(solution)/shard_map/ppermute | solution.py:139
  117.8 1.5 %correlate.10.refs_0_ = f32[2,32,256]{2,1,0:T(8,128)S(1)} custom-call(bf16[10240,512]{1,0:T(8,128)(2,1)S(1)} %place.1.placed_ref, bf16[2,32,7680]{2,1,0:T(8,128)(2,1)S(1)} %collective-permute-done.8.block_ref, f32[2,224,256]{2,1,0:T(8,128)S(1)} %pad_maximum_fusion.refs_0_.refs_1_), custom_call_target="tpu_custom_call" | custom-call | bytes 1024 | tf_op jit(solution)/shard_map/correlate/pallas_call | solution.py:119
  119.9 2.2 %collective-permute-start.15 = (f32[2,32,256]{2,1,0:T(8,128)S(1)}, f32[2,32,256]{2,1,0:T(8,128)S(1)}, u32[]{:S(2)}, u32[]{:S(2)}) collective-permute-start(f32[2,32,256]{2,1,0:T(8,128)S(1)} %get-tuple-element.20), channel_id=1, source_target_pairs={{0,2},{1,3},{2,0},{3,1},{4,6},{5,7},{6,4},{7,5},{8,10},{9,11},{10,... | collective-permute-start | bytes 196616 | tf_op jit(solution)/shard_map/ppermute | solution.py:151
  122.1 5.0 %collective-permute-done.15 = f32[2,32,256]{2,1,0:T(8,128)S(1)} collective-permute-done((f32[2,32,256]{2,1,0:T(8,128)S(1)}, f32[2,32,256]{2,1,0:T(8,128)S(1)}, u32[]{:S(2)}, u32[]{:S(2)}) %collective-permute-start.15) | collective-permute-done | bytes 65568 | tf_op jit(solution)/shard_map/ppermute | solution.py:151
  127.9 2.1 %collective-permute-start.16 = (f32[2,32,256]{2,1,0:T(8,128)S(1)}, f32[2,32,256]{2,1,0:T(8,128)S(1)}, u32[]{:S(2)}, u32[]{:S(2)}) collective-permute-start(f32[2,32,256]{2,1,0:T(8,128)S(1)} %add.35.refs_2_), channel_id=1, source_target_pairs={{0,1},{1,0},{2,3},{3,2},{4,5},{5,4},{6,7},{7,6},{8,9},{9,8},{10,11... | collective-permute-start | bytes 196616 | tf_op jit(solution)/shard_map/ppermute | solution.py:153
  130.0 2.3 %collective-permute-done.18.refs_5_ = f32[2,32,256]{2,1,0:T(8,128)S(1)} collective-permute-done((f32[2,32,256]{2,1,0:T(8,128)S(1)}, f32[2,32,256]{2,1,0:T(8,128)S(1)}, u32[]{:S(2)}, u32[]{:S(2)}) %collective-permute-start.18) | collective-permute-done | bytes 65568 | tf_op jit(solution)/shard_map/ppermute | solution.py:155
  (32 shorter events, 8.4 us)
Async XLA Ops:
  2.2 45.6 %collective-permute-start.2 = (bf16[2,96,10240]{2,1,0:T(8,128)(2,1)S(1)}, bf16[2,96,10240]{2,1,0:T(8,128)(2,1)S(1)}, u32[]{:S(2)}, u32[]{:S(2)}) collective-permute-start(bf16[2,96,10240]{2,1,0:T(8,128)(2,1)S(1)} %cut.6.refs_1_), channel_id=1, source_target_pairs={{0,12},{4,0},{8,4},{12,8},{1,13},{5,1},{9,5},{13,9},{2,14},{6,2},{... | collective-permute-start | bytes 11796488 | tf_op jit(solution)/shard_map/ppermute | solution.py:19
  6.3 69.6 %collective-permute-start.1 = (bf16[2,64,10240]{2,1,0:T(8,128)(2,1)S(1)}, bf16[2,64,10240]{2,1,0:T(8,128)(2,1)S(1)}, u32[]{:S(2)}, u32[]{:S(2)}) collective-permute-start(bf16[2,64,10240]{2,1,0:T(8,128)(2,1)S(1)} %cut.7.refs_1_), channel_id=1, source_target_pairs={{0,12},{4,0},{8,4},{12,8},{1,13},{5,1},{9,5},{13,9},{2,14},{6,2},{... | collective-permute-start | bytes 7864328 | tf_op jit(solution)/shard_map/ppermute | solution.py:19
  8.4 84.2 %collective-permute-start = (bf16[2,32,10240]{2,1,0:T(8,128)(2,1)S(1)}, bf16[2,32,10240]{2,1,0:T(8,128)(2,1)S(1)}, u32[]{:S(2)}, u32[]{:S(2)}) collective-permute-start(bf16[2,32,10240]{2,1,0:T(8,128)(2,1)S(1)} %cut.8.refs_1_), channel_id=1, source_target_pairs={{0,12},{4,0},{8,4},{12,8},{1,13},{5,1},{9,5},{13,9},{2,14},{6,2},{... | collective-permute-start | bytes 3932168 | tf_op jit(solution)/shard_map/ppermute | solution.py:19
  10.9 1.1 copy-start
  50.0 54.9 %collective-permute-start.11 = (bf16[2,32,10240]{2,1,0:T(8,128)(2,1)S(1)}, bf16[2,32,10240]{2,1,0:T(8,128)(2,1)S(1)}, u32[]{:S(2)}, u32[]{:S(2)}) collective-permute-start(bf16[2,32,10240]{2,1,0:T(8,128)(2,1)S(1)} %get-tuple-element.18), channel_id=1, source_target_pairs={{0,12},{4,0},{8,4},{12,8},{1,13},{5,1},{9,5},{13,9},{2,14},{6,2},{... | collective-permute-start | bytes 3932168 | tf_op jit(solution)/shard_map/ppermute | solution.py:19
  52.0 10.9 %collective-permute-start.3 = (f32[2,96,256]{2,1,0:T(8,128)S(1)}, f32[2,96,256]{2,1,0:T(8,128)S(1)}, u32[]{:S(2)}, u32[]{:S(2)}) collective-permute-start(f32[2,96,256]{2,1,0:T(8,128)S(1)} %get-tuple-element.13), channel_id=1, source_target_pairs={{0,2},{1,3},{2,0},{3,1},{4,6},{5,7},{6,4},{7,5},{8,10},{9,11},{10,... | collective-permute-start | bytes 589832 | tf_op jit(solution)/shard_map/ppermute | solution.py:139
  62.9 5.8 %collective-permute-start.4 = (f32[2,96,256]{2,1,0:T(8,128)S(1)}, f32[2,96,256]{2,1,0:T(8,128)S(1)}, u32[]{:S(2)}, u32[]{:S(2)}) collective-permute-start(f32[2,96,256]{2,1,0:T(8,128)S(1)} %add.27), channel_id=1, source_target_pairs={{0,1},{1,0},{2,3},{3,2},{4,5},{5,4},{6,7},{7,6},{8,9},{9,8},{10,11... | collective-permute-start | bytes 589832 | tf_op jit(solution)/shard_map/ppermute | solution.py:139
  77.4 40.4 %collective-permute-start.8 = (bf16[2,32,7680]{2,1,0:T(8,128)(2,1)S(1)}, bf16[2,32,7680]{2,1,0:T(8,128)(2,1)S(1)}, u32[]{:S(2)}, u32[]{:S(2)}) collective-permute-start(bf16[2,32,7680]{2,1,0:T(8,128)(2,1)S(1)} %get-tuple-element.16), channel_id=1, source_target_pairs={{0,12},{4,0},{8,4},{12,8},{1,13},{5,1},{9,5},{13,9},{2,14},{6,2},{... | collective-permute-start | bytes 2949128 | tf_op jit(solution)/shard_map/ppermute | solution.py:19
  79.4 8.1 %collective-permute-start.5 = (f32[2,64,256]{2,1,0:T(8,128)S(1)}, f32[2,64,256]{2,1,0:T(8,128)S(1)}, u32[]{:S(2)}, u32[]{:S(2)}) collective-permute-start(f32[2,64,256]{2,1,0:T(8,128)S(1)} %get-tuple-element.14), channel_id=1, source_target_pairs={{0,2},{1,3},{2,0},{3,1},{4,6},{5,7},{6,4},{7,5},{8,10},{9,11},{10,... | collective-permute-start | bytes 393224 | tf_op jit(solution)/shard_map/ppermute | solution.py:139
  87.5 5.0 %collective-permute-start.6 = (f32[2,64,256]{2,1,0:T(8,128)S(1)}, f32[2,64,256]{2,1,0:T(8,128)S(1)}, u32[]{:S(2)}, u32[]{:S(2)}) collective-permute-start(f32[2,64,256]{2,1,0:T(8,128)S(1)} %add.29), channel_id=1, source_target_pairs={{0,1},{1,0},{2,3},{3,2},{4,5},{5,4},{6,7},{7,6},{8,9},{9,8},{10,11... | collective-permute-start | bytes 393224 | tf_op jit(solution)/shard_map/ppermute | solution.py:139
  94.5 6.0 %collective-permute-start.9 = (f32[2,32,256]{2,1,0:T(8,128)S(1)}, f32[2,32,256]{2,1,0:T(8,128)S(1)}, u32[]{:S(2)}, u32[]{:S(2)}) collective-permute-start(f32[2,32,256]{2,1,0:T(8,128)S(1)} %get-tuple-element.17), channel_id=1, source_target_pairs={{0,2},{1,3},{2,0},{3,1},{4,6},{5,7},{6,4},{7,5},{8,10},{9,11},{10,... | collective-permute-start | bytes 196616 | tf_op jit(solution)/shard_map/ppermute | solution.py:139
  96.7 22.6 %collective-permute-start.7 = (bf16[2,32,2560]{2,1,0:T(8,128)(2,1)S(1)}, bf16[2,32,2560]{2,1,0:T(8,128)(2,1)S(1)}, u32[]{:S(2)}, u32[]{:S(2)}) collective-permute-start(bf16[2,32,2560]{2,1,0:T(8,128)(2,1)S(1)} %get-tuple-element.15), channel_id=1, source_target_pairs={{0,12},{4,0},{8,4},{12,8},{1,13},{5,1},{9,5},{13,9},{2,14},{6,2},{... | collective-permute-start | bytes 983048 | tf_op jit(solution)/shard_map/ppermute | solution.py:19
  100.5 4.3 %collective-permute-start.10 = (f32[2,32,256]{2,1,0:T(8,128)S(1)}, f32[2,32,256]{2,1,0:T(8,128)S(1)}, u32[]{:S(2)}, u32[]{:S(2)}) collective-permute-start(f32[2,32,256]{2,1,0:T(8,128)S(1)} %add.31), channel_id=1, source_target_pairs={{0,1},{1,0},{2,3},{3,2},{4,5},{5,4},{6,7},{7,6},{8,9},{9,8},{10,11... | collective-permute-start | bytes 196616 | tf_op jit(solution)/shard_map/ppermute | solution.py:139
  106.8 6.6 %collective-permute-start.12 = (f32[2,32,256]{2,1,0:T(8,128)S(1)}, f32[2,32,256]{2,1,0:T(8,128)S(1)}, u32[]{:S(2)}, u32[]{:S(2)}) collective-permute-start(f32[2,32,256]{2,1,0:T(8,128)S(1)} %correlate.9), channel_id=1, source_target_pairs={{0,2},{1,3},{2,0},{3,1},{4,6},{5,7},{6,4},{7,5},{8,10},{9,11},{10,... | collective-permute-start | bytes 196616 | tf_op jit(solution)/shard_map/ppermute | solution.py:139
  113.4 4.3 %collective-permute-start.13 = (f32[2,32,256]{2,1,0:T(8,128)S(1)}, f32[2,32,256]{2,1,0:T(8,128)S(1)}, u32[]{:S(2)}, u32[]{:S(2)}) collective-permute-start(f32[2,32,256]{2,1,0:T(8,128)S(1)} %add.33), channel_id=1, source_target_pairs={{0,1},{1,0},{2,3},{3,2},{4,5},{5,4},{6,7},{7,6},{8,9},{9,8},{10,11... | collective-permute-start | bytes 196616 | tf_op jit(solution)/shard_map/ppermute | solution.py:139
  119.9 13.0 %collective-permute-start.14 = (f32[2,224,256]{2,1,0:T(8,128)S(1)}, f32[2,224,256]{2,1,0:T(8,128)S(1)}, u32[]{:S(2)}, u32[]{:S(2)}) collective-permute-start(f32[2,224,256]{2,1,0:T(8,128)S(1)} %get-tuple-element.19.refs_0_), channel_id=1, source_target_pairs={{0,4},{4,8},{8,12},{12,0},{1,5},{5,9},{9,13},{13,1},{2,6},{6,10},{... | collective-permute-start | bytes 1376264 | tf_op jit(solution)/shard_map/ppermute | solution.py:19
  119.9 7.1 %collective-permute-start.15 = (f32[2,32,256]{2,1,0:T(8,128)S(1)}, f32[2,32,256]{2,1,0:T(8,128)S(1)}, u32[]{:S(2)}, u32[]{:S(2)}) collective-permute-start(f32[2,32,256]{2,1,0:T(8,128)S(1)} %get-tuple-element.20), channel_id=1, source_target_pairs={{0,2},{1,3},{2,0},{3,1},{4,6},{5,7},{6,4},{7,5},{8,10},{9,11},{10,... | collective-permute-start | bytes 196616 | tf_op jit(solution)/shard_map/ppermute | solution.py:151
  127.1 5.3 %collective-permute-start.18 = (f32[2,32,256]{2,1,0:T(8,128)S(1)}, f32[2,32,256]{2,1,0:T(8,128)S(1)}, u32[]{:S(2)}, u32[]{:S(2)}) collective-permute-start(f32[2,32,256]{2,1,0:T(8,128)S(1)} %add.35.refs_2_), channel_id=1, source_target_pairs={{0,5},{1,4},{2,7},{3,6},{4,9},{5,8},{6,11},{7,10},{8,13},{9,12},{1... | collective-permute-start | bytes 196616 | tf_op jit(solution)/shard_map/ppermute | solution.py:155
  127.3 5.0 %collective-permute-start.17 = (f32[2,32,256]{2,1,0:T(8,128)S(1)}, f32[2,32,256]{2,1,0:T(8,128)S(1)}, u32[]{:S(2)}, u32[]{:S(2)}) collective-permute-start(f32[2,32,256]{2,1,0:T(8,128)S(1)} %add.35.refs_2_), channel_id=1, source_target_pairs={{0,4},{4,8},{8,12},{12,0},{1,5},{5,9},{9,13},{13,1},{2,6},{6,10},{... | collective-permute-start | bytes 196616 | tf_op jit(solution)/shard_map/ppermute | solution.py:19
  127.9 5.0 %collective-permute-start.16 = (f32[2,32,256]{2,1,0:T(8,128)S(1)}, f32[2,32,256]{2,1,0:T(8,128)S(1)}, u32[]{:S(2)}, u32[]{:S(2)}) collective-permute-start(f32[2,32,256]{2,1,0:T(8,128)S(1)} %add.35.refs_2_), channel_id=1, source_target_pairs={{0,1},{1,0},{2,3},{3,2},{4,5},{5,4},{6,7},{7,6},{8,9},{9,8},{10,11... | collective-permute-start | bytes 196616 | tf_op jit(solution)/shard_map/ppermute | solution.py:153

commit v11 on v10

--- a/solution.py
+++ b/solution.py
@@ -223,9 +223,10 @@
             arrived.append(moved(waiting, "ka", -1))
         whole.append(summed_over_pw(partial))
     most = jnp.concatenate(whole, axis=1)
-    last = correlate(placed, arrived[4], most)
-    last, most = correlate(placed, arrived[5], first=late, begun=last, held=[most])
-    return assembled([most], [moved(most, "ka", 1)], *sums_here_and_next(last))
+    last, most = correlate(placed, arrived[4], held=[most])
+    most_before = moved(most, "ka", 1)
+    last = correlate(placed, arrived[5], first=late, begun=last)
+    return assembled([most], [most_before], *sums_here_and_next(last))
 
 
 def solution(mesh):

time: 134 us -> 134 us (level)
  no operation moved by 1% of the time
where the time goes in v11:
time: 134 us
  waiting for transfers between devices  80 us (60%)
  Pallas kernels  28.6 us (21%)
  starting transfers between devices  25 us (19%)
    ppermute x8, waiting for transfers between devices, summed_over_pw(): lax.ppermute(partial, 'pw', [(i, i ^ distance) for i in range(pw)])  38.5 us
    ppermute x8, waiting for transfers between devices, moved(): lax.ppermute(block, axis, [(i, (i + distance) % count) for i in range(cou...  33.6 us
    ppermute x8, starting transfers between devices, summed_over_pw(): lax.ppermute(partial, 'pw', [(i, i ^ distance) for i in range(pw)])  11.8 us
    pallas_call x6, Pallas kernels, correlate(): pl.pallas_call(functools.partial(correlate_kernel, first, depth, begun is...  9.54 us
    pallas_call x1, Pallas kernels, placed_bands(): pl.pallas_call(place_kernel, grid=(width // step,), out_shape=pltpu.VMEM(...  9.33 us
    ppermute x8, starting transfers between devices, moved(): lax.ppermute(block, axis, [(i, (i + distance) % count) for i in range(cou...  8.9 us
    pallas_call x6, Pallas kernels, cut(): pl.pallas_call(functools.partial(cut_kernel, bands, waves), out_shape=jax...  8.73 us
    ppermute x1, waiting for transfers between devices, sums_here_and_next(): lax.ppermute(partial, 'pw', [(i, i ^ distance) for i in range(pw)])  4.21 us
  transfers between devices with their start and end apart: 19, of which 13 were waited for; matrix products, arithmetic and copies ran while one was open for 0% of the time, Pallas kernels for 19%

profile of v11, /device:TPU:0, one launch (start us, length us, event | category | flops | bytes accessed | tf_op | source)
XLA Modules:
  0.0 134.0 jit_solution(18417226090056733070)
XLA Ops:
  0.0 2.2 %cut.6.refs_1_ = bf16[2,96,10240]{2,1,0:T(8,128)(2,1)S(1)} custom-call(bf16[1,2,256,10240]{3,2,1,0:T(8,128)(2,1)} %own_ref.1), custom_call_target="tpu_custom_call" | custom-call | bytes 1024 | tf_op jit(solution)/shard_map/cut/pallas_call | solution.py:36
  2.2 2.4 %collective-permute-start.1 = (bf16[2,96,10240]{2,1,0:T(8,128)(2,1)S(1)}, bf16[2,96,10240]{2,1,0:T(8,128)(2,1)S(1)}, u32[]{:S(2)}, u32[]{:S(2)}) collective-permute-start(bf16[2,96,10240]{2,1,0:T(8,128)(2,1)S(1)} %cut.6.refs_1_), channel_id=1, source_target_pairs={{0,12},{4,0},{8,4},{12,8},{1,13},{5,1},{9,5},{13,9},{2,14},{6,2},{... | collective-permute-start | bytes 11796488 | tf_op jit(solution)/shard_map/ppermute | solution.py:19
  4.6 1.7 %cut.7.refs_1_ = bf16[2,64,10240]{2,1,0:T(8,128)(2,1)S(1)} custom-call(bf16[1,2,256,10240]{3,2,1,0:T(8,128)(2,1)} %own_ref.1, bf16[2,96,10240]{2,1,0:T(8,128)(2,1)S(1)} %cut.6.refs_1_), custom_call_target="tpu_custom_call" | custom-call | bytes 1024 | tf_op jit(solution)/shard_map/cut/pallas_call | solution.py:36
  7.1 1.3 cut.8.refs_1_
  8.4 1.3 cut.9.refs_1_.refs_0_
  9.7 1.2 cut.10.refs_1_
  11.0 1.0 cut.11.refs_0_.refs_1_
  12.0 9.3 %place.1.placed_ref = bf16[10240,512]{1,0:T(8,128)(2,1)S(1)} custom-call(bf16[1,2,256,10240]{3,2,1,0:T(8,128)(2,1)} %own_ref.1, s32[1,2,10240]{2,1,0:T(2,128)S(1)} %copy-done, bf16[2,32,2560]{2,1,0:T(8,128)(2,1)S(1)} %cut.11.refs_0_.refs_1_), custom_call_target="tpu_custom_call" | custom-call | bytes 1024 | tf_op jit(solution)/shard_map/place/pallas_call | solution.py:68
  21.4 26.4 %collective-permute-done.1.block_ref = bf16[2,96,10240]{2,1,0:T(8,128)(2,1)S(1)} collective-permute-done((bf16[2,96,10240]{2,1,0:T(8,128)(2,1)S(1)}, bf16[2,96,10240]{2,1,0:T(8,128)(2,1)S(1)}, u32[]{:S(2)}, u32[]{:S(2)}) %collective-permute-start.1) | collective-permute-done | bytes 3932192 | tf_op jit(solution)/shard_map/ppermute | solution.py:19
  47.8 2.2 %correlate.6 = (f32[2,96,256]{2,1,0:T(8,128)S(1)}, bf16[2,32,10240]{2,1,0:T(8,128)(2,1)S(1)}) custom-call(bf16[10240,512]{1,0:T(8,128)(2,1)S(1)} %place.1.placed_ref, bf16[2,96,10240]{2,1,0:T(8,128)(2,1)S(1)} %collective-permute-done.1.block_ref, bf16[2,32,10240]{2,1,0:T(8,128)(2,1)S(1)} %cut.9.refs_1_.refs_0_), custom_call_target="tpu_custom_call", output_to_operand_aliasing={{1}: (2, {})} | custom-call | bytes 1024 | tf_op jit(solution)/shard_map/correlate/pallas_call | solution.py:119
  50.0 2.0 %collective-permute-start.10 = (bf16[2,32,10240]{2,1,0:T(8,128)(2,1)S(1)}, bf16[2,32,10240]{2,1,0:T(8,128)(2,1)S(1)}, u32[]{:S(2)}, u32[]{:S(2)}) collective-permute-start(bf16[2,32,10240]{2,1,0:T(8,128)(2,1)S(1)} %get-tuple-element.17), channel_id=1, source_target_pairs={{0,12},{4,0},{8,4},{12,8},{1,13},{5,1},{9,5},{13,9},{2,14},{6,2},{... | collective-permute-start | bytes 3932168 | tf_op jit(solution)/shard_map/ppermute | solution.py:19
  52.0 2.6 %collective-permute-start.2 = (f32[2,96,256]{2,1,0:T(8,128)S(1)}, f32[2,96,256]{2,1,0:T(8,128)S(1)}, u32[]{:S(2)}, u32[]{:S(2)}) collective-permute-start(f32[2,96,256]{2,1,0:T(8,128)S(1)} %get-tuple-element.13), channel_id=1, source_target_pairs={{0,2},{1,3},{2,0},{3,1},{4,6},{5,7},{6,4},{7,5},{8,10},{9,11},{10,... | collective-permute-start | bytes 589832 | tf_op jit(solution)/shard_map/ppermute | solution.py:139
  54.6 8.3 %collective-permute-done.2 = f32[2,96,256]{2,1,0:T(8,128)S(1)} collective-permute-done((f32[2,96,256]{2,1,0:T(8,128)S(1)}, f32[2,96,256]{2,1,0:T(8,128)S(1)}, u32[]{:S(2)}, u32[]{:S(2)}) %collective-permute-start.2) | collective-permute-done | bytes 196640 | tf_op jit(solution)/shard_map/ppermute | solution.py:139
  63.7 5.1 %collective-permute-done.3 = f32[2,96,256]{2,1,0:T(8,128)S(1)} collective-permute-done((f32[2,96,256]{2,1,0:T(8,128)S(1)}, f32[2,96,256]{2,1,0:T(8,128)S(1)}, u32[]{:S(2)}, u32[]{:S(2)}) %collective-permute-start.3) | collective-permute-done | bytes 196640 | tf_op jit(solution)/shard_map/ppermute | solution.py:139
  68.8 7.1 %collective-permute-done.block_ref = bf16[2,64,10240]{2,1,0:T(8,128)(2,1)S(1)} collective-permute-done((bf16[2,64,10240]{2,1,0:T(8,128)(2,1)S(1)}, bf16[2,64,10240]{2,1,0:T(8,128)(2,1)S(1)}, u32[]{:S(2)}, u32[]{:S(2)}) %collective-permute-start) | collective-permute-done | bytes 2621472 | tf_op jit(solution)/shard_map/ppermute | solution.py:19
  75.9 1.5 %correlate.7 = (f32[2,64,256]{2,1,0:T(8,128)S(1)}, bf16[2,32,7680]{2,1,0:T(8,128)(2,1)S(1)}) custom-call(bf16[10240,512]{1,0:T(8,128)(2,1)S(1)} %place.1.placed_ref, bf16[2,64,10240]{2,1,0:T(8,128)(2,1)S(1)} %collective-permute-done.block_ref, f32[2,96,256]{2,1,0:T(8,128)S(1)} %add.28.refs_0_, ...), custom_call_target="tpu_custom_call", output_to_operand_aliasing={{1}: (3, {})} | custom-call | bytes 1024 | tf_op jit(solution)/shard_map/correlate/pallas_call | solution.py:119
  77.4 2.0 %collective-permute-start.4 = (bf16[2,32,7680]{2,1,0:T(8,128)(2,1)S(1)}, bf16[2,32,7680]{2,1,0:T(8,128)(2,1)S(1)}, u32[]{:S(2)}, u32[]{:S(2)}) collective-permute-start(bf16[2,32,7680]{2,1,0:T(8,128)(2,1)S(1)} %get-tuple-element.14), channel_id=1, source_target_pairs={{0,12},{4,0},{8,4},{12,8},{1,13},{5,1},{9,5},{13,9},{2,14},{6,2},{... | collective-permute-start | bytes 2949128 | tf_op jit(solution)/shard_map/ppermute | solution.py:19
  79.4 2.6 %collective-permute-start.5 = (f32[2,64,256]{2,1,0:T(8,128)S(1)}, f32[2,64,256]{2,1,0:T(8,128)S(1)}, u32[]{:S(2)}, u32[]{:S(2)}) collective-permute-start(f32[2,64,256]{2,1,0:T(8,128)S(1)} %get-tuple-element.15), channel_id=1, source_target_pairs={{0,2},{1,3},{2,0},{3,1},{4,6},{5,7},{6,4},{7,5},{8,10},{9,11},{10,... | collective-permute-start | bytes 393224 | tf_op jit(solution)/shard_map/ppermute | solution.py:139
  82.0 5.5 %collective-permute-done.5 = f32[2,64,256]{2,1,0:T(8,128)S(1)} collective-permute-done((f32[2,64,256]{2,1,0:T(8,128)S(1)}, f32[2,64,256]{2,1,0:T(8,128)S(1)}, u32[]{:S(2)}, u32[]{:S(2)}) %collective-permute-start.5) | collective-permute-done | bytes 131104 | tf_op jit(solution)/shard_map/ppermute | solution.py:139
  88.3 4.3 %collective-permute-done.6 = f32[2,64,256]{2,1,0:T(8,128)S(1)} collective-permute-done((f32[2,64,256]{2,1,0:T(8,128)S(1)}, f32[2,64,256]{2,1,0:T(8,128)S(1)}, u32[]{:S(2)}, u32[]{:S(2)}) %collective-permute-start.6) | collective-permute-done | bytes 131104 | tf_op jit(solution)/shard_map/ppermute | solution.py:139
  92.6 1.9 %correlate.8 = (f32[2,32,256]{2,1,0:T(8,128)S(1)}, bf16[2,32,2560]{2,1,0:T(8,128)(2,1)S(1)}) custom-call(bf16[10240,512]{1,0:T(8,128)(2,1)S(1)} %place.1.placed_ref, bf16[2,32,10240]{2,1,0:T(8,128)(2,1)S(1)} %collective-permute-done.7.block_ref, f32[2,64,256]{2,1,0:T(8,128)S(1)} %add.30.refs_0_, ...), custom_call_target="tpu_custom_call", output_to_operand_aliasing={{1}: (3, {})} | custom-call | bytes 1024 | tf_op jit(solution)/shard_map/correlate/pallas_call | solution.py:119
  94.5 2.2 %collective-permute-start.8 = (f32[2,32,256]{2,1,0:T(8,128)S(1)}, f32[2,32,256]{2,1,0:T(8,128)S(1)}, u32[]{:S(2)}, u32[]{:S(2)}) collective-permute-start(f32[2,32,256]{2,1,0:T(8,128)S(1)} %get-tuple-element.16), channel_id=1, source_target_pairs={{0,2},{1,3},{2,0},{3,1},{4,6},{5,7},{6,4},{7,5},{8,10},{9,11},{10,... | collective-permute-start | bytes 196616 | tf_op jit(solution)/shard_map/ppermute | solution.py:139
  96.7 3.7 %collective-permute-done.8 = f32[2,32,256]{2,1,0:T(8,128)S(1)} collective-permute-done((f32[2,32,256]{2,1,0:T(8,128)S(1)}, f32[2,32,256]{2,1,0:T(8,128)S(1)}, u32[]{:S(2)}, u32[]{:S(2)}) %collective-permute-start.8) | collective-permute-done | bytes 65568 | tf_op jit(solution)/shard_map/ppermute | solution.py:139
  101.0 3.7 %collective-permute-done.9 = f32[2,32,256]{2,1,0:T(8,128)S(1)} collective-permute-done((f32[2,32,256]{2,1,0:T(8,128)S(1)}, f32[2,32,256]{2,1,0:T(8,128)S(1)}, u32[]{:S(2)}, u32[]{:S(2)}) %collective-permute-start.9) | collective-permute-done | bytes 65568 | tf_op jit(solution)/shard_map/ppermute | solution.py:139
  104.8 1.9 %correlate.9 = f32[2,32,256]{2,1,0:T(8,128)S(1)} custom-call(bf16[10240,512]{1,0:T(8,128)(2,1)S(1)} %place.1.placed_ref, bf16[2,32,10240]{2,1,0:T(8,128)(2,1)S(1)} %collective-permute-done.10.block_ref, f32[2,32,256]{2,1,0:T(8,128)S(1)} %add.32.refs_0_), custom_call_target="tpu_custom_call" | custom-call | bytes 1024 | tf_op jit(solution)/shard_map/correlate/pallas_call | solution.py:119
  106.7 1.8 %collective-permute-start.11 = (f32[2,32,256]{2,1,0:T(8,128)S(1)}, f32[2,32,256]{2,1,0:T(8,128)S(1)}, u32[]{:S(2)}, u32[]{:S(2)}) collective-permute-start(f32[2,32,256]{2,1,0:T(8,128)S(1)} %correlate.9), channel_id=1, source_target_pairs={{0,2},{1,3},{2,0},{3,1},{4,6},{5,7},{6,4},{7,5},{8,10},{9,11},{10,... | collective-permute-start | bytes 196616 | tf_op jit(solution)/shard_map/ppermute | solution.py:139
  108.5 4.8 %collective-permute-done.11 = f32[2,32,256]{2,1,0:T(8,128)S(1)} collective-permute-done((f32[2,32,256]{2,1,0:T(8,128)S(1)}, f32[2,32,256]{2,1,0:T(8,128)S(1)}, u32[]{:S(2)}, u32[]{:S(2)}) %collective-permute-start.11) | collective-permute-done | bytes 65568 | tf_op jit(solution)/shard_map/ppermute | solution.py:139
  114.7 3.0 %collective-permute-done.12 = f32[2,32,256]{2,1,0:T(8,128)S(1)} collective-permute-done((f32[2,32,256]{2,1,0:T(8,128)S(1)}, f32[2,32,256]{2,1,0:T(8,128)S(1)}, u32[]{:S(2)}, u32[]{:S(2)}) %collective-permute-start.12) | collective-permute-done | bytes 65568 | tf_op jit(solution)/shard_map/ppermute | solution.py:139
  117.8 1.5 %correlate.10 = (f32[2,32,256]{2,1,0:T(8,128)S(1)}, f32[2,224,256]{2,1,0:T(8,128)S(1)}) custom-call(bf16[10240,512]{1,0:T(8,128)(2,1)S(1)} %place.1.placed_ref, bf16[2,32,7680]{2,1,0:T(8,128)(2,1)S(1)} %collective-permute-done.4.block_ref, f32[2,224,256]{2,1,0:T(8,128)S(1)} %pad_maximum_fusion.refs_0_), custom_call_target="tpu_custom_call", output_to_operand_aliasing={{1}: (2, {})} | custom-call | bytes 1024 | tf_op jit(solution)/shard_map/correlate/pallas_call | solution.py:119
  119.9 3.4 %collective-permute-start.15 = (f32[2,32,256]{2,1,0:T(8,128)S(1)}, f32[2,32,256]{2,1,0:T(8,128)S(1)}, u32[]{:S(2)}, u32[]{:S(2)}) collective-permute-start(f32[2,32,256]{2,1,0:T(8,128)S(1)} %correlate.11), channel_id=1, source_target_pairs={{0,2},{1,3},{2,0},{3,1},{4,6},{5,7},{6,4},{7,5},{8,10},{9,11},{10,... | collective-permute-start | bytes 196616 | tf_op jit(solution)/shard_map/ppermute | solution.py:151
  123.3 4.2 %collective-permute-done.15 = f32[2,32,256]{2,1,0:T(8,128)S(1)} collective-permute-done((f32[2,32,256]{2,1,0:T(8,128)S(1)}, f32[2,32,256]{2,1,0:T(8,128)S(1)}, u32[]{:S(2)}, u32[]{:S(2)}) %collective-permute-start.15) | collective-permute-done | bytes 65568 | tf_op jit(solution)/shard_map/ppermute | solution.py:151
  129.3 3.2 %collective-permute-done.18.refs_5_ = f32[2,32,256]{2,1,0:T(8,128)S(1)} collective-permute-done((f32[2,32,256]{2,1,0:T(8,128)S(1)}, f32[2,32,256]{2,1,0:T(8,128)S(1)}, u32[]{:S(2)}, u32[]{:S(2)}) %collective-permute-start.18) | collective-permute-done | bytes 65568 | tf_op jit(solution)/shard_map/ppermute | solution.py:155
  (32 shorter events, 8.3 us)
Async XLA Ops:
  2.2 45.6 %collective-permute-start.1 = (bf16[2,96,10240]{2,1,0:T(8,128)(2,1)S(1)}, bf16[2,96,10240]{2,1,0:T(8,128)(2,1)S(1)}, u32[]{:S(2)}, u32[]{:S(2)}) collective-permute-start(bf16[2,96,10240]{2,1,0:T(8,128)(2,1)S(1)} %cut.6.refs_1_), channel_id=1, source_target_pairs={{0,12},{4,0},{8,4},{12,8},{1,13},{5,1},{9,5},{13,9},{2,14},{6,2},{... | collective-permute-start | bytes 11796488 | tf_op jit(solution)/shard_map/ppermute | solution.py:19
  6.3 69.6 %collective-permute-start = (bf16[2,64,10240]{2,1,0:T(8,128)(2,1)S(1)}, bf16[2,64,10240]{2,1,0:T(8,128)(2,1)S(1)}, u32[]{:S(2)}, u32[]{:S(2)}) collective-permute-start(bf16[2,64,10240]{2,1,0:T(8,128)(2,1)S(1)} %cut.7.refs_1_), channel_id=1, source_target_pairs={{0,12},{4,0},{8,4},{12,8},{1,13},{5,1},{9,5},{13,9},{2,14},{6,2},{... | collective-permute-start | bytes 7864328 | tf_op jit(solution)/shard_map/ppermute | solution.py:19
  8.4 84.2 %collective-permute-start.7 = (bf16[2,32,10240]{2,1,0:T(8,128)(2,1)S(1)}, bf16[2,32,10240]{2,1,0:T(8,128)(2,1)S(1)}, u32[]{:S(2)}, u32[]{:S(2)}) collective-permute-start(bf16[2,32,10240]{2,1,0:T(8,128)(2,1)S(1)} %cut.8.refs_1_), channel_id=1, source_target_pairs={{0,12},{4,0},{8,4},{12,8},{1,13},{5,1},{9,5},{13,9},{2,14},{6,2},{... | collective-permute-start | bytes 3932168 | tf_op jit(solution)/shard_map/ppermute | solution.py:19
  10.9 1.1 copy-start
  50.0 54.8 %collective-permute-start.10 = (bf16[2,32,10240]{2,1,0:T(8,128)(2,1)S(1)}, bf16[2,32,10240]{2,1,0:T(8,128)(2,1)S(1)}, u32[]{:S(2)}, u32[]{:S(2)}) collective-permute-start(bf16[2,32,10240]{2,1,0:T(8,128)(2,1)S(1)} %get-tuple-element.17), channel_id=1, source_target_pairs={{0,12},{4,0},{8,4},{12,8},{1,13},{5,1},{9,5},{13,9},{2,14},{6,2},{... | collective-permute-start | bytes 3932168 | tf_op jit(solution)/shard_map/ppermute | solution.py:19
  52.0 10.9 %collective-permute-start.2 = (f32[2,96,256]{2,1,0:T(8,128)S(1)}, f32[2,96,256]{2,1,0:T(8,128)S(1)}, u32[]{:S(2)}, u32[]{:S(2)}) collective-permute-start(f32[2,96,256]{2,1,0:T(8,128)S(1)} %get-tuple-element.13), channel_id=1, source_target_pairs={{0,2},{1,3},{2,0},{3,1},{4,6},{5,7},{6,4},{7,5},{8,10},{9,11},{10,... | collective-permute-start | bytes 589832 | tf_op jit(solution)/shard_map/ppermute | solution.py:139
  62.9 5.8 %collective-permute-start.3 = (f32[2,96,256]{2,1,0:T(8,128)S(1)}, f32[2,96,256]{2,1,0:T(8,128)S(1)}, u32[]{:S(2)}, u32[]{:S(2)}) collective-permute-start(f32[2,96,256]{2,1,0:T(8,128)S(1)} %add.27), channel_id=1, source_target_pairs={{0,1},{1,0},{2,3},{3,2},{4,5},{5,4},{6,7},{7,6},{8,9},{9,8},{10,11... | collective-permute-start | bytes 589832 | tf_op jit(solution)/shard_map/ppermute | solution.py:139
  77.4 40.3 %collective-permute-start.4 = (bf16[2,32,7680]{2,1,0:T(8,128)(2,1)S(1)}, bf16[2,32,7680]{2,1,0:T(8,128)(2,1)S(1)}, u32[]{:S(2)}, u32[]{:S(2)}) collective-permute-start(bf16[2,32,7680]{2,1,0:T(8,128)(2,1)S(1)} %get-tuple-element.14), channel_id=1, source_target_pairs={{0,12},{4,0},{8,4},{12,8},{1,13},{5,1},{9,5},{13,9},{2,14},{6,2},{... | collective-permute-start | bytes 2949128 | tf_op jit(solution)/shard_map/ppermute | solution.py:19
  79.4 8.1 %collective-permute-start.5 = (f32[2,64,256]{2,1,0:T(8,128)S(1)}, f32[2,64,256]{2,1,0:T(8,128)S(1)}, u32[]{:S(2)}, u32[]{:S(2)}) collective-permute-start(f32[2,64,256]{2,1,0:T(8,128)S(1)} %get-tuple-element.15), channel_id=1, source_target_pairs={{0,2},{1,3},{2,0},{3,1},{4,6},{5,7},{6,4},{7,5},{8,10},{9,11},{10,... | collective-permute-start | bytes 393224 | tf_op jit(solution)/shard_map/ppermute | solution.py:139
  87.5 5.0 %collective-permute-start.6 = (f32[2,64,256]{2,1,0:T(8,128)S(1)}, f32[2,64,256]{2,1,0:T(8,128)S(1)}, u32[]{:S(2)}, u32[]{:S(2)}) collective-permute-start(f32[2,64,256]{2,1,0:T(8,128)S(1)} %add.29), channel_id=1, source_target_pairs={{0,1},{1,0},{2,3},{3,2},{4,5},{5,4},{6,7},{7,6},{8,9},{9,8},{10,11... | collective-permute-start | bytes 393224 | tf_op jit(solution)/shard_map/ppermute | solution.py:139
  94.5 5.9 %collective-permute-start.8 = (f32[2,32,256]{2,1,0:T(8,128)S(1)}, f32[2,32,256]{2,1,0:T(8,128)S(1)}, u32[]{:S(2)}, u32[]{:S(2)}) collective-permute-start(f32[2,32,256]{2,1,0:T(8,128)S(1)} %get-tuple-element.16), channel_id=1, source_target_pairs={{0,2},{1,3},{2,0},{3,1},{4,6},{5,7},{6,4},{7,5},{8,10},{9,11},{10,... | collective-permute-start | bytes 196616 | tf_op jit(solution)/shard_map/ppermute | solution.py:139
  100.5 4.3 %collective-permute-start.9 = (f32[2,32,256]{2,1,0:T(8,128)S(1)}, f32[2,32,256]{2,1,0:T(8,128)S(1)}, u32[]{:S(2)}, u32[]{:S(2)}) collective-permute-start(f32[2,32,256]{2,1,0:T(8,128)S(1)} %add.31), channel_id=1, source_target_pairs={{0,1},{1,0},{2,3},{3,2},{4,5},{5,4},{6,7},{7,6},{8,9},{9,8},{10,11... | collective-permute-start | bytes 196616 | tf_op jit(solution)/shard_map/ppermute | solution.py:139
  106.7 6.6 %collective-permute-start.11 = (f32[2,32,256]{2,1,0:T(8,128)S(1)}, f32[2,32,256]{2,1,0:T(8,128)S(1)}, u32[]{:S(2)}, u32[]{:S(2)}) collective-permute-start(f32[2,32,256]{2,1,0:T(8,128)S(1)} %correlate.9), channel_id=1, source_target_pairs={{0,2},{1,3},{2,0},{3,1},{4,6},{5,7},{6,4},{7,5},{8,10},{9,11},{10,... | collective-permute-start | bytes 196616 | tf_op jit(solution)/shard_map/ppermute | solution.py:139
  113.4 4.3 %collective-permute-start.12 = (f32[2,32,256]{2,1,0:T(8,128)S(1)}, f32[2,32,256]{2,1,0:T(8,128)S(1)}, u32[]{:S(2)}, u32[]{:S(2)}) collective-permute-start(f32[2,32,256]{2,1,0:T(8,128)S(1)} %add.33), channel_id=1, source_target_pairs={{0,1},{1,0},{2,3},{3,2},{4,5},{5,4},{6,7},{7,6},{8,9},{9,8},{10,11... | collective-permute-start | bytes 196616 | tf_op jit(solution)/shard_map/ppermute | solution.py:139
  113.9 5.4 %collective-permute-start.14 = (bf16[2,32,2560]{2,1,0:T(8,128)(2,1)S(1)}, bf16[2,32,2560]{2,1,0:T(8,128)(2,1)S(1)}, u32[]{:S(2)}, u32[]{:S(2)}) collective-permute-start(bf16[2,32,2560]{2,1,0:T(8,128)(2,1)S(1)} %get-tuple-element.19), channel_id=1, source_target_pairs={{0,12},{4,0},{8,4},{12,8},{1,13},{5,1},{9,5},{13,9},{2,14},{6,2},{... | collective-permute-start | bytes 983048 | tf_op jit(solution)/shard_map/ppermute | solution.py:19
  119.2 13.7 %collective-permute-start.13 = (f32[2,224,256]{2,1,0:T(8,128)S(1)}, f32[2,224,256]{2,1,0:T(8,128)S(1)}, u32[]{:S(2)}, u32[]{:S(2)}) collective-permute-start(f32[2,224,256]{2,1,0:T(8,128)S(1)} %get-tuple-element.18.refs_0_), channel_id=1, source_target_pairs={{0,4},{4,8},{8,12},{12,0},{1,5},{5,9},{9,13},{13,1},{2,6},{6,10},{... | collective-permute-start | bytes 1376264 | tf_op jit(solution)/shard_map/ppermute | solution.py:19
  119.9 7.6 %collective-permute-start.15 = (f32[2,32,256]{2,1,0:T(8,128)S(1)}, f32[2,32,256]{2,1,0:T(8,128)S(1)}, u32[]{:S(2)}, u32[]{:S(2)}) collective-permute-start(f32[2,32,256]{2,1,0:T(8,128)S(1)} %correlate.11), channel_id=1, source_target_pairs={{0,2},{1,3},{2,0},{3,1},{4,6},{5,7},{6,4},{7,5},{8,10},{9,11},{10,... | collective-permute-start | bytes 196616 | tf_op jit(solution)/shard_map/ppermute | solution.py:151
  127.5 5.0 %collective-permute-start.18 = (f32[2,32,256]{2,1,0:T(8,128)S(1)}, f32[2,32,256]{2,1,0:T(8,128)S(1)}, u32[]{:S(2)}, u32[]{:S(2)}) collective-permute-start(f32[2,32,256]{2,1,0:T(8,128)S(1)} %add.35.refs_2_), channel_id=1, source_target_pairs={{0,5},{1,4},{2,7},{3,6},{4,9},{5,8},{6,11},{7,10},{8,13},{9,12},{1... | collective-permute-start | bytes 196616 | tf_op jit(solution)/shard_map/ppermute | solution.py:155
  127.6 4.9 %collective-permute-start.17 = (f32[2,32,256]{2,1,0:T(8,128)S(1)}, f32[2,32,256]{2,1,0:T(8,128)S(1)}, u32[]{:S(2)}, u32[]{:S(2)}) collective-permute-start(f32[2,32,256]{2,1,0:T(8,128)S(1)} %add.35.refs_2_), channel_id=1, source_target_pairs={{0,4},{4,8},{8,12},{12,0},{1,5},{5,9},{9,13},{13,1},{2,6},{6,10},{... | collective-permute-start | bytes 196616 | tf_op jit(solution)/shard_map/ppermute | solution.py:19
  128.5 4.5 %collective-permute-start.16 = (f32[2,32,256]{2,1,0:T(8,128)S(1)}, f32[2,32,256]{2,1,0:T(8,128)S(1)}, u32[]{:S(2)}, u32[]{:S(2)}) collective-permute-start(f32[2,32,256]{2,1,0:T(8,128)S(1)} %add.35.refs_2_), channel_id=1, source_target_pairs={{0,1},{1,0},{2,3},{3,2},{4,5},{5,4},{6,7},{7,6},{8,9},{9,8},{10,11... | collective-permute-start | bytes 196616 | tf_op jit(solution)/shard_map/ppermute | solution.py:153

commit v12 on v11

--- a/solution.py
+++ b/solution.py
@@ -8,8 +8,9 @@
 from jax.sharding import PartitionSpec as P
 
 PWB = 256
-SIXTEENTHS = (6, 4, 2, 2, 2)
+SIXTEENTHS = (2, 6, 4, 2, 2)
 MIB = 1 << 20
+PLACE_FLOPS = 1 << 36
 ANYWHERE = pl.BlockSpec(memory_space=pl.ANY)
 WHOLE = pl.BlockSpec(memory_space=pltpu.VMEM)
 
@@ -76,7 +77,7 @@
         + [ANYWHERE] * len(others),
         out_specs=WHOLE,
         compiler_params=pltpu.CompilerParams(vmem_limit_bytes=16 * MIB),
-        cost_estimate=pl.CostEstimate(flops=0, bytes_accessed=1024, transcendentals=0),
+        cost_estimate=pl.CostEstimate(flops=PLACE_FLOPS, bytes_accessed=1024, transcendentals=0),
         name="place",
     )(coefficients, shifts, *others)
 
@@ -216,7 +217,7 @@
     arrived = [moved(block, "ka", -1) for block in blocks[:3]]
     whole = []
     for chunk in range(4):
-        waiting = blocks[3 + chunk : 4 + chunk]
+        waiting = blocks[2 + chunk : 3 + chunk] if chunk else []
         partial = correlate(placed, arrived[chunk], *whole[-1:], held=waiting)
         if waiting:
             partial, waiting = partial

time: 134 us -> 135 us (level)
  starting transfers between devices: 25 us -> 26.7 us
    ppermute x1, waiting for transfers between devices: 3.18 us -> 0.52 us  [sums_here_and_next(): lax.ppermute(partial, ('ka', 'pw'), across)]
    ppermute x1, waiting for transfers between devices: 0.45 us -> 1.98 us  [sums_here_and_next(): here = lax.ppermute(partial, 'pw', [(i, i ^ 1) for i in range(pw)])]
  transfers between devices with their start and end apart: 19 -> 19, of which waited for: 13 -> 14; matrix products, arithmetic and copies ran while one was open for 0% -> 0% of each run, Pallas kernels for 19% -> 20%
where the time goes in v12:
time: 135 us; the launch traced here: 134 us
  waiting for transfers between devices  78.8 us (58%)
  Pallas kernels  28.6 us (21%)
  starting transfers between devices  26.7 us (20%)
    ppermute x8, waiting for transfers between devices, summed_over_pw(): lax.ppermute(partial, 'pw', [(i, i ^ distance) for i in range(pw)])  38.5 us
    ppermute x8, waiting for transfers between devices, moved(): lax.ppermute(block, axis, [(i, (i + distance) % count) for i in range(cou...  34.3 us
    ppermute x8, starting transfers between devices, summed_over_pw(): lax.ppermute(partial, 'pw', [(i, i ^ distance) for i in range(pw)])  12.9 us
    pallas_call x6, Pallas kernels, correlate(): pl.pallas_call(functools.partial(correlate_kernel, first, depth, begun is...  9.54 us
    pallas_call x1, Pallas kernels, placed_bands(): pl.pallas_call(place_kernel, grid=(width // step,), out_shape=pltpu.VMEM(...  9.35 us
    pallas_call x6, Pallas kernels, cut(): pl.pallas_call(functools.partial(cut_kernel, bands, waves), out_shape=jax...  8.73 us
    ppermute x8, starting transfers between devices, moved(): lax.ppermute(block, axis, [(i, (i + distance) % count) for i in range(cou...  8.57 us
    ppermute x1, waiting for transfers between devices, sums_here_and_next(): lax.ppermute(partial, 'pw', [(i, i ^ distance) for i in range(pw)])  3.54 us
  transfers between devices with their start and end apart: 19, of which 14 were waited for; matrix products, arithmetic and copies ran while one was open for 0% of the time, Pallas kernels for 20%

profile of v12, /device:TPU:0, one launch (start us, length us, event | category | flops | bytes accessed | tf_op | source)
XLA Modules:
  0.0 134.5 jit_solution(3148426753071179144)
XLA Ops:
  0.0 1.3 cut.6.refs_1_
  1.3 2.4 %collective-permute-start.2 = (bf16[2,32,10240]{2,1,0:T(8,128)(2,1)S(1)}, bf16[2,32,10240]{2,1,0:T(8,128)(2,1)S(1)}, u32[]{:S(2)}, u32[]{:S(2)}) collective-permute-start(bf16[2,32,10240]{2,1,0:T(8,128)(2,1)S(1)} %cut.6.refs_1_), channel_id=1, source_target_pairs={{0,12},{4,0},{8,4},{12,8},{1,13},{5,1},{9,5},{13,9},{2,14},{6,2},{... | collective-permute-start | bytes 3932168 | tf_op jit(solution)/shard_map/ppermute | solution.py:20
  3.7 2.2 %cut.7.refs_1_ = bf16[2,96,10240]{2,1,0:T(8,128)(2,1)S(1)} custom-call(bf16[1,2,256,10240]{3,2,1,0:T(8,128)(2,1)} %own_ref.1, bf16[2,32,10240]{2,1,0:T(8,128)(2,1)S(1)} %cut.6.refs_1_), custom_call_target="tpu_custom_call" | custom-call | bytes 1024 | tf_op jit(solution)/shard_map/cut/pallas_call | solution.py:37
  6.6 1.7 %cut.8.refs_1_ = bf16[2,64,10240]{2,1,0:T(8,128)(2,1)S(1)} custom-call(bf16[1,2,256,10240]{3,2,1,0:T(8,128)(2,1)} %own_ref.1, bf16[2,96,10240]{2,1,0:T(8,128)(2,1)S(1)} %cut.7.refs_1_), custom_call_target="tpu_custom_call" | custom-call | bytes 1024 | tf_op jit(solution)/shard_map/cut/pallas_call | solution.py:37
  8.4 1.3 cut.9.refs_1_
  12.0 9.4 %place.1.placed_ref = bf16[10240,512]{1,0:T(8,128)(2,1)S(1)} custom-call(bf16[1,2,256,10240]{3,2,1,0:T(8,128)(2,1)} %own_ref.1, s32[1,2,10240]{2,1,0:T(2,128)S(1)} %copy-done, bf16[2,32,2560]{2,1,0:T(8,128)(2,1)S(1)} %cut.11.refs_0_.refs_1_), custom_call_target="tpu_custom_call" | custom-call | flops 68719476736 | bytes 1024 | tf_op jit(solution)/shard_map/place/pallas_call | solution.py:69
  21.4 1.9 %correlate.6 = f32[2,32,256]{2,1,0:T(8,128)S(1)} custom-call(bf16[10240,512]{1,0:T(8,128)(2,1)S(1)} %place.1.placed_ref, bf16[2,32,10240]{2,1,0:T(8,128)(2,1)S(1)} %collective-permute-done.2.block_ref), custom_call_target="tpu_custom_call" | custom-call | bytes 1024 | tf_op jit(solution)/shard_map/correlate/pallas_call | solution.py:120
  23.3 2.6 %collective-permute-start.3 = (f32[2,32,256]{2,1,0:T(8,128)S(1)}, f32[2,32,256]{2,1,0:T(8,128)S(1)}, u32[]{:S(2)}, u32[]{:S(2)}) collective-permute-start(f32[2,32,256]{2,1,0:T(8,128)S(1)} %correlate.6), channel_id=1, source_target_pairs={{0,2},{1,3},{2,0},{3,1},{4,6},{5,7},{6,4},{7,5},{8,10},{9,11},{10,... | collective-permute-start | bytes 196616 | tf_op jit(solution)/shard_map/ppermute | solution.py:140
  26.0 4.2 %collective-permute-done.3 = f32[2,32,256]{2,1,0:T(8,128)S(1)} collective-permute-done((f32[2,32,256]{2,1,0:T(8,128)S(1)}, f32[2,32,256]{2,1,0:T(8,128)S(1)}, u32[]{:S(2)}, u32[]{:S(2)}) %collective-permute-start.3) | collective-permute-done | bytes 65568 | tf_op jit(solution)/shard_map/ppermute | solution.py:140
  30.9 3.6 %collective-permute-done.4 = f32[2,32,256]{2,1,0:T(8,128)S(1)} collective-permute-done((f32[2,32,256]{2,1,0:T(8,128)S(1)}, f32[2,32,256]{2,1,0:T(8,128)S(1)}, u32[]{:S(2)}, u32[]{:S(2)}) %collective-permute-start.4) | collective-permute-done | bytes 65568 | tf_op jit(solution)/shard_map/ppermute | solution.py:140
  34.5 26.5 %collective-permute-done.1.block_ref = bf16[2,96,10240]{2,1,0:T(8,128)(2,1)S(1)} collective-permute-done((bf16[2,96,10240]{2,1,0:T(8,128)(2,1)S(1)}, bf16[2,96,10240]{2,1,0:T(8,128)(2,1)S(1)}, u32[]{:S(2)}, u32[]{:S(2)}) %collective-permute-start.1) | collective-permute-done | bytes 3932192 | tf_op jit(solution)/shard_map/ppermute | solution.py:20
  61.0 2.2 %correlate.7 = (f32[2,96,256]{2,1,0:T(8,128)S(1)}, bf16[2,32,10240]{2,1,0:T(8,128)(2,1)S(1)}) custom-call(bf16[10240,512]{1,0:T(8,128)(2,1)S(1)} %place.1.placed_ref, bf16[2,96,10240]{2,1,0:T(8,128)(2,1)S(1)} %collective-permute-done.1.block_ref, f32[2,32,256]{2,1,0:T(8,128)S(1)} %add.28.refs_0_, ...), custom_call_target="tpu_custom_call", output_to_operand_aliasing={{1}: (3, {})} | custom-call | bytes 1024 | tf_op jit(solution)/shard_map/correlate/pallas_call | solution.py:120
  63.2 2.0 %collective-permute-start.10 = (bf16[2,32,10240]{2,1,0:T(8,128)(2,1)S(1)}, bf16[2,32,10240]{2,1,0:T(8,128)(2,1)S(1)}, u32[]{:S(2)}, u32[]{:S(2)}) collective-permute-start(bf16[2,32,10240]{2,1,0:T(8,128)(2,1)S(1)} %get-tuple-element.16), channel_id=1, source_target_pairs={{0,12},{4,0},{8,4},{12,8},{1,13},{5,1},{9,5},{13,9},{2,14},{6,2},{... | collective-permute-start | bytes 3932168 | tf_op jit(solution)/shard_map/ppermute | solution.py:20
  65.2 2.6 %collective-permute-start.5 = (f32[2,96,256]{2,1,0:T(8,128)S(1)}, f32[2,96,256]{2,1,0:T(8,128)S(1)}, u32[]{:S(2)}, u32[]{:S(2)}) collective-permute-start(f32[2,96,256]{2,1,0:T(8,128)S(1)} %get-tuple-element.13), channel_id=1, source_target_pairs={{0,2},{1,3},{2,0},{3,1},{4,6},{5,7},{6,4},{7,5},{8,10},{9,11},{10,... | collective-permute-start | bytes 589832 | tf_op jit(solution)/shard_map/ppermute | solution.py:140
  67.8 8.3 %collective-permute-done.5 = f32[2,96,256]{2,1,0:T(8,128)S(1)} collective-permute-done((f32[2,96,256]{2,1,0:T(8,128)S(1)}, f32[2,96,256]{2,1,0:T(8,128)S(1)}, u32[]{:S(2)}, u32[]{:S(2)}) %collective-permute-start.5) | collective-permute-done | bytes 196640 | tf_op jit(solution)/shard_map/ppermute | solution.py:140
  76.9 5.1 %collective-permute-done.6 = f32[2,96,256]{2,1,0:T(8,128)S(1)} collective-permute-done((f32[2,96,256]{2,1,0:T(8,128)S(1)}, f32[2,96,256]{2,1,0:T(8,128)S(1)}, u32[]{:S(2)}, u32[]{:S(2)}) %collective-permute-start.6) | collective-permute-done | bytes 196640 | tf_op jit(solution)/shard_map/ppermute | solution.py:140
  82.0 7.1 %collective-permute-done.block_ref = bf16[2,64,10240]{2,1,0:T(8,128)(2,1)S(1)} collective-permute-done((bf16[2,64,10240]{2,1,0:T(8,128)(2,1)S(1)}, bf16[2,64,10240]{2,1,0:T(8,128)(2,1)S(1)}, u32[]{:S(2)}, u32[]{:S(2)}) %collective-permute-start) | collective-permute-done | bytes 2621472 | tf_op jit(solution)/shard_map/ppermute | solution.py:20
  89.1 1.5 %correlate.8 = (f32[2,64,256]{2,1,0:T(8,128)S(1)}, bf16[2,32,7680]{2,1,0:T(8,128)(2,1)S(1)}) custom-call(bf16[10240,512]{1,0:T(8,128)(2,1)S(1)} %place.1.placed_ref, bf16[2,64,10240]{2,1,0:T(8,128)(2,1)S(1)} %collective-permute-done.block_ref, f32[2,96,256]{2,1,0:T(8,128)S(1)} %add.30.refs_0_, ...), custom_call_target="tpu_custom_call", output_to_operand_aliasing={{1}: (3, {})} | custom-call | bytes 1024 | tf_op jit(solution)/shard_map/correlate/pallas_call | solution.py:120
  90.6 2.0 %collective-permute-start.7 = (bf16[2,32,7680]{2,1,0:T(8,128)(2,1)S(1)}, bf16[2,32,7680]{2,1,0:T(8,128)(2,1)S(1)}, u32[]{:S(2)}, u32[]{:S(2)}) collective-permute-start(bf16[2,32,7680]{2,1,0:T(8,128)(2,1)S(1)} %get-tuple-element.14), channel_id=1, source_target_pairs={{0,12},{4,0},{8,4},{12,8},{1,13},{5,1},{9,5},{13,9},{2,14},{6,2},{... | collective-permute-start | bytes 2949128 | tf_op jit(solution)/shard_map/ppermute | solution.py:20
  92.6 2.6 %collective-permute-start.8 = (f32[2,64,256]{2,1,0:T(8,128)S(1)}, f32[2,64,256]{2,1,0:T(8,128)S(1)}, u32[]{:S(2)}, u32[]{:S(2)}) collective-permute-start(f32[2,64,256]{2,1,0:T(8,128)S(1)} %get-tuple-element.15), channel_id=1, source_target_pairs={{0,2},{1,3},{2,0},{3,1},{4,6},{5,7},{6,4},{7,5},{8,10},{9,11},{10,... | collective-permute-start | bytes 393224 | tf_op jit(solution)/shard_map/ppermute | solution.py:140
  95.2 5.5 %collective-permute-done.8 = f32[2,64,256]{2,1,0:T(8,128)S(1)} collective-permute-done((f32[2,64,256]{2,1,0:T(8,128)S(1)}, f32[2,64,256]{2,1,0:T(8,128)S(1)}, u32[]{:S(2)}, u32[]{:S(2)}) %collective-permute-start.8) | collective-permute-done | bytes 131104 | tf_op jit(solution)/shard_map/ppermute | solution.py:140
  101.5 4.3 %collective-permute-done.9 = f32[2,64,256]{2,1,0:T(8,128)S(1)} collective-permute-done((f32[2,64,256]{2,1,0:T(8,128)S(1)}, f32[2,64,256]{2,1,0:T(8,128)S(1)}, u32[]{:S(2)}, u32[]{:S(2)}) %collective-permute-start.9) | collective-permute-done | bytes 131104 | tf_op jit(solution)/shard_map/ppermute | solution.py:140
  105.8 1.9 %correlate.9 = (f32[2,32,256]{2,1,0:T(8,128)S(1)}, bf16[2,32,2560]{2,1,0:T(8,128)(2,1)S(1)}) custom-call(bf16[10240,512]{1,0:T(8,128)(2,1)S(1)} %place.1.placed_ref, bf16[2,32,10240]{2,1,0:T(8,128)(2,1)S(1)} %collective-permute-done.10.block_ref, f32[2,64,256]{2,1,0:T(8,128)S(1)} %add.32.refs_0_, ...), custom_call_target="tpu_custom_call", output_to_operand_aliasing={{1}: (3, {})} | custom-call | bytes 1024 | tf_op jit(solution)/shard_map/correlate/pallas_call | solution.py:120
  107.7 2.2 %collective-permute-start.11 = (f32[2,32,256]{2,1,0:T(8,128)S(1)}, f32[2,32,256]{2,1,0:T(8,128)S(1)}, u32[]{:S(2)}, u32[]{:S(2)}) collective-permute-start(f32[2,32,256]{2,1,0:T(8,128)S(1)} %get-tuple-element.17), channel_id=1, source_target_pairs={{0,2},{1,3},{2,0},{3,1},{4,6},{5,7},{6,4},{7,5},{8,10},{9,11},{10,... | collective-permute-start | bytes 196616 | tf_op jit(solution)/shard_map/ppermute | solution.py:140
  109.9 3.7 %collective-permute-done.11 = f32[2,32,256]{2,1,0:T(8,128)S(1)} collective-permute-done((f32[2,32,256]{2,1,0:T(8,128)S(1)}, f32[2,32,256]{2,1,0:T(8,128)S(1)}, u32[]{:S(2)}, u32[]{:S(2)}) %collective-permute-start.11) | collective-permute-done | bytes 65568 | tf_op jit(solution)/shard_map/ppermute | solution.py:140
  114.2 3.7 %collective-permute-done.12 = f32[2,32,256]{2,1,0:T(8,128)S(1)} collective-permute-done((f32[2,32,256]{2,1,0:T(8,128)S(1)}, f32[2,32,256]{2,1,0:T(8,128)S(1)}, u32[]{:S(2)}, u32[]{:S(2)}) %collective-permute-start.12) | collective-permute-done | bytes 65568 | tf_op jit(solution)/shard_map/ppermute | solution.py:140
  118.0 1.5 %correlate.10 = (f32[2,32,256]{2,1,0:T(8,128)S(1)}, f32[2,224,256]{2,1,0:T(8,128)S(1)}) custom-call(bf16[10240,512]{1,0:T(8,128)(2,1)S(1)} %place.1.placed_ref, bf16[2,32,7680]{2,1,0:T(8,128)(2,1)S(1)} %collective-permute-done.7.block_ref, f32[2,224,256]{2,1,0:T(8,128)S(1)} %pad_maximum_fusion.refs_0_), custom_call_target="tpu_custom_call", output_to_operand_aliasing={{1}: (2, {})} | custom-call | bytes 1024 | tf_op jit(solution)/shard_map/correlate/pallas_call | solution.py:120
  120.2 2.4 %collective-permute-start.15 = (f32[2,32,256]{2,1,0:T(8,128)S(1)}, f32[2,32,256]{2,1,0:T(8,128)S(1)}, u32[]{:S(2)}, u32[]{:S(2)}) collective-permute-start(f32[2,32,256]{2,1,0:T(8,128)S(1)} %correlate.11), channel_id=1, source_target_pairs={{0,2},{1,3},{2,0},{3,1},{4,6},{5,7},{6,4},{7,5},{8,10},{9,11},{10,... | collective-permute-start | bytes 196616 | tf_op jit(solution)/shard_map/ppermute | solution.py:152
  122.5 3.5 %collective-permute-done.15 = f32[2,32,256]{2,1,0:T(8,128)S(1)} collective-permute-done((f32[2,32,256]{2,1,0:T(8,128)S(1)}, f32[2,32,256]{2,1,0:T(8,128)S(1)}, u32[]{:S(2)}, u32[]{:S(2)}) %collective-permute-start.15) | collective-permute-done | bytes 65568 | tf_op jit(solution)/shard_map/ppermute | solution.py:152
  127.1 1.4 %collective-permute-start.17 = (f32[2,32,256]{2,1,0:T(8,128)S(1)}, f32[2,32,256]{2,1,0:T(8,128)S(1)}, u32[]{:S(2)}, u32[]{:S(2)}) collective-permute-start(f32[2,32,256]{2,1,0:T(8,128)S(1)} %add.35.refs_2_), channel_id=1, source_target_pairs={{0,4},{4,8},{8,12},{12,0},{1,5},{5,9},{9,13},{13,1},{2,6},{6,10},{... | collective-permute-start | bytes 196616 | tf_op jit(solution)/shard_map/ppermute | solution.py:20
  128.5 1.8 %collective-permute-start.16 = (f32[2,32,256]{2,1,0:T(8,128)S(1)}, f32[2,32,256]{2,1,0:T(8,128)S(1)}, u32[]{:S(2)}, u32[]{:S(2)}) collective-permute-start(f32[2,32,256]{2,1,0:T(8,128)S(1)} %add.35.refs_2_), channel_id=1, source_target_pairs={{0,1},{1,0},{2,3},{3,2},{4,5},{5,4},{6,7},{7,6},{8,9},{9,8},{10,11... | collective-permute-start | bytes 196616 | tf_op jit(solution)/shard_map/ppermute | solution.py:154
  131.4 2.0 %collective-permute-done.16.refs_3_ = f32[2,32,256]{2,1,0:T(8,128)S(1)} collective-permute-done((f32[2,32,256]{2,1,0:T(8,128)S(1)}, f32[2,32,256]{2,1,0:T(8,128)S(1)}, u32[]{:S(2)}, u32[]{:S(2)}) %collective-permute-start.16) | collective-permute-done | bytes 65568 | tf_op jit(solution)/shard_map/ppermute | solution.py:154
  (32 shorter events, 9.9 us)
Async XLA Ops:
  1.3 20.1 %collective-permute-start.2 = (bf16[2,32,10240]{2,1,0:T(8,128)(2,1)S(1)}, bf16[2,32,10240]{2,1,0:T(8,128)(2,1)S(1)}, u32[]{:S(2)}, u32[]{:S(2)}) collective-permute-start(bf16[2,32,10240]{2,1,0:T(8,128)(2,1)S(1)} %cut.6.refs_1_), channel_id=1, source_target_pairs={{0,12},{4,0},{8,4},{12,8},{1,13},{5,1},{9,5},{13,9},{2,14},{6,2},{... | collective-permute-start | bytes 3932168 | tf_op jit(solution)/shard_map/ppermute | solution.py:20
  5.9 55.1 %collective-permute-start.1 = (bf16[2,96,10240]{2,1,0:T(8,128)(2,1)S(1)}, bf16[2,96,10240]{2,1,0:T(8,128)(2,1)S(1)}, u32[]{:S(2)}, u32[]{:S(2)}) collective-permute-start(bf16[2,96,10240]{2,1,0:T(8,128)(2,1)S(1)} %cut.7.refs_1_), channel_id=1, source_target_pairs={{0,12},{4,0},{8,4},{12,8},{1,13},{5,1},{9,5},{13,9},{2,14},{6,2},{... | collective-permute-start | bytes 11796488 | tf_op jit(solution)/shard_map/ppermute | solution.py:20
  8.4 80.7 %collective-permute-start = (bf16[2,64,10240]{2,1,0:T(8,128)(2,1)S(1)}, bf16[2,64,10240]{2,1,0:T(8,128)(2,1)S(1)}, u32[]{:S(2)}, u32[]{:S(2)}) collective-permute-start(bf16[2,64,10240]{2,1,0:T(8,128)(2,1)S(1)} %cut.8.refs_1_), channel_id=1, source_target_pairs={{0,12},{4,0},{8,4},{12,8},{1,13},{5,1},{9,5},{13,9},{2,14},{6,2},{... | collective-permute-start | bytes 7864328 | tf_op jit(solution)/shard_map/ppermute | solution.py:20
  10.9 1.1 copy-start
  23.3 6.8 %collective-permute-start.3 = (f32[2,32,256]{2,1,0:T(8,128)S(1)}, f32[2,32,256]{2,1,0:T(8,128)S(1)}, u32[]{:S(2)}, u32[]{:S(2)}) collective-permute-start(f32[2,32,256]{2,1,0:T(8,128)S(1)} %correlate.6), channel_id=1, source_target_pairs={{0,2},{1,3},{2,0},{3,1},{4,6},{5,7},{6,4},{7,5},{8,10},{9,11},{10,... | collective-permute-start | bytes 196616 | tf_op jit(solution)/shard_map/ppermute | solution.py:140
  30.2 4.3 %collective-permute-start.4 = (f32[2,32,256]{2,1,0:T(8,128)S(1)}, f32[2,32,256]{2,1,0:T(8,128)S(1)}, u32[]{:S(2)}, u32[]{:S(2)}) collective-permute-start(f32[2,32,256]{2,1,0:T(8,128)S(1)} %add.27), channel_id=1, source_target_pairs={{0,1},{1,0},{2,3},{3,2},{4,5},{5,4},{6,7},{7,6},{8,9},{9,8},{10,11... | collective-permute-start | bytes 196616 | tf_op jit(solution)/shard_map/ppermute | solution.py:140
  63.2 42.6 %collective-permute-start.10 = (bf16[2,32,10240]{2,1,0:T(8,128)(2,1)S(1)}, bf16[2,32,10240]{2,1,0:T(8,128)(2,1)S(1)}, u32[]{:S(2)}, u32[]{:S(2)}) collective-permute-start(bf16[2,32,10240]{2,1,0:T(8,128)(2,1)S(1)} %get-tuple-element.16), channel_id=1, source_target_pairs={{0,12},{4,0},{8,4},{12,8},{1,13},{5,1},{9,5},{13,9},{2,14},{6,2},{... | collective-permute-start | bytes 3932168 | tf_op jit(solution)/shard_map/ppermute | solution.py:20
  65.2 10.9 %collective-permute-start.5 = (f32[2,96,256]{2,1,0:T(8,128)S(1)}, f32[2,96,256]{2,1,0:T(8,128)S(1)}, u32[]{:S(2)}, u32[]{:S(2)}) collective-permute-start(f32[2,96,256]{2,1,0:T(8,128)S(1)} %get-tuple-element.13), channel_id=1, source_target_pairs={{0,2},{1,3},{2,0},{3,1},{4,6},{5,7},{6,4},{7,5},{8,10},{9,11},{10,... | collective-permute-start | bytes 589832 | tf_op jit(solution)/shard_map/ppermute | solution.py:140
  76.1 5.8 %collective-permute-start.6 = (f32[2,96,256]{2,1,0:T(8,128)S(1)}, f32[2,96,256]{2,1,0:T(8,128)S(1)}, u32[]{:S(2)}, u32[]{:S(2)}) collective-permute-start(f32[2,96,256]{2,1,0:T(8,128)S(1)} %add.29), channel_id=1, source_target_pairs={{0,1},{1,0},{2,3},{3,2},{4,5},{5,4},{6,7},{7,6},{8,9},{9,8},{10,11... | collective-permute-start | bytes 589832 | tf_op jit(solution)/shard_map/ppermute | solution.py:140
  90.6 27.4 %collective-permute-start.7 = (bf16[2,32,7680]{2,1,0:T(8,128)(2,1)S(1)}, bf16[2,32,7680]{2,1,0:T(8,128)(2,1)S(1)}, u32[]{:S(2)}, u32[]{:S(2)}) collective-permute-start(bf16[2,32,7680]{2,1,0:T(8,128)(2,1)S(1)} %get-tuple-element.14), channel_id=1, source_target_pairs={{0,12},{4,0},{8,4},{12,8},{1,13},{5,1},{9,5},{13,9},{2,14},{6,2},{... | collective-permute-start | bytes 2949128 | tf_op jit(solution)/shard_map/ppermute | solution.py:20
  92.6 8.1 %collective-permute-start.8 = (f32[2,64,256]{2,1,0:T(8,128)S(1)}, f32[2,64,256]{2,1,0:T(8,128)S(1)}, u32[]{:S(2)}, u32[]{:S(2)}) collective-permute-start(f32[2,64,256]{2,1,0:T(8,128)S(1)} %get-tuple-element.15), channel_id=1, source_target_pairs={{0,2},{1,3},{2,0},{3,1},{4,6},{5,7},{6,4},{7,5},{8,10},{9,11},{10,... | collective-permute-start | bytes 393224 | tf_op jit(solution)/shard_map/ppermute | solution.py:140
  100.7 5.0 %collective-permute-start.9 = (f32[2,64,256]{2,1,0:T(8,128)S(1)}, f32[2,64,256]{2,1,0:T(8,128)S(1)}, u32[]{:S(2)}, u32[]{:S(2)}) collective-permute-start(f32[2,64,256]{2,1,0:T(8,128)S(1)} %add.31), channel_id=1, source_target_pairs={{0,1},{1,0},{2,3},{3,2},{4,5},{5,4},{6,7},{7,6},{8,9},{9,8},{10,11... | collective-permute-start | bytes 393224 | tf_op jit(solution)/shard_map/ppermute | solution.py:140
  107.7 5.9 %collective-permute-start.11 = (f32[2,32,256]{2,1,0:T(8,128)S(1)}, f32[2,32,256]{2,1,0:T(8,128)S(1)}, u32[]{:S(2)}, u32[]{:S(2)}) collective-permute-start(f32[2,32,256]{2,1,0:T(8,128)S(1)} %get-tuple-element.17), channel_id=1, source_target_pairs={{0,2},{1,3},{2,0},{3,1},{4,6},{5,7},{6,4},{7,5},{8,10},{9,11},{10,... | collective-permute-start | bytes 196616 | tf_op jit(solution)/shard_map/ppermute | solution.py:140
  113.6 4.3 %collective-permute-start.12 = (f32[2,32,256]{2,1,0:T(8,128)S(1)}, f32[2,32,256]{2,1,0:T(8,128)S(1)}, u32[]{:S(2)}, u32[]{:S(2)}) collective-permute-start(f32[2,32,256]{2,1,0:T(8,128)S(1)} %add.33), channel_id=1, source_target_pairs={{0,1},{1,0},{2,3},{3,2},{4,5},{5,4},{6,7},{7,6},{8,9},{9,8},{10,11... | collective-permute-start | bytes 196616 | tf_op jit(solution)/shard_map/ppermute | solution.py:140
  114.2 5.3 %collective-permute-start.14 = (bf16[2,32,2560]{2,1,0:T(8,128)(2,1)S(1)}, bf16[2,32,2560]{2,1,0:T(8,128)(2,1)S(1)}, u32[]{:S(2)}, u32[]{:S(2)}) collective-permute-start(bf16[2,32,2560]{2,1,0:T(8,128)(2,1)S(1)} %get-tuple-element.19), channel_id=1, source_target_pairs={{0,12},{4,0},{8,4},{12,8},{1,13},{5,1},{9,5},{13,9},{2,14},{6,2},{... | collective-permute-start | bytes 983048 | tf_op jit(solution)/shard_map/ppermute | solution.py:20
  119.5 13.9 %collective-permute-start.13 = (f32[2,224,256]{2,1,0:T(8,128)S(1)}, f32[2,224,256]{2,1,0:T(8,128)S(1)}, u32[]{:S(2)}, u32[]{:S(2)}) collective-permute-start(f32[2,224,256]{2,1,0:T(8,128)S(1)} %get-tuple-element.18.refs_0_), channel_id=1, source_target_pairs={{0,4},{4,8},{8,12},{12,0},{1,5},{5,9},{9,13},{13,1},{2,6},{6,10},{... | collective-permute-start | bytes 1376264 | tf_op jit(solution)/shard_map/ppermute | solution.py:20
  120.2 5.9 %collective-permute-start.15 = (f32[2,32,256]{2,1,0:T(8,128)S(1)}, f32[2,32,256]{2,1,0:T(8,128)S(1)}, u32[]{:S(2)}, u32[]{:S(2)}) collective-permute-start(f32[2,32,256]{2,1,0:T(8,128)S(1)} %correlate.11), channel_id=1, source_target_pairs={{0,2},{1,3},{2,0},{3,1},{4,6},{5,7},{6,4},{7,5},{8,10},{9,11},{10,... | collective-permute-start | bytes 196616 | tf_op jit(solution)/shard_map/ppermute | solution.py:152
  126.1 4.7 %collective-permute-start.18 = (f32[2,32,256]{2,1,0:T(8,128)S(1)}, f32[2,32,256]{2,1,0:T(8,128)S(1)}, u32[]{:S(2)}, u32[]{:S(2)}) collective-permute-start(f32[2,32,256]{2,1,0:T(8,128)S(1)} %add.35.refs_2_), channel_id=1, source_target_pairs={{0,5},{1,4},{2,7},{3,6},{4,9},{5,8},{6,11},{7,10},{8,13},{9,12},{1... | collective-permute-start | bytes 196616 | tf_op jit(solution)/shard_map/ppermute | solution.py:156
  127.1 4.3 %collective-permute-start.17 = (f32[2,32,256]{2,1,0:T(8,128)S(1)}, f32[2,32,256]{2,1,0:T(8,128)S(1)}, u32[]{:S(2)}, u32[]{:S(2)}) collective-permute-start(f32[2,32,256]{2,1,0:T(8,128)S(1)} %add.35.refs_2_), channel_id=1, source_target_pairs={{0,4},{4,8},{8,12},{12,0},{1,5},{5,9},{9,13},{13,1},{2,6},{6,10},{... | collective-permute-start | bytes 196616 | tf_op jit(solution)/shard_map/ppermute | solution.py:20
  128.5 5.0 %collective-permute-start.16 = (f32[2,32,256]{2,1,0:T(8,128)S(1)}, f32[2,32,256]{2,1,0:T(8,128)S(1)}, u32[]{:S(2)}, u32[]{:S(2)}) collective-permute-start(f32[2,32,256]{2,1,0:T(8,128)S(1)} %add.35.refs_2_), channel_id=1, source_target_pairs={{0,1},{1,0},{2,3},{3,2},{4,5},{5,4},{6,7},{7,6},{8,9},{9,8},{10,11... | collective-permute-start | bytes 196616 | tf_op jit(solution)/shard_map/ppermute | solution.py:154

commit v13 on v12

--- a/solution.py
+++ b/solution.py
@@ -8,7 +8,7 @@
 from jax.sharding import PartitionSpec as P
 
 PWB = 256
-SIXTEENTHS = (2, 6, 4, 2, 2)
+SIXTEENTHS = (2, 7, 3, 2, 2)
 MIB = 1 << 20
 PLACE_FLOPS = 1 << 36
 ANYWHERE = pl.BlockSpec(memory_space=pl.ANY)

time: 135 us -> 136 us (level)
  starting transfers between devices: 26.7 us -> 29.3 us
  waiting for transfers between devices: 78.8 us -> 76.5 us
    ppermute x8, starting transfers between devices: 12.9 us -> 15.4 us  [summed_over_pw(): lax.ppermute(partial, 'pw', [(i, i ^ distance) for i in range(pw)])]
    ppermute x8, starting transfers between devices: 8.57 us -> 6.28 us  [moved(): lax.ppermute(block, axis, [(i, (i + distance) % count) for i in range(cou...]
    ppermute x1, starting transfers between devices: 1.01 us -> 2.69 us  [sums_here_and_next(): lax.ppermute(partial, ('ka', 'pw'), across)]
  transfers between devices with their start and end apart: 19 -> 19, of which waited for: 14 -> 13; matrix products, arithmetic and copies ran while one was open for 0% -> 0% of each run, Pallas kernels for 20% -> 20%
where the time goes in v13:
time: 136 us
  waiting for transfers between devices  76.5 us (56%)
  Pallas kernels  29.8 us (22%)
  starting transfers between devices  29.3 us (22%)
    ppermute x8, waiting for transfers between devices, summed_over_pw(): lax.ppermute(partial, 'pw', [(i, i ^ distance) for i in range(pw)])  37.7 us
    ppermute x8, waiting for transfers between devices, moved(): lax.ppermute(block, axis, [(i, (i + distance) % count) for i in range(cou...  34.9 us
    ppermute x8, starting transfers between devices, summed_over_pw(): lax.ppermute(partial, 'pw', [(i, i ^ distance) for i in range(pw)])  15.4 us
    pallas_call x6, Pallas kernels, correlate(): pl.pallas_call(functools.partial(correlate_kernel, first, depth, begun is...  10.7 us
    pallas_call x1, Pallas kernels, placed_bands(): pl.pallas_call(place_kernel, grid=(width // step,), out_shape=pltpu.VMEM(...  9.35 us
    pallas_call x6, Pallas kernels, cut(): pl.pallas_call(functools.partial(cut_kernel, bands, waves), out_shape=jax...  8.71 us
    ppermute x8, starting transfers between devices, moved(): lax.ppermute(block, axis, [(i, (i + distance) % count) for i in range(cou...  6.28 us
    ppermute x1, starting transfers between devices, sums_here_and_next(): lax.ppermute(partial, 'pw', [(i, i ^ distance) for i in range(pw)])  3.41 us
  transfers between devices with their start and end apart: 19, of which 13 were waited for; matrix products, arithmetic and copies ran while one was open for 0% of the time, Pallas kernels for 20%

profile of v13, /device:TPU:0, one launch (start us, length us, event | category | flops | bytes accessed | tf_op | source)
XLA Modules:
  0.0 135.9 jit_solution(8186660956032228723)
XLA Ops:
  0.0 1.3 cut.6.refs_1_
  1.3 2.4 %collective-permute-start.2 = (bf16[2,32,10240]{2,1,0:T(8,128)(2,1)S(1)}, bf16[2,32,10240]{2,1,0:T(8,128)(2,1)S(1)}, u32[]{:S(2)}, u32[]{:S(2)}) collective-permute-start(bf16[2,32,10240]{2,1,0:T(8,128)(2,1)S(1)} %cut.6.refs_1_), channel_id=1, source_target_pairs={{0,12},{4,0},{8,4},{12,8},{1,13},{5,1},{9,5},{13,9},{2,14},{6,2},{... | collective-permute-start | bytes 3932168 | tf_op jit(solution)/shard_map/ppermute | solution.py:20
  3.7 2.4 %cut.7.refs_1_ = bf16[2,112,10240]{2,1,0:T(8,128)(2,1)S(1)} custom-call(bf16[1,2,256,10240]{3,2,1,0:T(8,128)(2,1)} %own_ref.1, bf16[2,32,10240]{2,1,0:T(8,128)(2,1)S(1)} %cut.6.refs_1_), custom_call_target="tpu_custom_call" | custom-call | bytes 1024 | tf_op jit(solution)/shard_map/cut/pallas_call | solution.py:37
  6.8 1.5 %cut.8.refs_1_ = bf16[2,48,10240]{2,1,0:T(8,128)(2,1)S(1)} custom-call(bf16[1,2,256,10240]{3,2,1,0:T(8,128)(2,1)} %own_ref.1, bf16[2,112,10240]{2,1,0:T(8,128)(2,1)S(1)} %cut.7.refs_1_), custom_call_target="tpu_custom_call" | custom-call | bytes 1024 | tf_op jit(solution)/shard_map/cut/pallas_call | solution.py:37
  8.4 1.3 cut.9.refs_1_
  12.0 9.3 %place.1.placed_ref = bf16[10240,512]{1,0:T(8,128)(2,1)S(1)} custom-call(bf16[1,2,256,10240]{3,2,1,0:T(8,128)(2,1)} %own_ref.1, s32[1,2,10240]{2,1,0:T(2,128)S(1)} %copy-done, bf16[2,32,2560]{2,1,0:T(8,128)(2,1)S(1)} %cut.11.refs_0_.refs_1_), custom_call_target="tpu_custom_call" | custom-call | flops 68719476736 | bytes 1024 | tf_op jit(solution)/shard_map/place/pallas_call | solution.py:69
  21.4 1.9 %correlate.6 = f32[2,32,256]{2,1,0:T(8,128)S(1)} custom-call(bf16[10240,512]{1,0:T(8,128)(2,1)S(1)} %place.1.placed_ref, bf16[2,32,10240]{2,1,0:T(8,128)(2,1)S(1)} %collective-permute-done.2.block_ref), custom_call_target="tpu_custom_call" | custom-call | bytes 1024 | tf_op jit(solution)/shard_map/correlate/pallas_call | solution.py:120
  23.3 2.7 %collective-permute-start.3 = (f32[2,32,256]{2,1,0:T(8,128)S(1)}, f32[2,32,256]{2,1,0:T(8,128)S(1)}, u32[]{:S(2)}, u32[]{:S(2)}) collective-permute-start(f32[2,32,256]{2,1,0:T(8,128)S(1)} %correlate.6), channel_id=1, source_target_pairs={{0,2},{1,3},{2,0},{3,1},{4,6},{5,7},{6,4},{7,5},{8,10},{9,11},{10,... | collective-permute-start | bytes 196616 | tf_op jit(solution)/shard_map/ppermute | solution.py:140
  25.9 4.2 %collective-permute-done.3 = f32[2,32,256]{2,1,0:T(8,128)S(1)} collective-permute-done((f32[2,32,256]{2,1,0:T(8,128)S(1)}, f32[2,32,256]{2,1,0:T(8,128)S(1)}, u32[]{:S(2)}, u32[]{:S(2)}) %collective-permute-start.3) | collective-permute-done | bytes 65568 | tf_op jit(solution)/shard_map/ppermute | solution.py:140
  30.9 3.6 %collective-permute-done.4 = f32[2,32,256]{2,1,0:T(8,128)S(1)} collective-permute-done((f32[2,32,256]{2,1,0:T(8,128)S(1)}, f32[2,32,256]{2,1,0:T(8,128)S(1)}, u32[]{:S(2)}, u32[]{:S(2)}) %collective-permute-start.4) | collective-permute-done | bytes 65568 | tf_op jit(solution)/shard_map/ppermute | solution.py:140
  34.5 33.5 %collective-permute-done.1.block_ref = bf16[2,112,10240]{2,1,0:T(8,128)(2,1)S(1)} collective-permute-done((bf16[2,112,10240]{2,1,0:T(8,128)(2,1)S(1)}, bf16[2,112,10240]{2,1,0:T(8,128)(2,1)S(1)}, u32[]{:S(2)}, u32[]{:S(2)}) %collective-permute-start.1) | collective-permute-done | bytes 4587552 | tf_op jit(solution)/shard_map/ppermute | solution.py:20
  68.0 3.0 %correlate.7 = (f32[2,112,256]{2,1,0:T(8,128)S(1)}, bf16[2,32,10240]{2,1,0:T(8,128)(2,1)S(1)}) custom-call(bf16[10240,512]{1,0:T(8,128)(2,1)S(1)} %place.1.placed_ref, bf16[2,112,10240]{2,1,0:T(8,128)(2,1)S(1)} %collective-permute-done.1.block_ref, f32[2,32,256]{2,1,0:T(8,128)S(1)} %add.28.refs_0_, ...), custom_call_target="tpu_custom_call", output_to_operand_aliasing={{1}: (3, {})} | custom-call | bytes 1024 | tf_op jit(solution)/shard_map/correlate/pallas_call | solution.py:120
  71.1 2.0 %collective-permute-start.10 = (bf16[2,32,10240]{2,1,0:T(8,128)(2,1)S(1)}, bf16[2,32,10240]{2,1,0:T(8,128)(2,1)S(1)}, u32[]{:S(2)}, u32[]{:S(2)}) collective-permute-start(bf16[2,32,10240]{2,1,0:T(8,128)(2,1)S(1)} %get-tuple-element.16), channel_id=1, source_target_pairs={{0,12},{4,0},{8,4},{12,8},{1,13},{5,1},{9,5},{13,9},{2,14},{6,2},{... | collective-permute-start | bytes 3932168 | tf_op jit(solution)/shard_map/ppermute | solution.py:20
  73.0 2.6 %collective-permute-start.5 = (f32[2,112,256]{2,1,0:T(8,128)S(1)}, f32[2,112,256]{2,1,0:T(8,128)S(1)}, u32[]{:S(2)}, u32[]{:S(2)}) collective-permute-start(f32[2,112,256]{2,1,0:T(8,128)S(1)} %get-tuple-element.13), channel_id=1, source_target_pairs={{0,2},{1,3},{2,0},{3,1},{4,6},{5,7},{6,4},{7,5},{8,10},{9,11},{10,... | collective-permute-start | bytes 688136 | tf_op jit(solution)/shard_map/ppermute | solution.py:140
  75.6 9.7 %collective-permute-done.5 = f32[2,112,256]{2,1,0:T(8,128)S(1)} collective-permute-done((f32[2,112,256]{2,1,0:T(8,128)S(1)}, f32[2,112,256]{2,1,0:T(8,128)S(1)}, u32[]{:S(2)}, u32[]{:S(2)}) %collective-permute-start.5) | collective-permute-done | bytes 229408 | tf_op jit(solution)/shard_map/ppermute | solution.py:140
  86.1 5.8 %collective-permute-done.6 = f32[2,112,256]{2,1,0:T(8,128)S(1)} collective-permute-done((f32[2,112,256]{2,1,0:T(8,128)S(1)}, f32[2,112,256]{2,1,0:T(8,128)S(1)}, u32[]{:S(2)}, u32[]{:S(2)}) %collective-permute-start.6) | collective-permute-done | bytes 229408 | tf_op jit(solution)/shard_map/ppermute | solution.py:140
  92.0 1.8 %correlate.8 = (f32[2,48,256]{2,1,0:T(8,128)S(1)}, bf16[2,32,7680]{2,1,0:T(8,128)(2,1)S(1)}) custom-call(bf16[10240,512]{1,0:T(8,128)(2,1)S(1)} %place.1.placed_ref, bf16[2,48,10240]{2,1,0:T(8,128)(2,1)S(1)} %collective-permute-done.block_ref, f32[2,112,256]{2,1,0:T(8,128)S(1)} %add.30.refs_0_, ...), custom_call_target="tpu_custom_call", output_to_operand_aliasing={{1}: (3, {})} | custom-call | bytes 1024 | tf_op jit(solution)/shard_map/correlate/pallas_call | solution.py:120
  93.9 3.9 %collective-permute-start.8 = (f32[2,48,256]{2,1,0:T(8,128)S(1)}, f32[2,48,256]{2,1,0:T(8,128)S(1)}, u32[]{:S(2)}, u32[]{:S(2)}) collective-permute-start(f32[2,48,256]{2,1,0:T(8,128)S(1)} %get-tuple-element.15), channel_id=1, source_target_pairs={{0,2},{1,3},{2,0},{3,1},{4,6},{5,7},{6,4},{7,5},{8,10},{9,11},{10,... | collective-permute-start | bytes 294920 | tf_op jit(solution)/shard_map/ppermute | solution.py:140
  97.8 5.0 %collective-permute-done.8 = f32[2,48,256]{2,1,0:T(8,128)S(1)} collective-permute-done((f32[2,48,256]{2,1,0:T(8,128)S(1)}, f32[2,48,256]{2,1,0:T(8,128)S(1)}, u32[]{:S(2)}, u32[]{:S(2)}) %collective-permute-start.8) | collective-permute-done | bytes 98336 | tf_op jit(solution)/shard_map/ppermute | solution.py:140
  103.6 3.9 %collective-permute-done.9 = f32[2,48,256]{2,1,0:T(8,128)S(1)} collective-permute-done((f32[2,48,256]{2,1,0:T(8,128)S(1)}, f32[2,48,256]{2,1,0:T(8,128)S(1)}, u32[]{:S(2)}, u32[]{:S(2)}) %collective-permute-start.9) | collective-permute-done | bytes 98336 | tf_op jit(solution)/shard_map/ppermute | solution.py:140
  107.5 1.9 %correlate.9 = (f32[2,32,256]{2,1,0:T(8,128)S(1)}, bf16[2,32,2560]{2,1,0:T(8,128)(2,1)S(1)}) custom-call(bf16[10240,512]{1,0:T(8,128)(2,1)S(1)} %place.1.placed_ref, bf16[2,32,10240]{2,1,0:T(8,128)(2,1)S(1)} %collective-permute-done.10.block_ref, f32[2,48,256]{2,1,0:T(8,128)S(1)} %add.32.refs_0_, ...), custom_call_target="tpu_custom_call", output_to_operand_aliasing={{1}: (3, {})} | custom-call | bytes 1024 | tf_op jit(solution)/shard_map/correlate/pallas_call | solution.py:120
  109.4 2.6 %collective-permute-start.11 = (f32[2,32,256]{2,1,0:T(8,128)S(1)}, f32[2,32,256]{2,1,0:T(8,128)S(1)}, u32[]{:S(2)}, u32[]{:S(2)}) collective-permute-start(f32[2,32,256]{2,1,0:T(8,128)S(1)} %get-tuple-element.17), channel_id=1, source_target_pairs={{0,2},{1,3},{2,0},{3,1},{4,6},{5,7},{6,4},{7,5},{8,10},{9,11},{10,... | collective-permute-start | bytes 196616 | tf_op jit(solution)/shard_map/ppermute | solution.py:140
  112.0 2.7 %collective-permute-done.11 = f32[2,32,256]{2,1,0:T(8,128)S(1)} collective-permute-done((f32[2,32,256]{2,1,0:T(8,128)S(1)}, f32[2,32,256]{2,1,0:T(8,128)S(1)}, u32[]{:S(2)}, u32[]{:S(2)}) %collective-permute-start.11) | collective-permute-done | bytes 65568 | tf_op jit(solution)/shard_map/ppermute | solution.py:140
  114.6 1.4 %collective-permute-start.12 = (f32[2,32,256]{2,1,0:T(8,128)S(1)}, f32[2,32,256]{2,1,0:T(8,128)S(1)}, u32[]{:S(2)}, u32[]{:S(2)}) collective-permute-start(f32[2,32,256]{2,1,0:T(8,128)S(1)} %add.33), channel_id=1, source_target_pairs={{0,1},{1,0},{2,3},{3,2},{4,5},{5,4},{6,7},{7,6},{8,9},{9,8},{10,11... | collective-permute-start | bytes 196616 | tf_op jit(solution)/shard_map/ppermute | solution.py:140
  116.0 2.9 %collective-permute-done.12 = f32[2,32,256]{2,1,0:T(8,128)S(1)} collective-permute-done((f32[2,32,256]{2,1,0:T(8,128)S(1)}, f32[2,32,256]{2,1,0:T(8,128)S(1)}, u32[]{:S(2)}, u32[]{:S(2)}) %collective-permute-start.12) | collective-permute-done | bytes 65568 | tf_op jit(solution)/shard_map/ppermute | solution.py:140
  119.0 1.5 %correlate.10 = (f32[2,32,256]{2,1,0:T(8,128)S(1)}, f32[2,224,256]{2,1,0:T(8,128)S(1)}) custom-call(bf16[10240,512]{1,0:T(8,128)(2,1)S(1)} %place.1.placed_ref, bf16[2,32,7680]{2,1,0:T(8,128)(2,1)S(1)} %collective-permute-done.7.block_ref, f32[2,224,256]{2,1,0:T(8,128)S(1)} %pad_maximum_fusion.refs_0_), custom_call_target="tpu_custom_call", output_to_operand_aliasing={{1}: (2, {})} | custom-call | bytes 1024 | tf_op jit(solution)/shard_map/correlate/pallas_call | solution.py:120
  121.2 3.4 %collective-permute-start.15 = (f32[2,32,256]{2,1,0:T(8,128)S(1)}, f32[2,32,256]{2,1,0:T(8,128)S(1)}, u32[]{:S(2)}, u32[]{:S(2)}) collective-permute-start(f32[2,32,256]{2,1,0:T(8,128)S(1)} %correlate.11), channel_id=1, source_target_pairs={{0,2},{1,3},{2,0},{3,1},{4,6},{5,7},{6,4},{7,5},{8,10},{9,11},{10,... | collective-permute-start | bytes 196616 | tf_op jit(solution)/shard_map/ppermute | solution.py:152
  124.6 2.2 %collective-permute-done.15 = f32[2,32,256]{2,1,0:T(8,128)S(1)} collective-permute-done((f32[2,32,256]{2,1,0:T(8,128)S(1)}, f32[2,32,256]{2,1,0:T(8,128)S(1)}, u32[]{:S(2)}, u32[]{:S(2)}) %collective-permute-start.15) | collective-permute-done | bytes 65568 | tf_op jit(solution)/shard_map/ppermute | solution.py:152
  126.9 2.7 %collective-permute-start.18 = (f32[2,32,256]{2,1,0:T(8,128)S(1)}, f32[2,32,256]{2,1,0:T(8,128)S(1)}, u32[]{:S(2)}, u32[]{:S(2)}) collective-permute-start(f32[2,32,256]{2,1,0:T(8,128)S(1)} %add.35.refs_2_), channel_id=1, source_target_pairs={{0,5},{1,4},{2,7},{3,6},{4,9},{5,8},{6,11},{7,10},{8,13},{9,12},{1... | collective-permute-start | bytes 196616 | tf_op jit(solution)/shard_map/ppermute | solution.py:156
  130.5 1.4 %collective-permute-start.16 = (f32[2,32,256]{2,1,0:T(8,128)S(1)}, f32[2,32,256]{2,1,0:T(8,128)S(1)}, u32[]{:S(2)}, u32[]{:S(2)}) collective-permute-start(f32[2,32,256]{2,1,0:T(8,128)S(1)} %add.35.refs_2_), channel_id=1, source_target_pairs={{0,1},{1,0},{2,3},{3,2},{4,5},{5,4},{6,7},{7,6},{8,9},{9,8},{10,11... | collective-permute-start | bytes 196616 | tf_op jit(solution)/shard_map/ppermute | solution.py:154
  132.0 1.3 collective-permute-done.17.refs_4_
  133.2 1.7 %collective-permute-done.16.refs_3_ = f32[2,32,256]{2,1,0:T(8,128)S(1)} collective-permute-done((f32[2,32,256]{2,1,0:T(8,128)S(1)}, f32[2,32,256]{2,1,0:T(8,128)S(1)}, u32[]{:S(2)}, u32[]{:S(2)}) %collective-permute-start.16) | collective-permute-done | bytes 65568 | tf_op jit(solution)/shard_map/ppermute | solution.py:154
  (32 shorter events, 8.3 us)
Async XLA Ops:
  1.3 20.1 %collective-permute-start.2 = (bf16[2,32,10240]{2,1,0:T(8,128)(2,1)S(1)}, bf16[2,32,10240]{2,1,0:T(8,128)(2,1)S(1)}, u32[]{:S(2)}, u32[]{:S(2)}) collective-permute-start(bf16[2,32,10240]{2,1,0:T(8,128)(2,1)S(1)} %cut.6.refs_1_), channel_id=1, source_target_pairs={{0,12},{4,0},{8,4},{12,8},{1,13},{5,1},{9,5},{13,9},{2,14},{6,2},{... | collective-permute-start | bytes 3932168 | tf_op jit(solution)/shard_map/ppermute | solution.py:20
  6.1 61.9 %collective-permute-start.1 = (bf16[2,112,10240]{2,1,0:T(8,128)(2,1)S(1)}, bf16[2,112,10240]{2,1,0:T(8,128)(2,1)S(1)}, u32[]{:S(2)}, u32[]{:S(2)}) collective-permute-start(bf16[2,112,10240]{2,1,0:T(8,128)(2,1)S(1)} %cut.7.refs_1_), channel_id=1, source_target_pairs={{0,12},{4,0},{8,4},{12,8},{1,13},{5,1},{9,5},{13,9},{2,14},{6,2},{... | collective-permute-start | bytes 13762568 | tf_op jit(solution)/shard_map/ppermute | solution.py:20
  8.3 83.6 %collective-permute-start = (bf16[2,48,10240]{2,1,0:T(8,128)(2,1)S(1)}, bf16[2,48,10240]{2,1,0:T(8,128)(2,1)S(1)}, u32[]{:S(2)}, u32[]{:S(2)}) collective-permute-start(bf16[2,48,10240]{2,1,0:T(8,128)(2,1)S(1)} %cut.8.refs_1_), channel_id=1, source_target_pairs={{0,12},{4,0},{8,4},{12,8},{1,13},{5,1},{9,5},{13,9},{2,14},{6,2},{... | collective-permute-start | bytes 5898248 | tf_op jit(solution)/shard_map/ppermute | solution.py:20
  10.9 1.1 copy-start
  23.3 6.8 %collective-permute-start.3 = (f32[2,32,256]{2,1,0:T(8,128)S(1)}, f32[2,32,256]{2,1,0:T(8,128)S(1)}, u32[]{:S(2)}, u32[]{:S(2)}) collective-permute-start(f32[2,32,256]{2,1,0:T(8,128)S(1)} %correlate.6), channel_id=1, source_target_pairs={{0,2},{1,3},{2,0},{3,1},{4,6},{5,7},{6,4},{7,5},{8,10},{9,11},{10,... | collective-permute-start | bytes 196616 | tf_op jit(solution)/shard_map/ppermute | solution.py:140
  30.1 4.3 %collective-permute-start.4 = (f32[2,32,256]{2,1,0:T(8,128)S(1)}, f32[2,32,256]{2,1,0:T(8,128)S(1)}, u32[]{:S(2)}, u32[]{:S(2)}) collective-permute-start(f32[2,32,256]{2,1,0:T(8,128)S(1)} %add.27), channel_id=1, source_target_pairs={{0,1},{1,0},{2,3},{3,2},{4,5},{5,4},{6,7},{7,6},{8,9},{9,8},{10,11... | collective-permute-start | bytes 196616 | tf_op jit(solution)/shard_map/ppermute | solution.py:140
  71.1 36.4 %collective-permute-start.10 = (bf16[2,32,10240]{2,1,0:T(8,128)(2,1)S(1)}, bf16[2,32,10240]{2,1,0:T(8,128)(2,1)S(1)}, u32[]{:S(2)}, u32[]{:S(2)}) collective-permute-start(bf16[2,32,10240]{2,1,0:T(8,128)(2,1)S(1)} %get-tuple-element.16), channel_id=1, source_target_pairs={{0,12},{4,0},{8,4},{12,8},{1,13},{5,1},{9,5},{13,9},{2,14},{6,2},{... | collective-permute-start | bytes 3932168 | tf_op jit(solution)/shard_map/ppermute | solution.py:20
  73.0 12.3 %collective-permute-start.5 = (f32[2,112,256]{2,1,0:T(8,128)S(1)}, f32[2,112,256]{2,1,0:T(8,128)S(1)}, u32[]{:S(2)}, u32[]{:S(2)}) collective-permute-start(f32[2,112,256]{2,1,0:T(8,128)S(1)} %get-tuple-element.13), channel_id=1, source_target_pairs={{0,2},{1,3},{2,0},{3,1},{4,6},{5,7},{6,4},{7,5},{8,10},{9,11},{10,... | collective-permute-start | bytes 688136 | tf_op jit(solution)/shard_map/ppermute | solution.py:140
  85.4 6.5 %collective-permute-start.6 = (f32[2,112,256]{2,1,0:T(8,128)S(1)}, f32[2,112,256]{2,1,0:T(8,128)S(1)}, u32[]{:S(2)}, u32[]{:S(2)}) collective-permute-start(f32[2,112,256]{2,1,0:T(8,128)S(1)} %add.29), channel_id=1, source_target_pairs={{0,1},{1,0},{2,3},{3,2},{4,5},{5,4},{6,7},{7,6},{8,9},{9,8},{10,11... | collective-permute-start | bytes 688136 | tf_op jit(solution)/shard_map/ppermute | solution.py:140
  93.8 25.2 %collective-permute-start.7 = (bf16[2,32,7680]{2,1,0:T(8,128)(2,1)S(1)}, bf16[2,32,7680]{2,1,0:T(8,128)(2,1)S(1)}, u32[]{:S(2)}, u32[]{:S(2)}) collective-permute-start(bf16[2,32,7680]{2,1,0:T(8,128)(2,1)S(1)} %get-tuple-element.14), channel_id=1, source_target_pairs={{0,12},{4,0},{8,4},{12,8},{1,13},{5,1},{9,5},{13,9},{2,14},{6,2},{... | collective-permute-start | bytes 2949128 | tf_op jit(solution)/shard_map/ppermute | solution.py:20
  93.9 8.9 %collective-permute-start.8 = (f32[2,48,256]{2,1,0:T(8,128)S(1)}, f32[2,48,256]{2,1,0:T(8,128)S(1)}, u32[]{:S(2)}, u32[]{:S(2)}) collective-permute-start(f32[2,48,256]{2,1,0:T(8,128)S(1)} %get-tuple-element.15), channel_id=1, source_target_pairs={{0,2},{1,3},{2,0},{3,1},{4,6},{5,7},{6,4},{7,5},{8,10},{9,11},{10,... | collective-permute-start | bytes 294920 | tf_op jit(solution)/shard_map/ppermute | solution.py:140
  102.8 4.7 %collective-permute-start.9 = (f32[2,48,256]{2,1,0:T(8,128)S(1)}, f32[2,48,256]{2,1,0:T(8,128)S(1)}, u32[]{:S(2)}, u32[]{:S(2)}) collective-permute-start(f32[2,48,256]{2,1,0:T(8,128)S(1)} %add.31), channel_id=1, source_target_pairs={{0,1},{1,0},{2,3},{3,2},{4,5},{5,4},{6,7},{7,6},{8,9},{9,8},{10,11... | collective-permute-start | bytes 294920 | tf_op jit(solution)/shard_map/ppermute | solution.py:140
  109.4 5.2 %collective-permute-start.11 = (f32[2,32,256]{2,1,0:T(8,128)S(1)}, f32[2,32,256]{2,1,0:T(8,128)S(1)}, u32[]{:S(2)}, u32[]{:S(2)}) collective-permute-start(f32[2,32,256]{2,1,0:T(8,128)S(1)} %get-tuple-element.17), channel_id=1, source_target_pairs={{0,2},{1,3},{2,0},{3,1},{4,6},{5,7},{6,4},{7,5},{8,10},{9,11},{10,... | collective-permute-start | bytes 196616 | tf_op jit(solution)/shard_map/ppermute | solution.py:140
  114.6 4.3 %collective-permute-start.12 = (f32[2,32,256]{2,1,0:T(8,128)S(1)}, f32[2,32,256]{2,1,0:T(8,128)S(1)}, u32[]{:S(2)}, u32[]{:S(2)}) collective-permute-start(f32[2,32,256]{2,1,0:T(8,128)S(1)} %add.33), channel_id=1, source_target_pairs={{0,1},{1,0},{2,3},{3,2},{4,5},{5,4},{6,7},{7,6},{8,9},{9,8},{10,11... | collective-permute-start | bytes 196616 | tf_op jit(solution)/shard_map/ppermute | solution.py:140
  116.0 4.6 %collective-permute-start.14 = (bf16[2,32,2560]{2,1,0:T(8,128)(2,1)S(1)}, bf16[2,32,2560]{2,1,0:T(8,128)(2,1)S(1)}, u32[]{:S(2)}, u32[]{:S(2)}) collective-permute-start(bf16[2,32,2560]{2,1,0:T(8,128)(2,1)S(1)} %get-tuple-element.19), channel_id=1, source_target_pairs={{0,12},{4,0},{8,4},{12,8},{1,13},{5,1},{9,5},{13,9},{2,14},{6,2},{... | collective-permute-start | bytes 983048 | tf_op jit(solution)/shard_map/ppermute | solution.py:20
  120.5 14.4 %collective-permute-start.13 = (f32[2,224,256]{2,1,0:T(8,128)S(1)}, f32[2,224,256]{2,1,0:T(8,128)S(1)}, u32[]{:S(2)}, u32[]{:S(2)}) collective-permute-start(f32[2,224,256]{2,1,0:T(8,128)S(1)} %get-tuple-element.18.refs_0_), channel_id=1, source_target_pairs={{0,4},{4,8},{8,12},{12,0},{1,5},{5,9},{9,13},{13,1},{2,6},{6,10},{... | collective-permute-start | bytes 1376264 | tf_op jit(solution)/shard_map/ppermute | solution.py:20
  121.2 5.7 %collective-permute-start.15 = (f32[2,32,256]{2,1,0:T(8,128)S(1)}, f32[2,32,256]{2,1,0:T(8,128)S(1)}, u32[]{:S(2)}, u32[]{:S(2)}) collective-permute-start(f32[2,32,256]{2,1,0:T(8,128)S(1)} %correlate.11), channel_id=1, source_target_pairs={{0,2},{1,3},{2,0},{3,1},{4,6},{5,7},{6,4},{7,5},{8,10},{9,11},{10,... | collective-permute-start | bytes 196616 | tf_op jit(solution)/shard_map/ppermute | solution.py:152
  126.9 5.1 %collective-permute-start.18 = (f32[2,32,256]{2,1,0:T(8,128)S(1)}, f32[2,32,256]{2,1,0:T(8,128)S(1)}, u32[]{:S(2)}, u32[]{:S(2)}) collective-permute-start(f32[2,32,256]{2,1,0:T(8,128)S(1)} %add.35.refs_2_), channel_id=1, source_target_pairs={{0,5},{1,4},{2,7},{3,6},{4,9},{5,8},{6,11},{7,10},{8,13},{9,12},{1... | collective-permute-start | bytes 196616 | tf_op jit(solution)/shard_map/ppermute | solution.py:156
  129.6 3.7 %collective-permute-start.17 = (f32[2,32,256]{2,1,0:T(8,128)S(1)}, f32[2,32,256]{2,1,0:T(8,128)S(1)}, u32[]{:S(2)}, u32[]{:S(2)}) collective-permute-start(f32[2,32,256]{2,1,0:T(8,128)S(1)} %add.35.refs_2_), channel_id=1, source_target_pairs={{0,4},{4,8},{8,12},{12,0},{1,5},{5,9},{9,13},{13,1},{2,6},{6,10},{... | collective-permute-start | bytes 196616 | tf_op jit(solution)/shard_map/ppermute | solution.py:20
  130.5 4.4 %collective-permute-start.16 = (f32[2,32,256]{2,1,0:T(8,128)S(1)}, f32[2,32,256]{2,1,0:T(8,128)S(1)}, u32[]{:S(2)}, u32[]{:S(2)}) collective-permute-start(f32[2,32,256]{2,1,0:T(8,128)S(1)} %add.35.refs_2_), channel_id=1, source_target_pairs={{0,1},{1,0},{2,3},{3,2},{4,5},{5,4},{6,7},{7,6},{8,9},{9,8},{10,11... | collective-permute-start | bytes 196616 | tf_op jit(solution)/shard_map/ppermute | solution.py:154

commit v14 on v13

--- a/solution.py
+++ b/solution.py
@@ -8,7 +8,7 @@
 from jax.sharding import PartitionSpec as P
 
 PWB = 256
-SIXTEENTHS = (2, 7, 3, 2, 2)
+SIXTEENTHS = (2, 5, 3, 2, 2, 2)
 MIB = 1 << 20
 PLACE_FLOPS = 1 << 36
 ANYWHERE = pl.BlockSpec(memory_space=pl.ANY)
@@ -207,7 +207,7 @@
         edges.append(edges[-1] + size * unit)
     late = width // PWB * 3 // 4 * PWB
     coefficients = pltpu.with_memory_space_constraint(coefficients, pltpu.HBM)
-    ranges = [(chunk, 0, width) for chunk in range(4)] + [(4, 0, late), (4, late, width)]
+    ranges = [(chunk, 0, width) for chunk in range(5)] + [(5, 0, late), (5, late, width)]
     blocks = []
     for chunk, low, high in ranges:
         some = slice(edges[chunk], edges[chunk + 1])
@@ -216,7 +216,7 @@
     placed = pltpu.with_memory_space_constraint(placed, pltpu.VMEM)
     arrived = [moved(block, "ka", -1) for block in blocks[:3]]
     whole = []
-    for chunk in range(4):
+    for chunk in range(5):
         waiting = blocks[2 + chunk : 3 + chunk] if chunk else []
         partial = correlate(placed, arrived[chunk], *whole[-1:], held=waiting)
         if waiting:
@@ -224,9 +224,9 @@
             arrived.append(moved(waiting, "ka", -1))
         whole.append(summed_over_pw(partial))
     most = jnp.concatenate(whole, axis=1)
-    last, most = correlate(placed, arrived[4], held=[most])
+    last, most = correlate(placed, arrived[5], held=[most])
     most_before = moved(most, "ka", 1)
-    last = correlate(placed, arrived[5], first=late, begun=last)
+    last = correlate(placed, arrived[6], first=late, begun=last)
     return assembled([most], [most_before], *sums_here_and_next(last))
 
 

time: 136 us -> 134 us (0.985)
  waiting for transfers between devices: 76.5 us -> 69.8 us
  starting transfers between devices: 29.3 us -> 32 us
  Pallas kernels: 29.8 us -> 31.3 us
    ppermute x8 -> x9, waiting for transfers between devices: 34.9 us -> 21.2 us  [moved(): lax.ppermute(block, axis, [(i, (i + distance) % count) for i in range(cou...]
    ppermute x8 -> x9, starting transfers between devices: 6.28 us -> 9.78 us  [moved(): lax.ppermute(block, axis, [(i, (i + distance) % count) for i in range(cou...]
    ppermute x8 -> x10, waiting for transfers between devices: 37.7 us -> 40.9 us  [summed_over_pw(): lax.ppermute(partial, 'pw', [(i, i ^ distance) for i in range(pw)])]
    ppermute x1, waiting for transfers between devices: 0.01 us -> 2.87 us  [sums_here_and_next(): lax.ppermute(partial, ('ka', 'pw'), across)]
    ppermute x1, starting transfers between devices: 2.69 us -> 0.19 us  [sums_here_and_next(): lax.ppermute(partial, ('ka', 'pw'), across)]
    ppermute x8 -> x10, starting transfers between devices: 15.4 us -> 17.3 us  [summed_over_pw(): lax.ppermute(partial, 'pw', [(i, i ^ distance) for i in range(pw)])]
    ppermute x1, waiting for transfers between devices: 2.25 us -> 4.07 us  [sums_here_and_next(): lax.ppermute(partial, 'pw', [(i, i ^ distance) for i in range(pw)])]
    pallas_call x6 -> x7, Pallas kernels: 8.71 us -> 9.61 us  [cut(): pl.pallas_call(functools.partial(cut_kernel, bands, waves), out_shape=jax...]
  transfers between devices with their start and end apart: 19 -> 22, of which waited for: 13 -> 17; matrix products, arithmetic and copies ran while one was open for 0% -> 0% of each run, Pallas kernels for 20% -> 22%
where the time goes in v14:
time: 134 us; the launch traced here: 133 us
  waiting for transfers between devices  69.8 us (52%)
  starting transfers between devices  32 us (24%)
  Pallas kernels  31.3 us (23%)
    ppermute x10, waiting for transfers between devices, summed_over_pw(): lax.ppermute(partial, 'pw', [(i, i ^ distance) for i in range(pw)])  40.9 us
    ppermute x9, waiting for transfers between devices, moved(): lax.ppermute(block, axis, [(i, (i + distance) % count) for i in range(cou...  21.2 us
    ppermute x10, starting transfers between devices, summed_over_pw(): lax.ppermute(partial, 'pw', [(i, i ^ distance) for i in range(pw)])  17.3 us
    pallas_call x7, Pallas kernels, correlate(): pl.pallas_call(functools.partial(correlate_kernel, first, depth, begun is...  11.4 us
    ppermute x9, starting transfers between devices, moved(): lax.ppermute(block, axis, [(i, (i + distance) % count) for i in range(cou...  9.78 us
    pallas_call x7, Pallas kernels, cut(): pl.pallas_call(functools.partial(cut_kernel, bands, waves), out_shape=jax...  9.61 us
    pallas_call x1, Pallas kernels, placed_bands(): pl.pallas_call(place_kernel, grid=(width // step,), out_shape=pltpu.VMEM(...  9.34 us
    ppermute x1, waiting for transfers between devices, sums_here_and_next(): lax.ppermute(partial, 'pw', [(i, i ^ distance) for i in range(pw)])  4.07 us
  transfers between devices with their start and end apart: 22, of which 17 were waited for; matrix products, arithmetic and copies ran while one was open for 0% of the time, Pallas kernels for 22%

profile of v14, /device:TPU:0, one launch (start us, length us, event | category | flops | bytes accessed | tf_op | source)
XLA Modules:
  0.0 133.5 jit_solution(7420074796531365808)
XLA Ops:
  1.3 2.4 %collective-permute-start.1 = (bf16[2,32,10240]{2,1,0:T(8,128)(2,1)S(1)}, bf16[2,32,10240]{2,1,0:T(8,128)(2,1)S(1)}, u32[]{:S(2)}, u32[]{:S(2)}) collective-permute-start(bf16[2,32,10240]{2,1,0:T(8,128)(2,1)S(1)} %cut.7.refs_1_), channel_id=1, source_target_pairs={{0,12},{4,0},{8,4},{12,8},{1,13},{5,1},{9,5},{13,9},{2,14},{6,2},{... | collective-permute-start | bytes 3932168 | tf_op jit(solution)/shard_map/ppermute | solution.py:20
  3.7 1.9 %cut.8.refs_1_ = bf16[2,80,10240]{2,1,0:T(8,128)(2,1)S(1)} custom-call(bf16[1,2,256,10240]{3,2,1,0:T(8,128)(2,1)} %own_ref.1, bf16[2,32,10240]{2,1,0:T(8,128)(2,1)S(1)} %cut.7.refs_1_), custom_call_target="tpu_custom_call" | custom-call | bytes 1024 | tf_op jit(solution)/shard_map/cut/pallas_call | solution.py:37
  6.4 1.5 %cut.9.refs_1_ = bf16[2,48,10240]{2,1,0:T(8,128)(2,1)S(1)} custom-call(bf16[1,2,256,10240]{3,2,1,0:T(8,128)(2,1)} %own_ref.1, bf16[2,80,10240]{2,1,0:T(8,128)(2,1)S(1)} %cut.8.refs_1_), custom_call_target="tpu_custom_call" | custom-call | bytes 1024 | tf_op jit(solution)/shard_map/cut/pallas_call | solution.py:37
  12.9 9.3 %place.1.placed_ref = bf16[10240,512]{1,0:T(8,128)(2,1)S(1)} custom-call(bf16[1,2,256,10240]{3,2,1,0:T(8,128)(2,1)} %own_ref.1, s32[1,2,10240]{2,1,0:T(2,128)S(1)} %copy-done, bf16[2,32,2560]{2,1,0:T(8,128)(2,1)S(1)} %cut.13.refs_0_.refs_1_), custom_call_target="tpu_custom_call" | custom-call | flops 68719476736 | bytes 1024 | tf_op jit(solution)/shard_map/place/pallas_call | solution.py:69
  22.3 1.9 %correlate.7 = f32[2,32,256]{2,1,0:T(8,128)S(1)} custom-call(bf16[10240,512]{1,0:T(8,128)(2,1)S(1)} %place.1.placed_ref, bf16[2,32,10240]{2,1,0:T(8,128)(2,1)S(1)} %collective-permute-done.1.block_ref), custom_call_target="tpu_custom_call" | custom-call | bytes 1024 | tf_op jit(solution)/shard_map/correlate/pallas_call | solution.py:120
  24.2 2.7 %collective-permute-start.2 = (f32[2,32,256]{2,1,0:T(8,128)S(1)}, f32[2,32,256]{2,1,0:T(8,128)S(1)}, u32[]{:S(2)}, u32[]{:S(2)}) collective-permute-start(f32[2,32,256]{2,1,0:T(8,128)S(1)} %correlate.7), channel_id=1, source_target_pairs={{0,2},{1,3},{2,0},{3,1},{4,6},{5,7},{6,4},{7,5},{8,10},{9,11},{10,... | collective-permute-start | bytes 196616 | tf_op jit(solution)/shard_map/ppermute | solution.py:140
  26.8 4.2 %collective-permute-done.2 = f32[2,32,256]{2,1,0:T(8,128)S(1)} collective-permute-done((f32[2,32,256]{2,1,0:T(8,128)S(1)}, f32[2,32,256]{2,1,0:T(8,128)S(1)}, u32[]{:S(2)}, u32[]{:S(2)}) %collective-permute-start.2) | collective-permute-done | bytes 65568 | tf_op jit(solution)/shard_map/ppermute | solution.py:140
  31.8 3.6 %collective-permute-done.3 = f32[2,32,256]{2,1,0:T(8,128)S(1)} collective-permute-done((f32[2,32,256]{2,1,0:T(8,128)S(1)}, f32[2,32,256]{2,1,0:T(8,128)S(1)}, u32[]{:S(2)}, u32[]{:S(2)}) %collective-permute-start.3) | collective-permute-done | bytes 65568 | tf_op jit(solution)/shard_map/ppermute | solution.py:140
  35.4 18.6 %collective-permute-done.block_ref = bf16[2,80,10240]{2,1,0:T(8,128)(2,1)S(1)} collective-permute-done((bf16[2,80,10240]{2,1,0:T(8,128)(2,1)S(1)}, bf16[2,80,10240]{2,1,0:T(8,128)(2,1)S(1)}, u32[]{:S(2)}, u32[]{:S(2)}) %collective-permute-start) | collective-permute-done | bytes 3276832 | tf_op jit(solution)/shard_map/ppermute | solution.py:20
  54.0 1.9 %correlate.8 = (f32[2,80,256]{2,1,0:T(8,128)S(1)}, bf16[2,32,10240]{2,1,0:T(8,128)(2,1)S(1)}) custom-call(bf16[10240,512]{1,0:T(8,128)(2,1)S(1)} %place.1.placed_ref, bf16[2,80,10240]{2,1,0:T(8,128)(2,1)S(1)} %collective-permute-done.block_ref, f32[2,32,256]{2,1,0:T(8,128)S(1)} %get-tuple-element.32.refs_0_, ...), custom_call_target="tpu_custom_call", output_to_operand_aliasing={{1}: (3, {})} | custom-call | bytes 1024 | tf_op jit(solution)/shard_map/correlate/pallas_call | solution.py:120
  55.8 2.0 %collective-permute-start.4 = (bf16[2,32,10240]{2,1,0:T(8,128)(2,1)S(1)}, bf16[2,32,10240]{2,1,0:T(8,128)(2,1)S(1)}, u32[]{:S(2)}, u32[]{:S(2)}) collective-permute-start(bf16[2,32,10240]{2,1,0:T(8,128)(2,1)S(1)} %get-tuple-element.15), channel_id=1, source_target_pairs={{0,12},{4,0},{8,4},{12,8},{1,13},{5,1},{9,5},{13,9},{2,14},{6,2},{... | collective-permute-start | bytes 3932168 | tf_op jit(solution)/shard_map/ppermute | solution.py:20
  57.8 2.6 %collective-permute-start.6 = (f32[2,80,256]{2,1,0:T(8,128)S(1)}, f32[2,80,256]{2,1,0:T(8,128)S(1)}, u32[]{:S(2)}, u32[]{:S(2)}) collective-permute-start(f32[2,80,256]{2,1,0:T(8,128)S(1)} %get-tuple-element.16), channel_id=1, source_target_pairs={{0,2},{1,3},{2,0},{3,1},{4,6},{5,7},{6,4},{7,5},{8,10},{9,11},{10,... | collective-permute-start | bytes 491528 | tf_op jit(solution)/shard_map/ppermute | solution.py:140
  60.4 6.9 %collective-permute-done.6 = f32[2,80,256]{2,1,0:T(8,128)S(1)} collective-permute-done((f32[2,80,256]{2,1,0:T(8,128)S(1)}, f32[2,80,256]{2,1,0:T(8,128)S(1)}, u32[]{:S(2)}, u32[]{:S(2)}) %collective-permute-start.6) | collective-permute-done | bytes 163872 | tf_op jit(solution)/shard_map/ppermute | solution.py:140
  68.1 4.6 %collective-permute-done.7 = f32[2,80,256]{2,1,0:T(8,128)S(1)} collective-permute-done((f32[2,80,256]{2,1,0:T(8,128)S(1)}, f32[2,80,256]{2,1,0:T(8,128)S(1)}, u32[]{:S(2)}, u32[]{:S(2)}) %collective-permute-start.7) | collective-permute-done | bytes 163872 | tf_op jit(solution)/shard_map/ppermute | solution.py:140
  72.8 2.3 %collective-permute-done.5.block_ref = bf16[2,48,10240]{2,1,0:T(8,128)(2,1)S(1)} collective-permute-done((bf16[2,48,10240]{2,1,0:T(8,128)(2,1)S(1)}, bf16[2,48,10240]{2,1,0:T(8,128)(2,1)S(1)}, u32[]{:S(2)}, u32[]{:S(2)}) %collective-permute-start.5) | collective-permute-done | bytes 1966112 | tf_op jit(solution)/shard_map/ppermute | solution.py:20
  75.0 1.8 %correlate.9 = (f32[2,48,256]{2,1,0:T(8,128)S(1)}, bf16[2,32,10240]{2,1,0:T(8,128)(2,1)S(1)}) custom-call(bf16[10240,512]{1,0:T(8,128)(2,1)S(1)} %place.1.placed_ref, bf16[2,48,10240]{2,1,0:T(8,128)(2,1)S(1)} %collective-permute-done.5.block_ref, f32[2,80,256]{2,1,0:T(8,128)S(1)} %get-tuple-element.30.refs_0_, ...), custom_call_target="tpu_custom_call", output_to_operand_aliasing={{1}: (3, {})} | custom-call | bytes 1024 | tf_op jit(solution)/shard_map/correlate/pallas_call | solution.py:120
  76.8 2.0 %collective-permute-start.13 = (bf16[2,32,10240]{2,1,0:T(8,128)(2,1)S(1)}, bf16[2,32,10240]{2,1,0:T(8,128)(2,1)S(1)}, u32[]{:S(2)}, u32[]{:S(2)}) collective-permute-start(bf16[2,32,10240]{2,1,0:T(8,128)(2,1)S(1)} %get-tuple-element.20), channel_id=1, source_target_pairs={{0,12},{4,0},{8,4},{12,8},{1,13},{5,1},{9,5},{13,9},{2,14},{6,2},{... | collective-permute-start | bytes 3932168 | tf_op jit(solution)/shard_map/ppermute | solution.py:20
  78.8 2.6 %collective-permute-start.8 = (f32[2,48,256]{2,1,0:T(8,128)S(1)}, f32[2,48,256]{2,1,0:T(8,128)S(1)}, u32[]{:S(2)}, u32[]{:S(2)}) collective-permute-start(f32[2,48,256]{2,1,0:T(8,128)S(1)} %get-tuple-element.17), channel_id=1, source_target_pairs={{0,2},{1,3},{2,0},{3,1},{4,6},{5,7},{6,4},{7,5},{8,10},{9,11},{10,... | collective-permute-start | bytes 294920 | tf_op jit(solution)/shard_map/ppermute | solution.py:140
  81.4 4.2 %collective-permute-done.8 = f32[2,48,256]{2,1,0:T(8,128)S(1)} collective-permute-done((f32[2,48,256]{2,1,0:T(8,128)S(1)}, f32[2,48,256]{2,1,0:T(8,128)S(1)}, u32[]{:S(2)}, u32[]{:S(2)}) %collective-permute-start.8) | collective-permute-done | bytes 98336 | tf_op jit(solution)/shard_map/ppermute | solution.py:140
  86.3 4.0 %collective-permute-done.9 = f32[2,48,256]{2,1,0:T(8,128)S(1)} collective-permute-done((f32[2,48,256]{2,1,0:T(8,128)S(1)}, f32[2,48,256]{2,1,0:T(8,128)S(1)}, u32[]{:S(2)}, u32[]{:S(2)}) %collective-permute-start.9) | collective-permute-done | bytes 98336 | tf_op jit(solution)/shard_map/ppermute | solution.py:140
  90.4 1.9 %correlate.10 = (f32[2,32,256]{2,1,0:T(8,128)S(1)}, bf16[2,32,7680]{2,1,0:T(8,128)(2,1)S(1)}) custom-call(bf16[10240,512]{1,0:T(8,128)(2,1)S(1)} %place.1.placed_ref, bf16[2,32,10240]{2,1,0:T(8,128)(2,1)S(1)} %collective-permute-done.4.block_ref, f32[2,48,256]{2,1,0:T(8,128)S(1)} %get-tuple-element.28.refs_0_, ...), custom_call_target="tpu_custom_call", output_to_operand_aliasing={{1}: (3, {})} | custom-call | bytes 1024 | tf_op jit(solution)/shard_map/correlate/pallas_call | solution.py:120
  93.2 2.5 %collective-permute-start.11 = (f32[2,32,256]{2,1,0:T(8,128)S(1)}, f32[2,32,256]{2,1,0:T(8,128)S(1)}, u32[]{:S(2)}, u32[]{:S(2)}) collective-permute-start(f32[2,32,256]{2,1,0:T(8,128)S(1)} %get-tuple-element.19), channel_id=1, source_target_pairs={{0,2},{1,3},{2,0},{3,1},{4,6},{5,7},{6,4},{7,5},{8,10},{9,11},{10,... | collective-permute-start | bytes 196616 | tf_op jit(solution)/shard_map/ppermute | solution.py:140
  95.8 2.7 %collective-permute-done.11 = f32[2,32,256]{2,1,0:T(8,128)S(1)} collective-permute-done((f32[2,32,256]{2,1,0:T(8,128)S(1)}, f32[2,32,256]{2,1,0:T(8,128)S(1)}, u32[]{:S(2)}, u32[]{:S(2)}) %collective-permute-start.11) | collective-permute-done | bytes 65568 | tf_op jit(solution)/shard_map/ppermute | solution.py:140
  99.8 3.0 %collective-permute-done.12 = f32[2,32,256]{2,1,0:T(8,128)S(1)} collective-permute-done((f32[2,32,256]{2,1,0:T(8,128)S(1)}, f32[2,32,256]{2,1,0:T(8,128)S(1)}, u32[]{:S(2)}, u32[]{:S(2)}) %collective-permute-start.12) | collective-permute-done | bytes 65568 | tf_op jit(solution)/shard_map/ppermute | solution.py:140
  103.1 1.9 %correlate.11 = (f32[2,32,256]{2,1,0:T(8,128)S(1)}, bf16[2,32,2560]{2,1,0:T(8,128)(2,1)S(1)}) custom-call(bf16[10240,512]{1,0:T(8,128)(2,1)S(1)} %place.1.placed_ref, bf16[2,32,10240]{2,1,0:T(8,128)(2,1)S(1)} %collective-permute-done.13.block_ref, f32[2,32,256]{2,1,0:T(8,128)S(1)} %get-tuple-element.26.refs_0_, ...), custom_call_target="tpu_custom_call", output_to_operand_aliasing={{1}: (3, {})} | custom-call | bytes 1024 | tf_op jit(solution)/shard_map/correlate/pallas_call | solution.py:120
  105.0 2.7 %collective-permute-start.14 = (f32[2,32,256]{2,1,0:T(8,128)S(1)}, f32[2,32,256]{2,1,0:T(8,128)S(1)}, u32[]{:S(2)}, u32[]{:S(2)}) collective-permute-start(f32[2,32,256]{2,1,0:T(8,128)S(1)} %get-tuple-element.21), channel_id=1, source_target_pairs={{0,2},{1,3},{2,0},{3,1},{4,6},{5,7},{6,4},{7,5},{8,10},{9,11},{10,... | collective-permute-start | bytes 196616 | tf_op jit(solution)/shard_map/ppermute | solution.py:140
  107.7 4.6 %collective-permute-done.14 = f32[2,32,256]{2,1,0:T(8,128)S(1)} collective-permute-done((f32[2,32,256]{2,1,0:T(8,128)S(1)}, f32[2,32,256]{2,1,0:T(8,128)S(1)}, u32[]{:S(2)}, u32[]{:S(2)}) %collective-permute-start.14) | collective-permute-done | bytes 65568 | tf_op jit(solution)/shard_map/ppermute | solution.py:140
  113.6 2.9 %collective-permute-done.15 = f32[2,32,256]{2,1,0:T(8,128)S(1)} collective-permute-done((f32[2,32,256]{2,1,0:T(8,128)S(1)}, f32[2,32,256]{2,1,0:T(8,128)S(1)}, u32[]{:S(2)}, u32[]{:S(2)}) %collective-permute-start.15) | collective-permute-done | bytes 65568 | tf_op jit(solution)/shard_map/ppermute | solution.py:140
  116.6 1.5 %correlate.12 = (f32[2,32,256]{2,1,0:T(8,128)S(1)}, f32[2,224,256]{2,1,0:T(8,128)S(1)}) custom-call(bf16[10240,512]{1,0:T(8,128)(2,1)S(1)} %place.1.placed_ref, bf16[2,32,7680]{2,1,0:T(8,128)(2,1)S(1)} %collective-permute-done.10.block_ref, f32[2,224,256]{2,1,0:T(8,128)S(1)} %add_dynamic-update-slice_fusion.refs_0_), custom_call_target="tpu_custom_call", output_to_operand_aliasing={{1}: (2, {})} | custom-call | bytes 1024 | tf_op jit(solution)/shard_map/correlate/pallas_call | solution.py:120
  118.8 3.4 %collective-permute-start.18 = (f32[2,32,256]{2,1,0:T(8,128)S(1)}, f32[2,32,256]{2,1,0:T(8,128)S(1)}, u32[]{:S(2)}, u32[]{:S(2)}) collective-permute-start(f32[2,32,256]{2,1,0:T(8,128)S(1)} %correlate.13), channel_id=1, source_target_pairs={{0,2},{1,3},{2,0},{3,1},{4,6},{5,7},{6,4},{7,5},{8,10},{9,11},{10,... | collective-permute-start | bytes 196616 | tf_op jit(solution)/shard_map/ppermute | solution.py:152
  122.3 4.1 %collective-permute-done.18 = f32[2,32,256]{2,1,0:T(8,128)S(1)} collective-permute-done((f32[2,32,256]{2,1,0:T(8,128)S(1)}, f32[2,32,256]{2,1,0:T(8,128)S(1)}, u32[]{:S(2)}, u32[]{:S(2)}) %collective-permute-start.18) | collective-permute-done | bytes 65568 | tf_op jit(solution)/shard_map/ppermute | solution.py:152
  128.8 2.9 %collective-permute-done.21.refs_5_ = f32[2,32,256]{2,1,0:T(8,128)S(1)} collective-permute-done((f32[2,32,256]{2,1,0:T(8,128)S(1)}, f32[2,32,256]{2,1,0:T(8,128)S(1)}, u32[]{:S(2)}, u32[]{:S(2)}) %collective-permute-start.21) | collective-permute-done | bytes 65568 | tf_op jit(solution)/shard_map/ppermute | solution.py:156
  (41 shorter events, 18.1 us)
Async XLA Ops:
  1.3 21.0 %collective-permute-start.1 = (bf16[2,32,10240]{2,1,0:T(8,128)(2,1)S(1)}, bf16[2,32,10240]{2,1,0:T(8,128)(2,1)S(1)}, u32[]{:S(2)}, u32[]{:S(2)}) collective-permute-start(bf16[2,32,10240]{2,1,0:T(8,128)(2,1)S(1)} %cut.7.refs_1_), channel_id=1, source_target_pairs={{0,12},{4,0},{8,4},{12,8},{1,13},{5,1},{9,5},{13,9},{2,14},{6,2},{... | collective-permute-start | bytes 3932168 | tf_op jit(solution)/shard_map/ppermute | solution.py:20
  5.7 48.3 %collective-permute-start = (bf16[2,80,10240]{2,1,0:T(8,128)(2,1)S(1)}, bf16[2,80,10240]{2,1,0:T(8,128)(2,1)S(1)}, u32[]{:S(2)}, u32[]{:S(2)}) collective-permute-start(bf16[2,80,10240]{2,1,0:T(8,128)(2,1)S(1)} %cut.8.refs_1_), channel_id=1, source_target_pairs={{0,12},{4,0},{8,4},{12,8},{1,13},{5,1},{9,5},{13,9},{2,14},{6,2},{... | collective-permute-start | bytes 9830408 | tf_op jit(solution)/shard_map/ppermute | solution.py:20
  7.9 67.1 %collective-permute-start.5 = (bf16[2,48,10240]{2,1,0:T(8,128)(2,1)S(1)}, bf16[2,48,10240]{2,1,0:T(8,128)(2,1)S(1)}, u32[]{:S(2)}, u32[]{:S(2)}) collective-permute-start(bf16[2,48,10240]{2,1,0:T(8,128)(2,1)S(1)} %cut.9.refs_1_), channel_id=1, source_target_pairs={{0,12},{4,0},{8,4},{12,8},{1,13},{5,1},{9,5},{13,9},{2,14},{6,2},{... | collective-permute-start | bytes 5898248 | tf_op jit(solution)/shard_map/ppermute | solution.py:20
  11.8 1.1 copy-start
  24.2 6.9 %collective-permute-start.2 = (f32[2,32,256]{2,1,0:T(8,128)S(1)}, f32[2,32,256]{2,1,0:T(8,128)S(1)}, u32[]{:S(2)}, u32[]{:S(2)}) collective-permute-start(f32[2,32,256]{2,1,0:T(8,128)S(1)} %correlate.7), channel_id=1, source_target_pairs={{0,2},{1,3},{2,0},{3,1},{4,6},{5,7},{6,4},{7,5},{8,10},{9,11},{10,... | collective-permute-start | bytes 196616 | tf_op jit(solution)/shard_map/ppermute | solution.py:140
  31.1 4.3 %collective-permute-start.3 = (f32[2,32,256]{2,1,0:T(8,128)S(1)}, f32[2,32,256]{2,1,0:T(8,128)S(1)}, u32[]{:S(2)}, u32[]{:S(2)}) collective-permute-start(f32[2,32,256]{2,1,0:T(8,128)S(1)} %add.33), channel_id=1, source_target_pairs={{0,1},{1,0},{2,3},{3,2},{4,5},{5,4},{6,7},{7,6},{8,9},{9,8},{10,11... | collective-permute-start | bytes 196616 | tf_op jit(solution)/shard_map/ppermute | solution.py:140
  55.8 34.5 %collective-permute-start.4 = (bf16[2,32,10240]{2,1,0:T(8,128)(2,1)S(1)}, bf16[2,32,10240]{2,1,0:T(8,128)(2,1)S(1)}, u32[]{:S(2)}, u32[]{:S(2)}) collective-permute-start(bf16[2,32,10240]{2,1,0:T(8,128)(2,1)S(1)} %get-tuple-element.15), channel_id=1, source_target_pairs={{0,12},{4,0},{8,4},{12,8},{1,13},{5,1},{9,5},{13,9},{2,14},{6,2},{... | collective-permute-start | bytes 3932168 | tf_op jit(solution)/shard_map/ppermute | solution.py:20
  57.8 9.5 %collective-permute-start.6 = (f32[2,80,256]{2,1,0:T(8,128)S(1)}, f32[2,80,256]{2,1,0:T(8,128)S(1)}, u32[]{:S(2)}, u32[]{:S(2)}) collective-permute-start(f32[2,80,256]{2,1,0:T(8,128)S(1)} %get-tuple-element.16), channel_id=1, source_target_pairs={{0,2},{1,3},{2,0},{3,1},{4,6},{5,7},{6,4},{7,5},{8,10},{9,11},{10,... | collective-permute-start | bytes 491528 | tf_op jit(solution)/shard_map/ppermute | solution.py:140
  67.4 5.4 %collective-permute-start.7 = (f32[2,80,256]{2,1,0:T(8,128)S(1)}, f32[2,80,256]{2,1,0:T(8,128)S(1)}, u32[]{:S(2)}, u32[]{:S(2)}) collective-permute-start(f32[2,80,256]{2,1,0:T(8,128)S(1)} %add.35), channel_id=1, source_target_pairs={{0,1},{1,0},{2,3},{3,2},{4,5},{5,4},{6,7},{7,6},{8,9},{9,8},{10,11... | collective-permute-start | bytes 491528 | tf_op jit(solution)/shard_map/ppermute | solution.py:140
  76.8 26.3 %collective-permute-start.13 = (bf16[2,32,10240]{2,1,0:T(8,128)(2,1)S(1)}, bf16[2,32,10240]{2,1,0:T(8,128)(2,1)S(1)}, u32[]{:S(2)}, u32[]{:S(2)}) collective-permute-start(bf16[2,32,10240]{2,1,0:T(8,128)(2,1)S(1)} %get-tuple-element.20), channel_id=1, source_target_pairs={{0,12},{4,0},{8,4},{12,8},{1,13},{5,1},{9,5},{13,9},{2,14},{6,2},{... | collective-permute-start | bytes 3932168 | tf_op jit(solution)/shard_map/ppermute | solution.py:20
  78.8 6.9 %collective-permute-start.8 = (f32[2,48,256]{2,1,0:T(8,128)S(1)}, f32[2,48,256]{2,1,0:T(8,128)S(1)}, u32[]{:S(2)}, u32[]{:S(2)}) collective-permute-start(f32[2,48,256]{2,1,0:T(8,128)S(1)} %get-tuple-element.17), channel_id=1, source_target_pairs={{0,2},{1,3},{2,0},{3,1},{4,6},{5,7},{6,4},{7,5},{8,10},{9,11},{10,... | collective-permute-start | bytes 294920 | tf_op jit(solution)/shard_map/ppermute | solution.py:140
  85.7 4.7 %collective-permute-start.9 = (f32[2,48,256]{2,1,0:T(8,128)S(1)}, f32[2,48,256]{2,1,0:T(8,128)S(1)}, u32[]{:S(2)}, u32[]{:S(2)}) collective-permute-start(f32[2,48,256]{2,1,0:T(8,128)S(1)} %add.37), channel_id=1, source_target_pairs={{0,1},{1,0},{2,3},{3,2},{4,5},{5,4},{6,7},{7,6},{8,9},{9,8},{10,11... | collective-permute-start | bytes 294920 | tf_op jit(solution)/shard_map/ppermute | solution.py:140
  92.3 24.3 %collective-permute-start.10 = (bf16[2,32,7680]{2,1,0:T(8,128)(2,1)S(1)}, bf16[2,32,7680]{2,1,0:T(8,128)(2,1)S(1)}, u32[]{:S(2)}, u32[]{:S(2)}) collective-permute-start(bf16[2,32,7680]{2,1,0:T(8,128)(2,1)S(1)} %get-tuple-element.18), channel_id=1, source_target_pairs={{0,12},{4,0},{8,4},{12,8},{1,13},{5,1},{9,5},{13,9},{2,14},{6,2},{... | collective-permute-start | bytes 2949128 | tf_op jit(solution)/shard_map/ppermute | solution.py:20
  93.2 5.2 %collective-permute-start.11 = (f32[2,32,256]{2,1,0:T(8,128)S(1)}, f32[2,32,256]{2,1,0:T(8,128)S(1)}, u32[]{:S(2)}, u32[]{:S(2)}) collective-permute-start(f32[2,32,256]{2,1,0:T(8,128)S(1)} %get-tuple-element.19), channel_id=1, source_target_pairs={{0,2},{1,3},{2,0},{3,1},{4,6},{5,7},{6,4},{7,5},{8,10},{9,11},{10,... | collective-permute-start | bytes 196616 | tf_op jit(solution)/shard_map/ppermute | solution.py:140
  98.5 4.3 %collective-permute-start.12 = (f32[2,32,256]{2,1,0:T(8,128)S(1)}, f32[2,32,256]{2,1,0:T(8,128)S(1)}, u32[]{:S(2)}, u32[]{:S(2)}) collective-permute-start(f32[2,32,256]{2,1,0:T(8,128)S(1)} %add.39), channel_id=1, source_target_pairs={{0,1},{1,0},{2,3},{3,2},{4,5},{5,4},{6,7},{7,6},{8,9},{9,8},{10,11... | collective-permute-start | bytes 196616 | tf_op jit(solution)/shard_map/ppermute | solution.py:140
  105.0 7.2 %collective-permute-start.14 = (f32[2,32,256]{2,1,0:T(8,128)S(1)}, f32[2,32,256]{2,1,0:T(8,128)S(1)}, u32[]{:S(2)}, u32[]{:S(2)}) collective-permute-start(f32[2,32,256]{2,1,0:T(8,128)S(1)} %get-tuple-element.21), channel_id=1, source_target_pairs={{0,2},{1,3},{2,0},{3,1},{4,6},{5,7},{6,4},{7,5},{8,10},{9,11},{10,... | collective-permute-start | bytes 196616 | tf_op jit(solution)/shard_map/ppermute | solution.py:140
  112.3 4.3 %collective-permute-start.15 = (f32[2,32,256]{2,1,0:T(8,128)S(1)}, f32[2,32,256]{2,1,0:T(8,128)S(1)}, u32[]{:S(2)}, u32[]{:S(2)}) collective-permute-start(f32[2,32,256]{2,1,0:T(8,128)S(1)} %add.41), channel_id=1, source_target_pairs={{0,1},{1,0},{2,3},{3,2},{4,5},{5,4},{6,7},{7,6},{8,9},{9,8},{10,11... | collective-permute-start | bytes 196616 | tf_op jit(solution)/shard_map/ppermute | solution.py:140
  113.0 5.2 %collective-permute-start.17 = (bf16[2,32,2560]{2,1,0:T(8,128)(2,1)S(1)}, bf16[2,32,2560]{2,1,0:T(8,128)(2,1)S(1)}, u32[]{:S(2)}, u32[]{:S(2)}) collective-permute-start(bf16[2,32,2560]{2,1,0:T(8,128)(2,1)S(1)} %get-tuple-element.23), channel_id=1, source_target_pairs={{0,12},{4,0},{8,4},{12,8},{1,13},{5,1},{9,5},{13,9},{2,14},{6,2},{... | collective-permute-start | bytes 983048 | tf_op jit(solution)/shard_map/ppermute | solution.py:20
  118.1 14.4 %collective-permute-start.16 = (f32[2,224,256]{2,1,0:T(8,128)S(1)}, f32[2,224,256]{2,1,0:T(8,128)S(1)}, u32[]{:S(2)}, u32[]{:S(2)}) collective-permute-start(f32[2,224,256]{2,1,0:T(8,128)S(1)} %get-tuple-element.22.refs_0_), channel_id=1, source_target_pairs={{0,4},{4,8},{8,12},{12,0},{1,5},{5,9},{9,13},{13,1},{2,6},{6,10},{... | collective-permute-start | bytes 1376264 | tf_op jit(solution)/shard_map/ppermute | solution.py:20
  118.8 7.5 %collective-permute-start.18 = (f32[2,32,256]{2,1,0:T(8,128)S(1)}, f32[2,32,256]{2,1,0:T(8,128)S(1)}, u32[]{:S(2)}, u32[]{:S(2)}) collective-permute-start(f32[2,32,256]{2,1,0:T(8,128)S(1)} %correlate.13), channel_id=1, source_target_pairs={{0,2},{1,3},{2,0},{3,1},{4,6},{5,7},{6,4},{7,5},{8,10},{9,11},{10,... | collective-permute-start | bytes 196616 | tf_op jit(solution)/shard_map/ppermute | solution.py:152
  126.3 5.3 %collective-permute-start.21 = (f32[2,32,256]{2,1,0:T(8,128)S(1)}, f32[2,32,256]{2,1,0:T(8,128)S(1)}, u32[]{:S(2)}, u32[]{:S(2)}) collective-permute-start(f32[2,32,256]{2,1,0:T(8,128)S(1)} %add.43.refs_2_), channel_id=1, source_target_pairs={{0,5},{1,4},{2,7},{3,6},{4,9},{5,8},{6,11},{7,10},{8,13},{9,12},{1... | collective-permute-start | bytes 196616 | tf_op jit(solution)/shard_map/ppermute | solution.py:156
  126.5 5.1 %collective-permute-start.20 = (f32[2,32,256]{2,1,0:T(8,128)S(1)}, f32[2,32,256]{2,1,0:T(8,128)S(1)}, u32[]{:S(2)}, u32[]{:S(2)}) collective-permute-start(f32[2,32,256]{2,1,0:T(8,128)S(1)} %add.43.refs_2_), channel_id=1, source_target_pairs={{0,4},{4,8},{8,12},{12,0},{1,5},{5,9},{9,13},{13,1},{2,6},{6,10},{... | collective-permute-start | bytes 196616 | tf_op jit(solution)/shard_map/ppermute | solution.py:20
  127.5 4.9 %collective-permute-start.19 = (f32[2,32,256]{2,1,0:T(8,128)S(1)}, f32[2,32,256]{2,1,0:T(8,128)S(1)}, u32[]{:S(2)}, u32[]{:S(2)}) collective-permute-start(f32[2,32,256]{2,1,0:T(8,128)S(1)} %add.43.refs_2_), channel_id=1, source_target_pairs={{0,1},{1,0},{2,3},{3,2},{4,5},{5,4},{6,7},{7,6},{8,9},{9,8},{10,11... | collective-permute-start | bytes 196616 | tf_op jit(solution)/shard_map/ppermute | solution.py:154

commit v15 on v14

--- a/solution.py
+++ b/solution.py
@@ -8,7 +8,7 @@
 from jax.sharding import PartitionSpec as P
 
 PWB = 256
-SIXTEENTHS = (2, 5, 3, 2, 2, 2)
+SIXTEENTHS = (1, 6, 3, 2, 2, 2)
 MIB = 1 << 20
 PLACE_FLOPS = 1 << 36
 ANYWHERE = pl.BlockSpec(memory_space=pl.ANY)
@@ -217,11 +217,11 @@
     arrived = [moved(block, "ka", -1) for block in blocks[:3]]
     whole = []
     for chunk in range(5):
-        waiting = blocks[2 + chunk : 3 + chunk] if chunk else []
+        waiting = [[], blocks[3:4], blocks[4:5], blocks[5:7], []][chunk]
         partial = correlate(placed, arrived[chunk], *whole[-1:], held=waiting)
         if waiting:
-            partial, waiting = partial
-            arrived.append(moved(waiting, "ka", -1))
+            partial, *waiting = partial
+            arrived.extend(moved(block, "ka", -1) for block in waiting)
         whole.append(summed_over_pw(partial))
     most = jnp.concatenate(whole, axis=1)
     last, most = correlate(placed, arrived[5], held=[most])

time: 134 us -> 134 us (level)
  starting transfers between devices: 32 us -> 29 us
  waiting for transfers between devices: 69.8 us -> 72.2 us
    ppermute x10, waiting for transfers between devices: 40.9 us -> 43.6 us  [summed_over_pw(): lax.ppermute(partial, 'pw', [(i, i ^ distance) for i in range(pw)])]
    ppermute x9, starting transfers between devices: 9.78 us -> 8.18 us  [moved(): lax.ppermute(block, axis, [(i, (i + distance) % count) for i in range(cou...]
  transfers between devices with their start and end apart: 22 -> 22, of which waited for: 17 -> 14; matrix products, arithmetic and copies ran while one was open for 0% -> 0% of each run, Pallas kernels for 22% -> 22%
where the time goes in v15:
time: 134 us; the launch traced here: 133 us
  waiting for transfers between devices  72.2 us (54%)
  Pallas kernels  31.7 us (24%)
  starting transfers between devices  29 us (22%)
    ppermute x10, waiting for transfers between devices, summed_over_pw(): lax.ppermute(partial, 'pw', [(i, i ^ distance) for i in range(pw)])  43.6 us
    ppermute x9, waiting for transfers between devices, moved(): lax.ppermute(block, axis, [(i, (i + distance) % count) for i in range(cou...  20.9 us
    ppermute x10, starting transfers between devices, summed_over_pw(): lax.ppermute(partial, 'pw', [(i, i ^ distance) for i in range(pw)])  16 us
    pallas_call x7, Pallas kernels, correlate(): pl.pallas_call(functools.partial(correlate_kernel, first, depth, begun is...  11.7 us
    pallas_call x7, Pallas kernels, cut(): pl.pallas_call(functools.partial(cut_kernel, bands, waves), out_shape=jax...  9.61 us
    pallas_call x1, Pallas kernels, placed_bands(): pl.pallas_call(place_kernel, grid=(width // step,), out_shape=pltpu.VMEM(...  9.34 us
    ppermute x9, starting transfers between devices, moved(): lax.ppermute(block, axis, [(i, (i + distance) % count) for i in range(cou...  8.18 us
    ppermute x1, waiting for transfers between devices, sums_here_and_next(): lax.ppermute(partial, 'pw', [(i, i ^ distance) for i in range(pw)])  4.07 us
  transfers between devices with their start and end apart: 22, of which 14 were waited for; matrix products, arithmetic and copies ran while one was open for 0% of the time, Pallas kernels for 22%

profile of v15, /device:TPU:0, one launch (start us, length us, event | category | flops | bytes accessed | tf_op | source)
XLA Modules:
  0.0 133.3 jit_solution(10326842021206680415)
XLA Ops:
  1.1 2.4 %collective-permute-start.1 = (bf16[2,16,10240]{2,1,0:T(8,128)(2,1)S(1)}, bf16[2,16,10240]{2,1,0:T(8,128)(2,1)S(1)}, u32[]{:S(2)}, u32[]{:S(2)}) collective-permute-start(bf16[2,16,10240]{2,1,0:T(8,128)(2,1)S(1)} %cut.7.refs_1_), channel_id=1, source_target_pairs={{0,12},{4,0},{8,4},{12,8},{1,13},{5,1},{9,5},{13,9},{2,14},{6,2},{... | collective-permute-start | bytes 1966088 | tf_op jit(solution)/shard_map/ppermute | solution.py:20
  3.5 2.2 %cut.8.refs_1_ = bf16[2,96,10240]{2,1,0:T(8,128)(2,1)S(1)} custom-call(bf16[1,2,256,10240]{3,2,1,0:T(8,128)(2,1)} %own_ref.1, bf16[2,16,10240]{2,1,0:T(8,128)(2,1)S(1)} %cut.7.refs_1_), custom_call_target="tpu_custom_call" | custom-call | bytes 1024 | tf_op jit(solution)/shard_map/cut/pallas_call | solution.py:37
  6.4 1.5 %cut.9.refs_1_ = bf16[2,48,10240]{2,1,0:T(8,128)(2,1)S(1)} custom-call(bf16[1,2,256,10240]{3,2,1,0:T(8,128)(2,1)} %own_ref.1, bf16[2,96,10240]{2,1,0:T(8,128)(2,1)S(1)} %cut.8.refs_1_), custom_call_target="tpu_custom_call" | custom-call | bytes 1024 | tf_op jit(solution)/shard_map/cut/pallas_call | solution.py:37
  9.3 1.3 cut.11.refs_1_
  12.9 9.3 %place.1.placed_ref = bf16[10240,512]{1,0:T(8,128)(2,1)S(1)} custom-call(bf16[1,2,256,10240]{3,2,1,0:T(8,128)(2,1)} %own_ref.1, s32[1,2,10240]{2,1,0:T(2,128)S(1)} %copy-done, bf16[2,32,2560]{2,1,0:T(8,128)(2,1)S(1)} %cut.13.refs_0_.refs_2_), custom_call_target="tpu_custom_call" | custom-call | flops 68719476736 | bytes 1024 | tf_op jit(solution)/shard_map/place/pallas_call | solution.py:69
  22.3 1.9 %correlate.7 = f32[2,16,256]{2,1,0:T(8,128)S(1)} custom-call(bf16[10240,512]{1,0:T(8,128)(2,1)S(1)} %place.1.placed_ref, bf16[2,16,10240]{2,1,0:T(8,128)(2,1)S(1)} %collective-permute-done.1.block_ref), custom_call_target="tpu_custom_call" | custom-call | bytes 1024 | tf_op jit(solution)/shard_map/correlate/pallas_call | solution.py:120
  24.1 2.6 %collective-permute-start.2 = (f32[2,16,256]{2,1,0:T(8,128)S(1)}, f32[2,16,256]{2,1,0:T(8,128)S(1)}, u32[]{:S(2)}, u32[]{:S(2)}) collective-permute-start(f32[2,16,256]{2,1,0:T(8,128)S(1)} %correlate.7), channel_id=1, source_target_pairs={{0,2},{1,3},{2,0},{3,1},{4,6},{5,7},{6,4},{7,5},{8,10},{9,11},{10,... | collective-permute-start | bytes 98312 | tf_op jit(solution)/shard_map/ppermute | solution.py:140
  26.8 2.2 %collective-permute-done.2 = f32[2,16,256]{2,1,0:T(8,128)S(1)} collective-permute-done((f32[2,16,256]{2,1,0:T(8,128)S(1)}, f32[2,16,256]{2,1,0:T(8,128)S(1)}, u32[]{:S(2)}, u32[]{:S(2)}) %collective-permute-start.2) | collective-permute-done | bytes 32800 | tf_op jit(solution)/shard_map/ppermute | solution.py:140
  29.0 1.6 %collective-permute-start.3 = (f32[2,16,256]{2,1,0:T(8,128)S(1)}, f32[2,16,256]{2,1,0:T(8,128)S(1)}, u32[]{:S(2)}, u32[]{:S(2)}) collective-permute-start(f32[2,16,256]{2,1,0:T(8,128)S(1)} %add.33), channel_id=1, source_target_pairs={{0,1},{1,0},{2,3},{3,2},{4,5},{5,4},{6,7},{7,6},{8,9},{9,8},{10,11... | collective-permute-start | bytes 98312 | tf_op jit(solution)/shard_map/ppermute | solution.py:140
  30.6 2.3 %collective-permute-done.3 = f32[2,16,256]{2,1,0:T(8,128)S(1)} collective-permute-done((f32[2,16,256]{2,1,0:T(8,128)S(1)}, f32[2,16,256]{2,1,0:T(8,128)S(1)}, u32[]{:S(2)}, u32[]{:S(2)}) %collective-permute-start.3) | collective-permute-done | bytes 32800 | tf_op jit(solution)/shard_map/ppermute | solution.py:140
  32.9 20.9 %collective-permute-done.block_ref = bf16[2,96,10240]{2,1,0:T(8,128)(2,1)S(1)} collective-permute-done((bf16[2,96,10240]{2,1,0:T(8,128)(2,1)S(1)}, bf16[2,96,10240]{2,1,0:T(8,128)(2,1)S(1)}, u32[]{:S(2)}, u32[]{:S(2)}) %collective-permute-start) | collective-permute-done | bytes 3932192 | tf_op jit(solution)/shard_map/ppermute | solution.py:20
  53.8 2.2 %correlate.8 = (f32[2,96,256]{2,1,0:T(8,128)S(1)}, bf16[2,32,10240]{2,1,0:T(8,128)(2,1)S(1)}) custom-call(bf16[10240,512]{1,0:T(8,128)(2,1)S(1)} %place.1.placed_ref, bf16[2,96,10240]{2,1,0:T(8,128)(2,1)S(1)} %collective-permute-done.block_ref, f32[2,16,256]{2,1,0:T(8,128)S(1)} %get-tuple-element.30.refs_0_, ...), custom_call_target="tpu_custom_call", output_to_operand_aliasing={{1}: (3, {})} | custom-call | bytes 1024 | tf_op jit(solution)/shard_map/correlate/pallas_call | solution.py:120
  56.0 2.7 %collective-permute-start.6 = (f32[2,96,256]{2,1,0:T(8,128)S(1)}, f32[2,96,256]{2,1,0:T(8,128)S(1)}, u32[]{:S(2)}, u32[]{:S(2)}) collective-permute-start(f32[2,96,256]{2,1,0:T(8,128)S(1)} %get-tuple-element.15), channel_id=1, source_target_pairs={{0,2},{1,3},{2,0},{3,1},{4,6},{5,7},{6,4},{7,5},{8,10},{9,11},{10,... | collective-permute-start | bytes 589832 | tf_op jit(solution)/shard_map/ppermute | solution.py:140
  58.6 1.6 %collective-permute-start.4 = (bf16[2,32,10240]{2,1,0:T(8,128)(2,1)S(1)}, bf16[2,32,10240]{2,1,0:T(8,128)(2,1)S(1)}, u32[]{:S(2)}, u32[]{:S(2)}) collective-permute-start(bf16[2,32,10240]{2,1,0:T(8,128)(2,1)S(1)} %get-tuple-element.14), channel_id=1, source_target_pairs={{0,12},{4,0},{8,4},{12,8},{1,13},{5,1},{9,5},{13,9},{2,14},{6,2},{... | collective-permute-start | bytes 3932168 | tf_op jit(solution)/shard_map/ppermute | solution.py:20
  60.2 8.5 %collective-permute-done.6 = f32[2,96,256]{2,1,0:T(8,128)S(1)} collective-permute-done((f32[2,96,256]{2,1,0:T(8,128)S(1)}, f32[2,96,256]{2,1,0:T(8,128)S(1)}, u32[]{:S(2)}, u32[]{:S(2)}) %collective-permute-start.6) | collective-permute-done | bytes 196640 | tf_op jit(solution)/shard_map/ppermute | solution.py:140
  69.6 6.1 %collective-permute-done.7 = f32[2,96,256]{2,1,0:T(8,128)S(1)} collective-permute-done((f32[2,96,256]{2,1,0:T(8,128)S(1)}, f32[2,96,256]{2,1,0:T(8,128)S(1)}, u32[]{:S(2)}, u32[]{:S(2)}) %collective-permute-start.7) | collective-permute-done | bytes 196640 | tf_op jit(solution)/shard_map/ppermute | solution.py:140
  75.7 1.8 %correlate.9 = (f32[2,48,256]{2,1,0:T(8,128)S(1)}, bf16[2,32,10240]{2,1,0:T(8,128)(2,1)S(1)}) custom-call(bf16[10240,512]{1,0:T(8,128)(2,1)S(1)} %place.1.placed_ref, bf16[2,48,10240]{2,1,0:T(8,128)(2,1)S(1)} %collective-permute-done.5.block_ref, f32[2,96,256]{2,1,0:T(8,128)S(1)} %get-tuple-element.28.refs_0_, ...), custom_call_target="tpu_custom_call", output_to_operand_aliasing={{1}: (3, {})} | custom-call | bytes 1024 | tf_op jit(solution)/shard_map/correlate/pallas_call | solution.py:120
  78.6 2.6 %collective-permute-start.8 = (f32[2,48,256]{2,1,0:T(8,128)S(1)}, f32[2,48,256]{2,1,0:T(8,128)S(1)}, u32[]{:S(2)}, u32[]{:S(2)}) collective-permute-start(f32[2,48,256]{2,1,0:T(8,128)S(1)} %get-tuple-element.16), channel_id=1, source_target_pairs={{0,2},{1,3},{2,0},{3,1},{4,6},{5,7},{6,4},{7,5},{8,10},{9,11},{10,... | collective-permute-start | bytes 294920 | tf_op jit(solution)/shard_map/ppermute | solution.py:140
  81.2 4.6 %collective-permute-done.8 = f32[2,48,256]{2,1,0:T(8,128)S(1)} collective-permute-done((f32[2,48,256]{2,1,0:T(8,128)S(1)}, f32[2,48,256]{2,1,0:T(8,128)S(1)}, u32[]{:S(2)}, u32[]{:S(2)}) %collective-permute-start.8) | collective-permute-done | bytes 98336 | tf_op jit(solution)/shard_map/ppermute | solution.py:140
  86.4 4.1 %collective-permute-done.9 = f32[2,48,256]{2,1,0:T(8,128)S(1)} collective-permute-done((f32[2,48,256]{2,1,0:T(8,128)S(1)}, f32[2,48,256]{2,1,0:T(8,128)S(1)}, u32[]{:S(2)}, u32[]{:S(2)}) %collective-permute-start.9) | collective-permute-done | bytes 98336 | tf_op jit(solution)/shard_map/ppermute | solution.py:140
  90.5 1.9 %correlate.10 = (f32[2,32,256]{2,1,0:T(8,128)S(1)}, bf16[2,32,7680]{2,1,0:T(8,128)(2,1)S(1)}, bf16[2,32,2560]{2,1,0:T(8,128)(2,1)S(1)}) custom-call(bf16[10240,512]{1,0:T(8,128)(2,1)S(1)} %place.1.placed_ref, bf16[2,32,10240]{2,1,0:T(8,128)(2,1)S(1)} %collective-permute-done.4.block_ref, ...), custom_call_target="tpu_custom_call", output_to_operand_aliasing={{1}: (3, {}), {2}: (4, {})} | custom-call | bytes 1024 | tf_op jit(solution)/shard_map/correlate/pallas_call | solution.py:120
  93.0 2.5 %collective-permute-start.11 = (f32[2,32,256]{2,1,0:T(8,128)S(1)}, f32[2,32,256]{2,1,0:T(8,128)S(1)}, u32[]{:S(2)}, u32[]{:S(2)}) collective-permute-start(f32[2,32,256]{2,1,0:T(8,128)S(1)} %get-tuple-element.18), channel_id=1, source_target_pairs={{0,2},{1,3},{2,0},{3,1},{4,6},{5,7},{6,4},{7,5},{8,10},{9,11},{10,... | collective-permute-start | bytes 196616 | tf_op jit(solution)/shard_map/ppermute | solution.py:140
  95.6 3.7 %collective-permute-done.11 = f32[2,32,256]{2,1,0:T(8,128)S(1)} collective-permute-done((f32[2,32,256]{2,1,0:T(8,128)S(1)}, f32[2,32,256]{2,1,0:T(8,128)S(1)}, u32[]{:S(2)}, u32[]{:S(2)}) %collective-permute-start.11) | collective-permute-done | bytes 65568 | tf_op jit(solution)/shard_map/ppermute | solution.py:140
  99.6 4.0 %collective-permute-done.12 = f32[2,32,256]{2,1,0:T(8,128)S(1)} collective-permute-done((f32[2,32,256]{2,1,0:T(8,128)S(1)}, f32[2,32,256]{2,1,0:T(8,128)S(1)}, u32[]{:S(2)}, u32[]{:S(2)}) %collective-permute-start.12) | collective-permute-done | bytes 65568 | tf_op jit(solution)/shard_map/ppermute | solution.py:140
  103.7 1.9 %correlate.11 = f32[2,32,256]{2,1,0:T(8,128)S(1)} custom-call(bf16[10240,512]{1,0:T(8,128)(2,1)S(1)} %place.1.placed_ref, bf16[2,32,10240]{2,1,0:T(8,128)(2,1)S(1)} %collective-permute-done.13.block_ref, f32[2,32,256]{2,1,0:T(8,128)S(1)} %get-tuple-element.24.refs_0_), custom_call_target="tpu_custom_call" | custom-call | bytes 1024 | tf_op jit(solution)/shard_map/correlate/pallas_call | solution.py:120
  105.6 1.9 %collective-permute-start.14 = (f32[2,32,256]{2,1,0:T(8,128)S(1)}, f32[2,32,256]{2,1,0:T(8,128)S(1)}, u32[]{:S(2)}, u32[]{:S(2)}) collective-permute-start(f32[2,32,256]{2,1,0:T(8,128)S(1)} %correlate.11), channel_id=1, source_target_pairs={{0,2},{1,3},{2,0},{3,1},{4,6},{5,7},{6,4},{7,5},{8,10},{9,11},{10,... | collective-permute-start | bytes 196616 | tf_op jit(solution)/shard_map/ppermute | solution.py:140
  107.5 4.7 %collective-permute-done.14 = f32[2,32,256]{2,1,0:T(8,128)S(1)} collective-permute-done((f32[2,32,256]{2,1,0:T(8,128)S(1)}, f32[2,32,256]{2,1,0:T(8,128)S(1)}, u32[]{:S(2)}, u32[]{:S(2)}) %collective-permute-start.14) | collective-permute-done | bytes 65568 | tf_op jit(solution)/shard_map/ppermute | solution.py:140
  113.4 3.1 %collective-permute-done.15 = f32[2,32,256]{2,1,0:T(8,128)S(1)} collective-permute-done((f32[2,32,256]{2,1,0:T(8,128)S(1)}, f32[2,32,256]{2,1,0:T(8,128)S(1)}, u32[]{:S(2)}, u32[]{:S(2)}) %collective-permute-start.15) | collective-permute-done | bytes 65568 | tf_op jit(solution)/shard_map/ppermute | solution.py:140
  116.6 1.5 %correlate.12 = (f32[2,32,256]{2,1,0:T(8,128)S(1)}, f32[2,224,256]{2,1,0:T(8,128)S(1)}) custom-call(bf16[10240,512]{1,0:T(8,128)(2,1)S(1)} %place.1.placed_ref, bf16[2,32,7680]{2,1,0:T(8,128)(2,1)S(1)} %collective-permute-done.10.block_ref, f32[2,224,256]{2,1,0:T(8,128)S(1)} %add_dynamic-update-slice_fusion.refs_0_), custom_call_target="tpu_custom_call", output_to_operand_aliasing={{1}: (2, {})} | custom-call | bytes 1024 | tf_op jit(solution)/shard_map/correlate/pallas_call | solution.py:120
  118.7 3.3 %collective-permute-start.18 = (f32[2,32,256]{2,1,0:T(8,128)S(1)}, f32[2,32,256]{2,1,0:T(8,128)S(1)}, u32[]{:S(2)}, u32[]{:S(2)}) collective-permute-start(f32[2,32,256]{2,1,0:T(8,128)S(1)} %correlate.13), channel_id=1, source_target_pairs={{0,2},{1,3},{2,0},{3,1},{4,6},{5,7},{6,4},{7,5},{8,10},{9,11},{10,... | collective-permute-start | bytes 196616 | tf_op jit(solution)/shard_map/ppermute | solution.py:152
  122.0 4.1 %collective-permute-done.18 = f32[2,32,256]{2,1,0:T(8,128)S(1)} collective-permute-done((f32[2,32,256]{2,1,0:T(8,128)S(1)}, f32[2,32,256]{2,1,0:T(8,128)S(1)}, u32[]{:S(2)}, u32[]{:S(2)}) %collective-permute-start.18) | collective-permute-done | bytes 65568 | tf_op jit(solution)/shard_map/ppermute | solution.py:152
  128.6 2.8 %collective-permute-done.21.refs_5_ = f32[2,32,256]{2,1,0:T(8,128)S(1)} collective-permute-done((f32[2,32,256]{2,1,0:T(8,128)S(1)}, f32[2,32,256]{2,1,0:T(8,128)S(1)}, u32[]{:S(2)}, u32[]{:S(2)}) %collective-permute-start.21) | collective-permute-done | bytes 65568 | tf_op jit(solution)/shard_map/ppermute | solution.py:156
  (41 shorter events, 15.0 us)
Async XLA Ops:
  1.1 21.2 %collective-permute-start.1 = (bf16[2,16,10240]{2,1,0:T(8,128)(2,1)S(1)}, bf16[2,16,10240]{2,1,0:T(8,128)(2,1)S(1)}, u32[]{:S(2)}, u32[]{:S(2)}) collective-permute-start(bf16[2,16,10240]{2,1,0:T(8,128)(2,1)S(1)} %cut.7.refs_1_), channel_id=1, source_target_pairs={{0,12},{4,0},{8,4},{12,8},{1,13},{5,1},{9,5},{13,9},{2,14},{6,2},{... | collective-permute-start | bytes 1966088 | tf_op jit(solution)/shard_map/ppermute | solution.py:20
  5.7 48.1 %collective-permute-start = (bf16[2,96,10240]{2,1,0:T(8,128)(2,1)S(1)}, bf16[2,96,10240]{2,1,0:T(8,128)(2,1)S(1)}, u32[]{:S(2)}, u32[]{:S(2)}) collective-permute-start(bf16[2,96,10240]{2,1,0:T(8,128)(2,1)S(1)} %cut.8.refs_1_), channel_id=1, source_target_pairs={{0,12},{4,0},{8,4},{12,8},{1,13},{5,1},{9,5},{13,9},{2,14},{6,2},{... | collective-permute-start | bytes 11796488 | tf_op jit(solution)/shard_map/ppermute | solution.py:20
  7.9 67.8 %collective-permute-start.5 = (bf16[2,48,10240]{2,1,0:T(8,128)(2,1)S(1)}, bf16[2,48,10240]{2,1,0:T(8,128)(2,1)S(1)}, u32[]{:S(2)}, u32[]{:S(2)}) collective-permute-start(bf16[2,48,10240]{2,1,0:T(8,128)(2,1)S(1)} %cut.9.refs_1_), channel_id=1, source_target_pairs={{0,12},{4,0},{8,4},{12,8},{1,13},{5,1},{9,5},{13,9},{2,14},{6,2},{... | collective-permute-start | bytes 5898248 | tf_op jit(solution)/shard_map/ppermute | solution.py:20
  11.8 1.1 copy-start
  24.1 4.8 %collective-permute-start.2 = (f32[2,16,256]{2,1,0:T(8,128)S(1)}, f32[2,16,256]{2,1,0:T(8,128)S(1)}, u32[]{:S(2)}, u32[]{:S(2)}) collective-permute-start(f32[2,16,256]{2,1,0:T(8,128)S(1)} %correlate.7), channel_id=1, source_target_pairs={{0,2},{1,3},{2,0},{3,1},{4,6},{5,7},{6,4},{7,5},{8,10},{9,11},{10,... | collective-permute-start | bytes 98312 | tf_op jit(solution)/shard_map/ppermute | solution.py:140
  29.0 3.9 %collective-permute-start.3 = (f32[2,16,256]{2,1,0:T(8,128)S(1)}, f32[2,16,256]{2,1,0:T(8,128)S(1)}, u32[]{:S(2)}, u32[]{:S(2)}) collective-permute-start(f32[2,16,256]{2,1,0:T(8,128)S(1)} %add.33), channel_id=1, source_target_pairs={{0,1},{1,0},{2,3},{3,2},{4,5},{5,4},{6,7},{7,6},{8,9},{9,8},{10,11... | collective-permute-start | bytes 98312 | tf_op jit(solution)/shard_map/ppermute | solution.py:140
  56.0 12.8 %collective-permute-start.6 = (f32[2,96,256]{2,1,0:T(8,128)S(1)}, f32[2,96,256]{2,1,0:T(8,128)S(1)}, u32[]{:S(2)}, u32[]{:S(2)}) collective-permute-start(f32[2,96,256]{2,1,0:T(8,128)S(1)} %get-tuple-element.15), channel_id=1, source_target_pairs={{0,2},{1,3},{2,0},{3,1},{4,6},{5,7},{6,4},{7,5},{8,10},{9,11},{10,... | collective-permute-start | bytes 589832 | tf_op jit(solution)/shard_map/ppermute | solution.py:140
  58.6 31.9 %collective-permute-start.4 = (bf16[2,32,10240]{2,1,0:T(8,128)(2,1)S(1)}, bf16[2,32,10240]{2,1,0:T(8,128)(2,1)S(1)}, u32[]{:S(2)}, u32[]{:S(2)}) collective-permute-start(bf16[2,32,10240]{2,1,0:T(8,128)(2,1)S(1)} %get-tuple-element.14), channel_id=1, source_target_pairs={{0,12},{4,0},{8,4},{12,8},{1,13},{5,1},{9,5},{13,9},{2,14},{6,2},{... | collective-permute-start | bytes 3932168 | tf_op jit(solution)/shard_map/ppermute | solution.py:20
  68.8 6.9 %collective-permute-start.7 = (f32[2,96,256]{2,1,0:T(8,128)S(1)}, f32[2,96,256]{2,1,0:T(8,128)S(1)}, u32[]{:S(2)}, u32[]{:S(2)}) collective-permute-start(f32[2,96,256]{2,1,0:T(8,128)S(1)} %add.35), channel_id=1, source_target_pairs={{0,1},{1,0},{2,3},{3,2},{4,5},{5,4},{6,7},{7,6},{8,9},{9,8},{10,11... | collective-permute-start | bytes 589832 | tf_op jit(solution)/shard_map/ppermute | solution.py:140
  77.5 26.1 %collective-permute-start.13 = (bf16[2,32,10240]{2,1,0:T(8,128)(2,1)S(1)}, bf16[2,32,10240]{2,1,0:T(8,128)(2,1)S(1)}, u32[]{:S(2)}, u32[]{:S(2)}) collective-permute-start(bf16[2,32,10240]{2,1,0:T(8,128)(2,1)S(1)} %get-tuple-element.19), channel_id=1, source_target_pairs={{0,12},{4,0},{8,4},{12,8},{1,13},{5,1},{9,5},{13,9},{2,14},{6,2},{... | collective-permute-start | bytes 3932168 | tf_op jit(solution)/shard_map/ppermute | solution.py:20
  78.6 7.2 %collective-permute-start.8 = (f32[2,48,256]{2,1,0:T(8,128)S(1)}, f32[2,48,256]{2,1,0:T(8,128)S(1)}, u32[]{:S(2)}, u32[]{:S(2)}) collective-permute-start(f32[2,48,256]{2,1,0:T(8,128)S(1)} %get-tuple-element.16), channel_id=1, source_target_pairs={{0,2},{1,3},{2,0},{3,1},{4,6},{5,7},{6,4},{7,5},{8,10},{9,11},{10,... | collective-permute-start | bytes 294920 | tf_op jit(solution)/shard_map/ppermute | solution.py:140
  85.8 4.7 %collective-permute-start.9 = (f32[2,48,256]{2,1,0:T(8,128)S(1)}, f32[2,48,256]{2,1,0:T(8,128)S(1)}, u32[]{:S(2)}, u32[]{:S(2)}) collective-permute-start(f32[2,48,256]{2,1,0:T(8,128)S(1)} %add.37), channel_id=1, source_target_pairs={{0,1},{1,0},{2,3},{3,2},{4,5},{5,4},{6,7},{7,6},{8,9},{9,8},{10,11... | collective-permute-start | bytes 294920 | tf_op jit(solution)/shard_map/ppermute | solution.py:140
  92.4 24.1 %collective-permute-start.10 = (bf16[2,32,7680]{2,1,0:T(8,128)(2,1)S(1)}, bf16[2,32,7680]{2,1,0:T(8,128)(2,1)S(1)}, u32[]{:S(2)}, u32[]{:S(2)}) collective-permute-start(bf16[2,32,7680]{2,1,0:T(8,128)(2,1)S(1)} %get-tuple-element.17), channel_id=1, source_target_pairs={{0,12},{4,0},{8,4},{12,8},{1,13},{5,1},{9,5},{13,9},{2,14},{6,2},{... | collective-permute-start | bytes 2949128 | tf_op jit(solution)/shard_map/ppermute | solution.py:20
  93.0 6.3 %collective-permute-start.11 = (f32[2,32,256]{2,1,0:T(8,128)S(1)}, f32[2,32,256]{2,1,0:T(8,128)S(1)}, u32[]{:S(2)}, u32[]{:S(2)}) collective-permute-start(f32[2,32,256]{2,1,0:T(8,128)S(1)} %get-tuple-element.18), channel_id=1, source_target_pairs={{0,2},{1,3},{2,0},{3,1},{4,6},{5,7},{6,4},{7,5},{8,10},{9,11},{10,... | collective-permute-start | bytes 196616 | tf_op jit(solution)/shard_map/ppermute | solution.py:140
  99.3 4.3 %collective-permute-start.12 = (f32[2,32,256]{2,1,0:T(8,128)S(1)}, f32[2,32,256]{2,1,0:T(8,128)S(1)}, u32[]{:S(2)}, u32[]{:S(2)}) collective-permute-start(f32[2,32,256]{2,1,0:T(8,128)S(1)} %add.39), channel_id=1, source_target_pairs={{0,1},{1,0},{2,3},{3,2},{4,5},{5,4},{6,7},{7,6},{8,9},{9,8},{10,11... | collective-permute-start | bytes 196616 | tf_op jit(solution)/shard_map/ppermute | solution.py:140
  105.6 6.6 %collective-permute-start.14 = (f32[2,32,256]{2,1,0:T(8,128)S(1)}, f32[2,32,256]{2,1,0:T(8,128)S(1)}, u32[]{:S(2)}, u32[]{:S(2)}) collective-permute-start(f32[2,32,256]{2,1,0:T(8,128)S(1)} %correlate.11), channel_id=1, source_target_pairs={{0,2},{1,3},{2,0},{3,1},{4,6},{5,7},{6,4},{7,5},{8,10},{9,11},{10,... | collective-permute-start | bytes 196616 | tf_op jit(solution)/shard_map/ppermute | solution.py:140
  112.2 4.3 %collective-permute-start.15 = (f32[2,32,256]{2,1,0:T(8,128)S(1)}, f32[2,32,256]{2,1,0:T(8,128)S(1)}, u32[]{:S(2)}, u32[]{:S(2)}) collective-permute-start(f32[2,32,256]{2,1,0:T(8,128)S(1)} %add.41), channel_id=1, source_target_pairs={{0,1},{1,0},{2,3},{3,2},{4,5},{5,4},{6,7},{7,6},{8,9},{9,8},{10,11... | collective-permute-start | bytes 196616 | tf_op jit(solution)/shard_map/ppermute | solution.py:140
  112.8 5.3 %collective-permute-start.17 = (bf16[2,32,2560]{2,1,0:T(8,128)(2,1)S(1)}, bf16[2,32,2560]{2,1,0:T(8,128)(2,1)S(1)}, u32[]{:S(2)}, u32[]{:S(2)}) collective-permute-start(bf16[2,32,2560]{2,1,0:T(8,128)(2,1)S(1)} %get-tuple-element.21), channel_id=1, source_target_pairs={{0,12},{4,0},{8,4},{12,8},{1,13},{5,1},{9,5},{13,9},{2,14},{6,2},{... | collective-permute-start | bytes 983048 | tf_op jit(solution)/shard_map/ppermute | solution.py:20
  118.1 14.2 %collective-permute-start.16 = (f32[2,224,256]{2,1,0:T(8,128)S(1)}, f32[2,224,256]{2,1,0:T(8,128)S(1)}, u32[]{:S(2)}, u32[]{:S(2)}) collective-permute-start(f32[2,224,256]{2,1,0:T(8,128)S(1)} %get-tuple-element.20.refs_0_), channel_id=1, source_target_pairs={{0,4},{4,8},{8,12},{12,0},{1,5},{5,9},{9,13},{13,1},{2,6},{6,10},{... | collective-permute-start | bytes 1376264 | tf_op jit(solution)/shard_map/ppermute | solution.py:20
  118.7 7.4 %collective-permute-start.18 = (f32[2,32,256]{2,1,0:T(8,128)S(1)}, f32[2,32,256]{2,1,0:T(8,128)S(1)}, u32[]{:S(2)}, u32[]{:S(2)}) collective-permute-start(f32[2,32,256]{2,1,0:T(8,128)S(1)} %correlate.13), channel_id=1, source_target_pairs={{0,2},{1,3},{2,0},{3,1},{4,6},{5,7},{6,4},{7,5},{8,10},{9,11},{10,... | collective-permute-start | bytes 196616 | tf_op jit(solution)/shard_map/ppermute | solution.py:152
  126.1 5.3 %collective-permute-start.21 = (f32[2,32,256]{2,1,0:T(8,128)S(1)}, f32[2,32,256]{2,1,0:T(8,128)S(1)}, u32[]{:S(2)}, u32[]{:S(2)}) collective-permute-start(f32[2,32,256]{2,1,0:T(8,128)S(1)} %add.43.refs_2_), channel_id=1, source_target_pairs={{0,5},{1,4},{2,7},{3,6},{4,9},{5,8},{6,11},{7,10},{8,13},{9,12},{1... | collective-permute-start | bytes 196616 | tf_op jit(solution)/shard_map/ppermute | solution.py:156
  126.3 5.1 %collective-permute-start.20 = (f32[2,32,256]{2,1,0:T(8,128)S(1)}, f32[2,32,256]{2,1,0:T(8,128)S(1)}, u32[]{:S(2)}, u32[]{:S(2)}) collective-permute-start(f32[2,32,256]{2,1,0:T(8,128)S(1)} %add.43.refs_2_), channel_id=1, source_target_pairs={{0,4},{4,8},{8,12},{12,0},{1,5},{5,9},{9,13},{13,1},{2,6},{6,10},{... | collective-permute-start | bytes 196616 | tf_op jit(solution)/shard_map/ppermute | solution.py:20
  127.3 4.9 %collective-permute-start.19 = (f32[2,32,256]{2,1,0:T(8,128)S(1)}, f32[2,32,256]{2,1,0:T(8,128)S(1)}, u32[]{:S(2)}, u32[]{:S(2)}) collective-permute-start(f32[2,32,256]{2,1,0:T(8,128)S(1)} %add.43.refs_2_), channel_id=1, source_target_pairs={{0,1},{1,0},{2,3},{3,2},{4,5},{5,4},{6,7},{7,6},{8,9},{9,8},{10,11... | collective-permute-start | bytes 196616 | tf_op jit(solution)/shard_map/ppermute | solution.py:154
